TPU v7x, 256 devices: a whole 4x4x8 slice. The times are simulated.
256 devices in a mesh: rep: 2 (over x_lo), row: 8 (over y, core), col: 16 (over x_hi, z).
Axes of the slice: x: 4 (x_hi: 2, x_lo: 2; x = x_hi * 2 + x_lo), y: 4, z: 8, core: 2. Of those that a mesh axis runs over, the one named last changes fastest.
Arguments:
- pre_act: bfloat16 [2048, 24576], P(('rep', 'row'), 'col'), may hold values from -8 to 8
- out_grad: bfloat16 [2048, 12288], P(('rep', 'col'), 'row'), may hold values from -1.25 to 1.25
- down_weight: bfloat16 [12288, 24576], P('row', 'col'), may hold values from -0.0546875 to 0.0546875
Outputs:
- pre_grad: bfloat16 [2048, 24576], P(('rep', 'row'), 'col')
- weight_grad: bfloat16 [12288, 24576], P('row', 'col')
All inputs are finite; a program needn't handle non-finite values.
Results may differ from a plain program's by a relative error of at most 0.0048.
Values may be sent and summed in bfloat16 or wider, within the bound.
No kernel may reach another device: no remote copies, remote signals or barrier semaphores. Data moves between devices by JAX's collectives and lax.ppermute only.
A program may use at most 128 MiB of HBM per device.

v0:
```python
import jax
import jax.numpy as jnp
from jax import lax
from jax.sharding import PartitionSpec as P

root_coef = 0.7978845608
cube_coef = 0.044715


def gelu_tanh(value):
    inner = jnp.tanh(root_coef * (value + cube_coef * value * value * value))
    return 0.5 * value * (1.0 + inner)


def gelu_slope(value):
    inner = jnp.tanh(root_coef * (value + cube_coef * value * value * value))
    return 0.5 * (1.0 + inner) + 0.5 * value * (1.0 - inner * inner) * root_coef * (
        1.0 + 3.0 * cube_coef * value * value
    )


def make_folder(grad_rows, shard_rows):
    return lax.dot_general(
        grad_rows, shard_rows, (((0,), (0,)), ((), ())), preferred_element_type=jnp.float32
    )


def per_device(pre_act, out_grad, down_weight):
    pre_wide = pre_act.astype(jnp.float32)
    activation = gelu_tanh(pre_wide).astype(jnp.bfloat16)
    grads_all = lax.all_gather(out_grad, ("rep", "col"), axis=0, tiled=True)
    replica_rows = grads_all.shape[0] // lax.axis_size("rep")
    grads_replica = lax.dynamic_slice_in_dim(
        grads_all, lax.axis_index("rep") * replica_rows, replica_rows, 0
    )
    weight_sum = make_folder(
        grads_all, lax.all_gather(activation, ("rep", "row"), axis=0, tiled=True)
    )
    weight_grad = weight_sum.astype(jnp.bfloat16)
    grad_act = lax.psum_scatter(
        jnp.dot(grads_replica, down_weight, preferred_element_type=jnp.float32),
        "row",
        scatter_dimension=0,
        tiled=True,
    )
    pre_grad = (grad_act * gelu_slope(pre_wide)).astype(jnp.bfloat16)
    return (pre_grad, weight_grad)


def solution(mesh):
    placed = (P(("rep", "row"), "col"), P(("rep", "col"), "row"), P("row", "col"))
    return jax.shard_map(
        per_device,
        mesh=mesh,
        in_specs=placed,
        out_specs=(P(("rep", "row"), "col"), P("row", "col")),
        check_vma=False,
    )
```

profile of v0, /device:TPU:1, one launch (start us, length us, event | category | flops | bytes accessed | tf_op | source)
XLA Modules:
  0.0 299.4 jit_solution(1819823331620041493)
XLA Ops:
  7.2 0.0 all-gather.3.cloned.1.call-start
  7.2 0.7 all-gather.3.cloned.1.call-update
  7.9 0.0 reduce-scatter.2.cloned.1.call-start
  7.9 140.3 %all-gather.3.cloned.1.call-done = bf16[2048,1536]{1,0:T(8,128)(2,1)} async-done(((bf16[64,1536]{1,0:T(8,128)(2,1)}), bf16[2048,1536]{1,0:T(8,128)(2,1)}) %all-gather.3.cloned.1.call-update) | async-done | bytes 6291472 | tf_op jit(solution)/shard_map/all_gather | solution.py:31
  148.2 9.7 %fusion.1 = f32[1024,1536]{1,0:T(8,128)} fusion(bf16[1536,1536]{1,0:T(8,128)(2,1)} %param.5, bf16[2048,1536]{1,0:T(8,128)(2,1)} %all-gather.3.cloned.1.call-done, s32[]{:T(128)S(6)} %select_n.3), kind=kOutput, calls=%fused_computation.2 | convolution fusion | flops 4831838208 | bytes 14155780 | tf_op jit(solution)/shard_map/dot_general | solution.py:41
  157.9 0.0 copy-start
  157.9 0.0 reduce-scatter.2.cloned.1.call-update
  157.9 0.0 all-gather.5.cloned.1.call-start
  158.0 64.5 %reduce-scatter.2.cloned.1.call-done = f32[128,1536]{1,0:T(8,128)} async-done(((f32[1024,1536]{1,0:T(8,128)}), f32[128,1536]{1,0:T(8,128)}) %reduce-scatter.2.cloned.1.call-update) | async-done | bytes 786448 | tf_op jit(solution)/shard_map/reduce_scatter | solution.py:40
  222.5 0.0 copy-done
  222.5 2.6 fusion.10
  225.1 0.0 all-gather.5.cloned.1.call-update
  225.1 45.7 %all-gather.5.cloned.1.call-done = bf16[2048,1536]{1,0:T(8,128)(2,1)} async-done(((bf16[128,1536]{1,0:T(8,128)(2,1)}), bf16[2048,1536]{1,0:T(8,128)(2,1)}) %all-gather.5.cloned.1.call-update) | async-done | bytes 6291472 | tf_op jit(solution)/shard_map/all_gather | solution.py:37
  270.8 15.5 %fusion = bf16[1536,1536]{0,1:T(8,128)(2,1)} fusion(bf16[2048,1536]{1,0:T(8,128)(2,1)} %all-gather.5.cloned.1.call-done, bf16[2048,1536]{1,0:T(8,128)(2,1)} %all-gather.3.cloned.1.call-done), kind=kOutput, calls=%fused_computation.1 | convolution fusion | flops 9666035712 | bytes 17301504 | tf_op jit(solution)/shard_map/dot_general | solution.py:23
  286.3 6.6 %copy.5 = bf16[1536,1536]{1,0:T(8,128)(2,1)} copy(bf16[1536,1536]{0,1:T(8,128)(2,1)} %fusion) | data formatting | bytes 9437184
Async XLA Ops:
  7.2 141.1 %all-gather.3.cloned.1.call-start = ((), (), s32[]{:S(2)}) async-start(), calls=%async_computation.1 | async-start | bytes 6488064 | tf_op jit(solution)/shard_map/all_gather | solution.py:31
  7.9 214.6 %reduce-scatter.2.cloned.1.call-start = ((), (), s32[]{:S(2)}) async-start(), calls=%async_computation.2 | async-start | bytes 7077888 | tf_op jit(solution)/shard_map/reduce_scatter | solution.py:40
  157.9 64.6 %copy-start = (bf16[128,1536]{1,0:T(8,128)(2,1)S(1)}, bf16[128,1536]{1,0:T(8,128)(2,1)}, u32[]{:S(2)}) copy-start(bf16[128,1536]{1,0:T(8,128)(2,1)} %param.3) | copy-start | bytes 1179652
  157.9 112.9 %all-gather.5.cloned.1.call-start = ((), (), s32[]{:S(2)}) async-start(), calls=%async_computation.3 | async-start | bytes 6684672 | tf_op jit(solution)/shard_map/all_gather | solution.py:37
Sparse Core Ops, SparseCore 0:
  9.8 138.3 all-gather.2
  158.1 64.4 reduce-scatter.1
  225.2 45.5 all-gather.4
where the time goes:
time: 300 us; the launch traced here: 299 us
  waiting for transfers between devices  251 us (84%)
  matrix products  25.2 us (8%)
  between operations  13.7 us (5%)
  local copies, waits for them, and re-layouts  6.61 us (2%)
    all_gather x1, waiting for transfers between devices, per_device(): grads_all = lax.all_gather(out_grad, ('rep', 'col'), axis=0, tiled=True)  140 us
    reduce_scatter x1, waiting for transfers between devices, per_device(): lax.psum_scatter(jnp.dot(grads_replica, down_weight, preferred_element_ty...  64.5 us
    all_gather x1, waiting for transfers between devices, per_device(): lax.all_gather(activation, ('rep', 'row'), axis=0, tiled=True)  45.7 us
    dot_general x1, matrix products, make_folder(): lax.dot_general(grad_rows, shard_rows, (((0,), (0,)), ((), ())), preferre...  15.5 us
    dot_general x1, matrix products, per_device(): jnp.dot(grads_replica, down_weight, preferred_element_type=jnp.float32)  9.68 us
    unnamed x3, local copies, waits for them, and re-layouts  6.61 us
  transfers between devices with their start and end apart: 3, of which 3 were waited for; matrix products, arithmetic and copies ran while one was open for 0% of the time, Pallas kernels for 0%

commit v1 on v0

v1 whole, which is shorter than its diff:
```python
import jax
import jax.numpy as jnp
from jax import lax
from jax.experimental import pallas as pl
from jax.experimental.pallas import tpu as pltpu
from jax.sharding import Mesh, PartitionSpec as P

root_coef = 0.7978845608
cube_coef = 0.044715

XL, Y, C, XH, Z = 2, 4, 2, 2, 8
AXES = ("xl", "y", "c", "xh", "z")
HALF = 32
BF, F32 = jnp.bfloat16, jnp.float32
ANY = pl.BlockSpec(memory_space=pl.ANY)


def gelu_tanh(value):
    inner = jnp.tanh(root_coef * (value + cube_coef * value * value * value))
    return 0.5 * value * (1.0 + inner)


def gelu_slope(value):
    inner = jnp.tanh(root_coef * (value + cube_coef * value * value * value))
    return 0.5 * (1.0 + inner) + 0.5 * value * (1.0 - inner * inner) * root_coef * (
        1.0 + 3.0 * cube_coef * value * value
    )


def along_z(a, d):
    return lax.ppermute(a, "z", [(i, (i + d) % Z) for i in range(Z)])


def along_x(a, d):
    def place(x):
        return (x % 2) * XH + x // 2

    return lax.ppermute(a, ("xl", "xh"), [(place(x), place((x + d) % 4)) for x in range(4)])


def along_y(a, d):
    return lax.ppermute(a, "y", [(i, (i + d) % Y) for i in range(Y)])


def round_y(a):
    pairs = [((y, c), ((y + (1 if c == 0 else -1)) % Y, c)) for y in range(Y) for c in range(C)]
    return lax.ppermute(a, ("y", "c"), [(s[0] * C + s[1], t[0] * C + t[1]) for s, t in pairs])


def swap(a, axis):
    return lax.ppermute(a, axis, [(0, 1), (1, 0)])


def rows(offset, count):
    return pl.ds(pl.multiple_of(offset, count), count)


def place_all(moves, whole, sem):
    for source, target in moves:
        pltpu.make_async_copy(source, target, sem).start()
    for source, target in moves:
        pltpu.make_async_copy(source, target, sem).wait()


def grad_moves(ring, cols, relay_a, relay_b, spot, replicas):
    z = lax.axis_index("z")
    moves = []
    for j in range(8):
        zp = lax.rem(z + 8 - j, 8)
        ref = ring[j]
        order = (0, 2, 3, 1) if replicas else (0, 2)
        first, second = ref if isinstance(ref, tuple) else (ref, None)
        sources = [first.at[pl.ds(0, 32)], first.at[pl.ds(32, 32)]]
        if replicas and second is not None:
            sources += [second.at[pl.ds(0, 32)], second.at[pl.ds(32, 32)]]
        elif replicas:
            sources += [first.at[pl.ds(64, 32)], first.at[pl.ds(96, 32)]]
        for k, dx in enumerate(order):
            moves.append((sources[k], spot(dx, zp, 0)))
        for dx, ref in cols:
            moves.append((ref.at[pl.ds(32 * j, 32)], spot(dx, zp, 1)))
        ref = relay_a if j < 4 else relay_b
        moves.append((ref.at[pl.ds(32 * (j % 4), 32)], spot(2, zp, 1)))
    return moves


def partial_kernel(*refs):
    ring = list(refs[:8])
    col, relay_a, relay_b, w_ref, mine_ref, other_ref, held, sem = refs[8:]
    y, c, xh = lax.axis_index("y"), lax.axis_index("c"), lax.axis_index("xh")

    def spot(dx, zp, half):
        xp = xh if dx == 0 else 1 - xh
        yp, cp = 2 * xp + zp // 4, lax.rem(zp // 2, 2)
        away = lax.rem(cp + c, 2)
        return held.at[rows(away * 512 + lax.rem(yp + 4 - y, 4) * 128 + lax.rem(zp, 2) * 64 + half * 32, 32)]

    @pl.when(pl.program_id(0) == 0)
    def _():
        place_all(grad_moves(ring, [(0, col)], relay_a, relay_b, spot, False), held, sem)

    other_ref[...] = jnp.dot(held[512:, :], w_ref[...], preferred_element_type=F32).astype(BF)
    mine_ref[...] = jnp.dot(held[:512, :], w_ref[...], preferred_element_type=F32)


def partial_grad(ring, col, relay_a, relay_b, weight):
    step = 256
    return pl.pallas_call(
        partial_kernel,
        grid=(1536 // step,),
        in_specs=[ANY] * 11 + [pl.BlockSpec((1536, step), lambda n: (0, n))],
        out_specs=[pl.BlockSpec((512, step), lambda n: (0, n))] * 2,
        out_shape=[jax.ShapeDtypeStruct((512, 1536), F32), jax.ShapeDtypeStruct((512, 1536), BF)],
        scratch_shapes=[pltpu.VMEM((1024, 1536), BF), pltpu.SemaphoreType.DMA],
        compiler_params=pltpu.CompilerParams(vmem_limit_bytes=40 << 20),
        cost_estimate=pl.CostEstimate(flops=2 * 1024 * 1536 * 1536, bytes_accessed=13 << 20, transcendentals=0),
    )(*ring, col, relay_a, relay_b, weight)


def weight_kernel(*refs):
    ring = list(refs[:7]) + [(refs[7], refs[8])]
    ring = ring[:4] + [ring[7]] + ring[4:7]
    col, left, right, relay_a, relay_b, own, swapped = refs[9:16]
    out_ref, grads, acts, sem = refs[16:]
    y, c, xl, xh = (lax.axis_index(a) for a in ("y", "c", "xl", "xh"))
    x = 2 * xh + xl

    def spot(dx, zp, half):
        xp = lax.rem(x + dx, 4)
        return grads.at[rows(lax.rem(xp, 2) * 1024 + (xp // 2) * 512 + zp * 64 + half * 32, 32)]

    def act_spot(other_rep, yp, cp):
        rep = 1 - xl if other_rep else xl
        return acts.at[rows(rep * 1024 + (lax.rem(yp + 4, 4) * 2 + cp) * 128, 128)]

    @pl.when(pl.program_id(0) == 0)
    def _():
        moves = grad_moves(ring, [(0, col), (3, left), (1, right)], relay_a, relay_b, spot, True)
        back = 2 * c - 1
        for ref, owner, ahead in ((own, c, back), (swapped, 1 - c, -back)):
            if ref is own:
                spots = [(0, c), (0, 1 - c), (ahead, c), (ahead, 1 - c), (2, c)]
            else:
                spots = [(ahead, 1 - c), (ahead, c), (2, 1 - c)]
            for k, (dy, cp) in enumerate(spots):
                for other in range(2):
                    moves.append((ref.at[pl.ds(256 * k + 128 * other, 128)], act_spot(other, y + dy, cp)))
        place_all(moves, grads, sem)

    lanes = pl.ds(pl.multiple_of(pl.program_id(0) * 256, 256), 256)
    out_ref[...] = lax.dot_general(
        grads[:, lanes], acts[...], (((0,), (0,)), ((), ())), preferred_element_type=F32
    ).astype(BF)


def weight_gradient(*arrays):
    step = 256
    return pl.pallas_call(
        weight_kernel,
        grid=(1536 // step,),
        in_specs=[ANY] * len(arrays),
        out_specs=pl.BlockSpec((step, 1536), lambda m: (m, 0)),
        out_shape=jax.ShapeDtypeStruct((1536, 1536), BF),
        scratch_shapes=[pltpu.VMEM((2048, 1536), BF), pltpu.VMEM((2048, 1536), BF), pltpu.SemaphoreType.DMA],
        compiler_params=pltpu.CompilerParams(vmem_limit_bytes=48 << 20),
        cost_estimate=pl.CostEstimate(flops=2 * 2048 * 1536 * 1536, bytes_accessed=17 << 20, transcendentals=0),
    )(*arrays)


def per_device(pre_act, out_grad, down_weight):
    pre_wide = pre_act.astype(F32)
    first, second = out_grad[:HALF], out_grad[HALF:]

    activation = gelu_tanh(pre_wide).astype(BF)
    two = jnp.concatenate([activation, swap(activation, "xl")])
    chip = jnp.concatenate([two, swap(two, "c")])
    near = round_y(chip)
    far = round_y(near[:256])
    came = jnp.concatenate([near, far])
    own_acts = jnp.concatenate([chip, came])
    swapped_acts = swap(came, "c")

    x_left, x_right = along_x(first, 1), along_x(first, -1)
    x_far = [along_x(x_left[:16], 1), along_x(x_right[16:], -1)]
    bundle = jnp.concatenate([first, *x_far, x_left, x_right])
    up, down = [bundle], [bundle]
    for _ in range(3):
        up.append(along_z(up[-1], 1))
        down.append(along_z(down[-1], -1))
    opposite = (along_z(up[-1][:64], 1), along_z(down[-1][64:], -1))

    z_up, z_down = [second], [second]
    for _ in range(3):
        z_up.append(along_z(z_up[-1], 1))
        z_down.append(along_z(z_down[-1], -1))
    z_far = [along_z(z_up[-1][:16], 1), along_z(z_down[-1][16:], -1)]
    column = jnp.concatenate([*z_up, *z_far, z_down[3], z_down[2], z_down[1]])
    left, right = along_x(column, 1), along_x(column, -1)
    relay_a, relay_b = along_x(left[:128], 1), along_x(right[128:], -1)

    ring = [up[0], up[1], up[2], up[3], opposite[0], down[3], down[2], down[1]]
    mine, other = partial_grad(ring, column, relay_a, relay_b, down_weight)
    other = swap(other, "c")

    def summed(block):
        return mine[128 * block : 128 * block + 128] + other[128 * block : 128 * block + 128].astype(F32)

    across = summed(2).astype(BF)
    from_below, from_above = along_y(across[:64], 1), along_y(across[64:], -1)
    empty = jnp.zeros((64, 1536), F32)
    upward = (summed(1) + jnp.concatenate([from_below.astype(F32), empty])).astype(BF)
    downward = (summed(3) + jnp.concatenate([empty, from_above.astype(F32)])).astype(BF)
    grad_act = summed(0) + along_y(upward, 1).astype(F32) + along_y(downward, -1).astype(F32)
    pre_grad = (grad_act * gelu_slope(pre_wide)).astype(BF)

    weight_grad = weight_gradient(
        up[0], up[1], up[2], up[3], down[3], down[2], down[1], *opposite,
        column, left, right, relay_a, relay_b, own_acts, swapped_acts,
    )
    return (pre_grad, weight_grad)


def solution(mesh):
    physical = Mesh(mesh.devices.reshape(XL, Y, C, XH, Z), AXES)
    rep, row, col = "xl", ("y", "c"), ("xh", "z")
    return jax.shard_map(
        per_device,
        mesh=physical,
        in_specs=(P((rep, *row), col), P((rep, *col), row), P(row, col)),
        out_specs=(P((rep, *row), col), P(row, col)),
        check_vma=False,
    )
```

time: 300 us -> 189 us (0.63)
  waiting for transfers between devices: 251 us -> 84.6 us
  starting transfers between devices: 0.12 us -> 62.2 us
  Pallas kernels: 0 us -> 35.2 us
  matrix products: 25.2 us -> 0 us
  between operations: 13.7 us -> 1.13 us
  local copies, waits for them, and re-layouts: 6.61 us -> 3.1 us
    all_gather x2 -> x0, waiting for transfers between devices: 186 us -> none  [the longest x1 140 us: per_device(): grads_all = lax.all_gather(out_grad, ('rep', 'col'), axis=0, tiled=True)]
    ppermute x0 -> x34, waiting for transfers between devices: none -> 84.6 us  [the longest x16 29.1 us: along_z(): return lax.ppermute(a, 'z', [(i, (i + d) % Z) for i in range(Z)])]
    reduce_scatter x1 -> x0, waiting for transfers between devices: 64.5 us -> none  [per_device(): lax.psum_scatter(jnp.dot(grads_replica, down_weight, preferred_element_ty...]
    ppermute x0 -> x34, starting transfers between devices: none -> 62.2 us  [the longest x16 23 us: along_z(): return lax.ppermute(a, 'z', [(i, (i + d) % Z) for i in range(Z)])]
    pallas_call x0 -> x2, Pallas kernels: none -> 35.2 us  [the longest x1 23.3 us: weight_gradient(): pl.pallas_call(weight_kernel, grid=(1536 // step,), in_specs=[ANY] * len(...]
    dot_general x2 -> x0, matrix products: 25.2 us -> none  [the longest x1 15.5 us: make_folder(): lax.dot_general(grad_rows, shard_rows, (((0,), (0,)), ((), ())), preferre...]
    unnamed x3 -> x23, local copies, waits for them, and re-layouts: 6.61 us -> 1.74 us
  transfers between devices with their start and end apart: 3 -> 34, of which waited for: 3 -> 15; matrix products, arithmetic and copies ran while one was open for 0% -> 0% of each run, Pallas kernels for 0% -> 0%
where the time goes in v1:
time: 189 us
  waiting for transfers between devices  84.6 us (45%)
  starting transfers between devices  62.2 us (33%)
  Pallas kernels  35.2 us (19%)
  local copies, waits for them, and re-layouts  3.1 us (2%)
  other arithmetic  2.38 us (1%)
    ppermute x16, waiting for transfers between devices, along_z(): return lax.ppermute(a, 'z', [(i, (i + d) % Z) for i in range(Z)])  29.1 us
    ppermute x2, waiting for transfers between devices, round_y(): lax.ppermute(a, ('y', 'c'), [(s[0] * C + s[1], t[0] * C + t[1]) for s, t...  26.3 us
    pallas_call x1, Pallas kernels, weight_gradient(): pl.pallas_call(weight_kernel, grid=(1536 // step,), in_specs=[ANY] * len(...  23.3 us
    ppermute x16, starting transfers between devices, along_z(): return lax.ppermute(a, 'z', [(i, (i + d) % Z) for i in range(Z)])  23 us
    ppermute x4, starting transfers between devices, swap(): return lax.ppermute(a, axis, [(0, 1), (1, 0)])  14.4 us
    ppermute x8, starting transfers between devices, along_x(): lax.ppermute(a, ('xl', 'xh'), [(place(x), place((x + d) % 4)) for x in ra...  13.5 us
    ppermute x4, waiting for transfers between devices, swap(): return lax.ppermute(a, axis, [(0, 1), (1, 0)])  13.4 us
    ppermute x4, waiting for transfers between devices, along_y(): return lax.ppermute(a, 'y', [(i, (i + d) % Y) for i in range(Y)])  12.6 us
  transfers between devices with their start and end apart: 34, of which 15 were waited for; matrix products, arithmetic and copies ran while one was open for 0% of the time, Pallas kernels for 0%

profile of v1, /device:TPU:1, one launch (start us, length us, event | category | flops | bytes accessed | tf_op | source)
XLA Modules:
  0.0 188.5 jit_solution(1105984730587469966)
XLA Ops:
  1.8 3.4 %collective-permute-start.2 = (bf16[32,1536]{1,0:T(8,128)(2,1)S(1)}, bf16[32,1536]{1,0:T(8,128)(2,1)S(1)}, u32[]{:S(2)}, u32[]{:S(2)}) collective-permute-start(bf16[32,1536]{1,0:T(8,128)(2,1)S(1)} %get-tuple-element.15), channel_id=1, source_target_pairs={{0,136},{128,0},{8,128},{136,8},{1,137},{129,1},{9,129},{137,9},{2... | collective-permute-start | bytes 294920 | tf_op jit(solution)/shard_map/ppermute | solution.py:38
  5.2 5.6 %collective-permute-start.15 = (bf16[32,1536]{1,0:T(8,128)(2,1)S(1)}, bf16[32,1536]{1,0:T(8,128)(2,1)S(1)}, u32[]{:S(2)}, u32[]{:S(2)}) collective-permute-start(bf16[32,1536]{1,0:T(8,128)(2,1)S(1)} %get-tuple-element.12), channel_id=1, source_target_pairs={{0,7},{1,0},{2,1},{3,2},{4,3},{5,4},{6,5},{7,6},{8,15},{9,8},{10,9... | collective-permute-start | bytes 294920 | tf_op jit(solution)/shard_map/ppermute | solution.py:31
  10.7 2.8 %collective-permute-start.3 = (bf16[16,1536]{1,0:T(8,128)(2,1)S(1)}, bf16[16,1536]{1,0:T(8,128)(2,1)S(1)}, u32[]{:S(2)}, u32[]{:S(2)}) collective-permute-start(bf16[16,1536]{1,0:T(8,128)(2,1)S(1)} %slice.85), channel_id=1, source_target_pairs={{0,136},{128,0},{8,128},{136,8},{1,137},{129,1},{9,129},{137,9},{2... | collective-permute-start | bytes 147464 | tf_op jit(solution)/shard_map/ppermute | solution.py:38
  13.6 2.7 %collective-permute-start.16 = (bf16[32,1536]{1,0:T(8,128)(2,1)S(1)}, bf16[32,1536]{1,0:T(8,128)(2,1)S(1)}, u32[]{:S(2)}, u32[]{:S(2)}) collective-permute-start(bf16[32,1536]{1,0:T(8,128)(2,1)S(1)} %collective-permute-done.15), channel_id=1, source_target_pairs={{0,7},{1,0},{2,1},{3,2},{4,3},{5,4},{6,5},{7,6},{8,15},{9,8},{10,9... | collective-permute-start | bytes 294920 | tf_op jit(solution)/shard_map/ppermute | solution.py:31
  17.8 2.7 %collective-permute-start.8 = (bf16[128,1536]{1,0:T(8,128)(2,1)S(1)}, bf16[128,1536]{1,0:T(8,128)(2,1)S(1)}, u32[]{:S(2)}, u32[]{:S(2)}) collective-permute-start(bf16[128,1536]{1,0:T(8,128)(2,1)S(1)} %constant_dynamic-update-slice_fusion.refs_0_), channel_id=1, source_target_pairs={{0,7},{1,0},{2,1},{3,2},{4,3},{5,4},{6,5},{7,6},{8,15},{9,8},{10,9... | collective-permute-start | bytes 1179656 | tf_op jit(solution)/shard_map/ppermute | solution.py:31
  20.5 2.7 %collective-permute-start.17 = (bf16[32,1536]{1,0:T(8,128)(2,1)S(1)}, bf16[32,1536]{1,0:T(8,128)(2,1)S(1)}, u32[]{:S(2)}, u32[]{:S(2)}) collective-permute-start(bf16[32,1536]{1,0:T(8,128)(2,1)S(1)} %collective-permute-done.16), channel_id=1, source_target_pairs={{0,7},{1,0},{2,1},{3,2},{4,3},{5,4},{6,5},{7,6},{8,15},{9,8},{10,9... | collective-permute-start | bytes 294920 | tf_op jit(solution)/shard_map/ppermute | solution.py:31
  23.2 4.6 %collective-permute-done.17 = bf16[32,1536]{1,0:T(8,128)(2,1)S(1)} collective-permute-done((bf16[32,1536]{1,0:T(8,128)(2,1)S(1)}, bf16[32,1536]{1,0:T(8,128)(2,1)S(1)}, u32[]{:S(2)}, u32[]{:S(2)}) %collective-permute-start.17) | collective-permute-done | bytes 98336 | tf_op jit(solution)/shard_map/ppermute | solution.py:31
  27.8 3.4 %collective-permute-start.18 = (bf16[16,1536]{1,0:T(8,128)(2,1)S(1)}, bf16[16,1536]{1,0:T(8,128)(2,1)S(1)}, u32[]{:S(2)}, u32[]{:S(2)}) collective-permute-start(bf16[16,1536]{1,0:T(8,128)(2,1)S(1)} %slice.88), channel_id=1, source_target_pairs={{0,7},{1,0},{2,1},{3,2},{4,3},{5,4},{6,5},{7,6},{8,15},{9,8},{10,9... | collective-permute-start | bytes 147464 | tf_op jit(solution)/shard_map/ppermute | solution.py:31
  31.3 4.1 %collective-permute-done.14 = bf16[16,1536]{1,0:T(8,128)(2,1)S(1)} collective-permute-done((bf16[16,1536]{1,0:T(8,128)(2,1)S(1)}, bf16[16,1536]{1,0:T(8,128)(2,1)S(1)}, u32[]{:S(2)}, u32[]{:S(2)}) %collective-permute-start.14) | collective-permute-done | bytes 49184 | tf_op jit(solution)/shard_map/ppermute | solution.py:31
  35.5 3.7 %collective-permute-start.21 = (bf16[256,1536]{1,0:T(8,128)(2,1)S(1)}, bf16[256,1536]{1,0:T(8,128)(2,1)S(1)}, u32[]{:S(2)}, u32[]{:S(2)}) collective-permute-start(bf16[256,1536]{1,0:T(8,128)(2,1)S(1)} %constant_dynamic-update-slice_fusion.5.refs_8_.refs_9_), channel_id=1, source_target_pairs={{0,136},{128,0},{8,128},{136,8},{1,137},{129,1},{9,129},{137,9},{2... | collective-permute-start | bytes 2359304 | tf_op jit(solution)/shard_map/ppermute | solution.py:38
  39.2 2.7 %collective-permute-start.9 = (bf16[128,1536]{1,0:T(8,128)(2,1)S(1)}, bf16[128,1536]{1,0:T(8,128)(2,1)S(1)}, u32[]{:S(2)}, u32[]{:S(2)}) collective-permute-start(bf16[128,1536]{1,0:T(8,128)(2,1)S(1)} %collective-permute-done.8.refs_7_.refs_6_), channel_id=1, source_target_pairs={{0,7},{1,0},{2,1},{3,2},{4,3},{5,4},{6,5},{7,6},{8,15},{9,8},{10,9... | collective-permute-start | bytes 1179656 | tf_op jit(solution)/shard_map/ppermute | solution.py:31
  41.9 5.2 %collective-permute-done.5.refs_2_ = bf16[128,1536]{1,0:T(8,128)(2,1)S(1)} collective-permute-done((bf16[128,1536]{1,0:T(8,128)(2,1)S(1)}, bf16[128,1536]{1,0:T(8,128)(2,1)S(1)}, u32[]{:S(2)}, u32[]{:S(2)}) %collective-permute-start.5) | collective-permute-done | bytes 393248 | tf_op jit(solution)/shard_map/ppermute | solution.py:31
  47.1 3.0 %collective-permute-start.10 = (bf16[128,1536]{1,0:T(8,128)(2,1)S(1)}, bf16[128,1536]{1,0:T(8,128)(2,1)S(1)}, u32[]{:S(2)}, u32[]{:S(2)}) collective-permute-start(bf16[128,1536]{1,0:T(8,128)(2,1)S(1)} %collective-permute-done.9.refs_6_.refs_5_), channel_id=1, source_target_pairs={{0,7},{1,0},{2,1},{3,2},{4,3},{5,4},{6,5},{7,6},{8,15},{9,8},{10,9... | collective-permute-start | bytes 1179656 | tf_op jit(solution)/shard_map/ppermute | solution.py:31
  50.0 1.8 collective-permute-done.21.refs_11_
  51.8 3.5 %collective-permute-start.22 = (bf16[128,1536]{1,0:T(8,128)(2,1)S(1)}, bf16[128,1536]{1,0:T(8,128)(2,1)S(1)}, u32[]{:S(2)}, u32[]{:S(2)}) collective-permute-start(bf16[128,1536]{1,0:T(8,128)(2,1)S(1)} %slice.90), channel_id=1, source_target_pairs={{0,136},{128,0},{8,128},{136,8},{1,137},{129,1},{9,129},{137,9},{2... | collective-permute-start | bytes 1179656 | tf_op jit(solution)/shard_map/ppermute | solution.py:38
  56.7 7.9 %collective-permute-done.7.refs_4_.refs_7_ = bf16[64,1536]{1,0:T(8,128)(2,1)S(1)} collective-permute-done((bf16[64,1536]{1,0:T(8,128)(2,1)S(1)}, bf16[64,1536]{1,0:T(8,128)(2,1)S(1)}, u32[]{:S(2)}, u32[]{:S(2)}) %collective-permute-start.7) | collective-permute-done | bytes 196640 | tf_op jit(solution)/shard_map/ppermute | solution.py:31
  64.6 11.9 %shard_map.50 = (f32[512,1536]{1,0:T(8,128)S(1)}, bf16[512,1536]{1,0:T(8,128)(2,1)S(1)}) custom-call(bf16[128,1536]{1,0:T(8,128)(2,1)S(1)} %constant_dynamic-update-slice_fusion.refs_0_, bf16[128,1536]{1,0:T(8,128)(2,1)S(1)} %collective-permute-done.4.refs_1_, bf16[128,1536]{1,0:T(8,128)(2,1)S(1)} %collective-permute-done.5.refs_2_, ...), custom_call_target="tpu_custom_call" | custom-call | flops 4831838208 | bytes 13631488 | tf_op jit(solution)/shard_map/pallas_call | solution.py:108
  76.5 7.5 %collective-permute-start.23 = (bf16[512,1536]{1,0:T(8,128)(2,1)S(1)}, bf16[512,1536]{1,0:T(8,128)(2,1)S(1)}, u32[]{:S(2)}, u32[]{:S(2)}) collective-permute-start(bf16[512,1536]{1,0:T(8,128)(2,1)S(1)} %get-tuple-element.5), channel_id=1, source_target_pairs={{0,16},{16,0},{1,17},{17,1},{2,18},{18,2},{3,19},{19,3},{4,20},{20... | collective-permute-start | bytes 4718600 | tf_op jit(solution)/shard_map/ppermute | solution.py:51
  84.0 3.0 %collective-permute-done.23 = bf16[512,1536]{1,0:T(8,128)(2,1)S(1)} collective-permute-done((bf16[512,1536]{1,0:T(8,128)(2,1)S(1)}, bf16[512,1536]{1,0:T(8,128)(2,1)S(1)}, u32[]{:S(2)}, u32[]{:S(2)}) %collective-permute-start.23) | collective-permute-done | bytes 1572896 | tf_op jit(solution)/shard_map/ppermute | solution.py:51
  90.0 4.6 %collective-permute-done.24 = bf16[64,1536]{1,0:T(8,128)(2,1)S(1)} collective-permute-done((bf16[64,1536]{1,0:T(8,128)(2,1)S(1)}, bf16[64,1536]{1,0:T(8,128)(2,1)S(1)}, u32[]{:S(2)}, u32[]{:S(2)}) %collective-permute-start.24) | collective-permute-done | bytes 196640 | tf_op jit(solution)/shard_map/ppermute | solution.py:42
  95.9 1.8 collective-permute-start.27
  97.7 8.0 %collective-permute-done.25 = bf16[128,1536]{1,0:T(8,128)(2,1)S(1)} collective-permute-done((bf16[128,1536]{1,0:T(8,128)(2,1)S(1)}, bf16[128,1536]{1,0:T(8,128)(2,1)S(1)}, u32[]{:S(2)}, u32[]{:S(2)}) %collective-permute-start.25) | collective-permute-done | bytes 393248 | tf_op jit(solution)/shard_map/ppermute | solution.py:42
  107.3 8.4 %collective-permute-done.29 = bf16[128,1536]{1,0:T(8,128)(2,1)S(1)} collective-permute-done((bf16[128,1536]{1,0:T(8,128)(2,1)S(1)}, bf16[128,1536]{1,0:T(8,128)(2,1)S(1)}, u32[]{:S(2)}, u32[]{:S(2)}) %collective-permute-start.29) | collective-permute-done | bytes 393248 | tf_op jit(solution)/shard_map/ppermute | solution.py:51
  115.7 3.3 %collective-permute-start.30 = (bf16[256,1536]{1,0:T(8,128)(2,1)S(1)}, bf16[256,1536]{1,0:T(8,128)(2,1)S(1)}, u32[]{:S(2)}, u32[]{:S(2)}) collective-permute-start(bf16[256,1536]{1,0:T(8,128)(2,1)S(1)} %pad_maximum_fusion.2), channel_id=1, source_target_pairs={{0,16},{16,0},{1,17},{17,1},{2,18},{18,2},{3,19},{19,3},{4,20},{20... | collective-permute-start | bytes 2359304 | tf_op jit(solution)/shard_map/ppermute | solution.py:51
  119.0 1.9 %collective-permute-done.30 = bf16[256,1536]{1,0:T(8,128)(2,1)S(1)} collective-permute-done((bf16[256,1536]{1,0:T(8,128)(2,1)S(1)}, bf16[256,1536]{1,0:T(8,128)(2,1)S(1)}, u32[]{:S(2)}, u32[]{:S(2)}) %collective-permute-start.30) | collective-permute-done | bytes 786464 | tf_op jit(solution)/shard_map/ppermute | solution.py:51
  121.0 2.5 %collective-permute-start.31 = (bf16[512,1536]{1,0:T(8,128)(2,1)S(1)}, bf16[512,1536]{1,0:T(8,128)(2,1)S(1)}, u32[]{:S(2)}, u32[]{:S(2)}) collective-permute-start(bf16[512,1536]{1,0:T(8,128)(2,1)S(1)} %pad_maximum_fusion.1), channel_id=1, source_target_pairs={{0,32},{16,112},{32,64},{48,16},{64,96},{80,48},{96,0},{112,80},{1... | collective-permute-start | bytes 4718600 | tf_op jit(solution)/shard_map/ppermute | solution.py:47
  123.5 17.4 %collective-permute-done.31 = bf16[512,1536]{1,0:T(8,128)(2,1)S(1)} collective-permute-done((bf16[512,1536]{1,0:T(8,128)(2,1)S(1)}, bf16[512,1536]{1,0:T(8,128)(2,1)S(1)}, u32[]{:S(2)}, u32[]{:S(2)}) %collective-permute-start.31) | collective-permute-done | bytes 1572896 | tf_op jit(solution)/shard_map/ppermute | solution.py:47
  140.9 3.2 %collective-permute-start.32 = (bf16[256,1536]{1,0:T(8,128)(2,1)S(1)}, bf16[256,1536]{1,0:T(8,128)(2,1)S(1)}, u32[]{:S(2)}, u32[]{:S(2)}) collective-permute-start(bf16[256,1536]{1,0:T(8,128)(2,1)S(1)} %slice.98), channel_id=1, source_target_pairs={{0,32},{16,112},{32,64},{48,16},{64,96},{80,48},{96,0},{112,80},{1... | collective-permute-start | bytes 2359304 | tf_op jit(solution)/shard_map/ppermute | solution.py:47
  144.1 8.9 %collective-permute-done.32 = bf16[256,1536]{1,0:T(8,128)(2,1)S(1)} collective-permute-done((bf16[256,1536]{1,0:T(8,128)(2,1)S(1)}, bf16[256,1536]{1,0:T(8,128)(2,1)S(1)}, u32[]{:S(2)}, u32[]{:S(2)}) %collective-permute-start.32) | collective-permute-done | bytes 786464 | tf_op jit(solution)/shard_map/ppermute | solution.py:47
  153.2 3.5 %collective-permute-start.33 = (bf16[768,1536]{1,0:T(8,128)(2,1)S(1)}, bf16[768,1536]{1,0:T(8,128)(2,1)S(1)}, u32[]{:S(2)}, u32[]{:S(2)}) collective-permute-start(bf16[768,1536]{1,0:T(8,128)(2,1)S(1)} %pad_maximum_fusion), channel_id=1, source_target_pairs={{0,16},{16,0},{1,17},{17,1},{2,18},{18,2},{3,19},{19,3},{4,20},{20... | collective-permute-start | bytes 7077896 | tf_op jit(solution)/shard_map/ppermute | solution.py:51
  157.4 6.2 %collective-permute-done.28.refs_8_ = bf16[64,1536]{1,0:T(8,128)(2,1)S(1)} collective-permute-done((bf16[64,1536]{1,0:T(8,128)(2,1)S(1)}, bf16[64,1536]{1,0:T(8,128)(2,1)S(1)}, u32[]{:S(2)}, u32[]{:S(2)}) %collective-permute-start.28) | collective-permute-done | bytes 196640 | tf_op jit(solution)/shard_map/ppermute | solution.py:31
  165.1 23.3 %shard_map.51 = bf16[1536,1536]{1,0:T(8,128)(2,1)} custom-call(bf16[128,1536]{1,0:T(8,128)(2,1)S(1)} %constant_dynamic-update-slice_fusion.refs_0_, bf16[128,1536]{1,0:T(8,128)(2,1)S(1)} %collective-permute-done.4.refs_1_, bf16[128,1536]{1,0:T(8,128)(2,1)S(1)} %collective-permute-done.5.refs_2_, bf16[128,1536]{1,0:T(8,128)(2,1)S(1)} %collective-permute-done.6.refs_3_, ...), custom_call_target="tpu_custom_call" | custom-call | flops 9663676416 | bytes 17825792 | tf_op jit(solution)/shard_map/pallas_call | solution.py:158
  (82 shorter events, 12.5 us)
Async XLA Ops:
  1.8 9.0 %collective-permute-start.2 = (bf16[32,1536]{1,0:T(8,128)(2,1)S(1)}, bf16[32,1536]{1,0:T(8,128)(2,1)S(1)}, u32[]{:S(2)}, u32[]{:S(2)}) collective-permute-start(bf16[32,1536]{1,0:T(8,128)(2,1)S(1)} %get-tuple-element.15), channel_id=1, source_target_pairs={{0,136},{128,0},{8,128},{136,8},{1,137},{129,1},{9,129},{137,9},{2... | collective-permute-start | bytes 294920 | tf_op jit(solution)/shard_map/ppermute | solution.py:38
  5.1 8.3 %collective-permute-start = (bf16[32,1536]{1,0:T(8,128)(2,1)S(1)}, bf16[32,1536]{1,0:T(8,128)(2,1)S(1)}, u32[]{:S(2)}, u32[]{:S(2)}) collective-permute-start(bf16[32,1536]{1,0:T(8,128)(2,1)S(1)} %get-tuple-element.15), channel_id=1, source_target_pairs={{0,128},{128,8},{8,136},{136,0},{1,129},{129,9},{9,137},{137,1},{2... | collective-permute-start | bytes 294920 | tf_op jit(solution)/shard_map/ppermute | solution.py:38
  5.2 8.4 %collective-permute-start.15 = (bf16[32,1536]{1,0:T(8,128)(2,1)S(1)}, bf16[32,1536]{1,0:T(8,128)(2,1)S(1)}, u32[]{:S(2)}, u32[]{:S(2)}) collective-permute-start(bf16[32,1536]{1,0:T(8,128)(2,1)S(1)} %get-tuple-element.12), channel_id=1, source_target_pairs={{0,7},{1,0},{2,1},{3,2},{4,3},{5,4},{6,5},{7,6},{8,15},{9,8},{10,9... | collective-permute-start | bytes 294920 | tf_op jit(solution)/shard_map/ppermute | solution.py:31
  10.7 5.6 %collective-permute-start.11 = (bf16[32,1536]{1,0:T(8,128)(2,1)S(1)}, bf16[32,1536]{1,0:T(8,128)(2,1)S(1)}, u32[]{:S(2)}, u32[]{:S(2)}) collective-permute-start(bf16[32,1536]{1,0:T(8,128)(2,1)S(1)} %get-tuple-element.12), channel_id=1, source_target_pairs={{0,1},{1,2},{2,3},{3,4},{4,5},{5,6},{6,7},{7,0},{8,9},{9,10},{10,1... | collective-permute-start | bytes 294920 | tf_op jit(solution)/shard_map/ppermute | solution.py:31
  10.7 7.0 %collective-permute-start.3 = (bf16[16,1536]{1,0:T(8,128)(2,1)S(1)}, bf16[16,1536]{1,0:T(8,128)(2,1)S(1)}, u32[]{:S(2)}, u32[]{:S(2)}) collective-permute-start(bf16[16,1536]{1,0:T(8,128)(2,1)S(1)} %slice.85), channel_id=1, source_target_pairs={{0,136},{128,0},{8,128},{136,8},{1,137},{129,1},{9,129},{137,9},{2... | collective-permute-start | bytes 147464 | tf_op jit(solution)/shard_map/ppermute | solution.py:38
  13.6 6.9 %collective-permute-start.16 = (bf16[32,1536]{1,0:T(8,128)(2,1)S(1)}, bf16[32,1536]{1,0:T(8,128)(2,1)S(1)}, u32[]{:S(2)}, u32[]{:S(2)}) collective-permute-start(bf16[32,1536]{1,0:T(8,128)(2,1)S(1)} %collective-permute-done.15), channel_id=1, source_target_pairs={{0,7},{1,0},{2,1},{3,2},{4,3},{5,4},{6,5},{7,6},{8,15},{9,8},{10,9... | collective-permute-start | bytes 294920 | tf_op jit(solution)/shard_map/ppermute | solution.py:31
  16.3 6.9 %collective-permute-start.12 = (bf16[32,1536]{1,0:T(8,128)(2,1)S(1)}, bf16[32,1536]{1,0:T(8,128)(2,1)S(1)}, u32[]{:S(2)}, u32[]{:S(2)}) collective-permute-start(bf16[32,1536]{1,0:T(8,128)(2,1)S(1)} %collective-permute-done.11), channel_id=1, source_target_pairs={{0,1},{1,2},{2,3},{3,4},{4,5},{5,6},{6,7},{7,0},{8,9},{9,10},{10,1... | collective-permute-start | bytes 294920 | tf_op jit(solution)/shard_map/ppermute | solution.py:31
  17.8 21.4 %collective-permute-start.8 = (bf16[128,1536]{1,0:T(8,128)(2,1)S(1)}, bf16[128,1536]{1,0:T(8,128)(2,1)S(1)}, u32[]{:S(2)}, u32[]{:S(2)}) collective-permute-start(bf16[128,1536]{1,0:T(8,128)(2,1)S(1)} %constant_dynamic-update-slice_fusion.refs_0_), channel_id=1, source_target_pairs={{0,7},{1,0},{2,1},{3,2},{4,3},{5,4},{6,5},{7,6},{8,15},{9,8},{10,9... | collective-permute-start | bytes 1179656 | tf_op jit(solution)/shard_map/ppermute | solution.py:31
  20.5 18.7 %collective-permute-start.4 = (bf16[128,1536]{1,0:T(8,128)(2,1)S(1)}, bf16[128,1536]{1,0:T(8,128)(2,1)S(1)}, u32[]{:S(2)}, u32[]{:S(2)}) collective-permute-start(bf16[128,1536]{1,0:T(8,128)(2,1)S(1)} %constant_dynamic-update-slice_fusion.refs_0_), channel_id=1, source_target_pairs={{0,1},{1,2},{2,3},{3,4},{4,5},{5,6},{6,7},{7,0},{8,9},{9,10},{10,1... | collective-permute-start | bytes 1179656 | tf_op jit(solution)/shard_map/ppermute | solution.py:31
  20.5 7.3 %collective-permute-start.17 = (bf16[32,1536]{1,0:T(8,128)(2,1)S(1)}, bf16[32,1536]{1,0:T(8,128)(2,1)S(1)}, u32[]{:S(2)}, u32[]{:S(2)}) collective-permute-start(bf16[32,1536]{1,0:T(8,128)(2,1)S(1)} %collective-permute-done.16), channel_id=1, source_target_pairs={{0,7},{1,0},{2,1},{3,2},{4,3},{5,4},{6,5},{7,6},{8,15},{9,8},{10,9... | collective-permute-start | bytes 294920 | tf_op jit(solution)/shard_map/ppermute | solution.py:31
  23.2 8.0 %collective-permute-start.13 = (bf16[32,1536]{1,0:T(8,128)(2,1)S(1)}, bf16[32,1536]{1,0:T(8,128)(2,1)S(1)}, u32[]{:S(2)}, u32[]{:S(2)}) collective-permute-start(bf16[32,1536]{1,0:T(8,128)(2,1)S(1)} %collective-permute-done.12), channel_id=1, source_target_pairs={{0,1},{1,2},{2,3},{3,4},{4,5},{5,6},{6,7},{7,0},{8,9},{9,10},{10,1... | collective-permute-start | bytes 294920 | tf_op jit(solution)/shard_map/ppermute | solution.py:31
  27.8 7.7 %collective-permute-start.18 = (bf16[16,1536]{1,0:T(8,128)(2,1)S(1)}, bf16[16,1536]{1,0:T(8,128)(2,1)S(1)}, u32[]{:S(2)}, u32[]{:S(2)}) collective-permute-start(bf16[16,1536]{1,0:T(8,128)(2,1)S(1)} %slice.88), channel_id=1, source_target_pairs={{0,7},{1,0},{2,1},{3,2},{4,3},{5,4},{6,5},{7,6},{8,15},{9,8},{10,9... | collective-permute-start | bytes 147464 | tf_op jit(solution)/shard_map/ppermute | solution.py:31
  35.5 16.3 %collective-permute-start.21 = (bf16[256,1536]{1,0:T(8,128)(2,1)S(1)}, bf16[256,1536]{1,0:T(8,128)(2,1)S(1)}, u32[]{:S(2)}, u32[]{:S(2)}) collective-permute-start(bf16[256,1536]{1,0:T(8,128)(2,1)S(1)} %constant_dynamic-update-slice_fusion.5.refs_8_.refs_9_), channel_id=1, source_target_pairs={{0,136},{128,0},{8,128},{136,8},{1,137},{129,1},{9,129},{137,9},{2... | collective-permute-start | bytes 2359304 | tf_op jit(solution)/shard_map/ppermute | solution.py:38
  39.2 16.1 %collective-permute-start.19 = (bf16[256,1536]{1,0:T(8,128)(2,1)S(1)}, bf16[256,1536]{1,0:T(8,128)(2,1)S(1)}, u32[]{:S(2)}, u32[]{:S(2)}) collective-permute-start(bf16[256,1536]{1,0:T(8,128)(2,1)S(1)} %constant_dynamic-update-slice_fusion.5.refs_8_.refs_9_), channel_id=1, source_target_pairs={{0,128},{128,8},{8,136},{136,0},{1,129},{129,9},{9,137},{137,1},{2... | collective-permute-start | bytes 2359304 | tf_op jit(solution)/shard_map/ppermute | solution.py:38
  39.2 7.8 %collective-permute-start.5 = (bf16[128,1536]{1,0:T(8,128)(2,1)S(1)}, bf16[128,1536]{1,0:T(8,128)(2,1)S(1)}, u32[]{:S(2)}, u32[]{:S(2)}) collective-permute-start(bf16[128,1536]{1,0:T(8,128)(2,1)S(1)} %collective-permute-done.4.refs_1_), channel_id=1, source_target_pairs={{0,1},{1,2},{2,3},{3,4},{4,5},{5,6},{6,7},{7,0},{8,9},{9,10},{10,1... | collective-permute-start | bytes 1179656 | tf_op jit(solution)/shard_map/ppermute | solution.py:31
  39.2 7.8 %collective-permute-start.9 = (bf16[128,1536]{1,0:T(8,128)(2,1)S(1)}, bf16[128,1536]{1,0:T(8,128)(2,1)S(1)}, u32[]{:S(2)}, u32[]{:S(2)}) collective-permute-start(bf16[128,1536]{1,0:T(8,128)(2,1)S(1)} %collective-permute-done.8.refs_7_.refs_6_), channel_id=1, source_target_pairs={{0,7},{1,0},{2,1},{3,2},{4,3},{5,4},{6,5},{7,6},{8,15},{9,8},{10,9... | collective-permute-start | bytes 1179656 | tf_op jit(solution)/shard_map/ppermute | solution.py:31
  47.1 9.5 %collective-permute-start.6 = (bf16[128,1536]{1,0:T(8,128)(2,1)S(1)}, bf16[128,1536]{1,0:T(8,128)(2,1)S(1)}, u32[]{:S(2)}, u32[]{:S(2)}) collective-permute-start(bf16[128,1536]{1,0:T(8,128)(2,1)S(1)} %collective-permute-done.5.refs_2_), channel_id=1, source_target_pairs={{0,1},{1,2},{2,3},{3,4},{4,5},{5,6},{6,7},{7,0},{8,9},{9,10},{10,1... | collective-permute-start | bytes 1179656 | tf_op jit(solution)/shard_map/ppermute | solution.py:31
  47.1 9.6 %collective-permute-start.10 = (bf16[128,1536]{1,0:T(8,128)(2,1)S(1)}, bf16[128,1536]{1,0:T(8,128)(2,1)S(1)}, u32[]{:S(2)}, u32[]{:S(2)}) collective-permute-start(bf16[128,1536]{1,0:T(8,128)(2,1)S(1)} %collective-permute-done.9.refs_6_.refs_5_), channel_id=1, source_target_pairs={{0,7},{1,0},{2,1},{3,2},{4,3},{5,4},{6,5},{7,6},{8,15},{9,8},{10,9... | collective-permute-start | bytes 1179656 | tf_op jit(solution)/shard_map/ppermute | solution.py:31
  51.8 12.8 %collective-permute-start.22 = (bf16[128,1536]{1,0:T(8,128)(2,1)S(1)}, bf16[128,1536]{1,0:T(8,128)(2,1)S(1)}, u32[]{:S(2)}, u32[]{:S(2)}) collective-permute-start(bf16[128,1536]{1,0:T(8,128)(2,1)S(1)} %slice.90), channel_id=1, source_target_pairs={{0,136},{128,0},{8,128},{136,8},{1,137},{129,1},{9,129},{137,9},{2... | collective-permute-start | bytes 1179656 | tf_op jit(solution)/shard_map/ppermute | solution.py:38
  55.4 9.2 %collective-permute-start.20 = (bf16[128,1536]{1,0:T(8,128)(2,1)S(1)}, bf16[128,1536]{1,0:T(8,128)(2,1)S(1)}, u32[]{:S(2)}, u32[]{:S(2)}) collective-permute-start(bf16[128,1536]{1,0:T(8,128)(2,1)S(1)} %slice.89), channel_id=1, source_target_pairs={{0,128},{128,8},{8,136},{136,0},{1,129},{129,9},{9,137},{137,1},{2... | collective-permute-start | bytes 1179656 | tf_op jit(solution)/shard_map/ppermute | solution.py:38
  56.6 8.0 %collective-permute-start.7 = (bf16[64,1536]{1,0:T(8,128)(2,1)S(1)}, bf16[64,1536]{1,0:T(8,128)(2,1)S(1)}, u32[]{:S(2)}, u32[]{:S(2)}) collective-permute-start(bf16[64,1536]{1,0:T(8,128)(2,1)S(1)} %slice.86), channel_id=1, source_target_pairs={{0,1},{1,2},{2,3},{3,4},{4,5},{5,6},{6,7},{7,0},{8,9},{9,10},{10,1... | collective-permute-start | bytes 589832 | tf_op jit(solution)/shard_map/ppermute | solution.py:31
  76.5 10.5 %collective-permute-start.23 = (bf16[512,1536]{1,0:T(8,128)(2,1)S(1)}, bf16[512,1536]{1,0:T(8,128)(2,1)S(1)}, u32[]{:S(2)}, u32[]{:S(2)}) collective-permute-start(bf16[512,1536]{1,0:T(8,128)(2,1)S(1)} %get-tuple-element.5), channel_id=1, source_target_pairs={{0,16},{16,0},{1,17},{17,1},{2,18},{18,2},{3,19},{19,3},{4,20},{20... | collective-permute-start | bytes 4718600 | tf_op jit(solution)/shard_map/ppermute | solution.py:51
  87.1 7.5 %collective-permute-start.24 = (bf16[64,1536]{1,0:T(8,128)(2,1)S(1)}, bf16[64,1536]{1,0:T(8,128)(2,1)S(1)}, u32[]{:S(2)}, u32[]{:S(2)}) collective-permute-start(bf16[64,1536]{1,0:T(8,128)(2,1)S(1)} %get-tuple-element.10), channel_id=1, source_target_pairs={{0,32},{32,64},{64,96},{96,0},{1,33},{33,65},{65,97},{97,1},{2,34}... | collective-permute-start | bytes 589832 | tf_op jit(solution)/shard_map/ppermute | solution.py:42
  88.5 6.2 %collective-permute-start.26 = (bf16[64,1536]{1,0:T(8,128)(2,1)S(1)}, bf16[64,1536]{1,0:T(8,128)(2,1)S(1)}, u32[]{:S(2)}, u32[]{:S(2)}) collective-permute-start(bf16[64,1536]{1,0:T(8,128)(2,1)S(1)} %get-tuple-element.11), channel_id=1, source_target_pairs={{0,96},{32,0},{64,32},{96,64},{1,97},{33,1},{65,33},{97,65},{2,98}... | collective-permute-start | bytes 589832 | tf_op jit(solution)/shard_map/ppermute | solution.py:42
  94.9 10.7 %collective-permute-start.25 = (bf16[128,1536]{1,0:T(8,128)(2,1)S(1)}, bf16[128,1536]{1,0:T(8,128)(2,1)S(1)}, u32[]{:S(2)}, u32[]{:S(2)}) collective-permute-start(bf16[128,1536]{1,0:T(8,128)(2,1)S(1)} %get-tuple-element.6), channel_id=1, source_target_pairs={{0,32},{32,64},{64,96},{96,0},{1,33},{33,65},{65,97},{97,1},{2,34}... | collective-permute-start | bytes 1179656 | tf_op jit(solution)/shard_map/ppermute | solution.py:42
  95.9 9.7 %collective-permute-start.27 = (bf16[128,1536]{1,0:T(8,128)(2,1)S(1)}, bf16[128,1536]{1,0:T(8,128)(2,1)S(1)}, u32[]{:S(2)}, u32[]{:S(2)}) collective-permute-start(bf16[128,1536]{1,0:T(8,128)(2,1)S(1)} %get-tuple-element.7), channel_id=1, source_target_pairs={{0,96},{32,0},{64,32},{96,64},{1,97},{33,1},{65,33},{97,65},{2,98}... | collective-permute-start | bytes 1179656 | tf_op jit(solution)/shard_map/ppermute | solution.py:42
  107.1 8.5 %collective-permute-start.29 = (bf16[128,1536]{1,0:T(8,128)(2,1)S(1)}, bf16[128,1536]{1,0:T(8,128)(2,1)S(1)}, u32[]{:S(2)}, u32[]{:S(2)}) collective-permute-start(bf16[128,1536]{1,0:T(8,128)(2,1)S(1)} %get-tuple-element.8), channel_id=1, source_target_pairs={{0,128},{128,0},{1,129},{129,1},{2,130},{130,2},{3,131},{131,3},{4... | collective-permute-start | bytes 1179656 | tf_op jit(solution)/shard_map/ppermute | solution.py:51
  115.7 5.2 %collective-permute-start.30 = (bf16[256,1536]{1,0:T(8,128)(2,1)S(1)}, bf16[256,1536]{1,0:T(8,128)(2,1)S(1)}, u32[]{:S(2)}, u32[]{:S(2)}) collective-permute-start(bf16[256,1536]{1,0:T(8,128)(2,1)S(1)} %pad_maximum_fusion.2), channel_id=1, source_target_pairs={{0,16},{16,0},{1,17},{17,1},{2,18},{18,2},{3,19},{19,3},{4,20},{20... | collective-permute-start | bytes 2359304 | tf_op jit(solution)/shard_map/ppermute | solution.py:51
  121.0 19.8 %collective-permute-start.31 = (bf16[512,1536]{1,0:T(8,128)(2,1)S(1)}, bf16[512,1536]{1,0:T(8,128)(2,1)S(1)}, u32[]{:S(2)}, u32[]{:S(2)}) collective-permute-start(bf16[512,1536]{1,0:T(8,128)(2,1)S(1)} %pad_maximum_fusion.1), channel_id=1, source_target_pairs={{0,32},{16,112},{32,64},{48,16},{64,96},{80,48},{96,0},{112,80},{1... | collective-permute-start | bytes 4718600 | tf_op jit(solution)/shard_map/ppermute | solution.py:47
  140.9 12.1 %collective-permute-start.32 = (bf16[256,1536]{1,0:T(8,128)(2,1)S(1)}, bf16[256,1536]{1,0:T(8,128)(2,1)S(1)}, u32[]{:S(2)}, u32[]{:S(2)}) collective-permute-start(bf16[256,1536]{1,0:T(8,128)(2,1)S(1)} %slice.98), channel_id=1, source_target_pairs={{0,32},{16,112},{32,64},{48,16},{64,96},{80,48},{96,0},{112,80},{1... | collective-permute-start | bytes 2359304 | tf_op jit(solution)/shard_map/ppermute | solution.py:47
  153.2 10.4 %collective-permute-start.33 = (bf16[768,1536]{1,0:T(8,128)(2,1)S(1)}, bf16[768,1536]{1,0:T(8,128)(2,1)S(1)}, u32[]{:S(2)}, u32[]{:S(2)}) collective-permute-start(bf16[768,1536]{1,0:T(8,128)(2,1)S(1)} %pad_maximum_fusion), channel_id=1, source_target_pairs={{0,16},{16,0},{1,17},{17,1},{2,18},{18,2},{3,19},{19,3},{4,20},{20... | collective-permute-start | bytes 7077896 | tf_op jit(solution)/shard_map/ppermute | solution.py:51
  157.0 6.6 %collective-permute-start.28 = (bf16[64,1536]{1,0:T(8,128)(2,1)S(1)}, bf16[64,1536]{1,0:T(8,128)(2,1)S(1)}, u32[]{:S(2)}, u32[]{:S(2)}) collective-permute-start(bf16[64,1536]{1,0:T(8,128)(2,1)S(1)} %slice.97), channel_id=1, source_target_pairs={{0,7},{1,0},{2,1},{3,2},{4,3},{5,4},{6,5},{7,6},{8,15},{9,8},{10,9... | collective-permute-start | bytes 589832 | tf_op jit(solution)/shard_map/ppermute | solution.py:31
  (7 other events, 134.0 us)

commit v2 on v0

v2 whole, which is shorter than its diff:
```python
import jax
import jax.numpy as jnp
from jax import lax
from jax.experimental import pallas as pl
from jax.experimental.pallas import tpu as pltpu
from jax.sharding import Mesh, PartitionSpec as P

root_coef = 0.7978845608
cube_coef = 0.044715

XL, Y, C, XH, Z = 2, 4, 2, 2, 8
AXES = ("xl", "y", "c", "xh", "z")
BF, F32 = jnp.bfloat16, jnp.float32


def gelu_tanh(value):
    inner = jnp.tanh(root_coef * (value + cube_coef * value * value * value))
    return 0.5 * value * (1.0 + inner)


def gelu_slope(value):
    inner = jnp.tanh(root_coef * (value + cube_coef * value * value * value))
    return 0.5 * (1.0 + inner) + 0.5 * value * (1.0 - inner * inner) * root_coef * (
        1.0 + 3.0 * cube_coef * value * value
    )


def along_z(a, d):
    return lax.ppermute(a, "z", [(i, (i + d) % Z) for i in range(Z)])


def along_x(a, d):
    def place(x):
        return (x % 2) * XH + x // 2

    return lax.ppermute(a, ("xl", "xh"), [(place(x), place((x + d) % 4)) for x in range(4)])


def along_y(a, d):
    return lax.ppermute(a, "y", [(i, (i + d) % Y) for i in range(Y)])


def round_y(a):
    pairs = [((y, c), ((y + (1 if c == 0 else -1)) % Y, c)) for y in range(Y) for c in range(C)]
    return lax.ppermute(a, ("y", "c"), [(s[0] * C + s[1], t[0] * C + t[1]) for s, t in pairs])


def swap(a, axis):
    return lax.ppermute(a, axis, [(0, 1), (1, 0)])


def tie(*arrays):
    return lax.optimization_barrier(arrays)


OWN = [0, -1, 1, -2, 2, -3, 3, 4]


def partial_kernel(grads_ref, w_ref, mine_ref, other_ref, held):
    y, c, xh, z = (lax.axis_index(a) for a in ("y", "c", "xh", "z"))
    held_new = jnp.dot(grads_ref[...], w_ref[...], preferred_element_type=F32)
    for k in range(16):
        xp = xh if k < 8 else 1 - xh
        zp = lax.rem(z + OWN[k % 8] + 8, 8)
        yp, cp = 2 * xp + zp // 4, lax.rem(zp // 2, 2)
        spot = lax.rem(cp + c, 2) * 512 + lax.rem(yp + 4 - y, 4) * 128 + lax.rem(zp, 2) * 64
        held[pl.ds(pl.multiple_of(spot, 64), 64), :] = held_new[64 * k : 64 * k + 64]
    mine_ref[...] = held[:512]
    other_ref[...] = held[512:].astype(BF)


def partial_grad(grads, weight):
    step = 512
    return pl.pallas_call(
        partial_kernel,
        grid=(1536 // step,),
        in_specs=[pl.BlockSpec((1024, 1536), lambda n: (0, 0)), pl.BlockSpec((1536, step), lambda n: (0, n))],
        out_specs=[pl.BlockSpec((512, step), lambda n: (0, n))] * 2,
        out_shape=[jax.ShapeDtypeStruct((512, 1536), F32), jax.ShapeDtypeStruct((512, 1536), BF)],
        scratch_shapes=[pltpu.VMEM((1024, step), F32)],
        compiler_params=pltpu.CompilerParams(vmem_limit_bytes=28 << 20),
        cost_estimate=pl.CostEstimate(flops=2 * 1024 * 1536 * 1536, bytes_accessed=13 << 20, transcendentals=0),
    )(grads, weight)


def weight_kernel(grads_ref, acts_ref, out_ref, acts):
    y, c, xl, xh, z = (lax.axis_index(a) for a in ("y", "c", "xl", "xh", "z"))

    @pl.when(pl.program_id(0) == 0)
    def _():
        for k in range(32):
            dx = (0, 2, 3, 1)[k // 8]
            xp = lax.rem(2 * xh + xl + dx, 4)
            zp = lax.rem(z + OWN[k % 8] + 8, 8)
            dy = lax.rem(2 * (xp // 2) + zp // 4 + 4 - y, 4)
            away = lax.rem(lax.rem(zp // 2, 2) + c, 2)
            back = jnp.where(c == 0, 3, 1)
            block = jnp.where(
                dy == 0, away, jnp.where(dy == 2, 4 + 3 * away, jnp.where(dy == back, 2 + away, 6 - away))
            )
            start = block * 256 + (dx % 2) * 128 + lax.rem(zp, 2) * 64
            acts[64 * k : 64 * k + 64, :] = acts_ref[pl.ds(pl.multiple_of(start, 64), 64), :]

    out_ref[...] = lax.dot_general(
        grads_ref[...], acts[...], (((0,), (0,)), ((), ())), preferred_element_type=F32
    ).astype(BF)


def weight_gradient(grads, acts):
    step = 256
    return pl.pallas_call(
        weight_kernel,
        grid=(1536 // step,),
        in_specs=[pl.BlockSpec((2048, step), lambda m: (0, m)), pl.BlockSpec((2048, 1536), lambda m: (0, 0))],
        out_specs=pl.BlockSpec((step, 1536), lambda m: (m, 0)),
        out_shape=jax.ShapeDtypeStruct((1536, 1536), BF),
        scratch_shapes=[pltpu.VMEM((2048, 1536), BF)],
        compiler_params=pltpu.CompilerParams(vmem_limit_bytes=36 << 20),
        cost_estimate=pl.CostEstimate(flops=2 * 2048 * 1536 * 1536, bytes_accessed=17 << 20, transcendentals=0),
    )(grads, acts)


def per_device(pre_act, out_grad, down_weight):
    pre_wide = pre_act.astype(F32)
    g = out_grad
    activation = gelu_tanh(pre_wide).astype(BF)

    up1, down1, far = along_z(g, 1), along_z(g, -1), along_x(g, 2)
    other_rep = swap(activation, "xl")
    up1, down1, far, other_rep = tie(up1, down1, far, other_rep)

    up2 = along_z(jnp.concatenate([far, up1]), 1)
    down2 = along_z(jnp.concatenate([down1, far]), -1)
    near = jnp.concatenate([g, up1, down1])
    left_a, right_a = along_x(near, 1), along_x(near, -1)
    two = jnp.concatenate([activation, other_rep])
    two_c = swap(two, "c")
    up2, down2, left_a, right_a, two_c = tie(up2, down2, left_a, right_a, two_c)

    up3, down3 = along_z(up2, 1), along_z(down2, -1)
    pair = jnp.concatenate([up2[64:], down2[:64]])
    left_b, right_b = along_x(pair, 1), along_x(pair, -1)
    acts_1 = round_y(jnp.concatenate([two, two_c]))
    up3, down3, left_b, right_b, acts_1 = tie(up3, down3, left_b, right_b, acts_1)

    up4, down4 = along_z(up3[:96], 1), along_z(down3[32:], -1)
    pair = jnp.concatenate([up3[64:], down3[:64]])
    left_c, right_c = along_x(pair, 1), along_x(pair, -1)
    acts_2 = round_y(acts_1[:256])
    up4, down4, left_c, right_c, acts_2 = tie(up4, down4, left_c, right_c, acts_2)

    up5, down5 = along_z(up4[:32], 1), along_z(down4[64:], -1)
    last = jnp.concatenate([up4[64:], down4[:32]])
    left_d, right_d = along_x(last, 1), along_x(last, -1)
    came = jnp.concatenate([acts_1, acts_2])
    swapped = swap(came, "c")

    own = [g, up1, down1, up2[64:], down2[:64], up3[64:], down3[:64], last]
    second = [far, up2[:64], down2[64:], up3[:64], down3[64:], up4[:64], down4[32:], up5, down5]
    grads_own = jnp.concatenate(own + second)

    mine, other = partial_grad(grads_own, down_weight)
    other = swap(other, "c")
    _, left_d, right_d, swapped = tie(other, left_d, right_d, swapped)

    def summed(block):
        return mine[128 * block : 128 * block + 128] + other[128 * block : 128 * block + 128].astype(F32)

    from_below = along_y(summed(1).astype(BF), 1)
    from_above = along_y(summed(3).astype(BF), -1)
    from_across = along_y(summed(2).astype(BF), 2)
    grad_act = summed(0) + from_below.astype(F32) + from_above.astype(F32) + from_across.astype(F32)
    pre_grad = (grad_act * gelu_slope(pre_wide)).astype(BF)

    grads = jnp.concatenate([grads_own, left_a, left_b, left_c, left_d, right_a, right_b, right_c, right_d])
    acts = jnp.concatenate([two, two_c, came, swapped])
    weight_grad = weight_gradient(grads, acts)
    return (pre_grad, weight_grad)


def solution(mesh):
    physical = Mesh(mesh.devices.reshape(XL, Y, C, XH, Z), AXES)
    rep, row, col = "xl", ("y", "c"), ("xh", "z")
    return jax.shard_map(
        per_device,
        mesh=physical,
        in_specs=(P((rep, *row), col), P((rep, *col), row), P(row, col)),
        out_specs=(P((rep, *row), col), P(row, col)),
        check_vma=False,
    )
```

time: 300 us -> 130 us (0.43)
  waiting for transfers between devices: 251 us -> 53.8 us
  starting transfers between devices: 0.12 us -> 49.1 us
  matrix products: 25.2 us -> 0 us
  Pallas kernels: 0 us -> 19.4 us
  between operations: 13.7 us -> 1.13 us
  local copies, waits for them, and re-layouts: 6.61 us -> 2.26 us
    all_gather x2 -> x0, waiting for transfers between devices: 186 us -> none  [the longest x1 140 us: per_device(): grads_all = lax.all_gather(out_grad, ('rep', 'col'), axis=0, tiled=True)]
    reduce_scatter x1 -> x0, waiting for transfers between devices: 64.5 us -> none  [per_device(): lax.psum_scatter(jnp.dot(grads_replica, down_weight, preferred_element_ty...]
    ppermute x0 -> x28, waiting for transfers between devices: none -> 53.8 us  [the longest x10 25.4 us: along_z(): return lax.ppermute(a, 'z', [(i, (i + d) % Z) for i in range(Z)])]
    ppermute x0 -> x28, starting transfers between devices: none -> 49.1 us  [the longest x10 22.8 us: along_z(): return lax.ppermute(a, 'z', [(i, (i + d) % Z) for i in range(Z)])]
    dot_general x2 -> x0, matrix products: 25.2 us -> none  [the longest x1 15.5 us: make_folder(): lax.dot_general(grad_rows, shard_rows, (((0,), (0,)), ((), ())), preferre...]
    pallas_call x0 -> x2, Pallas kernels: none -> 19.4 us  [the longest x1 13 us: weight_gradient(): pl.pallas_call(weight_kernel, grid=(1536 // step,), in_specs=[pl.BlockSpe...]
    unnamed x3 -> x40, local copies, waits for them, and re-layouts: 6.61 us -> 1.95 us
  transfers between devices with their start and end apart: 3 -> 28, of which waited for: 3 -> 12; matrix products, arithmetic and copies ran while one was open for 0% -> 3% of each run, Pallas kernels for 0% -> 0%
where the time goes in v2:
time: 130 us
  waiting for transfers between devices  53.8 us (41%)
  starting transfers between devices  49.1 us (38%)
  Pallas kernels  19.4 us (15%)
  other arithmetic  3.81 us (3%)
  local copies, waits for them, and re-layouts  2.26 us (2%)
    ppermute x10, waiting for transfers between devices, along_z(): return lax.ppermute(a, 'z', [(i, (i + d) % Z) for i in range(Z)])  25.4 us
    ppermute x10, starting transfers between devices, along_z(): return lax.ppermute(a, 'z', [(i, (i + d) % Z) for i in range(Z)])  22.8 us
    ppermute x3, waiting for transfers between devices, along_y(): return lax.ppermute(a, 'y', [(i, (i + d) % Y) for i in range(Y)])  17.4 us
    pallas_call x1, Pallas kernels, weight_gradient(): pl.pallas_call(weight_kernel, grid=(1536 // step,), in_specs=[pl.BlockSpe...  13 us
    ppermute x9, starting transfers between devices, along_x(): lax.ppermute(a, ('xl', 'xh'), [(place(x), place((x + d) % 4)) for x in ra...  12.9 us
    ppermute x9, waiting for transfers between devices, along_x(): lax.ppermute(a, ('xl', 'xh'), [(place(x), place((x + d) % 4)) for x in ra...  7.82 us
    pallas_call x1, Pallas kernels, partial_grad(): pl.pallas_call(partial_kernel, grid=(1536 // step,), in_specs=[pl.BlockSp...  6.43 us
    ppermute x2, starting transfers between devices, round_y(): lax.ppermute(a, ('y', 'c'), [(s[0] * C + s[1], t[0] * C + t[1]) for s, t...  6 us
  transfers between devices with their start and end apart: 28, of which 12 were waited for; matrix products, arithmetic and copies ran while one was open for 3% of the time, Pallas kernels for 0%

profile of v2, /device:TPU:1, one launch (start us, length us, event | category | flops | bytes accessed | tf_op | source)
XLA Modules:
  0.0 129.5 jit_solution(3451476594702276315)
XLA Ops:
  0.6 1.3 fusion.2
  1.9 2.1 %collective-permute-start.3 = (bf16[128,1536]{1,0:T(8,128)(2,1)S(1)}, bf16[128,1536]{1,0:T(8,128)(2,1)S(1)}, u32[]{:S(2)}, u32[]{:S(2)}) collective-permute-start(bf16[128,1536]{1,0:T(8,128)(2,1)S(1)} %fusion.2), channel_id=1, source_target_pairs={{0,128},{128,0},{1,129},{129,1},{2,130},{130,2},{3,131},{131,3},{4... | collective-permute-start | bytes 1179656 | tf_op jit(solution)/shard_map/ppermute | solution.py:49
  4.0 1.6 %collective-permute-start = (bf16[64,1536]{1,0:T(8,128)(2,1)}, bf16[64,1536]{1,0:T(8,128)(2,1)S(1)}, u32[]{:S(2)}, u32[]{:S(2)}) collective-permute-start(bf16[64,1536]{1,0:T(8,128)(2,1)} %param.4), channel_id=1, source_target_pairs={{0,1},{1,2},{2,3},{3,4},{4,5},{5,6},{6,7},{7,0},{8,9},{9,10},{10,1... | collective-permute-start | bytes 589832 | tf_op jit(solution)/shard_map/ppermute | solution.py:29
  5.7 3.9 %collective-permute-start.1 = (bf16[64,1536]{1,0:T(8,128)(2,1)}, bf16[64,1536]{1,0:T(8,128)(2,1)S(1)}, u32[]{:S(2)}, u32[]{:S(2)}) collective-permute-start(bf16[64,1536]{1,0:T(8,128)(2,1)} %param.4), channel_id=1, source_target_pairs={{0,7},{1,0},{2,1},{3,2},{4,3},{5,4},{6,5},{7,6},{8,15},{9,8},{10,9... | collective-permute-start | bytes 589832 | tf_op jit(solution)/shard_map/ppermute | solution.py:29
  9.6 2.5 %collective-permute-start.2 = (bf16[64,1536]{1,0:T(8,128)(2,1)}, bf16[64,1536]{1,0:T(8,128)(2,1)S(1)}, u32[]{:S(2)}, u32[]{:S(2)}) collective-permute-start(bf16[64,1536]{1,0:T(8,128)(2,1)} %param.4), channel_id=1, source_target_pairs={{0,8},{128,136},{8,0},{136,128},{1,9},{129,137},{9,1},{137,129},{2... | collective-permute-start | bytes 589832 | tf_op jit(solution)/shard_map/ppermute | solution.py:36
  13.1 1.1 collective-permute-done
  14.1 5.1 %collective-permute-done.2 = bf16[64,1536]{1,0:T(8,128)(2,1)S(1)} collective-permute-done((bf16[64,1536]{1,0:T(8,128)(2,1)}, bf16[64,1536]{1,0:T(8,128)(2,1)S(1)}, u32[]{:S(2)}, u32[]{:S(2)}) %collective-permute-start.2) | collective-permute-done | bytes 196640 | tf_op jit(solution)/shard_map/ppermute | solution.py:36
  19.3 1.6 %collective-permute-start.8 = (bf16[256,1536]{1,0:T(8,128)(2,1)S(1)}, bf16[256,1536]{1,0:T(8,128)(2,1)S(1)}, u32[]{:S(2)}, u32[]{:S(2)}) collective-permute-start(bf16[256,1536]{1,0:T(8,128)(2,1)S(1)} %pad_maximum_fusion.2), channel_id=1, source_target_pairs={{0,16},{16,0},{1,17},{17,1},{2,18},{18,2},{3,19},{19,3},{4,20},{20... | collective-permute-start | bytes 2359304 | tf_op jit(solution)/shard_map/ppermute | solution.py:49
  21.1 2.7 %collective-permute-start.7 = (bf16[192,1536]{1,0:T(8,128)(2,1)S(1)}, bf16[192,1536]{1,0:T(8,128)(2,1)S(1)}, u32[]{:S(2)}, u32[]{:S(2)}) collective-permute-start(bf16[192,1536]{1,0:T(8,128)(2,1)S(1)} %get-tuple-element.81), channel_id=1, source_target_pairs={{0,136},{128,0},{8,128},{136,8},{1,137},{129,1},{9,129},{137,9},{2... | collective-permute-start | bytes 1769480 | tf_op jit(solution)/shard_map/ppermute | solution.py:36
  23.8 1.7 %collective-permute-start.4 = (bf16[128,1536]{1,0:T(8,128)(2,1)S(1)}, bf16[128,1536]{1,0:T(8,128)(2,1)S(1)}, u32[]{:S(2)}, u32[]{:S(2)}) collective-permute-start(bf16[128,1536]{1,0:T(8,128)(2,1)S(1)} %get-tuple-element.89), channel_id=1, source_target_pairs={{0,1},{1,2},{2,3},{3,4},{4,5},{5,6},{6,7},{7,0},{8,9},{9,10},{10,1... | collective-permute-start | bytes 1179656 | tf_op jit(solution)/shard_map/ppermute | solution.py:29
  25.5 4.0 %collective-permute-start.5 = (bf16[128,1536]{1,0:T(8,128)(2,1)S(1)}, bf16[128,1536]{1,0:T(8,128)(2,1)S(1)}, u32[]{:S(2)}, u32[]{:S(2)}) collective-permute-start(bf16[128,1536]{1,0:T(8,128)(2,1)S(1)} %get-tuple-element.88), channel_id=1, source_target_pairs={{0,7},{1,0},{2,1},{3,2},{4,3},{5,4},{6,5},{7,6},{8,15},{9,8},{10,9... | collective-permute-start | bytes 1179656 | tf_op jit(solution)/shard_map/ppermute | solution.py:29
  29.6 8.8 %collective-permute-done.4 = bf16[128,1536]{1,0:T(8,128)(2,1)S(1)} collective-permute-done((bf16[128,1536]{1,0:T(8,128)(2,1)S(1)}, bf16[128,1536]{1,0:T(8,128)(2,1)S(1)}, u32[]{:S(2)}, u32[]{:S(2)}) %collective-permute-start.4) | collective-permute-done | bytes 393248 | tf_op jit(solution)/shard_map/ppermute | solution.py:29
  38.6 2.8 %collective-permute-start.13 = (bf16[512,1536]{1,0:T(8,128)(2,1)S(1)}, bf16[512,1536]{1,0:T(8,128)(2,1)S(1)}, u32[]{:S(2)}, u32[]{:S(2)}) collective-permute-start(bf16[512,1536]{1,0:T(8,128)(2,1)S(1)} %pad_maximum_fusion.1), channel_id=1, source_target_pairs={{0,32},{16,112},{32,64},{48,16},{64,96},{80,48},{96,0},{112,80},{1... | collective-permute-start | bytes 4718600 | tf_op jit(solution)/shard_map/ppermute | solution.py:45
  41.8 3.9 %collective-permute-start.10 = (bf16[128,1536]{1,0:T(8,128)(2,1)S(1)}, bf16[128,1536]{1,0:T(8,128)(2,1)S(1)}, u32[]{:S(2)}, u32[]{:S(2)}) collective-permute-start(bf16[128,1536]{1,0:T(8,128)(2,1)S(1)} %collective-permute-done.5), channel_id=1, source_target_pairs={{0,7},{1,0},{2,1},{3,2},{4,3},{5,4},{6,5},{7,6},{8,15},{9,8},{10,9... | collective-permute-start | bytes 1179656 | tf_op jit(solution)/shard_map/ppermute | solution.py:29
  45.9 2.7 %collective-permute-start.12 = (bf16[128,1536]{1,0:T(8,128)(2,1)S(1)}, bf16[128,1536]{1,0:T(8,128)(2,1)S(1)}, u32[]{:S(2)}, u32[]{:S(2)}) collective-permute-start(bf16[128,1536]{1,0:T(8,128)(2,1)S(1)} %pad_maximum_fusion.5), channel_id=1, source_target_pairs={{0,136},{128,0},{8,128},{136,8},{1,137},{129,1},{9,129},{137,9},{2... | collective-permute-start | bytes 1179656 | tf_op jit(solution)/shard_map/ppermute | solution.py:36
  48.6 6.6 %collective-permute-done.9 = bf16[128,1536]{1,0:T(8,128)(2,1)S(1)} collective-permute-done((bf16[128,1536]{1,0:T(8,128)(2,1)S(1)}, bf16[128,1536]{1,0:T(8,128)(2,1)S(1)}, u32[]{:S(2)}, u32[]{:S(2)}) %collective-permute-start.9) | collective-permute-done | bytes 393248 | tf_op jit(solution)/shard_map/ppermute | solution.py:29
  55.2 2.7 %collective-permute-done.11 = bf16[128,1536]{1,0:T(8,128)(2,1)S(1)} collective-permute-done((bf16[128,1536]{1,0:T(8,128)(2,1)S(1)}, bf16[128,1536]{1,0:T(8,128)(2,1)S(1)}, u32[]{:S(2)}, u32[]{:S(2)}) %collective-permute-start.11) | collective-permute-done | bytes 393248 | tf_op jit(solution)/shard_map/ppermute | solution.py:36
  58.8 3.2 %collective-permute-start.18 = (bf16[256,1536]{1,0:T(8,128)(2,1)S(1)}, bf16[256,1536]{1,0:T(8,128)(2,1)S(1)}, u32[]{:S(2)}, u32[]{:S(2)}) collective-permute-start(bf16[256,1536]{1,0:T(8,128)(2,1)S(1)} %slice.85), channel_id=1, source_target_pairs={{0,32},{16,112},{32,64},{48,16},{64,96},{80,48},{96,0},{112,80},{1... | collective-permute-start | bytes 2359304 | tf_op jit(solution)/shard_map/ppermute | solution.py:45
  62.4 2.7 %collective-permute-start.17 = (bf16[128,1536]{1,0:T(8,128)(2,1)S(1)}, bf16[128,1536]{1,0:T(8,128)(2,1)S(1)}, u32[]{:S(2)}, u32[]{:S(2)}) collective-permute-start(bf16[128,1536]{1,0:T(8,128)(2,1)S(1)} %pad_maximum_fusion.6), channel_id=1, source_target_pairs={{0,136},{128,0},{8,128},{136,8},{1,137},{129,1},{9,129},{137,9},{2... | collective-permute-start | bytes 1179656 | tf_op jit(solution)/shard_map/ppermute | solution.py:36
  65.5 3.9 %collective-permute-start.15 = (bf16[96,1536]{1,0:T(8,128)(2,1)S(1)}, bf16[96,1536]{1,0:T(8,128)(2,1)S(1)}, u32[]{:S(2)}, u32[]{:S(2)}) collective-permute-start(bf16[96,1536]{1,0:T(8,128)(2,1)S(1)} %slice.84), channel_id=1, source_target_pairs={{0,7},{1,0},{2,1},{3,2},{4,3},{5,4},{6,5},{7,6},{8,15},{9,8},{10,9... | collective-permute-start | bytes 884744 | tf_op jit(solution)/shard_map/ppermute | solution.py:29
  69.7 6.9 %collective-permute-done.14 = bf16[96,1536]{1,0:T(8,128)(2,1)S(1)} collective-permute-done((bf16[96,1536]{1,0:T(8,128)(2,1)S(1)}, bf16[96,1536]{1,0:T(8,128)(2,1)S(1)}, u32[]{:S(2)}, u32[]{:S(2)}) %collective-permute-start.14) | collective-permute-done | bytes 294944 | tf_op jit(solution)/shard_map/ppermute | solution.py:29
  77.2 2.7 %collective-permute-start.20 = (bf16[32,1536]{1,0:T(8,128)(2,1)S(1)}, bf16[32,1536]{1,0:T(8,128)(2,1)S(1)}, u32[]{:S(2)}, u32[]{:S(2)}) collective-permute-start(bf16[32,1536]{1,0:T(8,128)(2,1)S(1)} %get-tuple-element.74), channel_id=1, source_target_pairs={{0,7},{1,0},{2,1},{3,2},{4,3},{5,4},{6,5},{7,6},{8,15},{9,8},{10,9... | collective-permute-start | bytes 294920 | tf_op jit(solution)/shard_map/ppermute | solution.py:29
  79.9 1.9 %collective-permute-done.19 = bf16[32,1536]{1,0:T(8,128)(2,1)S(1)} collective-permute-done((bf16[32,1536]{1,0:T(8,128)(2,1)S(1)}, bf16[32,1536]{1,0:T(8,128)(2,1)S(1)}, u32[]{:S(2)}, u32[]{:S(2)}) %collective-permute-start.19) | collective-permute-done | bytes 98336 | tf_op jit(solution)/shard_map/ppermute | solution.py:29
  81.9 6.4 %shard_map.50 = (f32[512,1536]{1,0:T(8,128)S(1)}, bf16[512,1536]{1,0:T(8,128)(2,1)S(1)}) custom-call(bf16[1024,1536]{1,0:T(8,128)(2,1)S(1)} %get-tuple-element.91.grads_ref, bf16[1536,1536]{1,0:T(8,128)(2,1)S(1)} %bitcast.1), custom_call_target="tpu_custom_call" | custom-call | flops 4831838208 | bytes 13631488 | tf_op jit(solution)/shard_map/pallas_call | solution.py:74
  88.3 2.0 %collective-permute-start.21 = (bf16[512,1536]{1,0:T(8,128)(2,1)S(1)}, bf16[512,1536]{1,0:T(8,128)(2,1)S(1)}, u32[]{:S(2)}, u32[]{:S(2)}) collective-permute-start(bf16[512,1536]{1,0:T(8,128)(2,1)S(1)} %get-tuple-element.39), channel_id=1, source_target_pairs={{0,16},{16,0},{1,17},{17,1},{2,18},{18,2},{3,19},{19,3},{4,20},{20... | collective-permute-start | bytes 4718600 | tf_op jit(solution)/shard_map/ppermute | solution.py:49
  91.0 2.3 %collective-permute-done.21 = bf16[512,1536]{1,0:T(8,128)(2,1)S(1)} collective-permute-done((bf16[512,1536]{1,0:T(8,128)(2,1)S(1)}, bf16[512,1536]{1,0:T(8,128)(2,1)S(1)}, u32[]{:S(2)}, u32[]{:S(2)}) %collective-permute-start.21) | collective-permute-done | bytes 1572896 | tf_op jit(solution)/shard_map/ppermute | solution.py:49
  95.4 10.3 %collective-permute-done.24 = bf16[128,1536]{1,0:T(8,128)(2,1)S(1)} collective-permute-done((bf16[128,1536]{1,0:T(8,128)(2,1)S(1)}, bf16[128,1536]{1,0:T(8,128)(2,1)S(1)}, u32[]{:S(2)}, u32[]{:S(2)}) %collective-permute-start.24) | collective-permute-done | bytes 393248 | tf_op jit(solution)/shard_map/ppermute | solution.py:40
  105.7 2.0 %collective-permute-start.26 = (bf16[64,1536]{1,0:T(8,128)(2,1)S(1)}, bf16[64,1536]{1,0:T(8,128)(2,1)S(1)}, u32[]{:S(2)}, u32[]{:S(2)}) collective-permute-start(bf16[64,1536]{1,0:T(8,128)(2,1)S(1)} %pad_maximum_fusion.7), channel_id=1, source_target_pairs={{0,136},{128,0},{8,128},{136,8},{1,137},{129,1},{9,129},{137,9},{2... | collective-permute-start | bytes 589832 | tf_op jit(solution)/shard_map/ppermute | solution.py:36
  107.6 4.1 %collective-permute-done.23 = bf16[128,1536]{1,0:T(8,128)(2,1)S(1)} collective-permute-done((bf16[128,1536]{1,0:T(8,128)(2,1)S(1)}, bf16[128,1536]{1,0:T(8,128)(2,1)S(1)}, u32[]{:S(2)}, u32[]{:S(2)}) %collective-permute-start.23) | collective-permute-done | bytes 393248 | tf_op jit(solution)/shard_map/ppermute | solution.py:40
  111.7 3.0 %collective-permute-done.22 = bf16[128,1536]{1,0:T(8,128)(2,1)S(1)} collective-permute-done((bf16[128,1536]{1,0:T(8,128)(2,1)S(1)}, bf16[128,1536]{1,0:T(8,128)(2,1)S(1)}, u32[]{:S(2)}, u32[]{:S(2)}) %collective-permute-start.22) | collective-permute-done | bytes 393248 | tf_op jit(solution)/shard_map/ppermute | solution.py:40
  114.7 1.5 %fusion.7 = bf16[128,1536]{1,0:T(8,128)(2,1)} fusion(bf16[128,1536]{1,0:T(8,128)(2,1)S(1)} %copy-done, bf16[128,1536]{1,0:T(8,128)(2,1)S(1)} %collective-permute-done.24, bf16[128,1536]{1,0:T(8,128)(2,1)S(1)} %collective-permute-done.23, bf16[128,1536]{1,0:T(8,128)(2,1)S(1)} %collective-permute-done.22, f32[512,1536]{1,0:T(8,128)S(1)} %get-tuple-element.38, ...), kind=kLoop, calls=%fused_computation.16 | loop fusion | flops 5505024 | bytes 3145728 | tf_op jit(solution)/shard_map/convert_element_type | solution.py:173
  116.6 13.0 %shard_map.51 = bf16[1536,1536]{1,0:T(8,128)(2,1)} custom-call(bf16[2048,1536]{1,0:T(8,128)(2,1)S(1)} %constant_dynamic-update-slice_fusion.15.grads_ref, bf16[2048,1536]{1,0:T(8,128)(2,1)S(1)} %constant_dynamic-update-slice_fusion.35.acts_ref), custom_call_target="tpu_custom_call" | custom-call | flops 9663676416 | bytes 17825792 | tf_op jit(solution)/shard_map/pallas_call | solution.py:111
  (85 shorter events, 7.3 us)
Async XLA Ops:
  1.9 17.3 %collective-permute-start.3 = (bf16[128,1536]{1,0:T(8,128)(2,1)S(1)}, bf16[128,1536]{1,0:T(8,128)(2,1)S(1)}, u32[]{:S(2)}, u32[]{:S(2)}) collective-permute-start(bf16[128,1536]{1,0:T(8,128)(2,1)S(1)} %fusion.2), channel_id=1, source_target_pairs={{0,128},{128,0},{1,129},{129,1},{2,130},{130,2},{3,131},{131,3},{4... | collective-permute-start | bytes 1179656 | tf_op jit(solution)/shard_map/ppermute | solution.py:49
  4.0 10.1 %collective-permute-start = (bf16[64,1536]{1,0:T(8,128)(2,1)}, bf16[64,1536]{1,0:T(8,128)(2,1)S(1)}, u32[]{:S(2)}, u32[]{:S(2)}) collective-permute-start(bf16[64,1536]{1,0:T(8,128)(2,1)} %param.4), channel_id=1, source_target_pairs={{0,1},{1,2},{2,3},{3,4},{4,5},{5,6},{6,7},{7,0},{8,9},{9,10},{10,1... | collective-permute-start | bytes 589832 | tf_op jit(solution)/shard_map/ppermute | solution.py:29
  5.7 8.5 %collective-permute-start.1 = (bf16[64,1536]{1,0:T(8,128)(2,1)}, bf16[64,1536]{1,0:T(8,128)(2,1)S(1)}, u32[]{:S(2)}, u32[]{:S(2)}) collective-permute-start(bf16[64,1536]{1,0:T(8,128)(2,1)} %param.4), channel_id=1, source_target_pairs={{0,7},{1,0},{2,1},{3,2},{4,3},{5,4},{6,5},{7,6},{8,15},{9,8},{10,9... | collective-permute-start | bytes 589832 | tf_op jit(solution)/shard_map/ppermute | solution.py:29
  9.6 9.6 %collective-permute-start.2 = (bf16[64,1536]{1,0:T(8,128)(2,1)}, bf16[64,1536]{1,0:T(8,128)(2,1)S(1)}, u32[]{:S(2)}, u32[]{:S(2)}) collective-permute-start(bf16[64,1536]{1,0:T(8,128)(2,1)} %param.4), channel_id=1, source_target_pairs={{0,8},{128,136},{8,0},{136,128},{1,9},{129,137},{9,1},{137,129},{2... | collective-permute-start | bytes 589832 | tf_op jit(solution)/shard_map/ppermute | solution.py:36
  19.3 19.2 %collective-permute-start.8 = (bf16[256,1536]{1,0:T(8,128)(2,1)S(1)}, bf16[256,1536]{1,0:T(8,128)(2,1)S(1)}, u32[]{:S(2)}, u32[]{:S(2)}) collective-permute-start(bf16[256,1536]{1,0:T(8,128)(2,1)S(1)} %pad_maximum_fusion.2), channel_id=1, source_target_pairs={{0,16},{16,0},{1,17},{17,1},{2,18},{18,2},{3,19},{19,3},{4,20},{20... | collective-permute-start | bytes 2359304 | tf_op jit(solution)/shard_map/ppermute | solution.py:49
  20.9 48.5 %copy-start = (bf16[128,1536]{1,0:T(8,128)(2,1)S(1)}, bf16[128,1536]{1,0:T(8,128)(2,1)}, u32[]{:S(2)}) copy-start(bf16[128,1536]{1,0:T(8,128)(2,1)} %param.3) | copy-start | bytes 1179652
  21.0 17.4 %collective-permute-start.6 = (bf16[192,1536]{1,0:T(8,128)(2,1)S(1)}, bf16[192,1536]{1,0:T(8,128)(2,1)S(1)}, u32[]{:S(2)}, u32[]{:S(2)}) collective-permute-start(bf16[192,1536]{1,0:T(8,128)(2,1)S(1)} %get-tuple-element.81), channel_id=1, source_target_pairs={{0,128},{128,8},{8,136},{136,0},{1,129},{129,9},{9,137},{137,1},{2... | collective-permute-start | bytes 1769480 | tf_op jit(solution)/shard_map/ppermute | solution.py:36
  21.1 17.3 %collective-permute-start.7 = (bf16[192,1536]{1,0:T(8,128)(2,1)S(1)}, bf16[192,1536]{1,0:T(8,128)(2,1)S(1)}, u32[]{:S(2)}, u32[]{:S(2)}) collective-permute-start(bf16[192,1536]{1,0:T(8,128)(2,1)S(1)} %get-tuple-element.81), channel_id=1, source_target_pairs={{0,136},{128,0},{8,128},{136,8},{1,137},{129,1},{9,129},{137,9},{2... | collective-permute-start | bytes 1769480 | tf_op jit(solution)/shard_map/ppermute | solution.py:36
  23.8 14.6 %collective-permute-start.4 = (bf16[128,1536]{1,0:T(8,128)(2,1)S(1)}, bf16[128,1536]{1,0:T(8,128)(2,1)S(1)}, u32[]{:S(2)}, u32[]{:S(2)}) collective-permute-start(bf16[128,1536]{1,0:T(8,128)(2,1)S(1)} %get-tuple-element.89), channel_id=1, source_target_pairs={{0,1},{1,2},{2,3},{3,4},{4,5},{5,6},{6,7},{7,0},{8,9},{9,10},{10,1... | collective-permute-start | bytes 1179656 | tf_op jit(solution)/shard_map/ppermute | solution.py:29
  25.5 12.9 %collective-permute-start.5 = (bf16[128,1536]{1,0:T(8,128)(2,1)S(1)}, bf16[128,1536]{1,0:T(8,128)(2,1)S(1)}, u32[]{:S(2)}, u32[]{:S(2)}) collective-permute-start(bf16[128,1536]{1,0:T(8,128)(2,1)S(1)} %get-tuple-element.88), channel_id=1, source_target_pairs={{0,7},{1,0},{2,1},{3,2},{4,3},{5,4},{6,5},{7,6},{8,15},{9,8},{10,9... | collective-permute-start | bytes 1179656 | tf_op jit(solution)/shard_map/ppermute | solution.py:29
  38.6 20.2 %collective-permute-start.13 = (bf16[512,1536]{1,0:T(8,128)(2,1)S(1)}, bf16[512,1536]{1,0:T(8,128)(2,1)S(1)}, u32[]{:S(2)}, u32[]{:S(2)}) collective-permute-start(bf16[512,1536]{1,0:T(8,128)(2,1)S(1)} %pad_maximum_fusion.1), channel_id=1, source_target_pairs={{0,32},{16,112},{32,64},{48,16},{64,96},{80,48},{96,0},{112,80},{1... | collective-permute-start | bytes 4718600 | tf_op jit(solution)/shard_map/ppermute | solution.py:45
  41.4 13.9 %collective-permute-start.9 = (bf16[128,1536]{1,0:T(8,128)(2,1)S(1)}, bf16[128,1536]{1,0:T(8,128)(2,1)S(1)}, u32[]{:S(2)}, u32[]{:S(2)}) collective-permute-start(bf16[128,1536]{1,0:T(8,128)(2,1)S(1)} %collective-permute-done.4), channel_id=1, source_target_pairs={{0,1},{1,2},{2,3},{3,4},{4,5},{5,6},{6,7},{7,0},{8,9},{9,10},{10,1... | collective-permute-start | bytes 1179656 | tf_op jit(solution)/shard_map/ppermute | solution.py:29
  41.8 13.4 %collective-permute-start.10 = (bf16[128,1536]{1,0:T(8,128)(2,1)S(1)}, bf16[128,1536]{1,0:T(8,128)(2,1)S(1)}, u32[]{:S(2)}, u32[]{:S(2)}) collective-permute-start(bf16[128,1536]{1,0:T(8,128)(2,1)S(1)} %collective-permute-done.5), channel_id=1, source_target_pairs={{0,7},{1,0},{2,1},{3,2},{4,3},{5,4},{6,5},{7,6},{8,15},{9,8},{10,9... | collective-permute-start | bytes 1179656 | tf_op jit(solution)/shard_map/ppermute | solution.py:29
  45.8 36.1 %slice-start = ((s8[4718592]{0:T(1024)(128)(4,1)}), s8[4194304]{0:T(1024)(128)(4,1)S(1)}, s32[]{:S(2)}) async-start(s8[4718592]{0:T(1024)(128)(4,1)} %bitcast), calls=%async_computation | async-start | bytes 8388608
  45.8 12.1 %collective-permute-start.11 = (bf16[128,1536]{1,0:T(8,128)(2,1)S(1)}, bf16[128,1536]{1,0:T(8,128)(2,1)S(1)}, u32[]{:S(2)}, u32[]{:S(2)}) collective-permute-start(bf16[128,1536]{1,0:T(8,128)(2,1)S(1)} %pad_maximum_fusion.5), channel_id=1, source_target_pairs={{0,128},{128,8},{8,136},{136,0},{1,129},{129,9},{9,137},{137,1},{2... | collective-permute-start | bytes 1179656 | tf_op jit(solution)/shard_map/ppermute | solution.py:36
  45.9 12.0 %collective-permute-start.12 = (bf16[128,1536]{1,0:T(8,128)(2,1)S(1)}, bf16[128,1536]{1,0:T(8,128)(2,1)S(1)}, u32[]{:S(2)}, u32[]{:S(2)}) collective-permute-start(bf16[128,1536]{1,0:T(8,128)(2,1)S(1)} %pad_maximum_fusion.5), channel_id=1, source_target_pairs={{0,136},{128,0},{8,128},{136,8},{1,137},{129,1},{9,129},{137,9},{2... | collective-permute-start | bytes 1179656 | tf_op jit(solution)/shard_map/ppermute | solution.py:36
  58.8 17.9 %collective-permute-start.18 = (bf16[256,1536]{1,0:T(8,128)(2,1)S(1)}, bf16[256,1536]{1,0:T(8,128)(2,1)S(1)}, u32[]{:S(2)}, u32[]{:S(2)}) collective-permute-start(bf16[256,1536]{1,0:T(8,128)(2,1)S(1)} %slice.85), channel_id=1, source_target_pairs={{0,32},{16,112},{32,64},{48,16},{64,96},{80,48},{96,0},{112,80},{1... | collective-permute-start | bytes 2359304 | tf_op jit(solution)/shard_map/ppermute | solution.py:45
  62.1 14.5 %collective-permute-start.16 = (bf16[128,1536]{1,0:T(8,128)(2,1)S(1)}, bf16[128,1536]{1,0:T(8,128)(2,1)S(1)}, u32[]{:S(2)}, u32[]{:S(2)}) collective-permute-start(bf16[128,1536]{1,0:T(8,128)(2,1)S(1)} %pad_maximum_fusion.6), channel_id=1, source_target_pairs={{0,128},{128,8},{8,136},{136,0},{1,129},{129,9},{9,137},{137,1},{2... | collective-permute-start | bytes 1179656 | tf_op jit(solution)/shard_map/ppermute | solution.py:36
  62.4 14.3 %collective-permute-start.17 = (bf16[128,1536]{1,0:T(8,128)(2,1)S(1)}, bf16[128,1536]{1,0:T(8,128)(2,1)S(1)}, u32[]{:S(2)}, u32[]{:S(2)}) collective-permute-start(bf16[128,1536]{1,0:T(8,128)(2,1)S(1)} %pad_maximum_fusion.6), channel_id=1, source_target_pairs={{0,136},{128,0},{8,128},{136,8},{1,137},{129,1},{9,129},{137,9},{2... | collective-permute-start | bytes 1179656 | tf_op jit(solution)/shard_map/ppermute | solution.py:36
  65.1 11.6 %collective-permute-start.14 = (bf16[96,1536]{1,0:T(8,128)(2,1)S(1)}, bf16[96,1536]{1,0:T(8,128)(2,1)S(1)}, u32[]{:S(2)}, u32[]{:S(2)}) collective-permute-start(bf16[96,1536]{1,0:T(8,128)(2,1)S(1)} %slice.83), channel_id=1, source_target_pairs={{0,1},{1,2},{2,3},{3,4},{4,5},{5,6},{6,7},{7,0},{8,9},{9,10},{10,1... | collective-permute-start | bytes 884744 | tf_op jit(solution)/shard_map/ppermute | solution.py:29
  65.5 11.2 %collective-permute-start.15 = (bf16[96,1536]{1,0:T(8,128)(2,1)S(1)}, bf16[96,1536]{1,0:T(8,128)(2,1)S(1)}, u32[]{:S(2)}, u32[]{:S(2)}) collective-permute-start(bf16[96,1536]{1,0:T(8,128)(2,1)S(1)} %slice.84), channel_id=1, source_target_pairs={{0,7},{1,0},{2,1},{3,2},{4,3},{5,4},{6,5},{7,6},{8,15},{9,8},{10,9... | collective-permute-start | bytes 884744 | tf_op jit(solution)/shard_map/ppermute | solution.py:29
  76.7 5.2 %slice-start.1 = ((s8[4718592]{0:T(1024)(128)(4,1)}), s8[524288]{0:T(1024)(128)(4,1)S(1)}, s32[]{:S(2)}) async-start(s8[4718592]{0:T(1024)(128)(4,1)} %bitcast), calls=%async_computation.1 | async-start | bytes 1048576
  77.1 4.8 %collective-permute-start.19 = (bf16[32,1536]{1,0:T(8,128)(2,1)S(1)}, bf16[32,1536]{1,0:T(8,128)(2,1)S(1)}, u32[]{:S(2)}, u32[]{:S(2)}) collective-permute-start(bf16[32,1536]{1,0:T(8,128)(2,1)S(1)} %get-tuple-element.71), channel_id=1, source_target_pairs={{0,1},{1,2},{2,3},{3,4},{4,5},{5,6},{6,7},{7,0},{8,9},{9,10},{10,1... | collective-permute-start | bytes 294920 | tf_op jit(solution)/shard_map/ppermute | solution.py:29
  77.2 4.7 %collective-permute-start.20 = (bf16[32,1536]{1,0:T(8,128)(2,1)S(1)}, bf16[32,1536]{1,0:T(8,128)(2,1)S(1)}, u32[]{:S(2)}, u32[]{:S(2)}) collective-permute-start(bf16[32,1536]{1,0:T(8,128)(2,1)S(1)} %get-tuple-element.74), channel_id=1, source_target_pairs={{0,7},{1,0},{2,1},{3,2},{4,3},{5,4},{6,5},{7,6},{8,15},{9,8},{10,9... | collective-permute-start | bytes 294920 | tf_op jit(solution)/shard_map/ppermute | solution.py:29
  88.3 5.0 %collective-permute-start.21 = (bf16[512,1536]{1,0:T(8,128)(2,1)S(1)}, bf16[512,1536]{1,0:T(8,128)(2,1)S(1)}, u32[]{:S(2)}, u32[]{:S(2)}) collective-permute-start(bf16[512,1536]{1,0:T(8,128)(2,1)S(1)} %get-tuple-element.39), channel_id=1, source_target_pairs={{0,16},{16,0},{1,17},{17,1},{2,18},{18,2},{3,19},{19,3},{4,20},{20... | collective-permute-start | bytes 4718600 | tf_op jit(solution)/shard_map/ppermute | solution.py:49
  90.6 25.7 %collective-permute-start.27 = (bf16[768,1536]{1,0:T(8,128)(2,1)S(1)}, bf16[768,1536]{1,0:T(8,128)(2,1)S(1)}, u32[]{:S(2)}, u32[]{:S(2)}) collective-permute-start(bf16[768,1536]{1,0:T(8,128)(2,1)S(1)} %pad_maximum_fusion), channel_id=1, source_target_pairs={{0,16},{16,0},{1,17},{17,1},{2,18},{18,2},{3,19},{19,3},{4,20},{20... | collective-permute-start | bytes 7077896 | tf_op jit(solution)/shard_map/ppermute | solution.py:49
  90.8 25.4 %collective-permute-start.25 = (bf16[64,1536]{1,0:T(8,128)(2,1)S(1)}, bf16[64,1536]{1,0:T(8,128)(2,1)S(1)}, u32[]{:S(2)}, u32[]{:S(2)}) collective-permute-start(bf16[64,1536]{1,0:T(8,128)(2,1)S(1)} %pad_maximum_fusion.7), channel_id=1, source_target_pairs={{0,128},{128,8},{8,136},{136,0},{1,129},{129,9},{9,137},{137,1},{2... | collective-permute-start | bytes 589832 | tf_op jit(solution)/shard_map/ppermute | solution.py:36
  93.7 12.0 %collective-permute-start.24 = (bf16[128,1536]{1,0:T(8,128)(2,1)S(1)}, bf16[128,1536]{1,0:T(8,128)(2,1)S(1)}, u32[]{:S(2)}, u32[]{:S(2)}) collective-permute-start(bf16[128,1536]{1,0:T(8,128)(2,1)S(1)} %get-tuple-element.51), channel_id=1, source_target_pairs={{0,64},{32,96},{64,0},{96,32},{1,65},{33,97},{65,1},{97,33},{2,66}... | collective-permute-start | bytes 1179656 | tf_op jit(solution)/shard_map/ppermute | solution.py:40
  93.8 17.9 %collective-permute-start.23 = (bf16[128,1536]{1,0:T(8,128)(2,1)S(1)}, bf16[128,1536]{1,0:T(8,128)(2,1)S(1)}, u32[]{:S(2)}, u32[]{:S(2)}) collective-permute-start(bf16[128,1536]{1,0:T(8,128)(2,1)S(1)} %get-tuple-element.52), channel_id=1, source_target_pairs={{0,96},{32,0},{64,32},{96,64},{1,97},{33,1},{65,33},{97,65},{2,98}... | collective-permute-start | bytes 1179656 | tf_op jit(solution)/shard_map/ppermute | solution.py:40
  94.8 20.0 %collective-permute-start.22 = (bf16[128,1536]{1,0:T(8,128)(2,1)S(1)}, bf16[128,1536]{1,0:T(8,128)(2,1)S(1)}, u32[]{:S(2)}, u32[]{:S(2)}) collective-permute-start(bf16[128,1536]{1,0:T(8,128)(2,1)S(1)} %get-tuple-element.50), channel_id=1, source_target_pairs={{0,32},{32,64},{64,96},{96,0},{1,33},{33,65},{65,97},{97,1},{2,34}... | collective-permute-start | bytes 1179656 | tf_op jit(solution)/shard_map/ppermute | solution.py:40
  105.7 10.6 %collective-permute-start.26 = (bf16[64,1536]{1,0:T(8,128)(2,1)S(1)}, bf16[64,1536]{1,0:T(8,128)(2,1)S(1)}, u32[]{:S(2)}, u32[]{:S(2)}) collective-permute-start(bf16[64,1536]{1,0:T(8,128)(2,1)S(1)} %pad_maximum_fusion.7), channel_id=1, source_target_pairs={{0,136},{128,0},{8,128},{136,8},{1,137},{129,1},{9,129},{137,9},{2... | collective-permute-start | bytes 589832 | tf_op jit(solution)/shard_map/ppermute | solution.py:36

commit v3 on v2

--- a/solution.py
+++ b/solution.py
@@ -95,10 +95,14 @@
             dy = lax.rem(2 * (xp // 2) + zp // 4 + 4 - y, 4)
             away = lax.rem(lax.rem(zp // 2, 2) + c, 2)
             back = jnp.where(c == 0, 3, 1)
+            other = dx % 2
             block = jnp.where(
-                dy == 0, away, jnp.where(dy == 2, 4 + 3 * away, jnp.where(dy == back, 2 + away, 6 - away))
+                dy == 0,
+                2 * other + away,
+                3 * other
+                + jnp.where(dy == 2, 6 + 6 * away, jnp.where(dy == back, 4 + away, 11 - away)),
             )
-            start = block * 256 + (dx % 2) * 128 + lax.rem(zp, 2) * 64
+            start = block * 128 + lax.rem(zp, 2) * 64
             acts[64 * k : 64 * k + 64, :] = acts_ref[pl.ds(pl.multiple_of(start, 64), 64), :]
 
     out_ref[...] = lax.dot_general(
@@ -126,34 +130,32 @@
     activation = gelu_tanh(pre_wide).astype(BF)
 
     up1, down1, far = along_z(g, 1), along_z(g, -1), along_x(g, 2)
-    other_rep = swap(activation, "xl")
-    up1, down1, far, other_rep = tie(up1, down1, far, other_rep)
+    act_c = swap(activation, "c")
+    activation, act_c, up1, down1, far = tie(activation, act_c, up1, down1, far)
 
     up2 = along_z(jnp.concatenate([far, up1]), 1)
     down2 = along_z(jnp.concatenate([down1, far]), -1)
+    other_rep = swap(activation, "xl")
+    chip = jnp.concatenate([activation, act_c])
+    hop_1 = round_y(chip)
+    up2, down2, other_rep, hop_1 = tie(up2, down2, other_rep, hop_1)
+
+    up3, down3 = along_z(up2, 1), along_z(down2, -1)
     near = jnp.concatenate([g, up1, down1])
     left_a, right_a = along_x(near, 1), along_x(near, -1)
-    two = jnp.concatenate([activation, other_rep])
-    two_c = swap(two, "c")
-    up2, down2, left_a, right_a, two_c = tie(up2, down2, left_a, right_a, two_c)
-
-    up3, down3 = along_z(up2, 1), along_z(down2, -1)
-    pair = jnp.concatenate([up2[64:], down2[:64]])
-    left_b, right_b = along_x(pair, 1), along_x(pair, -1)
-    acts_1 = round_y(jnp.concatenate([two, two_c]))
-    up3, down3, left_b, right_b, acts_1 = tie(up3, down3, left_b, right_b, acts_1)
+    other_chip = jnp.concatenate([other_rep, swap(other_rep, "c")])
+    hop_2 = round_y(jnp.concatenate([hop_1[:128], other_chip]))
+    up3, down3, left_a, right_a, other_chip = tie(up3, down3, left_a, right_a, other_chip)
 
     up4, down4 = along_z(up3[:96], 1), along_z(down3[32:], -1)
-    pair = jnp.concatenate([up3[64:], down3[:64]])
-    left_c, right_c = along_x(pair, 1), along_x(pair, -1)
-    acts_2 = round_y(acts_1[:256])
-    up4, down4, left_c, right_c, acts_2 = tie(up4, down4, left_c, right_c, acts_2)
+    middle = jnp.concatenate([up2[64:], down2[:64]])
+    left_b, right_b = along_x(middle, 1), along_x(middle, -1)
+    up4, down4, hop_2, left_b, right_b = tie(up4, down4, hop_2, left_b, right_b)
 
     up5, down5 = along_z(up4[:32], 1), along_z(down4[64:], -1)
     last = jnp.concatenate([up4[64:], down4[:32]])
-    left_d, right_d = along_x(last, 1), along_x(last, -1)
-    came = jnp.concatenate([acts_1, acts_2])
-    swapped = swap(came, "c")
+    hop_3 = round_y(hop_2[128:256])
+    up5, down5, hop_3 = tie(up5, down5, hop_3)
 
     own = [g, up1, down1, up2[64:], down2[:64], up3[64:], down3[:64], last]
     second = [far, up2[:64], down2[64:], up3[:64], down3[64:], up4[:64], down4[32:], up5, down5]
@@ -161,20 +163,25 @@
 
     mine, other = partial_grad(grads_own, down_weight)
     other = swap(other, "c")
-    _, left_d, right_d, swapped = tie(other, left_d, right_d, swapped)
+    third = jnp.concatenate([up3[64:], down3[:64], last])
+    left_c, right_c = along_x(third, 1), along_x(third, -1)
+    came = jnp.concatenate([hop_1, hop_2, hop_3])
+    swapped = swap(came, "c")
 
     def summed(block):
         return mine[128 * block : 128 * block + 128] + other[128 * block : 128 * block + 128].astype(F32)
 
-    from_below = along_y(summed(1).astype(BF), 1)
-    from_above = along_y(summed(3).astype(BF), -1)
-    from_across = along_y(summed(2).astype(BF), 2)
+    to_above, to_below, to_across = summed(1).astype(BF), summed(3).astype(BF), summed(2).astype(BF)
+    to_above, to_below, to_across, swapped = tie(to_above, to_below, to_across, swapped)
+    from_across = along_y(to_across, 2)
+    from_below, from_above = along_y(to_above, 1), along_y(to_below, -1)
+
+    grads = jnp.concatenate([grads_own, left_a, left_b, left_c, right_a, right_b, right_c])
+    acts = jnp.concatenate([chip, other_chip, came, swapped])
+    weight_grad = weight_gradient(grads, acts)
+    from_across, from_below, from_above, weight_grad = tie(from_across, from_below, from_above, weight_grad)
     grad_act = summed(0) + from_below.astype(F32) + from_above.astype(F32) + from_across.astype(F32)
     pre_grad = (grad_act * gelu_slope(pre_wide)).astype(BF)
-
-    grads = jnp.concatenate([grads_own, left_a, left_b, left_c, left_d, right_a, right_b, right_c, right_d])
-    acts = jnp.concatenate([two, two_c, came, swapped])
-    weight_grad = weight_gradient(grads, acts)
     return (pre_grad, weight_grad)
 
 

time: 130 us -> 118 us (0.908)
  waiting for transfers between devices: 53.8 us -> 35.9 us
  starting transfers between devices: 49.1 us -> 55.8 us
    ppermute x10, waiting for transfers between devices: 25.4 us -> 4.92 us  [along_z(): return lax.ppermute(a, 'z', [(i, (i + d) % Z) for i in range(Z)])]
    ppermute x2 -> x3, waiting for transfers between devices: 0.78 us -> 17.2 us  [round_y(): lax.ppermute(a, ('y', 'c'), [(s[0] * C + s[1], t[0] * C + t[1]) for s, t...]
    ppermute x3, waiting for transfers between devices: 17.4 us -> 4.44 us  [along_y(): return lax.ppermute(a, 'y', [(i, (i + d) % Y) for i in range(Y)])]
    ppermute x4 -> x5, starting transfers between devices: 5.83 us -> 17.8 us  [swap(): return lax.ppermute(a, axis, [(0, 1), (1, 0)])]
    ppermute x10, starting transfers between devices: 22.8 us -> 14.9 us  [along_z(): return lax.ppermute(a, 'z', [(i, (i + d) % Z) for i in range(Z)])]
    ppermute x9 -> x7, waiting for transfers between devices: 7.82 us -> 5.12 us  [along_x(): lax.ppermute(a, ('xl', 'xh'), [(place(x), place((x + d) % 4)) for x in ra...]
    ppermute x2 -> x3, starting transfers between devices: 6 us -> 8.58 us  [round_y(): lax.ppermute(a, ('y', 'c'), [(s[0] * C + s[1], t[0] * C + t[1]) for s, t...]
    ppermute x4 -> x5, waiting for transfers between devices: 2.36 us -> 4.27 us  [swap(): return lax.ppermute(a, axis, [(0, 1), (1, 0)])]
  transfers between devices with their start and end apart: 28 -> 28, of which waited for: 12 -> 10; matrix products, arithmetic and copies ran while one was open for 3% -> 2% of each run, Pallas kernels for 0% -> 16%
where the time goes in v3:
time: 118 us
  starting transfers between devices  55.8 us (47%)
  waiting for transfers between devices  35.9 us (30%)
  Pallas kernels  19.4 us (16%)
  other arithmetic  3.54 us (3%)
  local copies, waits for them, and re-layouts  2.27 us (2%)
    ppermute x5, starting transfers between devices, swap(): return lax.ppermute(a, axis, [(0, 1), (1, 0)])  17.8 us
    ppermute x3, waiting for transfers between devices, round_y(): lax.ppermute(a, ('y', 'c'), [(s[0] * C + s[1], t[0] * C + t[1]) for s, t...  17.2 us
    ppermute x10, starting transfers between devices, along_z(): return lax.ppermute(a, 'z', [(i, (i + d) % Z) for i in range(Z)])  14.9 us
    pallas_call x1, Pallas kernels, weight_gradient(): pl.pallas_call(weight_kernel, grid=(1536 // step,), in_specs=[pl.BlockSpe...  13 us
    ppermute x7, starting transfers between devices, along_x(): lax.ppermute(a, ('xl', 'xh'), [(place(x), place((x + d) % 4)) for x in ra...  11.1 us
    ppermute x3, starting transfers between devices, round_y(): lax.ppermute(a, ('y', 'c'), [(s[0] * C + s[1], t[0] * C + t[1]) for s, t...  8.58 us
    pallas_call x1, Pallas kernels, partial_grad(): pl.pallas_call(partial_kernel, grid=(1536 // step,), in_specs=[pl.BlockSp...  6.43 us
    ppermute x7, waiting for transfers between devices, along_x(): lax.ppermute(a, ('xl', 'xh'), [(place(x), place((x + d) % 4)) for x in ra...  5.12 us
  transfers between devices with their start and end apart: 28, of which 10 were waited for; matrix products, arithmetic and copies ran while one was open for 2% of the time, Pallas kernels for 16%

profile of v3, /device:TPU:1, one launch (start us, length us, event | category | flops | bytes accessed | tf_op | source)
XLA Modules:
  0.0 118.0 jit_solution(12040979558537007365)
XLA Ops:
  0.6 1.3 %fusion.2 = bf16[128,1536]{1,0:T(8,128)(2,1)S(1)} fusion(bf16[128,1536]{1,0:T(8,128)(2,1)} %param.3), kind=kLoop, calls=%fused_computation.11 | loop fusion | flops 1966080 | bytes 786432 | tf_op jit(solution)/shard_map/convert_element_type | solution.py:130
  1.9 3.3 %collective-permute-start = (bf16[128,1536]{1,0:T(8,128)(2,1)S(1)}, bf16[128,1536]{1,0:T(8,128)(2,1)S(1)}, u32[]{:S(2)}, u32[]{:S(2)}) collective-permute-start(bf16[128,1536]{1,0:T(8,128)(2,1)S(1)} %fusion.2), channel_id=1, source_target_pairs={{0,16},{16,0},{1,17},{17,1},{2,18},{18,2},{3,19},{19,3},{4,20},{20... | collective-permute-start | bytes 1179656 | tf_op jit(solution)/shard_map/ppermute | solution.py:49
  5.2 3.8 %collective-permute-start.2 = (bf16[64,1536]{1,0:T(8,128)(2,1)}, bf16[64,1536]{1,0:T(8,128)(2,1)S(1)}, u32[]{:S(2)}, u32[]{:S(2)}) collective-permute-start(bf16[64,1536]{1,0:T(8,128)(2,1)} %param.4), channel_id=1, source_target_pairs={{0,7},{1,0},{2,1},{3,2},{4,3},{5,4},{6,5},{7,6},{8,15},{9,8},{10,9... | collective-permute-start | bytes 589832 | tf_op jit(solution)/shard_map/ppermute | solution.py:29
  9.1 2.7 %collective-permute-start.3 = (bf16[64,1536]{1,0:T(8,128)(2,1)}, bf16[64,1536]{1,0:T(8,128)(2,1)S(1)}, u32[]{:S(2)}, u32[]{:S(2)}) collective-permute-start(bf16[64,1536]{1,0:T(8,128)(2,1)} %param.4), channel_id=1, source_target_pairs={{0,8},{128,136},{8,0},{136,128},{1,9},{129,137},{9,1},{137,129},{2... | collective-permute-start | bytes 589832 | tf_op jit(solution)/shard_map/ppermute | solution.py:36
  11.8 1.0 constant_dynamic-update-slice_fusion.32
  12.8 1.6 %collective-permute-done.1 = bf16[64,1536]{1,0:T(8,128)(2,1)S(1)} collective-permute-done((bf16[64,1536]{1,0:T(8,128)(2,1)}, bf16[64,1536]{1,0:T(8,128)(2,1)S(1)}, u32[]{:S(2)}, u32[]{:S(2)}) %collective-permute-start.1) | collective-permute-done | bytes 196640 | tf_op jit(solution)/shard_map/ppermute | solution.py:29
  14.5 2.3 %collective-permute-done.3 = bf16[64,1536]{1,0:T(8,128)(2,1)S(1)} collective-permute-done((bf16[64,1536]{1,0:T(8,128)(2,1)}, bf16[64,1536]{1,0:T(8,128)(2,1)S(1)}, u32[]{:S(2)}, u32[]{:S(2)}) %collective-permute-start.3) | collective-permute-done | bytes 196640 | tf_op jit(solution)/shard_map/ppermute | solution.py:36
  17.0 2.7 %collective-permute-start.5 = (bf16[128,1536]{1,0:T(8,128)(2,1)S(1)}, bf16[128,1536]{1,0:T(8,128)(2,1)S(1)}, u32[]{:S(2)}, u32[]{:S(2)}) collective-permute-start(bf16[128,1536]{1,0:T(8,128)(2,1)S(1)} %get-tuple-element.112), channel_id=1, source_target_pairs={{0,7},{1,0},{2,1},{3,2},{4,3},{5,4},{6,5},{7,6},{8,15},{9,8},{10,9... | collective-permute-start | bytes 1179656 | tf_op jit(solution)/shard_map/ppermute | solution.py:29
  19.6 1.2 %collective-permute-start.6 = (bf16[128,1536]{1,0:T(8,128)(2,1)S(1)}, bf16[128,1536]{1,0:T(8,128)(2,1)S(1)}, u32[]{:S(2)}, u32[]{:S(2)}) collective-permute-start(bf16[128,1536]{1,0:T(8,128)(2,1)S(1)} %fusion.2), channel_id=1, source_target_pairs={{0,128},{128,0},{1,129},{129,1},{2,130},{130,2},{3,131},{131,3},{4... | collective-permute-start | bytes 1179656 | tf_op jit(solution)/shard_map/ppermute | solution.py:49
  20.9 2.8 %collective-permute-start.7 = (bf16[256,1536]{1,0:T(8,128)(2,1)S(1)}, bf16[256,1536]{1,0:T(8,128)(2,1)S(1)}, u32[]{:S(2)}, u32[]{:S(2)}) collective-permute-start(bf16[256,1536]{1,0:T(8,128)(2,1)S(1)} %pad_maximum_fusion.2), channel_id=1, source_target_pairs={{0,32},{16,112},{32,64},{48,16},{64,96},{80,48},{96,0},{112,80},{1... | collective-permute-start | bytes 2359304 | tf_op jit(solution)/shard_map/ppermute | solution.py:45
  24.2 3.3 %collective-permute-done.4 = bf16[128,1536]{1,0:T(8,128)(2,1)S(1)} collective-permute-done((bf16[128,1536]{1,0:T(8,128)(2,1)S(1)}, bf16[128,1536]{1,0:T(8,128)(2,1)S(1)}, u32[]{:S(2)}, u32[]{:S(2)}) %collective-permute-start.4) | collective-permute-done | bytes 393248 | tf_op jit(solution)/shard_map/ppermute | solution.py:29
  27.5 2.5 %collective-permute-start.11 = (bf16[192,1536]{1,0:T(8,128)(2,1)S(1)}, bf16[192,1536]{1,0:T(8,128)(2,1)S(1)}, u32[]{:S(2)}, u32[]{:S(2)}) collective-permute-start(bf16[192,1536]{1,0:T(8,128)(2,1)S(1)} %get-tuple-element.105), channel_id=1, source_target_pairs={{0,136},{128,0},{8,128},{136,8},{1,137},{129,1},{9,129},{137,9},{2... | collective-permute-start | bytes 1769480 | tf_op jit(solution)/shard_map/ppermute | solution.py:36
  29.9 2.7 %collective-permute-done.7 = bf16[256,1536]{1,0:T(8,128)(2,1)S(1)} collective-permute-done((bf16[256,1536]{1,0:T(8,128)(2,1)S(1)}, bf16[256,1536]{1,0:T(8,128)(2,1)S(1)}, u32[]{:S(2)}, u32[]{:S(2)}) %collective-permute-start.7) | collective-permute-done | bytes 786464 | tf_op jit(solution)/shard_map/ppermute | solution.py:45
  32.6 2.7 %collective-permute-start.9 = (bf16[128,1536]{1,0:T(8,128)(2,1)S(1)}, bf16[128,1536]{1,0:T(8,128)(2,1)S(1)}, u32[]{:S(2)}, u32[]{:S(2)}) collective-permute-start(bf16[128,1536]{1,0:T(8,128)(2,1)S(1)} %collective-permute-done.5), channel_id=1, source_target_pairs={{0,7},{1,0},{2,1},{3,2},{4,3},{5,4},{6,5},{7,6},{8,15},{9,8},{10,9... | collective-permute-start | bytes 1179656 | tf_op jit(solution)/shard_map/ppermute | solution.py:29
  35.3 4.2 %collective-permute-start.12 = (bf16[128,1536]{1,0:T(8,128)(2,1)S(1)}, bf16[128,1536]{1,0:T(8,128)(2,1)S(1)}, u32[]{:S(2)}, u32[]{:S(2)}) collective-permute-start(bf16[128,1536]{1,0:T(8,128)(2,1)S(1)} %collective-permute-done.6), channel_id=1, source_target_pairs={{0,16},{16,0},{1,17},{17,1},{2,18},{18,2},{3,19},{19,3},{4,20},{20... | collective-permute-start | bytes 1179656 | tf_op jit(solution)/shard_map/ppermute | solution.py:49
  39.7 1.2 %collective-permute-done.12 = bf16[128,1536]{1,0:T(8,128)(2,1)S(1)} collective-permute-done((bf16[128,1536]{1,0:T(8,128)(2,1)S(1)}, bf16[128,1536]{1,0:T(8,128)(2,1)S(1)}, u32[]{:S(2)}, u32[]{:S(2)}) %collective-permute-start.12) | collective-permute-done | bytes 393248 | tf_op jit(solution)/shard_map/ppermute | solution.py:49
  41.2 2.5 %collective-permute-start.17 = (bf16[128,1536]{1,0:T(8,128)(2,1)S(1)}, bf16[128,1536]{1,0:T(8,128)(2,1)S(1)}, u32[]{:S(2)}, u32[]{:S(2)}) collective-permute-start(bf16[128,1536]{1,0:T(8,128)(2,1)S(1)} %pad_maximum_fusion.7), channel_id=1, source_target_pairs={{0,136},{128,0},{8,128},{136,8},{1,137},{129,1},{9,129},{137,9},{2... | collective-permute-start | bytes 1179656 | tf_op jit(solution)/shard_map/ppermute | solution.py:36
  44.1 2.7 %collective-permute-start.14 = (bf16[96,1536]{1,0:T(8,128)(2,1)S(1)}, bf16[96,1536]{1,0:T(8,128)(2,1)S(1)}, u32[]{:S(2)}, u32[]{:S(2)}) collective-permute-start(bf16[96,1536]{1,0:T(8,128)(2,1)S(1)} %slice.87), channel_id=1, source_target_pairs={{0,7},{1,0},{2,1},{3,2},{4,3},{5,4},{6,5},{7,6},{8,15},{9,8},{10,9... | collective-permute-start | bytes 884744 | tf_op jit(solution)/shard_map/ppermute | solution.py:29
  46.9 2.6 %collective-permute-start.15 = (bf16[384,1536]{1,0:T(8,128)(2,1)S(1)}, bf16[384,1536]{1,0:T(8,128)(2,1)S(1)}, u32[]{:S(2)}, u32[]{:S(2)}) collective-permute-start(bf16[384,1536]{1,0:T(8,128)(2,1)S(1)} %pad_maximum_fusion.1), channel_id=1, source_target_pairs={{0,32},{16,112},{32,64},{48,16},{64,96},{80,48},{96,0},{112,80},{1... | collective-permute-start | bytes 3538952 | tf_op jit(solution)/shard_map/ppermute | solution.py:45
  49.7 2.8 %collective-permute-done.16 = bf16[128,1536]{1,0:T(8,128)(2,1)S(1)} collective-permute-done((bf16[128,1536]{1,0:T(8,128)(2,1)S(1)}, bf16[128,1536]{1,0:T(8,128)(2,1)S(1)}, u32[]{:S(2)}, u32[]{:S(2)}) %collective-permute-start.16) | collective-permute-done | bytes 393248 | tf_op jit(solution)/shard_map/ppermute | solution.py:36
  52.5 10.1 %collective-permute-done.15 = bf16[384,1536]{1,0:T(8,128)(2,1)S(1)} collective-permute-done((bf16[384,1536]{1,0:T(8,128)(2,1)S(1)}, bf16[384,1536]{1,0:T(8,128)(2,1)S(1)}, u32[]{:S(2)}, u32[]{:S(2)}) %collective-permute-start.15) | collective-permute-done | bytes 1179680 | tf_op jit(solution)/shard_map/ppermute | solution.py:45
  62.8 2.7 %collective-permute-start.27 = (bf16[192,1536]{1,0:T(8,128)(2,1)S(1)}, bf16[192,1536]{1,0:T(8,128)(2,1)S(1)}, u32[]{:S(2)}, u32[]{:S(2)}) collective-permute-start(bf16[192,1536]{1,0:T(8,128)(2,1)S(1)} %pad_maximum_fusion.4), channel_id=1, source_target_pairs={{0,136},{128,0},{8,128},{136,8},{1,137},{129,1},{9,129},{137,9},{2... | collective-permute-start | bytes 1769480 | tf_op jit(solution)/shard_map/ppermute | solution.py:36
  65.5 2.7 %collective-permute-start.19 = (bf16[32,1536]{1,0:T(8,128)(2,1)S(1)}, bf16[32,1536]{1,0:T(8,128)(2,1)S(1)}, u32[]{:S(2)}, u32[]{:S(2)}) collective-permute-start(bf16[32,1536]{1,0:T(8,128)(2,1)S(1)} %get-tuple-element.96), channel_id=1, source_target_pairs={{0,7},{1,0},{2,1},{3,2},{4,3},{5,4},{6,5},{7,6},{8,15},{9,8},{10,9... | collective-permute-start | bytes 294920 | tf_op jit(solution)/shard_map/ppermute | solution.py:29
  68.2 3.2 %collective-permute-start.20 = (bf16[128,1536]{1,0:T(8,128)(2,1)S(1)}, bf16[128,1536]{1,0:T(8,128)(2,1)S(1)}, u32[]{:S(2)}, u32[]{:S(2)}) collective-permute-start(bf16[128,1536]{1,0:T(8,128)(2,1)S(1)} %slice.99), channel_id=1, source_target_pairs={{0,32},{16,112},{32,64},{48,16},{64,96},{80,48},{96,0},{112,80},{1... | collective-permute-start | bytes 1179656 | tf_op jit(solution)/shard_map/ppermute | solution.py:45
  71.8 4.3 %collective-permute-done.20 = bf16[128,1536]{1,0:T(8,128)(2,1)S(1)} collective-permute-done((bf16[128,1536]{1,0:T(8,128)(2,1)S(1)}, bf16[128,1536]{1,0:T(8,128)(2,1)S(1)}, u32[]{:S(2)}, u32[]{:S(2)}) %collective-permute-start.20) | collective-permute-done | bytes 393248 | tf_op jit(solution)/shard_map/ppermute | solution.py:45
  76.2 8.9 %collective-permute-start.22 = (bf16[768,1536]{1,0:T(8,128)(2,1)S(1)}, bf16[768,1536]{1,0:T(8,128)(2,1)S(1)}, u32[]{:S(2)}, u32[]{:S(2)}) collective-permute-start(bf16[768,1536]{1,0:T(8,128)(2,1)S(1)} %pad_maximum_fusion), channel_id=1, source_target_pairs={{0,16},{16,0},{1,17},{17,1},{2,18},{18,2},{3,19},{19,3},{4,20},{20... | collective-permute-start | bytes 7077896 | tf_op jit(solution)/shard_map/ppermute | solution.py:49
  85.2 6.4 %shard_map.50 = (f32[512,1536]{1,0:T(8,128)S(1)}, bf16[512,1536]{1,0:T(8,128)(2,1)S(1)}) custom-call(bf16[1024,1536]{1,0:T(8,128)(2,1)S(1)} %get-tuple-element.115.grads_ref, bf16[1536,1536]{1,0:T(8,128)(2,1)S(1)} %bitcast.1), custom_call_target="tpu_custom_call" | custom-call | flops 4831838208 | bytes 13631488 | tf_op jit(solution)/shard_map/pallas_call | solution.py:74
  92.1 3.1 %collective-permute-done.21 = bf16[512,1536]{1,0:T(8,128)(2,1)S(1)} collective-permute-done((bf16[512,1536]{1,0:T(8,128)(2,1)S(1)}, bf16[512,1536]{1,0:T(8,128)(2,1)S(1)}, u32[]{:S(2)}, u32[]{:S(2)}) %collective-permute-start.21) | collective-permute-done | bytes 1572896 | tf_op jit(solution)/shard_map/ppermute | solution.py:49
  96.7 2.3 %collective-permute-start.25 = (bf16[128,1536]{1,0:T(8,128)(2,1)S(1)}, bf16[128,1536]{1,0:T(8,128)(2,1)S(1)}, u32[]{:S(2)}, u32[]{:S(2)}) collective-permute-start(bf16[128,1536]{1,0:T(8,128)(2,1)S(1)} %get-tuple-element.55), channel_id=1, source_target_pairs={{0,96},{32,0},{64,32},{96,64},{1,97},{33,1},{65,33},{97,65},{2,98}... | collective-permute-start | bytes 1179656 | tf_op jit(solution)/shard_map/ppermute | solution.py:40
  99.1 13.0 %shard_map.51 = bf16[1536,1536]{1,0:T(8,128)(2,1)} custom-call(bf16[2048,1536]{1,0:T(8,128)(2,1)S(1)} %constant_dynamic-update-slice_fusion.15.grads_ref, bf16[2048,1536]{1,0:T(8,128)(2,1)S(1)} %constant_dynamic-update-slice_fusion.33.acts_ref), custom_call_target="tpu_custom_call" | custom-call | flops 9663676416 | bytes 17825792 | tf_op jit(solution)/shard_map/pallas_call | solution.py:115
  112.1 4.4 %collective-permute-done.24 = bf16[128,1536]{1,0:T(8,128)(2,1)S(1)} collective-permute-done((bf16[128,1536]{1,0:T(8,128)(2,1)S(1)}, bf16[128,1536]{1,0:T(8,128)(2,1)S(1)}, u32[]{:S(2)}, u32[]{:S(2)}) %collective-permute-start.24) | collective-permute-done | bytes 393248 | tf_op jit(solution)/shard_map/ppermute | solution.py:40
  116.6 1.5 %fusion.7 = bf16[128,1536]{1,0:T(8,128)(2,1)} fusion(bf16[128,1536]{1,0:T(8,128)(2,1)S(1)} %copy-done, bf16[128,1536]{1,0:T(8,128)(2,1)S(1)} %collective-permute-done.23, bf16[128,1536]{1,0:T(8,128)(2,1)S(1)} %collective-permute-done.25, bf16[128,1536]{1,0:T(8,128)(2,1)S(1)} %collective-permute-done.24, f32[512,1536]{1,0:T(8,128)S(1)} %get-tuple-element.50, ...), kind=kLoop, calls=%fused_computation.16 | loop fusion | flops 5505024 | bytes 3145728 | tf_op jit(solution)/shard_map/convert_element_type | solution.py:184
  (78 shorter events, 4.4 us)
Async XLA Ops:
  1.9 14.9 %collective-permute-start = (bf16[128,1536]{1,0:T(8,128)(2,1)S(1)}, bf16[128,1536]{1,0:T(8,128)(2,1)S(1)}, u32[]{:S(2)}, u32[]{:S(2)}) collective-permute-start(bf16[128,1536]{1,0:T(8,128)(2,1)S(1)} %fusion.2), channel_id=1, source_target_pairs={{0,16},{16,0},{1,17},{17,1},{2,18},{18,2},{3,19},{19,3},{4,20},{20... | collective-permute-start | bytes 1179656 | tf_op jit(solution)/shard_map/ppermute | solution.py:49
  5.2 9.2 %collective-permute-start.1 = (bf16[64,1536]{1,0:T(8,128)(2,1)}, bf16[64,1536]{1,0:T(8,128)(2,1)S(1)}, u32[]{:S(2)}, u32[]{:S(2)}) collective-permute-start(bf16[64,1536]{1,0:T(8,128)(2,1)} %param.4), channel_id=1, source_target_pairs={{0,1},{1,2},{2,3},{3,4},{4,5},{5,6},{6,7},{7,0},{8,9},{9,10},{10,1... | collective-permute-start | bytes 589832 | tf_op jit(solution)/shard_map/ppermute | solution.py:29
  5.2 9.2 %collective-permute-start.2 = (bf16[64,1536]{1,0:T(8,128)(2,1)}, bf16[64,1536]{1,0:T(8,128)(2,1)S(1)}, u32[]{:S(2)}, u32[]{:S(2)}) collective-permute-start(bf16[64,1536]{1,0:T(8,128)(2,1)} %param.4), channel_id=1, source_target_pairs={{0,7},{1,0},{2,1},{3,2},{4,3},{5,4},{6,5},{7,6},{8,15},{9,8},{10,9... | collective-permute-start | bytes 589832 | tf_op jit(solution)/shard_map/ppermute | solution.py:29
  9.1 7.7 %collective-permute-start.3 = (bf16[64,1536]{1,0:T(8,128)(2,1)}, bf16[64,1536]{1,0:T(8,128)(2,1)S(1)}, u32[]{:S(2)}, u32[]{:S(2)}) collective-permute-start(bf16[64,1536]{1,0:T(8,128)(2,1)} %param.4), channel_id=1, source_target_pairs={{0,8},{128,136},{8,0},{136,128},{1,9},{129,137},{9,1},{137,129},{2... | collective-permute-start | bytes 589832 | tf_op jit(solution)/shard_map/ppermute | solution.py:36
  16.9 10.6 %collective-permute-start.4 = (bf16[128,1536]{1,0:T(8,128)(2,1)S(1)}, bf16[128,1536]{1,0:T(8,128)(2,1)S(1)}, u32[]{:S(2)}, u32[]{:S(2)}) collective-permute-start(bf16[128,1536]{1,0:T(8,128)(2,1)S(1)} %get-tuple-element.113), channel_id=1, source_target_pairs={{0,1},{1,2},{2,3},{3,4},{4,5},{5,6},{6,7},{7,0},{8,9},{9,10},{10,1... | collective-permute-start | bytes 1179656 | tf_op jit(solution)/shard_map/ppermute | solution.py:29
  17.0 13.0 %collective-permute-start.5 = (bf16[128,1536]{1,0:T(8,128)(2,1)S(1)}, bf16[128,1536]{1,0:T(8,128)(2,1)S(1)}, u32[]{:S(2)}, u32[]{:S(2)}) collective-permute-start(bf16[128,1536]{1,0:T(8,128)(2,1)S(1)} %get-tuple-element.112), channel_id=1, source_target_pairs={{0,7},{1,0},{2,1},{3,2},{4,3},{5,4},{6,5},{7,6},{8,15},{9,8},{10,9... | collective-permute-start | bytes 1179656 | tf_op jit(solution)/shard_map/ppermute | solution.py:29
  19.6 10.3 %collective-permute-start.6 = (bf16[128,1536]{1,0:T(8,128)(2,1)S(1)}, bf16[128,1536]{1,0:T(8,128)(2,1)S(1)}, u32[]{:S(2)}, u32[]{:S(2)}) collective-permute-start(bf16[128,1536]{1,0:T(8,128)(2,1)S(1)} %fusion.2), channel_id=1, source_target_pairs={{0,128},{128,0},{1,129},{129,1},{2,130},{130,2},{3,131},{131,3},{4... | collective-permute-start | bytes 1179656 | tf_op jit(solution)/shard_map/ppermute | solution.py:49
  20.9 11.7 %collective-permute-start.7 = (bf16[256,1536]{1,0:T(8,128)(2,1)S(1)}, bf16[256,1536]{1,0:T(8,128)(2,1)S(1)}, u32[]{:S(2)}, u32[]{:S(2)}) collective-permute-start(bf16[256,1536]{1,0:T(8,128)(2,1)S(1)} %pad_maximum_fusion.2), channel_id=1, source_target_pairs={{0,32},{16,112},{32,64},{48,16},{64,96},{80,48},{96,0},{112,80},{1... | collective-permute-start | bytes 2359304 | tf_op jit(solution)/shard_map/ppermute | solution.py:45
  23.8 17.4 %collective-permute-start.10 = (bf16[192,1536]{1,0:T(8,128)(2,1)S(1)}, bf16[192,1536]{1,0:T(8,128)(2,1)S(1)}, u32[]{:S(2)}, u32[]{:S(2)}) collective-permute-start(bf16[192,1536]{1,0:T(8,128)(2,1)S(1)} %get-tuple-element.105), channel_id=1, source_target_pairs={{0,128},{128,8},{8,136},{136,0},{1,129},{129,9},{9,137},{137,1},{2... | collective-permute-start | bytes 1769480 | tf_op jit(solution)/shard_map/ppermute | solution.py:36
  27.5 16.3 %collective-permute-start.11 = (bf16[192,1536]{1,0:T(8,128)(2,1)S(1)}, bf16[192,1536]{1,0:T(8,128)(2,1)S(1)}, u32[]{:S(2)}, u32[]{:S(2)}) collective-permute-start(bf16[192,1536]{1,0:T(8,128)(2,1)S(1)} %get-tuple-element.105), channel_id=1, source_target_pairs={{0,136},{128,0},{8,128},{136,8},{1,137},{129,1},{9,129},{137,9},{2... | collective-permute-start | bytes 1769480 | tf_op jit(solution)/shard_map/ppermute | solution.py:36
  32.6 11.1 %collective-permute-start.8 = (bf16[128,1536]{1,0:T(8,128)(2,1)S(1)}, bf16[128,1536]{1,0:T(8,128)(2,1)S(1)}, u32[]{:S(2)}, u32[]{:S(2)}) collective-permute-start(bf16[128,1536]{1,0:T(8,128)(2,1)S(1)} %collective-permute-done.4), channel_id=1, source_target_pairs={{0,1},{1,2},{2,3},{3,4},{4,5},{5,6},{6,7},{7,0},{8,9},{9,10},{10,1... | collective-permute-start | bytes 1179656 | tf_op jit(solution)/shard_map/ppermute | solution.py:29
  32.6 11.1 %collective-permute-start.9 = (bf16[128,1536]{1,0:T(8,128)(2,1)S(1)}, bf16[128,1536]{1,0:T(8,128)(2,1)S(1)}, u32[]{:S(2)}, u32[]{:S(2)}) collective-permute-start(bf16[128,1536]{1,0:T(8,128)(2,1)S(1)} %collective-permute-done.5), channel_id=1, source_target_pairs={{0,7},{1,0},{2,1},{3,2},{4,3},{5,4},{6,5},{7,6},{8,15},{9,8},{10,9... | collective-permute-start | bytes 1179656 | tf_op jit(solution)/shard_map/ppermute | solution.py:29
  35.3 5.6 %collective-permute-start.12 = (bf16[128,1536]{1,0:T(8,128)(2,1)S(1)}, bf16[128,1536]{1,0:T(8,128)(2,1)S(1)}, u32[]{:S(2)}, u32[]{:S(2)}) collective-permute-start(bf16[128,1536]{1,0:T(8,128)(2,1)S(1)} %collective-permute-done.6), channel_id=1, source_target_pairs={{0,16},{16,0},{1,17},{17,1},{2,18},{18,2},{3,19},{19,3},{4,20},{20... | collective-permute-start | bytes 1179656 | tf_op jit(solution)/shard_map/ppermute | solution.py:49
  40.9 11.5 %collective-permute-start.16 = (bf16[128,1536]{1,0:T(8,128)(2,1)S(1)}, bf16[128,1536]{1,0:T(8,128)(2,1)S(1)}, u32[]{:S(2)}, u32[]{:S(2)}) collective-permute-start(bf16[128,1536]{1,0:T(8,128)(2,1)S(1)} %pad_maximum_fusion.7), channel_id=1, source_target_pairs={{0,128},{128,8},{8,136},{136,0},{1,129},{129,9},{9,137},{137,1},{2... | collective-permute-start | bytes 1179656 | tf_op jit(solution)/shard_map/ppermute | solution.py:36
  41.2 11.2 %collective-permute-start.17 = (bf16[128,1536]{1,0:T(8,128)(2,1)S(1)}, bf16[128,1536]{1,0:T(8,128)(2,1)S(1)}, u32[]{:S(2)}, u32[]{:S(2)}) collective-permute-start(bf16[128,1536]{1,0:T(8,128)(2,1)S(1)} %pad_maximum_fusion.7), channel_id=1, source_target_pairs={{0,136},{128,0},{8,128},{136,8},{1,137},{129,1},{9,129},{137,9},{2... | collective-permute-start | bytes 1179656 | tf_op jit(solution)/shard_map/ppermute | solution.py:36
  43.8 8.7 %collective-permute-start.13 = (bf16[96,1536]{1,0:T(8,128)(2,1)S(1)}, bf16[96,1536]{1,0:T(8,128)(2,1)S(1)}, u32[]{:S(2)}, u32[]{:S(2)}) collective-permute-start(bf16[96,1536]{1,0:T(8,128)(2,1)S(1)} %slice.86), channel_id=1, source_target_pairs={{0,1},{1,2},{2,3},{3,4},{4,5},{5,6},{6,7},{7,0},{8,9},{9,10},{10,1... | collective-permute-start | bytes 884744 | tf_op jit(solution)/shard_map/ppermute | solution.py:29
  44.1 8.4 %collective-permute-start.14 = (bf16[96,1536]{1,0:T(8,128)(2,1)S(1)}, bf16[96,1536]{1,0:T(8,128)(2,1)S(1)}, u32[]{:S(2)}, u32[]{:S(2)}) collective-permute-start(bf16[96,1536]{1,0:T(8,128)(2,1)S(1)} %slice.87), channel_id=1, source_target_pairs={{0,7},{1,0},{2,1},{3,2},{4,3},{5,4},{6,5},{7,6},{8,15},{9,8},{10,9... | collective-permute-start | bytes 884744 | tf_op jit(solution)/shard_map/ppermute | solution.py:29
  46.9 15.7 %collective-permute-start.15 = (bf16[384,1536]{1,0:T(8,128)(2,1)S(1)}, bf16[384,1536]{1,0:T(8,128)(2,1)S(1)}, u32[]{:S(2)}, u32[]{:S(2)}) collective-permute-start(bf16[384,1536]{1,0:T(8,128)(2,1)S(1)} %pad_maximum_fusion.1), channel_id=1, source_target_pairs={{0,32},{16,112},{32,64},{48,16},{64,96},{80,48},{96,0},{112,80},{1... | collective-permute-start | bytes 3538952 | tf_op jit(solution)/shard_map/ppermute | solution.py:45
  62.7 29.2 %collective-permute-start.26 = (bf16[192,1536]{1,0:T(8,128)(2,1)S(1)}, bf16[192,1536]{1,0:T(8,128)(2,1)S(1)}, u32[]{:S(2)}, u32[]{:S(2)}) collective-permute-start(bf16[192,1536]{1,0:T(8,128)(2,1)S(1)} %pad_maximum_fusion.4), channel_id=1, source_target_pairs={{0,128},{128,8},{8,136},{136,0},{1,129},{129,9},{9,137},{137,1},{2... | collective-permute-start | bytes 1769480 | tf_op jit(solution)/shard_map/ppermute | solution.py:36
  62.8 29.2 %collective-permute-start.27 = (bf16[192,1536]{1,0:T(8,128)(2,1)S(1)}, bf16[192,1536]{1,0:T(8,128)(2,1)S(1)}, u32[]{:S(2)}, u32[]{:S(2)}) collective-permute-start(bf16[192,1536]{1,0:T(8,128)(2,1)S(1)} %pad_maximum_fusion.4), channel_id=1, source_target_pairs={{0,136},{128,0},{8,128},{136,8},{1,137},{129,1},{9,129},{137,9},{2... | collective-permute-start | bytes 1769480 | tf_op jit(solution)/shard_map/ppermute | solution.py:36
  65.5 6.3 %collective-permute-start.18 = (bf16[32,1536]{1,0:T(8,128)(2,1)S(1)}, bf16[32,1536]{1,0:T(8,128)(2,1)S(1)}, u32[]{:S(2)}, u32[]{:S(2)}) collective-permute-start(bf16[32,1536]{1,0:T(8,128)(2,1)S(1)} %get-tuple-element.92), channel_id=1, source_target_pairs={{0,1},{1,2},{2,3},{3,4},{4,5},{5,6},{6,7},{7,0},{8,9},{9,10},{10,1... | collective-permute-start | bytes 294920 | tf_op jit(solution)/shard_map/ppermute | solution.py:29
  65.5 6.3 %collective-permute-start.19 = (bf16[32,1536]{1,0:T(8,128)(2,1)S(1)}, bf16[32,1536]{1,0:T(8,128)(2,1)S(1)}, u32[]{:S(2)}, u32[]{:S(2)}) collective-permute-start(bf16[32,1536]{1,0:T(8,128)(2,1)S(1)} %get-tuple-element.96), channel_id=1, source_target_pairs={{0,7},{1,0},{2,1},{3,2},{4,3},{5,4},{6,5},{7,6},{8,15},{9,8},{10,9... | collective-permute-start | bytes 294920 | tf_op jit(solution)/shard_map/ppermute | solution.py:29
  68.2 7.9 %collective-permute-start.20 = (bf16[128,1536]{1,0:T(8,128)(2,1)S(1)}, bf16[128,1536]{1,0:T(8,128)(2,1)S(1)}, u32[]{:S(2)}, u32[]{:S(2)}) collective-permute-start(bf16[128,1536]{1,0:T(8,128)(2,1)S(1)} %slice.99), channel_id=1, source_target_pairs={{0,32},{16,112},{32,64},{48,16},{64,96},{80,48},{96,0},{112,80},{1... | collective-permute-start | bytes 1179656 | tf_op jit(solution)/shard_map/ppermute | solution.py:45
  71.4 13.7 %slice-start = ((s8[4718592]{0:T(1024)(128)(4,1)}), s8[4194304]{0:T(1024)(128)(4,1)S(1)}, s32[]{:S(2)}) async-start(s8[4718592]{0:T(1024)(128)(4,1)} %bitcast), calls=%async_computation | async-start | bytes 8388608
  71.6 13.6 %slice-start.1 = ((s8[4718592]{0:T(1024)(128)(4,1)}), s8[524288]{0:T(1024)(128)(4,1)S(1)}, s32[]{:S(2)}) async-start(s8[4718592]{0:T(1024)(128)(4,1)} %bitcast), calls=%async_computation.1 | async-start | bytes 1048576
  76.2 19.2 %collective-permute-start.22 = (bf16[768,1536]{1,0:T(8,128)(2,1)S(1)}, bf16[768,1536]{1,0:T(8,128)(2,1)S(1)}, u32[]{:S(2)}, u32[]{:S(2)}) collective-permute-start(bf16[768,1536]{1,0:T(8,128)(2,1)S(1)} %pad_maximum_fusion), channel_id=1, source_target_pairs={{0,16},{16,0},{1,17},{17,1},{2,18},{18,2},{3,19},{19,3},{4,20},{20... | collective-permute-start | bytes 7077896 | tf_op jit(solution)/shard_map/ppermute | solution.py:49
  91.6 3.5 %collective-permute-start.21 = (bf16[512,1536]{1,0:T(8,128)(2,1)S(1)}, bf16[512,1536]{1,0:T(8,128)(2,1)S(1)}, u32[]{:S(2)}, u32[]{:S(2)}) collective-permute-start(bf16[512,1536]{1,0:T(8,128)(2,1)S(1)} %get-tuple-element.51), channel_id=1, source_target_pairs={{0,16},{16,0},{1,17},{17,1},{2,18},{18,2},{3,19},{19,3},{4,20},{20... | collective-permute-start | bytes 4718600 | tf_op jit(solution)/shard_map/ppermute | solution.py:49
  95.5 16.6 %collective-permute-start.23 = (bf16[128,1536]{1,0:T(8,128)(2,1)S(1)}, bf16[128,1536]{1,0:T(8,128)(2,1)S(1)}, u32[]{:S(2)}, u32[]{:S(2)}) collective-permute-start(bf16[128,1536]{1,0:T(8,128)(2,1)S(1)} %get-tuple-element.53), channel_id=1, source_target_pairs={{0,64},{32,96},{64,0},{96,32},{1,65},{33,97},{65,1},{97,33},{2,66}... | collective-permute-start | bytes 1179656 | tf_op jit(solution)/shard_map/ppermute | solution.py:40
  96.3 20.3 %collective-permute-start.24 = (bf16[128,1536]{1,0:T(8,128)(2,1)S(1)}, bf16[128,1536]{1,0:T(8,128)(2,1)S(1)}, u32[]{:S(2)}, u32[]{:S(2)}) collective-permute-start(bf16[128,1536]{1,0:T(8,128)(2,1)S(1)} %get-tuple-element.54), channel_id=1, source_target_pairs={{0,32},{32,64},{64,96},{96,0},{1,33},{33,65},{65,97},{97,1},{2,34}... | collective-permute-start | bytes 1179656 | tf_op jit(solution)/shard_map/ppermute | solution.py:40
  96.7 19.9 %collective-permute-start.25 = (bf16[128,1536]{1,0:T(8,128)(2,1)S(1)}, bf16[128,1536]{1,0:T(8,128)(2,1)S(1)}, u32[]{:S(2)}, u32[]{:S(2)}) collective-permute-start(bf16[128,1536]{1,0:T(8,128)(2,1)S(1)} %get-tuple-element.55), channel_id=1, source_target_pairs={{0,96},{32,0},{64,32},{96,64},{1,97},{33,1},{65,33},{97,65},{2,98}... | collective-permute-start | bytes 1179656 | tf_op jit(solution)/shard_map/ppermute | solution.py:40
  99.1 17.4 %copy-start = (bf16[128,1536]{1,0:T(8,128)(2,1)S(1)}, bf16[128,1536]{1,0:T(8,128)(2,1)}, u32[]{:S(2)}) copy-start(bf16[128,1536]{1,0:T(8,128)(2,1)} %param.3) | copy-start | bytes 1179652

commit v4 on v3

--- a/solution.py
+++ b/solution.py
@@ -56,31 +56,65 @@
 OWN = [0, -1, 1, -2, 2, -3, 3, 4]
 
 
-def partial_kernel(grads_ref, w_ref, mine_ref, other_ref, held):
+VMEM = pl.BlockSpec(memory_space=pltpu.VMEM)
+EARLY = [(0, k) for k in range(7)] + [(1, k) for k in range(5)]
+LATE = [(0, 7), (1, 5), (1, 6), (1, 7)]
+
+
+def early_kernel(grads_ref, w_ref, out_ref):
+    out_ref[...] = jnp.dot(grads_ref[...], w_ref[...], preferred_element_type=F32)
+
+
+def early_partial(grads, weight):
+    step = 512
+    count = 64 * len(EARLY)
+    return pl.pallas_call(
+        early_kernel,
+        grid=(1536 // step,),
+        in_specs=[pl.BlockSpec((count, 1536), lambda n: (0, 0)), pl.BlockSpec((1536, step), lambda n: (0, n))],
+        out_specs=pl.BlockSpec((count, step), lambda n: (0, n)),
+        out_shape=jax.ShapeDtypeStruct((count, 1536), F32),
+        compiler_params=pltpu.CompilerParams(vmem_limit_bytes=24 << 20),
+        cost_estimate=pl.CostEstimate(flops=2 * count * 1536 * 1536, bytes_accessed=12 << 20, transcendentals=0),
+    )(grads, weight)
+
+
+def late_kernel(early_ref, grads_ref, w_ref, mine_ref, other_ref, late):
     y, c, xh, z = (lax.axis_index(a) for a in ("y", "c", "xh", "z"))
-    held_new = jnp.dot(grads_ref[...], w_ref[...], preferred_element_type=F32)
-    for k in range(16):
-        xp = xh if k < 8 else 1 - xh
-        zp = lax.rem(z + OWN[k % 8] + 8, 8)
-        yp, cp = 2 * xp + zp // 4, lax.rem(zp // 2, 2)
-        spot = lax.rem(cp + c, 2) * 512 + lax.rem(yp + 4 - y, 4) * 128 + lax.rem(zp, 2) * 64
-        held[pl.ds(pl.multiple_of(spot, 64), 64), :] = held_new[64 * k : 64 * k + 64]
-    mine_ref[...] = held[:512]
-    other_ref[...] = held[512:].astype(BF)
-
-
-def partial_grad(grads, weight):
-    step = 512
+
+    def place(source, which):
+        for k, (far, j) in enumerate(which):
+            xp = 1 - xh if far else xh
+            zp = lax.rem(z + OWN[j] + 8, 8)
+            yp, cp = 2 * xp + zp // 4, lax.rem(zp // 2, 2)
+            start = pl.multiple_of(lax.rem(yp + 4 - y, 4) * 128 + lax.rem(zp, 2) * 64, 64)
+
+            @pl.when(cp == c)
+            def _():
+                mine_ref[pl.ds(start, 64), :] = source[64 * k : 64 * k + 64, :]
+
+            @pl.when(cp != c)
+            def _():
+                other_ref[pl.ds(start, 64), :] = source[64 * k : 64 * k + 64, :].astype(BF)
+
+    for n in range(3):
+        late[:, 512 * n : 512 * n + 512] = jnp.dot(
+            grads_ref[...], w_ref[:, 512 * n : 512 * n + 512], preferred_element_type=F32
+        )
+    place(early_ref, EARLY)
+    place(late, LATE)
+
+
+def late_partial(early, grads, weight):
     return pl.pallas_call(
-        partial_kernel,
-        grid=(1536 // step,),
-        in_specs=[pl.BlockSpec((1024, 1536), lambda n: (0, 0)), pl.BlockSpec((1536, step), lambda n: (0, n))],
-        out_specs=[pl.BlockSpec((512, step), lambda n: (0, n))] * 2,
+        late_kernel,
+        in_specs=[VMEM] * 3,
+        out_specs=[VMEM] * 2,
         out_shape=[jax.ShapeDtypeStruct((512, 1536), F32), jax.ShapeDtypeStruct((512, 1536), BF)],
-        scratch_shapes=[pltpu.VMEM((1024, step), F32)],
-        compiler_params=pltpu.CompilerParams(vmem_limit_bytes=28 << 20),
-        cost_estimate=pl.CostEstimate(flops=2 * 1024 * 1536 * 1536, bytes_accessed=13 << 20, transcendentals=0),
-    )(grads, weight)
+        scratch_shapes=[pltpu.VMEM((256, 1536), F32)],
+        compiler_params=pltpu.CompilerParams(vmem_limit_bytes=32 << 20),
+        cost_estimate=pl.CostEstimate(flops=2 * 256 * 1536 * 1536, bytes_accessed=8 << 20, transcendentals=0),
+    )(early, grads, weight)
 
 
 def weight_kernel(grads_ref, acts_ref, out_ref, acts):
@@ -144,39 +178,46 @@
     near = jnp.concatenate([g, up1, down1])
     left_a, right_a = along_x(near, 1), along_x(near, -1)
     other_chip = jnp.concatenate([other_rep, swap(other_rep, "c")])
-    hop_2 = round_y(jnp.concatenate([hop_1[:128], other_chip]))
-    up3, down3, left_a, right_a, other_chip = tie(up3, down3, left_a, right_a, other_chip)
+    hop_2 = round_y(hop_1[:128])
+    up3, down3, left_a, right_a, other_chip, hop_2 = tie(up3, down3, left_a, right_a, other_chip, hop_2)
 
     up4, down4 = along_z(up3[:96], 1), along_z(down3[32:], -1)
     middle = jnp.concatenate([up2[64:], down2[:64]])
     left_b, right_b = along_x(middle, 1), along_x(middle, -1)
-    up4, down4, hop_2, left_b, right_b = tie(up4, down4, hop_2, left_b, right_b)
+    hop_3 = round_y(other_chip)
+    up4, down4, left_b, right_b, hop_3 = tie(up4, down4, left_b, right_b, hop_3)
+    own = [g, up1, down1, up2[64:], down2[:64], up3[64:], down3[:64]]
+    second = [far, up2[:64], down2[64:], up3[:64], down3[64:]]
+    grads_early = jnp.concatenate(own + second)
+    early = early_partial(grads_early, down_weight)
 
     up5, down5 = along_z(up4[:32], 1), along_z(down4[64:], -1)
     last = jnp.concatenate([up4[64:], down4[:32]])
-    hop_3 = round_y(hop_2[128:256])
-    up5, down5, hop_3 = tie(up5, down5, hop_3)
-
-    own = [g, up1, down1, up2[64:], down2[:64], up3[64:], down3[:64], last]
-    second = [far, up2[:64], down2[64:], up3[:64], down3[64:], up4[:64], down4[32:], up5, down5]
-    grads_own = jnp.concatenate(own + second)
-
-    mine, other = partial_grad(grads_own, down_weight)
+    hop_4 = round_y(hop_3[:128])
+    third = jnp.concatenate([up3[64:], down3[:64]])
+    left_c, right_c = along_x(third, 1), along_x(third, -1)
+    up5, down5, early, hop_4 = tie(up5, down5, early, hop_4)
+
+    grads_late = jnp.concatenate([last, up4[:64], down4[32:], up5, down5])
+    mine, other = late_partial(early, grads_late, down_weight)
+    mine, other, left_c, right_c = tie(mine, other, left_c, right_c)
     other = swap(other, "c")
-    third = jnp.concatenate([up3[64:], down3[:64], last])
-    left_c, right_c = along_x(third, 1), along_x(third, -1)
-    came = jnp.concatenate([hop_1, hop_2, hop_3])
+    came = jnp.concatenate([hop_1, hop_2, hop_3, hop_4])
     swapped = swap(came, "c")
 
     def summed(block):
         return mine[128 * block : 128 * block + 128] + other[128 * block : 128 * block + 128].astype(F32)
 
     to_above, to_below, to_across = summed(1).astype(BF), summed(3).astype(BF), summed(2).astype(BF)
-    to_above, to_below, to_across, swapped = tie(to_above, to_below, to_across, swapped)
+    to_above, to_below, to_across, swapped, last = tie(to_above, to_below, to_across, swapped, last)
+    left_d, right_d = along_x(last, 1), along_x(last, -1)
     from_across = along_y(to_across, 2)
     from_below, from_above = along_y(to_above, 1), along_y(to_below, -1)
 
-    grads = jnp.concatenate([grads_own, left_a, left_b, left_c, right_a, right_b, right_c])
+    grads = jnp.concatenate(
+        [grads_early[:448], last, grads_early[448:], grads_late[64:], left_a, left_b, left_c, left_d]
+        + [right_a, right_b, right_c, right_d]
+    )
     acts = jnp.concatenate([chip, other_chip, came, swapped])
     weight_grad = weight_gradient(grads, acts)
     from_across, from_below, from_above, weight_grad = tie(from_across, from_below, from_above, weight_grad)

time: 118 us -> 127 us (1.076)
  local copies, waits for them, and re-layouts: 2.27 us -> 25.9 us
  waiting for transfers between devices: 35.9 us -> 24.6 us
  starting transfers between devices: 55.8 us -> 50.3 us
  other arithmetic: 3.54 us -> 5.2 us
    unnamed x31 -> x58, local copies, waits for them, and re-layouts: 1.85 us -> 23.6 us
    ppermute x3 -> x4, waiting for transfers between devices: 17.2 us -> 6.26 us  [round_y(): lax.ppermute(a, ('y', 'c'), [(s[0] * C + s[1], t[0] * C + t[1]) for s, t...]
    ppermute x3, waiting for transfers between devices: 4.44 us -> 0.01 us  [along_y(): return lax.ppermute(a, 'y', [(i, (i + d) % Y) for i in range(Y)])]
    ppermute x3 -> x4, starting transfers between devices: 8.58 us -> 4.83 us  [round_y(): lax.ppermute(a, ('y', 'c'), [(s[0] * C + s[1], t[0] * C + t[1]) for s, t...]
    ppermute x10, waiting for transfers between devices: 4.92 us -> 8.45 us  [along_z(): return lax.ppermute(a, 'z', [(i, (i + d) % Z) for i in range(Z)])]
    ppermute x5, starting transfers between devices: 17.8 us -> 14.6 us  [swap(): return lax.ppermute(a, axis, [(0, 1), (1, 0)])]
    ppermute x7 -> x9, starting transfers between devices: 11.1 us -> 13.4 us  [along_x(): lax.ppermute(a, ('xl', 'xh'), [(place(x), place((x + d) % 4)) for x in ra...]
    ppermute x7 -> x9, waiting for transfers between devices: 5.12 us -> 7 us  [along_x(): lax.ppermute(a, ('xl', 'xh'), [(place(x), place((x + d) % 4)) for x in ra...]
  transfers between devices with their start and end apart: 28 -> 31, of which waited for: 10 -> 8; matrix products, arithmetic and copies ran while one was open for 2% -> 20% of each run, Pallas kernels for 16% -> 16%
where the time goes in v4:
time: 127 us
  starting transfers between devices  50.3 us (40%)
  local copies, waits for them, and re-layouts  25.9 us (20%)
  waiting for transfers between devices  24.6 us (19%)
  Pallas kernels  19.7 us (16%)
  other arithmetic  5.2 us (4%)
    unnamed x58, local copies, waits for them, and re-layouts  23.6 us
    ppermute x10, starting transfers between devices, along_z(): return lax.ppermute(a, 'z', [(i, (i + d) % Z) for i in range(Z)])  14.8 us
    ppermute x5, starting transfers between devices, swap(): return lax.ppermute(a, axis, [(0, 1), (1, 0)])  14.6 us
    ppermute x9, starting transfers between devices, along_x(): lax.ppermute(a, ('xl', 'xh'), [(place(x), place((x + d) % 4)) for x in ra...  13.4 us
    pallas_call x1, Pallas kernels, weight_gradient(): pl.pallas_call(weight_kernel, grid=(1536 // step,), in_specs=[pl.BlockSpe...  13 us
    ppermute x10, waiting for transfers between devices, along_z(): return lax.ppermute(a, 'z', [(i, (i + d) % Z) for i in range(Z)])  8.45 us
    ppermute x9, waiting for transfers between devices, along_x(): lax.ppermute(a, ('xl', 'xh'), [(place(x), place((x + d) % 4)) for x in ra...  7 us
    ppermute x4, waiting for transfers between devices, round_y(): lax.ppermute(a, ('y', 'c'), [(s[0] * C + s[1], t[0] * C + t[1]) for s, t...  6.26 us
  transfers between devices with their start and end apart: 31, of which 8 were waited for; matrix products, arithmetic and copies ran while one was open for 20% of the time, Pallas kernels for 16%

profile of v4, /device:TPU:1, one launch (start us, length us, event | category | flops | bytes accessed | tf_op | source)
XLA Modules:
  0.0 126.8 jit_solution(4252502818884593996)
XLA Ops:
  0.6 1.3 %fusion.2 = bf16[128,1536]{1,0:T(8,128)(2,1)S(1)} fusion(bf16[128,1536]{1,0:T(8,128)(2,1)} %param.3), kind=kLoop, calls=%fused_computation.10 | loop fusion | flops 1966080 | bytes 786432 | tf_op jit(solution)/shard_map/convert_element_type | solution.py:164
  1.9 3.3 %collective-permute-start = (bf16[128,1536]{1,0:T(8,128)(2,1)S(1)}, bf16[128,1536]{1,0:T(8,128)(2,1)S(1)}, u32[]{:S(2)}, u32[]{:S(2)}) collective-permute-start(bf16[128,1536]{1,0:T(8,128)(2,1)S(1)} %fusion.2), channel_id=1, source_target_pairs={{0,16},{16,0},{1,17},{17,1},{2,18},{18,2},{3,19},{19,3},{4,20},{20... | collective-permute-start | bytes 1179656 | tf_op jit(solution)/shard_map/ppermute | solution.py:49
  5.2 3.8 %collective-permute-start.2 = (bf16[64,1536]{1,0:T(8,128)(2,1)}, bf16[64,1536]{1,0:T(8,128)(2,1)S(1)}, u32[]{:S(2)}, u32[]{:S(2)}) collective-permute-start(bf16[64,1536]{1,0:T(8,128)(2,1)} %param.4), channel_id=1, source_target_pairs={{0,7},{1,0},{2,1},{3,2},{4,3},{5,4},{6,5},{7,6},{8,15},{9,8},{10,9... | collective-permute-start | bytes 589832 | tf_op jit(solution)/shard_map/ppermute | solution.py:29
  9.1 2.7 %collective-permute-start.3 = (bf16[64,1536]{1,0:T(8,128)(2,1)}, bf16[64,1536]{1,0:T(8,128)(2,1)S(1)}, u32[]{:S(2)}, u32[]{:S(2)}) collective-permute-start(bf16[64,1536]{1,0:T(8,128)(2,1)} %param.4), channel_id=1, source_target_pairs={{0,8},{128,136},{8,0},{136,128},{1,9},{129,137},{9,1},{137,129},{2... | collective-permute-start | bytes 589832 | tf_op jit(solution)/shard_map/ppermute | solution.py:36
  11.8 1.7 %constant_dynamic-update-slice_fusion.33 = (bf16[2048,1536]{1,0:T(8,128)(2,1)}, bf16[192,1536]{1,0:T(8,128)(2,1)S(1)}, bf16[768,1536]{1,0:T(8,128)(2,1)S(1)}) fusion(bf16[64,1536]{1,0:T(8,128)(2,1)} %param.4), kind=kLoop, calls=%fused_computation.74 | loop fusion | bytes 786432
  14.5 2.3 %collective-permute-done.3 = bf16[64,1536]{1,0:T(8,128)(2,1)S(1)} collective-permute-done((bf16[64,1536]{1,0:T(8,128)(2,1)}, bf16[64,1536]{1,0:T(8,128)(2,1)S(1)}, u32[]{:S(2)}, u32[]{:S(2)}) %collective-permute-start.3) | collective-permute-done | bytes 196640 | tf_op jit(solution)/shard_map/ppermute | solution.py:36
  16.8 1.2 collective-permute-start.6
  18.1 2.8 %collective-permute-start.7 = (bf16[256,1536]{1,0:T(8,128)(2,1)S(1)}, bf16[256,1536]{1,0:T(8,128)(2,1)S(1)}, u32[]{:S(2)}, u32[]{:S(2)}) collective-permute-start(bf16[256,1536]{1,0:T(8,128)(2,1)S(1)} %pad_maximum_fusion.1), channel_id=1, source_target_pairs={{0,32},{16,112},{32,64},{48,16},{64,96},{80,48},{96,0},{112,80},{1... | collective-permute-start | bytes 2359304 | tf_op jit(solution)/shard_map/ppermute | solution.py:45
  21.0 2.7 %collective-permute-start.5 = (bf16[128,1536]{1,0:T(8,128)(2,1)S(1)}, bf16[128,1536]{1,0:T(8,128)(2,1)S(1)}, u32[]{:S(2)}, u32[]{:S(2)}) collective-permute-start(bf16[128,1536]{1,0:T(8,128)(2,1)S(1)} %get-tuple-element.110), channel_id=1, source_target_pairs={{0,7},{1,0},{2,1},{3,2},{4,3},{5,4},{6,5},{7,6},{8,15},{9,8},{10,9... | collective-permute-start | bytes 1179656 | tf_op jit(solution)/shard_map/ppermute | solution.py:29
  25.4 7.1 %collective-permute-done.4 = bf16[128,1536]{1,0:T(8,128)(2,1)S(1)} collective-permute-done((bf16[128,1536]{1,0:T(8,128)(2,1)S(1)}, bf16[128,1536]{1,0:T(8,128)(2,1)S(1)}, u32[]{:S(2)}, u32[]{:S(2)}) %collective-permute-start.4) | collective-permute-done | bytes 393248 | tf_op jit(solution)/shard_map/ppermute | solution.py:29
  32.5 1.8 %collective-permute-start.11 = (bf16[192,1536]{1,0:T(8,128)(2,1)S(1)}, bf16[192,1536]{1,0:T(8,128)(2,1)S(1)}, u32[]{:S(2)}, u32[]{:S(2)}) collective-permute-start(bf16[192,1536]{1,0:T(8,128)(2,1)S(1)} %get-tuple-element.103), channel_id=1, source_target_pairs={{0,136},{128,0},{8,128},{136,8},{1,137},{129,1},{9,129},{137,9},{2... | collective-permute-start | bytes 1769480 | tf_op jit(solution)/shard_map/ppermute | solution.py:36
  34.4 2.7 %collective-permute-start.9 = (bf16[128,1536]{1,0:T(8,128)(2,1)S(1)}, bf16[128,1536]{1,0:T(8,128)(2,1)S(1)}, u32[]{:S(2)}, u32[]{:S(2)}) collective-permute-start(bf16[128,1536]{1,0:T(8,128)(2,1)S(1)} %collective-permute-done.5), channel_id=1, source_target_pairs={{0,7},{1,0},{2,1},{3,2},{4,3},{5,4},{6,5},{7,6},{8,15},{9,8},{10,9... | collective-permute-start | bytes 1179656 | tf_op jit(solution)/shard_map/ppermute | solution.py:29
  37.1 2.1 %collective-permute-start.12 = (bf16[128,1536]{1,0:T(8,128)(2,1)S(1)}, bf16[128,1536]{1,0:T(8,128)(2,1)S(1)}, u32[]{:S(2)}, u32[]{:S(2)}) collective-permute-start(bf16[128,1536]{1,0:T(8,128)(2,1)S(1)} %collective-permute-done.6), channel_id=1, source_target_pairs={{0,16},{16,0},{1,17},{17,1},{2,18},{18,2},{3,19},{19,3},{4,20},{20... | collective-permute-start | bytes 1179656 | tf_op jit(solution)/shard_map/ppermute | solution.py:49
  41.4 4.7 %collective-permute-done.11 = bf16[192,1536]{1,0:T(8,128)(2,1)S(1)} collective-permute-done((bf16[192,1536]{1,0:T(8,128)(2,1)S(1)}, bf16[192,1536]{1,0:T(8,128)(2,1)S(1)}, u32[]{:S(2)}, u32[]{:S(2)}) %collective-permute-start.11) | collective-permute-done | bytes 589856 | tf_op jit(solution)/shard_map/ppermute | solution.py:36
  46.1 3.0 %collective-permute-start.17 = (bf16[128,1536]{1,0:T(8,128)(2,1)S(1)}, bf16[128,1536]{1,0:T(8,128)(2,1)S(1)}, u32[]{:S(2)}, u32[]{:S(2)}) collective-permute-start(bf16[128,1536]{1,0:T(8,128)(2,1)S(1)} %pad_maximum_fusion.5), channel_id=1, source_target_pairs={{0,136},{128,0},{8,128},{136,8},{1,137},{129,1},{9,129},{137,9},{2... | collective-permute-start | bytes 1179656 | tf_op jit(solution)/shard_map/ppermute | solution.py:36
  49.2 2.7 %collective-permute-start.15 = (bf16[96,1536]{1,0:T(8,128)(2,1)S(1)}, bf16[96,1536]{1,0:T(8,128)(2,1)S(1)}, u32[]{:S(2)}, u32[]{:S(2)}) collective-permute-start(bf16[96,1536]{1,0:T(8,128)(2,1)S(1)} %slice.90), channel_id=1, source_target_pairs={{0,7},{1,0},{2,1},{3,2},{4,3},{5,4},{6,5},{7,6},{8,15},{9,8},{10,9... | collective-permute-start | bytes 884744 | tf_op jit(solution)/shard_map/ppermute | solution.py:29
  54.6 4.8 %shard_map.50.early_ref = f32[768,1536]{1,0:T(8,128)S(1)} custom-call(bf16[768,1536]{1,0:T(8,128)(2,1)S(1)} %slice_dynamic-update-slice_fusion.5.grads_ref, bf16[1536,1536]{1,0:T(8,128)(2,1)S(1)} %bitcast.1), custom_call_target="tpu_custom_call" | custom-call | flops 3623878656 | bytes 12582912 | tf_op jit(solution)/shard_map/pallas_call | solution.py:71
  59.5 2.7 %collective-permute-start.23 = (bf16[128,1536]{1,0:T(8,128)(2,1)}, bf16[128,1536]{1,0:T(8,128)(2,1)}, u32[]{:S(2)}, u32[]{:S(2)}) collective-permute-start(bf16[128,1536]{1,0:T(8,128)(2,1)} %pad_maximum_fusion.6), channel_id=1, source_target_pairs={{0,136},{128,0},{8,128},{136,8},{1,137},{129,1},{9,129},{137,9},{2... | collective-permute-start | bytes 1179656 | tf_op jit(solution)/shard_map/ppermute | solution.py:36
  64.5 2.7 %collective-permute-start.20 = (bf16[32,1536]{1,0:T(8,128)(2,1)S(1)}, bf16[32,1536]{1,0:T(8,128)(2,1)S(1)}, u32[]{:S(2)}, u32[]{:S(2)}) collective-permute-start(bf16[32,1536]{1,0:T(8,128)(2,1)S(1)} %get-tuple-element.100), channel_id=1, source_target_pairs={{0,7},{1,0},{2,1},{3,2},{4,3},{5,4},{6,5},{7,6},{8,15},{9,8},{10,9... | collective-permute-start | bytes 294920 | tf_op jit(solution)/shard_map/ppermute | solution.py:29
  67.2 1.2 collective-permute-start.21
  68.9 5.3 %collective-permute-done.21 = bf16[128,1536]{1,0:T(8,128)(2,1)S(1)} collective-permute-done((bf16[128,1536]{1,0:T(8,128)(2,1)S(1)}, bf16[128,1536]{1,0:T(8,128)(2,1)S(1)}, u32[]{:S(2)}, u32[]{:S(2)}) %collective-permute-start.21) | collective-permute-done | bytes 393248 | tf_op jit(solution)/shard_map/ppermute | solution.py:45
  74.3 7.8 %collective-permute-start.25 = (bf16[768,1536]{1,0:T(8,128)(2,1)S(1)}, bf16[768,1536]{1,0:T(8,128)(2,1)S(1)}, u32[]{:S(2)}, u32[]{:S(2)}) collective-permute-start(bf16[768,1536]{1,0:T(8,128)(2,1)S(1)} %pad_maximum_fusion), channel_id=1, source_target_pairs={{0,16},{16,0},{1,17},{17,1},{2,18},{18,2},{3,19},{19,3},{4,20},{20... | collective-permute-start | bytes 7077896 | tf_op jit(solution)/shard_map/ppermute | solution.py:49
  82.2 2.0 %shard_map.51 = (f32[512,1536]{1,0:T(8,128)S(1)}, bf16[512,1536]{1,0:T(8,128)(2,1)S(1)}) custom-call(f32[768,1536]{1,0:T(8,128)S(1)} %shard_map.50.early_ref, bf16[256,1536]{1,0:T(8,128)(2,1)S(1)} %constant_dynamic-update-slice_fusion.11.grads_ref, bf16[1536,1536]{1,0:T(8,128)(2,1)S(1)} %bitcast.1), custom_call_target="tpu_custom_call" | custom-call | flops 1207959552 | bytes 8388608 | tf_op jit(solution)/shard_map/pallas_call | solution.py:109
  84.5 1.0 pad_maximum_fusion.7
  85.6 2.9 %collective-permute-done.24 = bf16[512,1536]{1,0:T(8,128)(2,1)S(1)} collective-permute-done((bf16[512,1536]{1,0:T(8,128)(2,1)S(1)}, bf16[512,1536]{1,0:T(8,128)(2,1)S(1)}, u32[]{:S(2)}, u32[]{:S(2)}) %collective-permute-start.24) | collective-permute-done | bytes 1572896 | tf_op jit(solution)/shard_map/ppermute | solution.py:49
  89.0 2.7 %collective-permute-start.30 = (bf16[64,1536]{1,0:T(8,128)(2,1)S(1)}, bf16[64,1536]{1,0:T(8,128)(2,1)S(1)}, u32[]{:S(2)}, u32[]{:S(2)}) collective-permute-start(bf16[64,1536]{1,0:T(8,128)(2,1)S(1)} %pad_maximum_fusion.7), channel_id=1, source_target_pairs={{0,136},{128,0},{8,128},{136,8},{1,137},{129,1},{9,129},{137,9},{2... | collective-permute-start | bytes 589832 | tf_op jit(solution)/shard_map/ppermute | solution.py:36
  91.6 2.7 %collective-permute-start.28 = (bf16[128,1536]{1,0:T(8,128)(2,1)S(1)}, bf16[128,1536]{1,0:T(8,128)(2,1)S(1)}, u32[]{:S(2)}, u32[]{:S(2)}) collective-permute-start(bf16[128,1536]{1,0:T(8,128)(2,1)S(1)} %get-tuple-element.67), channel_id=1, source_target_pairs={{0,96},{32,0},{64,32},{96,64},{1,97},{33,1},{65,33},{97,65},{2,98}... | collective-permute-start | bytes 1179656 | tf_op jit(solution)/shard_map/ppermute | solution.py:40
  102.9 1.8 %constant_dynamic-update-slice_fusion.20 = bf16[2048,1536]{1,0:T(8,128)(2,1)} fusion(bf16[2048,1536]{1,0:T(8,128)(2,1)} %constant_dynamic-update-slice_fusion.21, bf16[128,1536]{1,0:T(8,128)(2,1)} %collective-permute-done.22), kind=kLoop, calls=%fused_computation.61 | loop fusion | bytes 786432
  107.1 1.8 %constant_dynamic-update-slice_fusion.16 = bf16[2048,1536]{1,0:T(8,128)(2,1)} fusion(bf16[2048,1536]{1,0:T(8,128)(2,1)} %constant_dynamic-update-slice_fusion.17, bf16[128,1536]{1,0:T(8,128)(2,1)} %collective-permute-done.23), kind=kLoop, calls=%fused_computation.57 | loop fusion | bytes 786432
  109.5 2.8 %copy-done = bf16[2048,1536]{1,0:T(8,128)(2,1)S(1)} copy-done((bf16[2048,1536]{1,0:T(8,128)(2,1)S(1)}, bf16[2048,1536]{1,0:T(8,128)(2,1)}, u32[]{:S(2)}) %copy-start) | copy-done | bytes 6291480
  112.3 13.0 %shard_map.52 = bf16[1536,1536]{1,0:T(8,128)(2,1)} custom-call(bf16[2048,1536]{1,0:T(8,128)(2,1)S(1)} %copy-done, bf16[2048,1536]{1,0:T(8,128)(2,1)S(1)} %constant_dynamic-update-slice_fusion.34.acts_ref), custom_call_target="tpu_custom_call" | custom-call | flops 9663676416 | bytes 17825792 | tf_op jit(solution)/shard_map/pallas_call | solution.py:149
  125.3 1.5 %fusion.7 = bf16[128,1536]{1,0:T(8,128)(2,1)} fusion(bf16[128,1536]{1,0:T(8,128)(2,1)S(1)} %copy-done.1, bf16[128,1536]{1,0:T(8,128)(2,1)S(1)} %collective-permute-done.26, bf16[128,1536]{1,0:T(8,128)(2,1)S(1)} %collective-permute-done.28, bf16[128,1536]{1,0:T(8,128)(2,1)S(1)} %collective-permute-done.27, f32[512,1536]{1,0:T(8,128)S(1)} %get-tuple-element.61, ...), kind=kLoop, calls=%fused_computation.15 | loop fusion | flops 5505024 | bytes 3145728 | tf_op jit(solution)/shard_map/convert_element_type | solution.py:225
  (112 shorter events, 23.4 us)
Async XLA Ops:
  1.9 14.9 %collective-permute-start = (bf16[128,1536]{1,0:T(8,128)(2,1)S(1)}, bf16[128,1536]{1,0:T(8,128)(2,1)S(1)}, u32[]{:S(2)}, u32[]{:S(2)}) collective-permute-start(bf16[128,1536]{1,0:T(8,128)(2,1)S(1)} %fusion.2), channel_id=1, source_target_pairs={{0,16},{16,0},{1,17},{17,1},{2,18},{18,2},{3,19},{19,3},{4,20},{20... | collective-permute-start | bytes 1179656 | tf_op jit(solution)/shard_map/ppermute | solution.py:49
  5.2 9.2 %collective-permute-start.1 = (bf16[64,1536]{1,0:T(8,128)(2,1)}, bf16[64,1536]{1,0:T(8,128)(2,1)S(1)}, u32[]{:S(2)}, u32[]{:S(2)}) collective-permute-start(bf16[64,1536]{1,0:T(8,128)(2,1)} %param.4), channel_id=1, source_target_pairs={{0,1},{1,2},{2,3},{3,4},{4,5},{5,6},{6,7},{7,0},{8,9},{9,10},{10,1... | collective-permute-start | bytes 589832 | tf_op jit(solution)/shard_map/ppermute | solution.py:29
  5.2 9.2 %collective-permute-start.2 = (bf16[64,1536]{1,0:T(8,128)(2,1)}, bf16[64,1536]{1,0:T(8,128)(2,1)S(1)}, u32[]{:S(2)}, u32[]{:S(2)}) collective-permute-start(bf16[64,1536]{1,0:T(8,128)(2,1)} %param.4), channel_id=1, source_target_pairs={{0,7},{1,0},{2,1},{3,2},{4,3},{5,4},{6,5},{7,6},{8,15},{9,8},{10,9... | collective-permute-start | bytes 589832 | tf_op jit(solution)/shard_map/ppermute | solution.py:29
  9.1 7.7 %collective-permute-start.3 = (bf16[64,1536]{1,0:T(8,128)(2,1)}, bf16[64,1536]{1,0:T(8,128)(2,1)S(1)}, u32[]{:S(2)}, u32[]{:S(2)}) collective-permute-start(bf16[64,1536]{1,0:T(8,128)(2,1)} %param.4), channel_id=1, source_target_pairs={{0,8},{128,136},{8,0},{136,128},{1,9},{129,137},{9,1},{137,129},{2... | collective-permute-start | bytes 589832 | tf_op jit(solution)/shard_map/ppermute | solution.py:36
  16.8 17.5 %collective-permute-start.6 = (bf16[128,1536]{1,0:T(8,128)(2,1)S(1)}, bf16[128,1536]{1,0:T(8,128)(2,1)S(1)}, u32[]{:S(2)}, u32[]{:S(2)}) collective-permute-start(bf16[128,1536]{1,0:T(8,128)(2,1)S(1)} %fusion.2), channel_id=1, source_target_pairs={{0,128},{128,0},{1,129},{129,1},{2,130},{130,2},{3,131},{131,3},{4... | collective-permute-start | bytes 1179656 | tf_op jit(solution)/shard_map/ppermute | solution.py:49
  18.0 36.6 %slice-start = ((s8[4718592]{0:T(1024)(128)(4,1)}), s8[4194304]{0:T(1024)(128)(4,1)S(1)}, s32[]{:S(2)}) async-start(s8[4718592]{0:T(1024)(128)(4,1)} %bitcast), calls=%async_computation | async-start | bytes 8388608
  18.1 16.3 %collective-permute-start.7 = (bf16[256,1536]{1,0:T(8,128)(2,1)S(1)}, bf16[256,1536]{1,0:T(8,128)(2,1)S(1)}, u32[]{:S(2)}, u32[]{:S(2)}) collective-permute-start(bf16[256,1536]{1,0:T(8,128)(2,1)S(1)} %pad_maximum_fusion.1), channel_id=1, source_target_pairs={{0,32},{16,112},{32,64},{48,16},{64,96},{80,48},{96,0},{112,80},{1... | collective-permute-start | bytes 2359304 | tf_op jit(solution)/shard_map/ppermute | solution.py:45
  20.9 11.6 %collective-permute-start.4 = (bf16[128,1536]{1,0:T(8,128)(2,1)S(1)}, bf16[128,1536]{1,0:T(8,128)(2,1)S(1)}, u32[]{:S(2)}, u32[]{:S(2)}) collective-permute-start(bf16[128,1536]{1,0:T(8,128)(2,1)S(1)} %get-tuple-element.111), channel_id=1, source_target_pairs={{0,1},{1,2},{2,3},{3,4},{4,5},{5,6},{6,7},{7,0},{8,9},{9,10},{10,1... | collective-permute-start | bytes 1179656 | tf_op jit(solution)/shard_map/ppermute | solution.py:29
  21.0 13.3 %collective-permute-start.5 = (bf16[128,1536]{1,0:T(8,128)(2,1)S(1)}, bf16[128,1536]{1,0:T(8,128)(2,1)S(1)}, u32[]{:S(2)}, u32[]{:S(2)}) collective-permute-start(bf16[128,1536]{1,0:T(8,128)(2,1)S(1)} %get-tuple-element.110), channel_id=1, source_target_pairs={{0,7},{1,0},{2,1},{3,2},{4,3},{5,4},{6,5},{7,6},{8,15},{9,8},{10,9... | collective-permute-start | bytes 1179656 | tf_op jit(solution)/shard_map/ppermute | solution.py:29
  25.2 16.1 %collective-permute-start.10 = (bf16[192,1536]{1,0:T(8,128)(2,1)S(1)}, bf16[192,1536]{1,0:T(8,128)(2,1)S(1)}, u32[]{:S(2)}, u32[]{:S(2)}) collective-permute-start(bf16[192,1536]{1,0:T(8,128)(2,1)S(1)} %get-tuple-element.103), channel_id=1, source_target_pairs={{0,128},{128,8},{8,136},{136,0},{1,129},{129,9},{9,137},{137,1},{2... | collective-permute-start | bytes 1769480 | tf_op jit(solution)/shard_map/ppermute | solution.py:36
  32.5 13.6 %collective-permute-start.11 = (bf16[192,1536]{1,0:T(8,128)(2,1)S(1)}, bf16[192,1536]{1,0:T(8,128)(2,1)S(1)}, u32[]{:S(2)}, u32[]{:S(2)}) collective-permute-start(bf16[192,1536]{1,0:T(8,128)(2,1)S(1)} %get-tuple-element.103), channel_id=1, source_target_pairs={{0,136},{128,0},{8,128},{136,8},{1,137},{129,1},{9,129},{137,9},{2... | collective-permute-start | bytes 1769480 | tf_op jit(solution)/shard_map/ppermute | solution.py:36
  34.3 14.8 %collective-permute-start.8 = (bf16[128,1536]{1,0:T(8,128)(2,1)S(1)}, bf16[128,1536]{1,0:T(8,128)(2,1)S(1)}, u32[]{:S(2)}, u32[]{:S(2)}) collective-permute-start(bf16[128,1536]{1,0:T(8,128)(2,1)S(1)} %collective-permute-done.4), channel_id=1, source_target_pairs={{0,1},{1,2},{2,3},{3,4},{4,5},{5,6},{6,7},{7,0},{8,9},{9,10},{10,1... | collective-permute-start | bytes 1179656 | tf_op jit(solution)/shard_map/ppermute | solution.py:29
  34.4 14.7 %collective-permute-start.9 = (bf16[128,1536]{1,0:T(8,128)(2,1)S(1)}, bf16[128,1536]{1,0:T(8,128)(2,1)S(1)}, u32[]{:S(2)}, u32[]{:S(2)}) collective-permute-start(bf16[128,1536]{1,0:T(8,128)(2,1)S(1)} %collective-permute-done.5), channel_id=1, source_target_pairs={{0,7},{1,0},{2,1},{3,2},{4,3},{5,4},{6,5},{7,6},{8,15},{9,8},{10,9... | collective-permute-start | bytes 1179656 | tf_op jit(solution)/shard_map/ppermute | solution.py:29
  37.1 3.6 %collective-permute-start.12 = (bf16[128,1536]{1,0:T(8,128)(2,1)S(1)}, bf16[128,1536]{1,0:T(8,128)(2,1)S(1)}, u32[]{:S(2)}, u32[]{:S(2)}) collective-permute-start(bf16[128,1536]{1,0:T(8,128)(2,1)S(1)} %collective-permute-done.6), channel_id=1, source_target_pairs={{0,16},{16,0},{1,17},{17,1},{2,18},{18,2},{3,19},{19,3},{4,20},{20... | collective-permute-start | bytes 1179656 | tf_op jit(solution)/shard_map/ppermute | solution.py:49
  40.7 8.4 %collective-permute-start.13 = (bf16[128,1536]{1,0:T(8,128)(2,1)S(1)}, bf16[128,1536]{1,0:T(8,128)(2,1)S(1)}, u32[]{:S(2)}, u32[]{:S(2)}) collective-permute-start(bf16[128,1536]{1,0:T(8,128)(2,1)S(1)} %slice.88), channel_id=1, source_target_pairs={{0,32},{16,112},{32,64},{48,16},{64,96},{80,48},{96,0},{112,80},{1... | collective-permute-start | bytes 1179656 | tf_op jit(solution)/shard_map/ppermute | solution.py:45
  41.3 18.1 %collective-permute-start.16 = (bf16[128,1536]{1,0:T(8,128)(2,1)S(1)}, bf16[128,1536]{1,0:T(8,128)(2,1)S(1)}, u32[]{:S(2)}, u32[]{:S(2)}) collective-permute-start(bf16[128,1536]{1,0:T(8,128)(2,1)S(1)} %pad_maximum_fusion.5), channel_id=1, source_target_pairs={{0,128},{128,8},{8,136},{136,0},{1,129},{129,9},{9,137},{137,1},{2... | collective-permute-start | bytes 1179656 | tf_op jit(solution)/shard_map/ppermute | solution.py:36
  46.1 13.4 %collective-permute-start.17 = (bf16[128,1536]{1,0:T(8,128)(2,1)S(1)}, bf16[128,1536]{1,0:T(8,128)(2,1)S(1)}, u32[]{:S(2)}, u32[]{:S(2)}) collective-permute-start(bf16[128,1536]{1,0:T(8,128)(2,1)S(1)} %pad_maximum_fusion.5), channel_id=1, source_target_pairs={{0,136},{128,0},{8,128},{136,8},{1,137},{129,1},{9,129},{137,9},{2... | collective-permute-start | bytes 1179656 | tf_op jit(solution)/shard_map/ppermute | solution.py:36
  49.1 13.0 %collective-permute-start.14 = (bf16[96,1536]{1,0:T(8,128)(2,1)S(1)}, bf16[96,1536]{1,0:T(8,128)(2,1)S(1)}, u32[]{:S(2)}, u32[]{:S(2)}) collective-permute-start(bf16[96,1536]{1,0:T(8,128)(2,1)S(1)} %slice.89), channel_id=1, source_target_pairs={{0,1},{1,2},{2,3},{3,4},{4,5},{5,6},{6,7},{7,0},{8,9},{9,10},{10,1... | collective-permute-start | bytes 884744 | tf_op jit(solution)/shard_map/ppermute | solution.py:29
  49.2 12.9 %collective-permute-start.15 = (bf16[96,1536]{1,0:T(8,128)(2,1)S(1)}, bf16[96,1536]{1,0:T(8,128)(2,1)S(1)}, u32[]{:S(2)}, u32[]{:S(2)}) collective-permute-start(bf16[96,1536]{1,0:T(8,128)(2,1)S(1)} %slice.90), channel_id=1, source_target_pairs={{0,7},{1,0},{2,1},{3,2},{4,3},{5,4},{6,5},{7,6},{8,15},{9,8},{10,9... | collective-permute-start | bytes 884744 | tf_op jit(solution)/shard_map/ppermute | solution.py:29
  52.0 11.1 %collective-permute-start.18 = (bf16[256,1536]{1,0:T(8,128)(2,1)S(1)}, bf16[256,1536]{1,0:T(8,128)(2,1)S(1)}, u32[]{:S(2)}, u32[]{:S(2)}) collective-permute-start(bf16[256,1536]{1,0:T(8,128)(2,1)S(1)} %pad_maximum_fusion.2), channel_id=1, source_target_pairs={{0,32},{16,112},{32,64},{48,16},{64,96},{80,48},{96,0},{112,80},{1... | collective-permute-start | bytes 2359304 | tf_op jit(solution)/shard_map/ppermute | solution.py:45
  59.4 24.8 %collective-permute-start.22 = (bf16[128,1536]{1,0:T(8,128)(2,1)}, bf16[128,1536]{1,0:T(8,128)(2,1)}, u32[]{:S(2)}, u32[]{:S(2)}) collective-permute-start(bf16[128,1536]{1,0:T(8,128)(2,1)} %pad_maximum_fusion.6), channel_id=1, source_target_pairs={{0,128},{128,8},{8,136},{136,0},{1,129},{129,9},{9,137},{137,1},{2... | collective-permute-start | bytes 1179656 | tf_op jit(solution)/shard_map/ppermute | solution.py:36
  59.5 24.7 %collective-permute-start.23 = (bf16[128,1536]{1,0:T(8,128)(2,1)}, bf16[128,1536]{1,0:T(8,128)(2,1)}, u32[]{:S(2)}, u32[]{:S(2)}) collective-permute-start(bf16[128,1536]{1,0:T(8,128)(2,1)} %pad_maximum_fusion.6), channel_id=1, source_target_pairs={{0,136},{128,0},{8,128},{136,8},{1,137},{129,1},{9,129},{137,9},{2... | collective-permute-start | bytes 1179656 | tf_op jit(solution)/shard_map/ppermute | solution.py:36
  63.8 5.1 %collective-permute-start.19 = (bf16[32,1536]{1,0:T(8,128)(2,1)S(1)}, bf16[32,1536]{1,0:T(8,128)(2,1)S(1)}, u32[]{:S(2)}, u32[]{:S(2)}) collective-permute-start(bf16[32,1536]{1,0:T(8,128)(2,1)S(1)} %get-tuple-element.97), channel_id=1, source_target_pairs={{0,1},{1,2},{2,3},{3,4},{4,5},{5,6},{6,7},{7,0},{8,9},{9,10},{10,1... | collective-permute-start | bytes 294920 | tf_op jit(solution)/shard_map/ppermute | solution.py:29
  64.5 4.4 %collective-permute-start.20 = (bf16[32,1536]{1,0:T(8,128)(2,1)S(1)}, bf16[32,1536]{1,0:T(8,128)(2,1)S(1)}, u32[]{:S(2)}, u32[]{:S(2)}) collective-permute-start(bf16[32,1536]{1,0:T(8,128)(2,1)S(1)} %get-tuple-element.100), channel_id=1, source_target_pairs={{0,7},{1,0},{2,1},{3,2},{4,3},{5,4},{6,5},{7,6},{8,15},{9,8},{10,9... | collective-permute-start | bytes 294920 | tf_op jit(solution)/shard_map/ppermute | solution.py:29
  67.2 7.0 %collective-permute-start.21 = (bf16[128,1536]{1,0:T(8,128)(2,1)S(1)}, bf16[128,1536]{1,0:T(8,128)(2,1)S(1)}, u32[]{:S(2)}, u32[]{:S(2)}) collective-permute-start(bf16[128,1536]{1,0:T(8,128)(2,1)S(1)} %slice.101), channel_id=1, source_target_pairs={{0,32},{16,112},{32,64},{48,16},{64,96},{80,48},{96,0},{112,80},{1... | collective-permute-start | bytes 1179656 | tf_op jit(solution)/shard_map/ppermute | solution.py:45
  74.3 14.6 %collective-permute-start.25 = (bf16[768,1536]{1,0:T(8,128)(2,1)S(1)}, bf16[768,1536]{1,0:T(8,128)(2,1)S(1)}, u32[]{:S(2)}, u32[]{:S(2)}) collective-permute-start(bf16[768,1536]{1,0:T(8,128)(2,1)S(1)} %pad_maximum_fusion), channel_id=1, source_target_pairs={{0,16},{16,0},{1,17},{17,1},{2,18},{18,2},{3,19},{19,3},{4,20},{20... | collective-permute-start | bytes 7077896 | tf_op jit(solution)/shard_map/ppermute | solution.py:49
  84.2 4.3 %collective-permute-start.24 = (bf16[512,1536]{1,0:T(8,128)(2,1)S(1)}, bf16[512,1536]{1,0:T(8,128)(2,1)S(1)}, u32[]{:S(2)}, u32[]{:S(2)}) collective-permute-start(bf16[512,1536]{1,0:T(8,128)(2,1)S(1)} %get-tuple-element.62), channel_id=1, source_target_pairs={{0,16},{16,0},{1,17},{17,1},{2,18},{18,2},{3,19},{19,3},{4,20},{20... | collective-permute-start | bytes 4718600 | tf_op jit(solution)/shard_map/ppermute | solution.py:49
  88.9 15.8 %collective-permute-start.29 = (bf16[64,1536]{1,0:T(8,128)(2,1)S(1)}, bf16[64,1536]{1,0:T(8,128)(2,1)S(1)}, u32[]{:S(2)}, u32[]{:S(2)}) collective-permute-start(bf16[64,1536]{1,0:T(8,128)(2,1)S(1)} %pad_maximum_fusion.7), channel_id=1, source_target_pairs={{0,128},{128,8},{8,136},{136,0},{1,129},{129,9},{9,137},{137,1},{2... | collective-permute-start | bytes 589832 | tf_op jit(solution)/shard_map/ppermute | solution.py:36
  89.0 19.9 %collective-permute-start.30 = (bf16[64,1536]{1,0:T(8,128)(2,1)S(1)}, bf16[64,1536]{1,0:T(8,128)(2,1)S(1)}, u32[]{:S(2)}, u32[]{:S(2)}) collective-permute-start(bf16[64,1536]{1,0:T(8,128)(2,1)S(1)} %pad_maximum_fusion.7), channel_id=1, source_target_pairs={{0,136},{128,0},{8,128},{136,8},{1,137},{129,1},{9,129},{137,9},{2... | collective-permute-start | bytes 589832 | tf_op jit(solution)/shard_map/ppermute | solution.py:36
  91.6 33.6 %collective-permute-start.26 = (bf16[128,1536]{1,0:T(8,128)(2,1)S(1)}, bf16[128,1536]{1,0:T(8,128)(2,1)S(1)}, u32[]{:S(2)}, u32[]{:S(2)}) collective-permute-start(bf16[128,1536]{1,0:T(8,128)(2,1)S(1)} %get-tuple-element.65), channel_id=1, source_target_pairs={{0,64},{32,96},{64,0},{96,32},{1,65},{33,97},{65,1},{97,33},{2,66}... | collective-permute-start | bytes 1179656 | tf_op jit(solution)/shard_map/ppermute | solution.py:40
  91.6 33.6 %collective-permute-start.27 = (bf16[128,1536]{1,0:T(8,128)(2,1)S(1)}, bf16[128,1536]{1,0:T(8,128)(2,1)S(1)}, u32[]{:S(2)}, u32[]{:S(2)}) collective-permute-start(bf16[128,1536]{1,0:T(8,128)(2,1)S(1)} %get-tuple-element.66), channel_id=1, source_target_pairs={{0,32},{32,64},{64,96},{96,0},{1,33},{33,65},{65,97},{97,1},{2,34}... | collective-permute-start | bytes 1179656 | tf_op jit(solution)/shard_map/ppermute | solution.py:40
  91.6 33.6 %collective-permute-start.28 = (bf16[128,1536]{1,0:T(8,128)(2,1)S(1)}, bf16[128,1536]{1,0:T(8,128)(2,1)S(1)}, u32[]{:S(2)}, u32[]{:S(2)}) collective-permute-start(bf16[128,1536]{1,0:T(8,128)(2,1)S(1)} %get-tuple-element.67), channel_id=1, source_target_pairs={{0,96},{32,0},{64,32},{96,64},{1,97},{33,1},{65,33},{97,65},{2,98}... | collective-permute-start | bytes 1179656 | tf_op jit(solution)/shard_map/ppermute | solution.py:40
  (9 other events, 127.5 us)

commit v5 on v4

--- a/solution.py
+++ b/solution.py
@@ -74,7 +74,7 @@
         in_specs=[pl.BlockSpec((count, 1536), lambda n: (0, 0)), pl.BlockSpec((1536, step), lambda n: (0, n))],
         out_specs=pl.BlockSpec((count, step), lambda n: (0, n)),
         out_shape=jax.ShapeDtypeStruct((count, 1536), F32),
-        compiler_params=pltpu.CompilerParams(vmem_limit_bytes=24 << 20),
+        compiler_params=pltpu.CompilerParams(vmem_limit_bytes=16 << 20),
         cost_estimate=pl.CostEstimate(flops=2 * count * 1536 * 1536, bytes_accessed=12 << 20, transcendentals=0),
     )(grads, weight)
 
@@ -112,50 +112,71 @@
         out_specs=[VMEM] * 2,
         out_shape=[jax.ShapeDtypeStruct((512, 1536), F32), jax.ShapeDtypeStruct((512, 1536), BF)],
         scratch_shapes=[pltpu.VMEM((256, 1536), F32)],
-        compiler_params=pltpu.CompilerParams(vmem_limit_bytes=32 << 20),
+        compiler_params=pltpu.CompilerParams(vmem_limit_bytes=8 << 20),
         cost_estimate=pl.CostEstimate(flops=2 * 256 * 1536 * 1536, bytes_accessed=8 << 20, transcendentals=0),
     )(early, grads, weight)
 
 
-def weight_kernel(grads_ref, acts_ref, out_ref, acts):
+PIECES = [
+    [(2 * far, OWN[j]) for far, j in EARLY],
+    [(2 * far, OWN[j]) for far, j in LATE],
+    *[[(dx, OWN[j]) for j in group] for dx in (3, 1) for group in ((0, 1, 2), (3, 4), (5, 6), (7,))],
+]
+
+
+def weight_kernel(*refs):
+    pieces, acts_refs = refs[:10], refs[10:14]
+    out_ref, grads, acts = refs[14:]
     y, c, xl, xh, z = (lax.axis_index(a) for a in ("y", "c", "xl", "xh", "z"))
 
     @pl.when(pl.program_id(0) == 0)
     def _():
-        for k in range(32):
-            dx = (0, 2, 3, 1)[k // 8]
+        for k, (dx, dz) in enumerate(shard for piece in PIECES for shard in piece):
             xp = lax.rem(2 * xh + xl + dx, 4)
-            zp = lax.rem(z + OWN[k % 8] + 8, 8)
+            zp = lax.rem(z + dz + 8, 8)
             dy = lax.rem(2 * (xp // 2) + zp // 4 + 4 - y, 4)
             away = lax.rem(lax.rem(zp // 2, 2) + c, 2)
             back = jnp.where(c == 0, 3, 1)
             other = dx % 2
-            block = jnp.where(
-                dy == 0,
-                2 * other + away,
-                3 * other
-                + jnp.where(dy == 2, 6 + 6 * away, jnp.where(dy == back, 4 + away, 11 - away)),
-            )
-            start = block * 128 + lax.rem(zp, 2) * 64
-            acts[64 * k : 64 * k + 64, :] = acts_ref[pl.ds(pl.multiple_of(start, 64), 64), :]
-
+            half = lax.rem(zp, 2) * 64
+
+            def copy(which, block):
+                acts[64 * k : 64 * k + 64, :] = acts_refs[which][pl.ds(pl.multiple_of(block * 128 + half, 64), 64), :]
+
+            @pl.when(dy == 0)
+            def _():
+                copy(other, away)
+
+            @pl.when((dy == back) | ((dy == 2) & (away == 0)))
+            def _():
+                copy(2, 3 * other + jnp.where(dy == 2, 2, away))
+
+            @pl.when((dy == 4 - back) | ((dy == 2) & (away == 1)))
+            def _():
+                copy(3, 3 * other + jnp.where(dy == 2, 2, 1 - away))
+
+    lanes = pl.ds(pl.multiple_of(pl.program_id(0) * 256, 256), 256)
+    start = 0
+    for piece, ref in zip(PIECES, pieces):
+        grads[start : start + 64 * len(piece), :] = ref[:, lanes]
+        start += 64 * len(piece)
     out_ref[...] = lax.dot_general(
-        grads_ref[...], acts[...], (((0,), (0,)), ((), ())), preferred_element_type=F32
+        grads[...], acts[...], (((0,), (0,)), ((), ())), preferred_element_type=F32
     ).astype(BF)
 
 
-def weight_gradient(grads, acts):
+def weight_gradient(pieces, acts):
     step = 256
     return pl.pallas_call(
         weight_kernel,
         grid=(1536 // step,),
-        in_specs=[pl.BlockSpec((2048, step), lambda m: (0, m)), pl.BlockSpec((2048, 1536), lambda m: (0, 0))],
+        in_specs=[VMEM] * 14,
         out_specs=pl.BlockSpec((step, 1536), lambda m: (m, 0)),
         out_shape=jax.ShapeDtypeStruct((1536, 1536), BF),
-        scratch_shapes=[pltpu.VMEM((2048, 1536), BF)],
-        compiler_params=pltpu.CompilerParams(vmem_limit_bytes=36 << 20),
+        scratch_shapes=[pltpu.VMEM((2048, step), BF), pltpu.VMEM((2048, 1536), BF)],
+        compiler_params=pltpu.CompilerParams(vmem_limit_bytes=18 << 20),
         cost_estimate=pl.CostEstimate(flops=2 * 2048 * 1536 * 1536, bytes_accessed=17 << 20, transcendentals=0),
-    )(grads, acts)
+    )(*pieces, *acts)
 
 
 def per_device(pre_act, out_grad, down_weight):
@@ -214,12 +235,8 @@
     from_across = along_y(to_across, 2)
     from_below, from_above = along_y(to_above, 1), along_y(to_below, -1)
 
-    grads = jnp.concatenate(
-        [grads_early[:448], last, grads_early[448:], grads_late[64:], left_a, left_b, left_c, left_d]
-        + [right_a, right_b, right_c, right_d]
-    )
-    acts = jnp.concatenate([chip, other_chip, came, swapped])
-    weight_grad = weight_gradient(grads, acts)
+    arrived = [left_a, left_b, left_c, left_d, right_a, right_b, right_c, right_d]
+    weight_grad = weight_gradient([grads_early, grads_late, *arrived], [chip, other_chip, came, swapped])
     from_across, from_below, from_above, weight_grad = tie(from_across, from_below, from_above, weight_grad)
     grad_act = summed(0) + from_below.astype(F32) + from_above.astype(F32) + from_across.astype(F32)
     pre_grad = (grad_act * gelu_slope(pre_wide)).astype(BF)

time: 127 us -> 109 us (0.86)
  local copies, waits for them, and re-layouts: 25.9 us -> 0.68 us
  waiting for transfers between devices: 24.6 us -> 35 us
  other arithmetic: 5.2 us -> 3.34 us
  starting transfers between devices: 50.3 us -> 48.5 us
    unnamed x58 -> x24, local copies, waits for them, and re-layouts: 23.6 us -> 0.41 us
    ppermute x5, waiting for transfers between devices: 2.92 us -> 9.31 us  [swap(): return lax.ppermute(a, axis, [(0, 1), (1, 0)])]
    ppermute x10, waiting for transfers between devices: 8.45 us -> 11.8 us  [along_z(): return lax.ppermute(a, 'z', [(i, (i + d) % Z) for i in range(Z)])]
    ppermute x9, waiting for transfers between devices: 7 us -> 10.3 us  [along_x(): lax.ppermute(a, ('xl', 'xh'), [(place(x), place((x + d) % 4)) for x in ra...]
    ppermute x4, waiting for transfers between devices: 6.26 us -> 3.64 us  [round_y(): lax.ppermute(a, ('y', 'c'), [(s[0] * C + s[1], t[0] * C + t[1]) for s, t...]
    ppermute x5, starting transfers between devices: 14.6 us -> 12.4 us  [swap(): return lax.ppermute(a, axis, [(0, 1), (1, 0)])]
    slice x2, local copies, waits for them, and re-layouts: 1.33 us -> 0.04 us  [per_device(): last = jnp.concatenate([up4[64:], down4[:32]])]
  transfers between devices with their start and end apart: 31 -> 31, of which waited for: 8 -> 15; matrix products, arithmetic and copies ran while one was open for 20% -> 1% of each run, Pallas kernels for 16% -> 19%
where the time goes in v5:
time: 109 us
  starting transfers between devices  48.5 us (44%)
  waiting for transfers between devices  35 us (32%)
  Pallas kernels  20.2 us (19%)
  other arithmetic  3.34 us (3%)
    ppermute x10, starting transfers between devices, along_z(): return lax.ppermute(a, 'z', [(i, (i + d) % Z) for i in range(Z)])  14.2 us
    ppermute x9, starting transfers between devices, along_x(): lax.ppermute(a, ('xl', 'xh'), [(place(x), place((x + d) % 4)) for x in ra...  14 us
    pallas_call x1, Pallas kernels, weight_gradient(): pl.pallas_call(weight_kernel, grid=(1536 // step,), in_specs=[VMEM] * 14,...  13.5 us
    ppermute x5, starting transfers between devices, swap(): return lax.ppermute(a, axis, [(0, 1), (1, 0)])  12.4 us
    ppermute x10, waiting for transfers between devices, along_z(): return lax.ppermute(a, 'z', [(i, (i + d) % Z) for i in range(Z)])  11.8 us
    ppermute x9, waiting for transfers between devices, along_x(): lax.ppermute(a, ('xl', 'xh'), [(place(x), place((x + d) % 4)) for x in ra...  10.3 us
    ppermute x5, waiting for transfers between devices, swap(): return lax.ppermute(a, axis, [(0, 1), (1, 0)])  9.31 us
    ppermute x4, starting transfers between devices, round_y(): lax.ppermute(a, ('y', 'c'), [(s[0] * C + s[1], t[0] * C + t[1]) for s, t...  5.27 us
  transfers between devices with their start and end apart: 31, of which 15 were waited for; matrix products, arithmetic and copies ran while one was open for 1% of the time, Pallas kernels for 19%

profile of v5, /device:TPU:1, one launch (start us, length us, event | category | flops | bytes accessed | tf_op | source)
XLA Modules:
  0.0 108.8 jit_solution(5760540916605324544)
XLA Ops:
  0.6 1.3 %fusion.2 = bf16[128,1536]{1,0:T(8,128)(2,1)S(1)} fusion(bf16[128,1536]{1,0:T(8,128)(2,1)} %param.3), kind=kLoop, calls=%fused_computation.9 | loop fusion | flops 1966080 | bytes 786432 | tf_op jit(solution)/shard_map/convert_element_type | solution.py:185
  2.0 3.3 %collective-permute-start = (bf16[128,1536]{1,0:T(8,128)(2,1)S(1)}, bf16[128,1536]{1,0:T(8,128)(2,1)S(1)}, u32[]{:S(2)}, u32[]{:S(2)}) collective-permute-start(bf16[128,1536]{1,0:T(8,128)(2,1)S(1)} %fusion.2), channel_id=1, source_target_pairs={{0,16},{16,0},{1,17},{17,1},{2,18},{18,2},{3,19},{19,3},{4,20},{20... | collective-permute-start | bytes 1179656 | tf_op jit(solution)/shard_map/ppermute | solution.py:49
  5.3 3.9 %collective-permute-start.2 = (bf16[64,1536]{1,0:T(8,128)(2,1)}, bf16[64,1536]{1,0:T(8,128)(2,1)S(1)}, u32[]{:S(2)}, u32[]{:S(2)}) collective-permute-start(bf16[64,1536]{1,0:T(8,128)(2,1)} %param.4), channel_id=1, source_target_pairs={{0,7},{1,0},{2,1},{3,2},{4,3},{5,4},{6,5},{7,6},{8,15},{9,8},{10,9... | collective-permute-start | bytes 589832 | tf_op jit(solution)/shard_map/ppermute | solution.py:29
  9.1 2.7 %collective-permute-start.3 = (bf16[64,1536]{1,0:T(8,128)(2,1)}, bf16[64,1536]{1,0:T(8,128)(2,1)S(1)}, u32[]{:S(2)}, u32[]{:S(2)}) collective-permute-start(bf16[64,1536]{1,0:T(8,128)(2,1)} %param.4), channel_id=1, source_target_pairs={{0,8},{128,136},{8,0},{136,128},{1,9},{129,137},{9,1},{137,129},{2... | collective-permute-start | bytes 589832 | tf_op jit(solution)/shard_map/ppermute | solution.py:36
  11.9 1.8 %collective-permute-done.2 = bf16[64,1536]{1,0:T(8,128)(2,1)S(1)} collective-permute-done((bf16[64,1536]{1,0:T(8,128)(2,1)}, bf16[64,1536]{1,0:T(8,128)(2,1)S(1)}, u32[]{:S(2)}, u32[]{:S(2)}) %collective-permute-start.2) | collective-permute-done | bytes 196640 | tf_op jit(solution)/shard_map/ppermute | solution.py:29
  13.7 3.0 %collective-permute-done.1 = bf16[64,1536]{1,0:T(8,128)(2,1)S(1)} collective-permute-done((bf16[64,1536]{1,0:T(8,128)(2,1)}, bf16[64,1536]{1,0:T(8,128)(2,1)S(1)}, u32[]{:S(2)}, u32[]{:S(2)}) %collective-permute-start.1) | collective-permute-done | bytes 196640 | tf_op jit(solution)/shard_map/ppermute | solution.py:29
  17.1 2.8 %collective-permute-start.7 = (bf16[256,1536]{1,0:T(8,128)(2,1)S(1)}, bf16[256,1536]{1,0:T(8,128)(2,1)S(1)}, u32[]{:S(2)}, u32[]{:S(2)}) collective-permute-start(bf16[256,1536]{1,0:T(8,128)(2,1)S(1)} %constant_dynamic-update-slice_fusion.refs_10_), channel_id=1, source_target_pairs={{0,32},{16,112},{32,64},{48,16},{64,96},{80,48},{96,0},{112,80},{1... | collective-permute-start | bytes 2359304 | tf_op jit(solution)/shard_map/ppermute | solution.py:45
  21.3 2.4 %collective-permute-start.5 = (bf16[128,1536]{1,0:T(8,128)(2,1)S(1)}, bf16[128,1536]{1,0:T(8,128)(2,1)S(1)}, u32[]{:S(2)}, u32[]{:S(2)}) collective-permute-start(bf16[128,1536]{1,0:T(8,128)(2,1)S(1)} %get-tuple-element.103), channel_id=1, source_target_pairs={{0,7},{1,0},{2,1},{3,2},{4,3},{5,4},{6,5},{7,6},{8,15},{9,8},{10,9... | collective-permute-start | bytes 1179656 | tf_op jit(solution)/shard_map/ppermute | solution.py:29
  23.8 1.9 %collective-permute-start.11 = (bf16[192,1536]{1,0:T(8,128)(2,1)S(1)}, bf16[192,1536]{1,0:T(8,128)(2,1)S(1)}, u32[]{:S(2)}, u32[]{:S(2)}) collective-permute-start(bf16[192,1536]{1,0:T(8,128)(2,1)S(1)} %get-tuple-element.98), channel_id=1, source_target_pairs={{0,136},{128,0},{8,128},{136,8},{1,137},{129,1},{9,129},{137,9},{2... | collective-permute-start | bytes 1769480 | tf_op jit(solution)/shard_map/ppermute | solution.py:36
  25.7 5.1 %collective-permute-done.6 = bf16[128,1536]{1,0:T(8,128)(2,1)S(1)} collective-permute-done((bf16[128,1536]{1,0:T(8,128)(2,1)S(1)}, bf16[128,1536]{1,0:T(8,128)(2,1)S(1)}, u32[]{:S(2)}, u32[]{:S(2)}) %collective-permute-start.6) | collective-permute-done | bytes 393248 | tf_op jit(solution)/shard_map/ppermute | solution.py:49
  31.9 2.7 %collective-permute-done.4 = bf16[128,1536]{1,0:T(8,128)(2,1)S(1)} collective-permute-done((bf16[128,1536]{1,0:T(8,128)(2,1)S(1)}, bf16[128,1536]{1,0:T(8,128)(2,1)S(1)}, u32[]{:S(2)}, u32[]{:S(2)}) %collective-permute-start.4) | collective-permute-done | bytes 393248 | tf_op jit(solution)/shard_map/ppermute | solution.py:29
  34.6 1.8 %collective-permute-start.12 = (bf16[128,1536]{1,0:T(8,128)(2,1)S(1)}, bf16[128,1536]{1,0:T(8,128)(2,1)S(1)}, u32[]{:S(2)}, u32[]{:S(2)}) collective-permute-start(bf16[128,1536]{1,0:T(8,128)(2,1)S(1)} %collective-permute-done.6), channel_id=1, source_target_pairs={{0,16},{16,0},{1,17},{17,1},{2,18},{18,2},{3,19},{19,3},{4,20},{20... | collective-permute-start | bytes 1179656 | tf_op jit(solution)/shard_map/ppermute | solution.py:49
  36.4 2.7 %collective-permute-start.9 = (bf16[128,1536]{1,0:T(8,128)(2,1)S(1)}, bf16[128,1536]{1,0:T(8,128)(2,1)S(1)}, u32[]{:S(2)}, u32[]{:S(2)}) collective-permute-start(bf16[128,1536]{1,0:T(8,128)(2,1)S(1)} %collective-permute-done.5), channel_id=1, source_target_pairs={{0,7},{1,0},{2,1},{3,2},{4,3},{5,4},{6,5},{7,6},{8,15},{9,8},{10,9... | collective-permute-start | bytes 1179656 | tf_op jit(solution)/shard_map/ppermute | solution.py:29
  39.9 3.5 %collective-permute-done.11.refs_6_ = bf16[192,1536]{1,0:T(8,128)(2,1)S(1)} collective-permute-done((bf16[192,1536]{1,0:T(8,128)(2,1)S(1)}, bf16[192,1536]{1,0:T(8,128)(2,1)S(1)}, u32[]{:S(2)}, u32[]{:S(2)}) %collective-permute-start.11) | collective-permute-done | bytes 589856 | tf_op jit(solution)/shard_map/ppermute | solution.py:36
  43.4 2.2 %collective-permute-done.10.refs_2_ = bf16[192,1536]{1,0:T(8,128)(2,1)S(1)} collective-permute-done((bf16[192,1536]{1,0:T(8,128)(2,1)S(1)}, bf16[192,1536]{1,0:T(8,128)(2,1)S(1)}, u32[]{:S(2)}, u32[]{:S(2)}) %collective-permute-start.10) | collective-permute-done | bytes 589856 | tf_op jit(solution)/shard_map/ppermute | solution.py:36
  46.2 2.2 %collective-permute-done.8 = bf16[128,1536]{1,0:T(8,128)(2,1)S(1)} collective-permute-done((bf16[128,1536]{1,0:T(8,128)(2,1)S(1)}, bf16[128,1536]{1,0:T(8,128)(2,1)S(1)}, u32[]{:S(2)}, u32[]{:S(2)}) %collective-permute-start.8) | collective-permute-done | bytes 393248 | tf_op jit(solution)/shard_map/ppermute | solution.py:29
  48.7 1.9 %collective-permute-start.17 = (bf16[128,1536]{1,0:T(8,128)(2,1)S(1)}, bf16[128,1536]{1,0:T(8,128)(2,1)S(1)}, u32[]{:S(2)}, u32[]{:S(2)}) collective-permute-start(bf16[128,1536]{1,0:T(8,128)(2,1)S(1)} %pad_maximum_fusion.3), channel_id=1, source_target_pairs={{0,136},{128,0},{8,128},{136,8},{1,137},{129,1},{9,129},{137,9},{2... | collective-permute-start | bytes 1179656 | tf_op jit(solution)/shard_map/ppermute | solution.py:36
  50.6 2.4 %collective-permute-start.15 = (bf16[96,1536]{1,0:T(8,128)(2,1)S(1)}, bf16[96,1536]{1,0:T(8,128)(2,1)S(1)}, u32[]{:S(2)}, u32[]{:S(2)}) collective-permute-start(bf16[96,1536]{1,0:T(8,128)(2,1)S(1)} %slice.84), channel_id=1, source_target_pairs={{0,7},{1,0},{2,1},{3,2},{4,3},{5,4},{6,5},{7,6},{8,15},{9,8},{10,9... | collective-permute-start | bytes 884744 | tf_op jit(solution)/shard_map/ppermute | solution.py:29
  53.5 4.8 %shard_map.50.early_ref = f32[768,1536]{1,0:T(8,128)S(1)} custom-call(bf16[768,1536]{1,0:T(8,128)(2,1)S(1)} %slice_dynamic-update-slice_fusion.2.grads_ref.refs_0_, bf16[1536,1536]{1,0:T(8,128)(2,1)S(1)} %bitcast.1), custom_call_target="tpu_custom_call" | custom-call | flops 3623878656 | bytes 12582912 | tf_op jit(solution)/shard_map/pallas_call | solution.py:71
  58.3 2.8 %collective-permute-start.23 = (bf16[128,1536]{1,0:T(8,128)(2,1)S(1)}, bf16[128,1536]{1,0:T(8,128)(2,1)S(1)}, u32[]{:S(2)}, u32[]{:S(2)}) collective-permute-start(bf16[128,1536]{1,0:T(8,128)(2,1)S(1)} %pad_maximum_fusion.4), channel_id=1, source_target_pairs={{0,136},{128,0},{8,128},{136,8},{1,137},{129,1},{9,129},{137,9},{2... | collective-permute-start | bytes 1179656 | tf_op jit(solution)/shard_map/ppermute | solution.py:36
  61.5 2.5 %collective-permute-done.18 = bf16[256,1536]{1,0:T(8,128)(2,1)S(1)} collective-permute-done((bf16[256,1536]{1,0:T(8,128)(2,1)S(1)}, bf16[256,1536]{1,0:T(8,128)(2,1)S(1)}, u32[]{:S(2)}, u32[]{:S(2)}) %collective-permute-start.18) | collective-permute-done | bytes 786464 | tf_op jit(solution)/shard_map/ppermute | solution.py:45
  64.1 1.5 %collective-permute-start.21 = (bf16[128,1536]{1,0:T(8,128)(2,1)S(1)}, bf16[128,1536]{1,0:T(8,128)(2,1)S(1)}, u32[]{:S(2)}, u32[]{:S(2)}) collective-permute-start(bf16[128,1536]{1,0:T(8,128)(2,1)S(1)} %slice.95), channel_id=1, source_target_pairs={{0,32},{16,112},{32,64},{48,16},{64,96},{80,48},{96,0},{112,80},{1... | collective-permute-start | bytes 1179656 | tf_op jit(solution)/shard_map/ppermute | solution.py:45
  65.7 2.7 %collective-permute-start.20 = (bf16[32,1536]{1,0:T(8,128)(2,1)S(1)}, bf16[32,1536]{1,0:T(8,128)(2,1)S(1)}, u32[]{:S(2)}, u32[]{:S(2)}) collective-permute-start(bf16[32,1536]{1,0:T(8,128)(2,1)S(1)} %get-tuple-element.96), channel_id=1, source_target_pairs={{0,7},{1,0},{2,1},{3,2},{4,3},{5,4},{6,5},{7,6},{8,15},{9,8},{10,9... | collective-permute-start | bytes 294920 | tf_op jit(solution)/shard_map/ppermute | solution.py:29
  68.5 2.1 %collective-permute-done.19 = bf16[32,1536]{1,0:T(8,128)(2,1)S(1)} collective-permute-done((bf16[32,1536]{1,0:T(8,128)(2,1)S(1)}, bf16[32,1536]{1,0:T(8,128)(2,1)S(1)}, u32[]{:S(2)}, u32[]{:S(2)}) %collective-permute-start.19) | collective-permute-done | bytes 98336 | tf_op jit(solution)/shard_map/ppermute | solution.py:29
  71.1 5.9 %collective-permute-start.25 = (bf16[768,1536]{1,0:T(8,128)(2,1)S(1)}, bf16[768,1536]{1,0:T(8,128)(2,1)S(1)}, u32[]{:S(2)}, u32[]{:S(2)}) collective-permute-start(bf16[768,1536]{1,0:T(8,128)(2,1)S(1)} %constant_dynamic-update-slice_fusion.17.refs_12_), channel_id=1, source_target_pairs={{0,16},{16,0},{1,17},{17,1},{2,18},{18,2},{3,19},{19,3},{4,20},{20... | collective-permute-start | bytes 7077896 | tf_op jit(solution)/shard_map/ppermute | solution.py:49
  77.0 2.0 %shard_map.51 = (f32[512,1536]{1,0:T(8,128)S(1)}, bf16[512,1536]{1,0:T(8,128)(2,1)S(1)}) custom-call(f32[768,1536]{1,0:T(8,128)S(1)} %shard_map.50.early_ref, bf16[256,1536]{1,0:T(8,128)(2,1)S(1)} %constant_dynamic-update-slice_fusion.13.grads_ref.refs_1_, bf16[1536,1536]{1,0:T(8,128)(2,1)S(1)} %bitcast.1), custom_call_target="tpu_custom_call" | custom-call | flops 1207959552 | bytes 8388608 | tf_op jit(solution)/shard_map/pallas_call | solution.py:109
  79.1 4.2 %collective-permute-done.24 = bf16[512,1536]{1,0:T(8,128)(2,1)S(1)} collective-permute-done((bf16[512,1536]{1,0:T(8,128)(2,1)S(1)}, bf16[512,1536]{1,0:T(8,128)(2,1)S(1)}, u32[]{:S(2)}, u32[]{:S(2)}) %collective-permute-start.24) | collective-permute-done | bytes 1572896 | tf_op jit(solution)/shard_map/ppermute | solution.py:49
  83.8 3.0 %collective-permute-start.30 = (bf16[64,1536]{1,0:T(8,128)(2,1)S(1)}, bf16[64,1536]{1,0:T(8,128)(2,1)S(1)}, u32[]{:S(2)}, u32[]{:S(2)}) collective-permute-start(bf16[64,1536]{1,0:T(8,128)(2,1)S(1)} %pad_maximum_fusion.5), channel_id=1, source_target_pairs={{0,136},{128,0},{8,128},{136,8},{1,137},{129,1},{9,129},{137,9},{2... | collective-permute-start | bytes 589832 | tf_op jit(solution)/shard_map/ppermute | solution.py:36
  87.3 2.2 %collective-permute-start.28 = (bf16[128,1536]{1,0:T(8,128)(2,1)S(1)}, bf16[128,1536]{1,0:T(8,128)(2,1)S(1)}, u32[]{:S(2)}, u32[]{:S(2)}) collective-permute-start(bf16[128,1536]{1,0:T(8,128)(2,1)S(1)} %get-tuple-element.67), channel_id=1, source_target_pairs={{0,96},{32,0},{64,32},{96,64},{1,97},{33,1},{65,33},{97,65},{2,98}... | collective-permute-start | bytes 1179656 | tf_op jit(solution)/shard_map/ppermute | solution.py:40
  90.8 3.1 %collective-permute-done.29.refs_5_ = bf16[64,1536]{1,0:T(8,128)(2,1)S(1)} collective-permute-done((bf16[64,1536]{1,0:T(8,128)(2,1)S(1)}, bf16[64,1536]{1,0:T(8,128)(2,1)S(1)}, u32[]{:S(2)}, u32[]{:S(2)}) %collective-permute-start.29) | collective-permute-done | bytes 196640 | tf_op jit(solution)/shard_map/ppermute | solution.py:36
  93.8 13.5 %shard_map.52 = bf16[1536,1536]{1,0:T(8,128)(2,1)} custom-call(bf16[768,1536]{1,0:T(8,128)(2,1)S(1)} %slice_dynamic-update-slice_fusion.2.grads_ref.refs_0_, bf16[256,1536]{1,0:T(8,128)(2,1)S(1)} %constant_dynamic-update-slice_fusion.13.grads_ref.refs_1_, bf16[192,1536]{1,0:T(8,128)(2,1)S(1)} %collective-permute-done.10.refs_2_, ...), custom_call_target="tpu_custom_call" | custom-call | flops 9663676416 | bytes 17825792 | tf_op jit(solution)/shard_map/pallas_call | solution.py:170
  107.3 1.5 %fusion.7 = bf16[128,1536]{1,0:T(8,128)(2,1)} fusion(bf16[128,1536]{1,0:T(8,128)(2,1)S(1)} %copy-done, bf16[128,1536]{1,0:T(8,128)(2,1)S(1)} %collective-permute-done.26, bf16[128,1536]{1,0:T(8,128)(2,1)S(1)} %collective-permute-done.28, bf16[128,1536]{1,0:T(8,128)(2,1)S(1)} %collective-permute-done.27, f32[512,1536]{1,0:T(8,128)S(1)} %get-tuple-element.61, ...), kind=kLoop, calls=%fused_computation.14 | loop fusion | flops 5505024 | bytes 3145728 | tf_op jit(solution)/shard_map/convert_element_type | solution.py:242
  (78 shorter events, 8.6 us)
Async XLA Ops:
  2.0 15.0 %collective-permute-start = (bf16[128,1536]{1,0:T(8,128)(2,1)S(1)}, bf16[128,1536]{1,0:T(8,128)(2,1)S(1)}, u32[]{:S(2)}, u32[]{:S(2)}) collective-permute-start(bf16[128,1536]{1,0:T(8,128)(2,1)S(1)} %fusion.2), channel_id=1, source_target_pairs={{0,16},{16,0},{1,17},{17,1},{2,18},{18,2},{3,19},{19,3},{4,20},{20... | collective-permute-start | bytes 1179656 | tf_op jit(solution)/shard_map/ppermute | solution.py:49
  5.3 8.4 %collective-permute-start.2 = (bf16[64,1536]{1,0:T(8,128)(2,1)}, bf16[64,1536]{1,0:T(8,128)(2,1)S(1)}, u32[]{:S(2)}, u32[]{:S(2)}) collective-permute-start(bf16[64,1536]{1,0:T(8,128)(2,1)} %param.4), channel_id=1, source_target_pairs={{0,7},{1,0},{2,1},{3,2},{4,3},{5,4},{6,5},{7,6},{8,15},{9,8},{10,9... | collective-permute-start | bytes 589832 | tf_op jit(solution)/shard_map/ppermute | solution.py:29
  9.1 7.6 %collective-permute-start.1 = (bf16[64,1536]{1,0:T(8,128)(2,1)}, bf16[64,1536]{1,0:T(8,128)(2,1)S(1)}, u32[]{:S(2)}, u32[]{:S(2)}) collective-permute-start(bf16[64,1536]{1,0:T(8,128)(2,1)} %param.4), channel_id=1, source_target_pairs={{0,1},{1,2},{2,3},{3,4},{4,5},{5,6},{6,7},{7,0},{8,9},{9,10},{10,1... | collective-permute-start | bytes 589832 | tf_op jit(solution)/shard_map/ppermute | solution.py:29
  9.1 7.8 %collective-permute-start.3 = (bf16[64,1536]{1,0:T(8,128)(2,1)}, bf16[64,1536]{1,0:T(8,128)(2,1)S(1)}, u32[]{:S(2)}, u32[]{:S(2)}) collective-permute-start(bf16[64,1536]{1,0:T(8,128)(2,1)} %param.4), channel_id=1, source_target_pairs={{0,8},{128,136},{8,0},{136,128},{1,9},{129,137},{9,1},{137,129},{2... | collective-permute-start | bytes 589832 | tf_op jit(solution)/shard_map/ppermute | solution.py:36
  17.1 17.6 %collective-permute-start.7 = (bf16[256,1536]{1,0:T(8,128)(2,1)S(1)}, bf16[256,1536]{1,0:T(8,128)(2,1)S(1)}, u32[]{:S(2)}, u32[]{:S(2)}) collective-permute-start(bf16[256,1536]{1,0:T(8,128)(2,1)S(1)} %constant_dynamic-update-slice_fusion.refs_10_), channel_id=1, source_target_pairs={{0,32},{16,112},{32,64},{48,16},{64,96},{80,48},{96,0},{112,80},{1... | collective-permute-start | bytes 2359304 | tf_op jit(solution)/shard_map/ppermute | solution.py:45
  19.9 33.6 %slice-start = ((s8[4718592]{0:T(1024)(128)(4,1)}), s8[4194304]{0:T(1024)(128)(4,1)S(1)}, s32[]{:S(2)}) async-start(s8[4718592]{0:T(1024)(128)(4,1)} %bitcast), calls=%async_computation | async-start | bytes 8388608
  19.9 10.8 %collective-permute-start.6 = (bf16[128,1536]{1,0:T(8,128)(2,1)S(1)}, bf16[128,1536]{1,0:T(8,128)(2,1)S(1)}, u32[]{:S(2)}, u32[]{:S(2)}) collective-permute-start(bf16[128,1536]{1,0:T(8,128)(2,1)S(1)} %fusion.2), channel_id=1, source_target_pairs={{0,128},{128,0},{1,129},{129,1},{2,130},{130,2},{3,131},{131,3},{4... | collective-permute-start | bytes 1179656 | tf_op jit(solution)/shard_map/ppermute | solution.py:49
  21.3 10.7 %collective-permute-start.5 = (bf16[128,1536]{1,0:T(8,128)(2,1)S(1)}, bf16[128,1536]{1,0:T(8,128)(2,1)S(1)}, u32[]{:S(2)}, u32[]{:S(2)}) collective-permute-start(bf16[128,1536]{1,0:T(8,128)(2,1)S(1)} %get-tuple-element.103), channel_id=1, source_target_pairs={{0,7},{1,0},{2,1},{3,2},{4,3},{5,4},{6,5},{7,6},{8,15},{9,8},{10,9... | collective-permute-start | bytes 1179656 | tf_op jit(solution)/shard_map/ppermute | solution.py:29
  23.7 10.9 %collective-permute-start.4 = (bf16[128,1536]{1,0:T(8,128)(2,1)S(1)}, bf16[128,1536]{1,0:T(8,128)(2,1)S(1)}, u32[]{:S(2)}, u32[]{:S(2)}) collective-permute-start(bf16[128,1536]{1,0:T(8,128)(2,1)S(1)} %get-tuple-element.104), channel_id=1, source_target_pairs={{0,1},{1,2},{2,3},{3,4},{4,5},{5,6},{6,7},{7,0},{8,9},{9,10},{10,1... | collective-permute-start | bytes 1179656 | tf_op jit(solution)/shard_map/ppermute | solution.py:29
  23.8 19.6 %collective-permute-start.11 = (bf16[192,1536]{1,0:T(8,128)(2,1)S(1)}, bf16[192,1536]{1,0:T(8,128)(2,1)S(1)}, u32[]{:S(2)}, u32[]{:S(2)}) collective-permute-start(bf16[192,1536]{1,0:T(8,128)(2,1)S(1)} %get-tuple-element.98), channel_id=1, source_target_pairs={{0,136},{128,0},{8,128},{136,8},{1,137},{129,1},{9,129},{137,9},{2... | collective-permute-start | bytes 1769480 | tf_op jit(solution)/shard_map/ppermute | solution.py:36
  30.7 14.8 %collective-permute-start.10 = (bf16[192,1536]{1,0:T(8,128)(2,1)S(1)}, bf16[192,1536]{1,0:T(8,128)(2,1)S(1)}, u32[]{:S(2)}, u32[]{:S(2)}) collective-permute-start(bf16[192,1536]{1,0:T(8,128)(2,1)S(1)} %get-tuple-element.98), channel_id=1, source_target_pairs={{0,128},{128,8},{8,136},{136,0},{1,129},{129,9},{9,137},{137,1},{2... | collective-permute-start | bytes 1769480 | tf_op jit(solution)/shard_map/ppermute | solution.py:36
  34.6 4.6 %collective-permute-start.12 = (bf16[128,1536]{1,0:T(8,128)(2,1)S(1)}, bf16[128,1536]{1,0:T(8,128)(2,1)S(1)}, u32[]{:S(2)}, u32[]{:S(2)}) collective-permute-start(bf16[128,1536]{1,0:T(8,128)(2,1)S(1)} %collective-permute-done.6), channel_id=1, source_target_pairs={{0,16},{16,0},{1,17},{17,1},{2,18},{18,2},{3,19},{19,3},{4,20},{20... | collective-permute-start | bytes 1179656 | tf_op jit(solution)/shard_map/ppermute | solution.py:49
  36.4 12.0 %collective-permute-start.8 = (bf16[128,1536]{1,0:T(8,128)(2,1)S(1)}, bf16[128,1536]{1,0:T(8,128)(2,1)S(1)}, u32[]{:S(2)}, u32[]{:S(2)}) collective-permute-start(bf16[128,1536]{1,0:T(8,128)(2,1)S(1)} %collective-permute-done.4), channel_id=1, source_target_pairs={{0,1},{1,2},{2,3},{3,4},{4,5},{5,6},{6,7},{7,0},{8,9},{9,10},{10,1... | collective-permute-start | bytes 1179656 | tf_op jit(solution)/shard_map/ppermute | solution.py:29
  36.4 12.0 %collective-permute-start.9 = (bf16[128,1536]{1,0:T(8,128)(2,1)S(1)}, bf16[128,1536]{1,0:T(8,128)(2,1)S(1)}, u32[]{:S(2)}, u32[]{:S(2)}) collective-permute-start(bf16[128,1536]{1,0:T(8,128)(2,1)S(1)} %collective-permute-done.5), channel_id=1, source_target_pairs={{0,7},{1,0},{2,1},{3,2},{4,3},{5,4},{6,5},{7,6},{8,15},{9,8},{10,9... | collective-permute-start | bytes 1179656 | tf_op jit(solution)/shard_map/ppermute | solution.py:29
  39.2 7.0 %collective-permute-start.13 = (bf16[128,1536]{1,0:T(8,128)(2,1)S(1)}, bf16[128,1536]{1,0:T(8,128)(2,1)S(1)}, u32[]{:S(2)}, u32[]{:S(2)}) collective-permute-start(bf16[128,1536]{1,0:T(8,128)(2,1)S(1)} %slice.82), channel_id=1, source_target_pairs={{0,32},{16,112},{32,64},{48,16},{64,96},{80,48},{96,0},{112,80},{1... | collective-permute-start | bytes 1179656 | tf_op jit(solution)/shard_map/ppermute | solution.py:45
  48.7 12.9 %collective-permute-start.17 = (bf16[128,1536]{1,0:T(8,128)(2,1)S(1)}, bf16[128,1536]{1,0:T(8,128)(2,1)S(1)}, u32[]{:S(2)}, u32[]{:S(2)}) collective-permute-start(bf16[128,1536]{1,0:T(8,128)(2,1)S(1)} %pad_maximum_fusion.3), channel_id=1, source_target_pairs={{0,136},{128,0},{8,128},{136,8},{1,137},{129,1},{9,129},{137,9},{2... | collective-permute-start | bytes 1179656 | tf_op jit(solution)/shard_map/ppermute | solution.py:36
  50.5 11.0 %collective-permute-start.16 = (bf16[128,1536]{1,0:T(8,128)(2,1)S(1)}, bf16[128,1536]{1,0:T(8,128)(2,1)S(1)}, u32[]{:S(2)}, u32[]{:S(2)}) collective-permute-start(bf16[128,1536]{1,0:T(8,128)(2,1)S(1)} %pad_maximum_fusion.3), channel_id=1, source_target_pairs={{0,128},{128,8},{8,136},{136,0},{1,129},{129,9},{9,137},{137,1},{2... | collective-permute-start | bytes 1179656 | tf_op jit(solution)/shard_map/ppermute | solution.py:36
  50.6 7.7 %collective-permute-start.15 = (bf16[96,1536]{1,0:T(8,128)(2,1)S(1)}, bf16[96,1536]{1,0:T(8,128)(2,1)S(1)}, u32[]{:S(2)}, u32[]{:S(2)}) collective-permute-start(bf16[96,1536]{1,0:T(8,128)(2,1)S(1)} %slice.84), channel_id=1, source_target_pairs={{0,7},{1,0},{2,1},{3,2},{4,3},{5,4},{6,5},{7,6},{8,15},{9,8},{10,9... | collective-permute-start | bytes 884744 | tf_op jit(solution)/shard_map/ppermute | solution.py:29
  52.9 8.1 %collective-permute-start.14 = (bf16[96,1536]{1,0:T(8,128)(2,1)S(1)}, bf16[96,1536]{1,0:T(8,128)(2,1)S(1)}, u32[]{:S(2)}, u32[]{:S(2)}) collective-permute-start(bf16[96,1536]{1,0:T(8,128)(2,1)S(1)} %slice.83), channel_id=1, source_target_pairs={{0,1},{1,2},{2,3},{3,4},{4,5},{5,6},{6,7},{7,0},{8,9},{9,10},{10,1... | collective-permute-start | bytes 884744 | tf_op jit(solution)/shard_map/ppermute | solution.py:29
  52.9 11.1 %collective-permute-start.18 = (bf16[256,1536]{1,0:T(8,128)(2,1)S(1)}, bf16[256,1536]{1,0:T(8,128)(2,1)S(1)}, u32[]{:S(2)}, u32[]{:S(2)}) collective-permute-start(bf16[256,1536]{1,0:T(8,128)(2,1)S(1)} %pad_maximum_fusion.refs_11_), channel_id=1, source_target_pairs={{0,32},{16,112},{32,64},{48,16},{64,96},{80,48},{96,0},{112,80},{1... | collective-permute-start | bytes 2359304 | tf_op jit(solution)/shard_map/ppermute | solution.py:45
  58.3 20.7 %collective-permute-start.23 = (bf16[128,1536]{1,0:T(8,128)(2,1)S(1)}, bf16[128,1536]{1,0:T(8,128)(2,1)S(1)}, u32[]{:S(2)}, u32[]{:S(2)}) collective-permute-start(bf16[128,1536]{1,0:T(8,128)(2,1)S(1)} %pad_maximum_fusion.4), channel_id=1, source_target_pairs={{0,136},{128,0},{8,128},{136,8},{1,137},{129,1},{9,129},{137,9},{2... | collective-permute-start | bytes 1179656 | tf_op jit(solution)/shard_map/ppermute | solution.py:36
  61.1 18.0 %collective-permute-start.22 = (bf16[128,1536]{1,0:T(8,128)(2,1)S(1)}, bf16[128,1536]{1,0:T(8,128)(2,1)S(1)}, u32[]{:S(2)}, u32[]{:S(2)}) collective-permute-start(bf16[128,1536]{1,0:T(8,128)(2,1)S(1)} %pad_maximum_fusion.4), channel_id=1, source_target_pairs={{0,128},{128,8},{8,136},{136,0},{1,129},{129,9},{9,137},{137,1},{2... | collective-permute-start | bytes 1179656 | tf_op jit(solution)/shard_map/ppermute | solution.py:36
  64.1 7.0 %collective-permute-start.21 = (bf16[128,1536]{1,0:T(8,128)(2,1)S(1)}, bf16[128,1536]{1,0:T(8,128)(2,1)S(1)}, u32[]{:S(2)}, u32[]{:S(2)}) collective-permute-start(bf16[128,1536]{1,0:T(8,128)(2,1)S(1)} %slice.95), channel_id=1, source_target_pairs={{0,32},{16,112},{32,64},{48,16},{64,96},{80,48},{96,0},{112,80},{1... | collective-permute-start | bytes 1179656 | tf_op jit(solution)/shard_map/ppermute | solution.py:45
  65.6 5.1 %collective-permute-start.19 = (bf16[32,1536]{1,0:T(8,128)(2,1)S(1)}, bf16[32,1536]{1,0:T(8,128)(2,1)S(1)}, u32[]{:S(2)}, u32[]{:S(2)}) collective-permute-start(bf16[32,1536]{1,0:T(8,128)(2,1)S(1)} %get-tuple-element.93), channel_id=1, source_target_pairs={{0,1},{1,2},{2,3},{3,4},{4,5},{5,6},{6,7},{7,0},{8,9},{9,10},{10,1... | collective-permute-start | bytes 294920 | tf_op jit(solution)/shard_map/ppermute | solution.py:29
  65.7 4.9 %collective-permute-start.20 = (bf16[32,1536]{1,0:T(8,128)(2,1)S(1)}, bf16[32,1536]{1,0:T(8,128)(2,1)S(1)}, u32[]{:S(2)}, u32[]{:S(2)}) collective-permute-start(bf16[32,1536]{1,0:T(8,128)(2,1)S(1)} %get-tuple-element.96), channel_id=1, source_target_pairs={{0,7},{1,0},{2,1},{3,2},{4,3},{5,4},{6,5},{7,6},{8,15},{9,8},{10,9... | collective-permute-start | bytes 294920 | tf_op jit(solution)/shard_map/ppermute | solution.py:29
  71.1 12.7 %collective-permute-start.25 = (bf16[768,1536]{1,0:T(8,128)(2,1)S(1)}, bf16[768,1536]{1,0:T(8,128)(2,1)S(1)}, u32[]{:S(2)}, u32[]{:S(2)}) collective-permute-start(bf16[768,1536]{1,0:T(8,128)(2,1)S(1)} %constant_dynamic-update-slice_fusion.17.refs_12_), channel_id=1, source_target_pairs={{0,16},{16,0},{1,17},{17,1},{2,18},{18,2},{3,19},{19,3},{4,20},{20... | collective-permute-start | bytes 7077896 | tf_op jit(solution)/shard_map/ppermute | solution.py:49
  79.0 4.4 %collective-permute-start.24 = (bf16[512,1536]{1,0:T(8,128)(2,1)S(1)}, bf16[512,1536]{1,0:T(8,128)(2,1)S(1)}, u32[]{:S(2)}, u32[]{:S(2)}) collective-permute-start(bf16[512,1536]{1,0:T(8,128)(2,1)S(1)} %get-tuple-element.62), channel_id=1, source_target_pairs={{0,16},{16,0},{1,17},{17,1},{2,18},{18,2},{3,19},{19,3},{4,20},{20... | collective-permute-start | bytes 4718600 | tf_op jit(solution)/shard_map/ppermute | solution.py:49
  83.8 6.9 %collective-permute-start.30 = (bf16[64,1536]{1,0:T(8,128)(2,1)S(1)}, bf16[64,1536]{1,0:T(8,128)(2,1)S(1)}, u32[]{:S(2)}, u32[]{:S(2)}) collective-permute-start(bf16[64,1536]{1,0:T(8,128)(2,1)S(1)} %pad_maximum_fusion.5), channel_id=1, source_target_pairs={{0,136},{128,0},{8,128},{136,8},{1,137},{129,1},{9,129},{137,9},{2... | collective-permute-start | bytes 589832 | tf_op jit(solution)/shard_map/ppermute | solution.py:36
  86.8 7.0 %collective-permute-start.29 = (bf16[64,1536]{1,0:T(8,128)(2,1)S(1)}, bf16[64,1536]{1,0:T(8,128)(2,1)S(1)}, u32[]{:S(2)}, u32[]{:S(2)}) collective-permute-start(bf16[64,1536]{1,0:T(8,128)(2,1)S(1)} %pad_maximum_fusion.5), channel_id=1, source_target_pairs={{0,128},{128,8},{8,136},{136,0},{1,129},{129,9},{9,137},{137,1},{2... | collective-permute-start | bytes 589832 | tf_op jit(solution)/shard_map/ppermute | solution.py:36
  86.8 20.5 %collective-permute-start.26 = (bf16[128,1536]{1,0:T(8,128)(2,1)S(1)}, bf16[128,1536]{1,0:T(8,128)(2,1)S(1)}, u32[]{:S(2)}, u32[]{:S(2)}) collective-permute-start(bf16[128,1536]{1,0:T(8,128)(2,1)S(1)} %get-tuple-element.65), channel_id=1, source_target_pairs={{0,64},{32,96},{64,0},{96,32},{1,65},{33,97},{65,1},{97,33},{2,66}... | collective-permute-start | bytes 1179656 | tf_op jit(solution)/shard_map/ppermute | solution.py:40
  86.8 20.5 %collective-permute-start.27 = (bf16[128,1536]{1,0:T(8,128)(2,1)S(1)}, bf16[128,1536]{1,0:T(8,128)(2,1)S(1)}, u32[]{:S(2)}, u32[]{:S(2)}) collective-permute-start(bf16[128,1536]{1,0:T(8,128)(2,1)S(1)} %get-tuple-element.66), channel_id=1, source_target_pairs={{0,32},{32,64},{64,96},{96,0},{1,33},{33,65},{65,97},{97,1},{2,34}... | collective-permute-start | bytes 1179656 | tf_op jit(solution)/shard_map/ppermute | solution.py:40
  87.3 20.0 %collective-permute-start.28 = (bf16[128,1536]{1,0:T(8,128)(2,1)S(1)}, bf16[128,1536]{1,0:T(8,128)(2,1)S(1)}, u32[]{:S(2)}, u32[]{:S(2)}) collective-permute-start(bf16[128,1536]{1,0:T(8,128)(2,1)S(1)} %get-tuple-element.67), channel_id=1, source_target_pairs={{0,96},{32,0},{64,32},{96,64},{1,97},{33,1},{65,33},{97,65},{2,98}... | collective-permute-start | bytes 1179656 | tf_op jit(solution)/shard_map/ppermute | solution.py:40
  (3 other events, 56.5 us)

commit v6 on v5

--- a/solution.py
+++ b/solution.py
@@ -186,6 +186,7 @@
 
     up1, down1, far = along_z(g, 1), along_z(g, -1), along_x(g, 2)
     act_c = swap(activation, "c")
+    hop_2 = along_y(activation, 2)
     activation, act_c, up1, down1, far = tie(activation, act_c, up1, down1, far)
 
     up2 = along_z(jnp.concatenate([far, up1]), 1)
@@ -193,20 +194,21 @@
     other_rep = swap(activation, "xl")
     chip = jnp.concatenate([activation, act_c])
     hop_1 = round_y(chip)
-    up2, down2, other_rep, hop_1 = tie(up2, down2, other_rep, hop_1)
+    up2, down2, other_rep, hop_1, hop_2 = tie(up2, down2, other_rep, hop_1, hop_2)
 
     up3, down3 = along_z(up2, 1), along_z(down2, -1)
     near = jnp.concatenate([g, up1, down1])
     left_a, right_a = along_x(near, 1), along_x(near, -1)
+    hop_4 = along_y(other_rep, 2)
+    other_rep, left_a, right_a = tie(other_rep, left_a, right_a)
     other_chip = jnp.concatenate([other_rep, swap(other_rep, "c")])
-    hop_2 = round_y(hop_1[:128])
-    up3, down3, left_a, right_a, other_chip, hop_2 = tie(up3, down3, left_a, right_a, other_chip, hop_2)
+    up3, down3, left_a, right_a, other_chip, hop_4 = tie(up3, down3, left_a, right_a, other_chip, hop_4)
 
     up4, down4 = along_z(up3[:96], 1), along_z(down3[32:], -1)
     middle = jnp.concatenate([up2[64:], down2[:64]])
     left_b, right_b = along_x(middle, 1), along_x(middle, -1)
     hop_3 = round_y(other_chip)
-    up4, down4, left_b, right_b, hop_3 = tie(up4, down4, left_b, right_b, hop_3)
+    up4, down4 = tie(up4, down4)
     own = [g, up1, down1, up2[64:], down2[:64], up3[64:], down3[:64]]
     second = [far, up2[:64], down2[64:], up3[:64], down3[64:]]
     grads_early = jnp.concatenate(own + second)
@@ -214,10 +216,9 @@
 
     up5, down5 = along_z(up4[:32], 1), along_z(down4[64:], -1)
     last = jnp.concatenate([up4[64:], down4[:32]])
-    hop_4 = round_y(hop_3[:128])
     third = jnp.concatenate([up3[64:], down3[:64]])
     left_c, right_c = along_x(third, 1), along_x(third, -1)
-    up5, down5, early, hop_4 = tie(up5, down5, early, hop_4)
+    up5, down5, early, hop_3, left_b, right_b = tie(up5, down5, early, hop_3, left_b, right_b)
 
     grads_late = jnp.concatenate([last, up4[:64], down4[32:], up5, down5])
     mine, other = late_partial(early, grads_late, down_weight)

time: 109 us -> 102 us (0.936)
  waiting for transfers between devices: 35 us -> 18.2 us
  starting transfers between devices: 48.5 us -> 57.1 us
    ppermute x3 -> x5, starting transfers between devices: 2.68 us -> 8.82 us  [along_y(): return lax.ppermute(a, 'y', [(i, (i + d) % Y) for i in range(Y)])]
    ppermute x9, waiting for transfers between devices: 10.3 us -> 4.27 us  [along_x(): lax.ppermute(a, ('xl', 'xh'), [(place(x), place((x + d) % 4)) for x in ra...]
    ppermute x5, waiting for transfers between devices: 9.31 us -> 3.9 us  [swap(): return lax.ppermute(a, axis, [(0, 1), (1, 0)])]
    ppermute x5, starting transfers between devices: 12.4 us -> 17.1 us  [swap(): return lax.ppermute(a, axis, [(0, 1), (1, 0)])]
    ppermute x10, waiting for transfers between devices: 11.8 us -> 7.82 us  [along_z(): return lax.ppermute(a, 'z', [(i, (i + d) % Z) for i in range(Z)])]
    ppermute x4 -> x2, waiting for transfers between devices: 3.64 us -> 0.01 us  [round_y(): lax.ppermute(a, ('y', 'c'), [(s[0] * C + s[1], t[0] * C + t[1]) for s, t...]
    ppermute x9, starting transfers between devices: 14 us -> 11.7 us  [along_x(): lax.ppermute(a, ('xl', 'xh'), [(place(x), place((x + d) % 4)) for x in ra...]
    ppermute x3 -> x5, waiting for transfers between devices: 0.01 us -> 2.19 us  [along_y(): return lax.ppermute(a, 'y', [(i, (i + d) % Y) for i in range(Y)])]
  transfers between devices with their start and end apart: 31 -> 31, of which waited for: 15 -> 11; matrix products, arithmetic and copies ran while one was open for 1% -> 2% of each run, Pallas kernels for 19% -> 20%
where the time goes in v6:
time: 102 us; the launch traced here: 101 us
  starting transfers between devices  57.1 us (56%)
  Pallas kernels  20.2 us (20%)
  waiting for transfers between devices  18.2 us (18%)
  other arithmetic  3.3 us (3%)
  local copies, waits for them, and re-layouts  1.55 us (2%)
  between operations  1.02 us (1%)
    ppermute x5, starting transfers between devices, swap(): return lax.ppermute(a, axis, [(0, 1), (1, 0)])  17.1 us
    ppermute x10, starting transfers between devices, along_z(): return lax.ppermute(a, 'z', [(i, (i + d) % Z) for i in range(Z)])  14.2 us
    pallas_call x1, Pallas kernels, weight_gradient(): pl.pallas_call(weight_kernel, grid=(1536 // step,), in_specs=[VMEM] * 14,...  13.5 us
    ppermute x9, starting transfers between devices, along_x(): lax.ppermute(a, ('xl', 'xh'), [(place(x), place((x + d) % 4)) for x in ra...  11.7 us
    ppermute x5, starting transfers between devices, along_y(): return lax.ppermute(a, 'y', [(i, (i + d) % Y) for i in range(Y)])  8.82 us
    ppermute x10, waiting for transfers between devices, along_z(): return lax.ppermute(a, 'z', [(i, (i + d) % Z) for i in range(Z)])  7.82 us
    ppermute x2, starting transfers between devices, round_y(): lax.ppermute(a, ('y', 'c'), [(s[0] * C + s[1], t[0] * C + t[1]) for s, t...  5.2 us
    pallas_call x1, Pallas kernels, early_partial(): pl.pallas_call(early_kernel, grid=(1536 // step,), in_specs=[pl.BlockSpec...  4.78 us
  transfers between devices with their start and end apart: 31, of which 11 were waited for; matrix products, arithmetic and copies ran while one was open for 2% of the time, Pallas kernels for 20%

profile of v6, /device:TPU:1, one launch (start us, length us, event | category | flops | bytes accessed | tf_op | source)
XLA Modules:
  0.0 101.4 jit_solution(13776613832993686387)
XLA Ops:
  0.6 1.3 %fusion.2 = bf16[128,1536]{1,0:T(8,128)(2,1)S(1)} fusion(bf16[128,1536]{1,0:T(8,128)(2,1)} %param.3), kind=kLoop, calls=%fused_computation.9 | loop fusion | flops 1966080 | bytes 786432 | tf_op jit(solution)/shard_map/convert_element_type | solution.py:185
  1.9 3.3 %collective-permute-start = (bf16[128,1536]{1,0:T(8,128)(2,1)S(1)}, bf16[128,1536]{1,0:T(8,128)(2,1)S(1)}, u32[]{:S(2)}, u32[]{:S(2)}) collective-permute-start(bf16[128,1536]{1,0:T(8,128)(2,1)S(1)} %fusion.2), channel_id=1, source_target_pairs={{0,16},{16,0},{1,17},{17,1},{2,18},{18,2},{3,19},{19,3},{4,20},{20... | collective-permute-start | bytes 1179656 | tf_op jit(solution)/shard_map/ppermute | solution.py:49
  5.2 3.9 %collective-permute-start.2 = (bf16[64,1536]{1,0:T(8,128)(2,1)}, bf16[64,1536]{1,0:T(8,128)(2,1)S(1)}, u32[]{:S(2)}, u32[]{:S(2)}) collective-permute-start(bf16[64,1536]{1,0:T(8,128)(2,1)} %param.4), channel_id=1, source_target_pairs={{0,7},{1,0},{2,1},{3,2},{4,3},{5,4},{6,5},{7,6},{8,15},{9,8},{10,9... | collective-permute-start | bytes 589832 | tf_op jit(solution)/shard_map/ppermute | solution.py:29
  9.1 2.7 %collective-permute-start.3 = (bf16[64,1536]{1,0:T(8,128)(2,1)}, bf16[64,1536]{1,0:T(8,128)(2,1)S(1)}, u32[]{:S(2)}, u32[]{:S(2)}) collective-permute-start(bf16[64,1536]{1,0:T(8,128)(2,1)} %param.4), channel_id=1, source_target_pairs={{0,8},{128,136},{8,0},{136,128},{1,9},{129,137},{9,1},{137,129},{2... | collective-permute-start | bytes 589832 | tf_op jit(solution)/shard_map/ppermute | solution.py:36
  11.8 2.9 %collective-permute-start.8 = (bf16[128,1536]{1,0:T(8,128)(2,1)S(1)}, bf16[128,1536]{1,0:T(8,128)(2,1)S(1)}, u32[]{:S(2)}, u32[]{:S(2)}) collective-permute-start(bf16[128,1536]{1,0:T(8,128)(2,1)S(1)} %fusion.2), channel_id=1, source_target_pairs={{0,64},{32,96},{64,0},{96,32},{1,65},{33,97},{65,1},{97,33},{2,66}... | collective-permute-start | bytes 1179656 | tf_op jit(solution)/shard_map/ppermute | solution.py:40
  16.9 1.2 %collective-permute-start.6 = (bf16[128,1536]{1,0:T(8,128)(2,1)S(1)}, bf16[128,1536]{1,0:T(8,128)(2,1)S(1)}, u32[]{:S(2)}, u32[]{:S(2)}) collective-permute-start(bf16[128,1536]{1,0:T(8,128)(2,1)S(1)} %fusion.2), channel_id=1, source_target_pairs={{0,128},{128,0},{1,129},{129,1},{2,130},{130,2},{3,131},{131,3},{4... | collective-permute-start | bytes 1179656 | tf_op jit(solution)/shard_map/ppermute | solution.py:49
  18.2 2.8 %collective-permute-start.7 = (bf16[256,1536]{1,0:T(8,128)(2,1)S(1)}, bf16[256,1536]{1,0:T(8,128)(2,1)S(1)}, u32[]{:S(2)}, u32[]{:S(2)}) collective-permute-start(bf16[256,1536]{1,0:T(8,128)(2,1)S(1)} %constant_dynamic-update-slice_fusion.refs_10_), channel_id=1, source_target_pairs={{0,32},{16,112},{32,64},{48,16},{64,96},{80,48},{96,0},{112,80},{1... | collective-permute-start | bytes 2359304 | tf_op jit(solution)/shard_map/ppermute | solution.py:45
  21.1 2.4 %collective-permute-start.5 = (bf16[128,1536]{1,0:T(8,128)(2,1)S(1)}, bf16[128,1536]{1,0:T(8,128)(2,1)S(1)}, u32[]{:S(2)}, u32[]{:S(2)}) collective-permute-start(bf16[128,1536]{1,0:T(8,128)(2,1)S(1)} %get-tuple-element.109), channel_id=1, source_target_pairs={{0,7},{1,0},{2,1},{3,2},{4,3},{5,4},{6,5},{7,6},{8,15},{9,8},{10,9... | collective-permute-start | bytes 1179656 | tf_op jit(solution)/shard_map/ppermute | solution.py:29
  23.6 1.9 %collective-permute-start.12 = (bf16[192,1536]{1,0:T(8,128)(2,1)S(1)}, bf16[192,1536]{1,0:T(8,128)(2,1)S(1)}, u32[]{:S(2)}, u32[]{:S(2)}) collective-permute-start(bf16[192,1536]{1,0:T(8,128)(2,1)S(1)} %get-tuple-element.104), channel_id=1, source_target_pairs={{0,136},{128,0},{8,128},{136,8},{1,137},{129,1},{9,129},{137,9},{2... | collective-permute-start | bytes 1769480 | tf_op jit(solution)/shard_map/ppermute | solution.py:36
  26.4 1.2 %collective-permute-start.11 = (bf16[192,1536]{1,0:T(8,128)(2,1)S(1)}, bf16[192,1536]{1,0:T(8,128)(2,1)S(1)}, u32[]{:S(2)}, u32[]{:S(2)}) collective-permute-start(bf16[192,1536]{1,0:T(8,128)(2,1)S(1)} %get-tuple-element.104), channel_id=1, source_target_pairs={{0,128},{128,8},{8,136},{136,0},{1,129},{129,9},{9,137},{137,1},{2... | collective-permute-start | bytes 1769480 | tf_op jit(solution)/shard_map/ppermute | solution.py:36
  27.6 4.0 %collective-permute-done.5 = bf16[128,1536]{1,0:T(8,128)(2,1)S(1)} collective-permute-done((bf16[128,1536]{1,0:T(8,128)(2,1)S(1)}, bf16[128,1536]{1,0:T(8,128)(2,1)S(1)}, u32[]{:S(2)}, u32[]{:S(2)}) %collective-permute-start.5) | collective-permute-done | bytes 393248 | tf_op jit(solution)/shard_map/ppermute | solution.py:29
  31.6 2.9 %collective-permute-done.4 = bf16[128,1536]{1,0:T(8,128)(2,1)S(1)} collective-permute-done((bf16[128,1536]{1,0:T(8,128)(2,1)S(1)}, bf16[128,1536]{1,0:T(8,128)(2,1)S(1)}, u32[]{:S(2)}, u32[]{:S(2)}) %collective-permute-start.4) | collective-permute-done | bytes 393248 | tf_op jit(solution)/shard_map/ppermute | solution.py:29
  34.8 2.7 %collective-permute-start.10 = (bf16[128,1536]{1,0:T(8,128)(2,1)S(1)}, bf16[128,1536]{1,0:T(8,128)(2,1)S(1)}, u32[]{:S(2)}, u32[]{:S(2)}) collective-permute-start(bf16[128,1536]{1,0:T(8,128)(2,1)S(1)} %collective-permute-done.5), channel_id=1, source_target_pairs={{0,7},{1,0},{2,1},{3,2},{4,3},{5,4},{6,5},{7,6},{8,15},{9,8},{10,9... | collective-permute-start | bytes 1179656 | tf_op jit(solution)/shard_map/ppermute | solution.py:29
  37.5 1.5 %collective-permute-done.12.refs_6_ = bf16[192,1536]{1,0:T(8,128)(2,1)S(1)} collective-permute-done((bf16[192,1536]{1,0:T(8,128)(2,1)S(1)}, bf16[192,1536]{1,0:T(8,128)(2,1)S(1)}, u32[]{:S(2)}, u32[]{:S(2)}) %collective-permute-start.12) | collective-permute-done | bytes 589856 | tf_op jit(solution)/shard_map/ppermute | solution.py:36
  39.1 4.2 %collective-permute-start.13 = (bf16[128,1536]{1,0:T(8,128)(2,1)S(1)}, bf16[128,1536]{1,0:T(8,128)(2,1)S(1)}, u32[]{:S(2)}, u32[]{:S(2)}) collective-permute-start(bf16[128,1536]{1,0:T(8,128)(2,1)S(1)} %collective-permute-done.6), channel_id=1, source_target_pairs={{0,16},{16,0},{1,17},{17,1},{2,18},{18,2},{3,19},{19,3},{4,20},{20... | collective-permute-start | bytes 1179656 | tf_op jit(solution)/shard_map/ppermute | solution.py:49
  43.4 1.3 %collective-permute-start.21 = (bf16[128,1536]{1,0:T(8,128)(2,1)S(1)}, bf16[128,1536]{1,0:T(8,128)(2,1)S(1)}, u32[]{:S(2)}, u32[]{:S(2)}) collective-permute-start(bf16[128,1536]{1,0:T(8,128)(2,1)S(1)} %pad_maximum_fusion.3), channel_id=1, source_target_pairs={{0,136},{128,0},{8,128},{136,8},{1,137},{129,1},{9,129},{137,9},{2... | collective-permute-start | bytes 1179656 | tf_op jit(solution)/shard_map/ppermute | solution.py:36
  45.4 2.5 %collective-permute-start.16 = (bf16[96,1536]{1,0:T(8,128)(2,1)S(1)}, bf16[96,1536]{1,0:T(8,128)(2,1)S(1)}, u32[]{:S(2)}, u32[]{:S(2)}) collective-permute-start(bf16[96,1536]{1,0:T(8,128)(2,1)S(1)} %slice.77), channel_id=1, source_target_pairs={{0,7},{1,0},{2,1},{3,2},{4,3},{5,4},{6,5},{7,6},{8,15},{9,8},{10,9... | collective-permute-start | bytes 884744 | tf_op jit(solution)/shard_map/ppermute | solution.py:29
  47.9 2.4 %collective-permute-start.19 = (bf16[256,1536]{1,0:T(8,128)(2,1)S(1)}, bf16[256,1536]{1,0:T(8,128)(2,1)S(1)}, u32[]{:S(2)}, u32[]{:S(2)}) collective-permute-start(bf16[256,1536]{1,0:T(8,128)(2,1)S(1)} %pad_maximum_fusion.refs_11_), channel_id=1, source_target_pairs={{0,32},{16,112},{32,64},{48,16},{64,96},{80,48},{96,0},{112,80},{1... | collective-permute-start | bytes 2359304 | tf_op jit(solution)/shard_map/ppermute | solution.py:45
  50.5 4.8 %shard_map.50.early_ref = f32[768,1536]{1,0:T(8,128)S(1)} custom-call(bf16[768,1536]{1,0:T(8,128)(2,1)S(1)} %slice_dynamic-update-slice_fusion.2.grads_ref.refs_0_, bf16[1536,1536]{1,0:T(8,128)(2,1)S(1)} %bitcast.1), custom_call_target="tpu_custom_call" | custom-call | flops 3623878656 | bytes 12582912 | tf_op jit(solution)/shard_map/pallas_call | solution.py:71
  55.5 2.7 %collective-permute-start.18 = (bf16[32,1536]{1,0:T(8,128)(2,1)S(1)}, bf16[32,1536]{1,0:T(8,128)(2,1)S(1)}, u32[]{:S(2)}, u32[]{:S(2)}) collective-permute-start(bf16[32,1536]{1,0:T(8,128)(2,1)S(1)} %get-tuple-element.102), channel_id=1, source_target_pairs={{0,7},{1,0},{2,1},{3,2},{4,3},{5,4},{6,5},{7,6},{8,15},{9,8},{10,9... | collective-permute-start | bytes 294920 | tf_op jit(solution)/shard_map/ppermute | solution.py:29
  58.3 2.6 %collective-permute-start.23 = (bf16[128,1536]{1,0:T(8,128)(2,1)S(1)}, bf16[128,1536]{1,0:T(8,128)(2,1)S(1)}, u32[]{:S(2)}, u32[]{:S(2)}) collective-permute-start(bf16[128,1536]{1,0:T(8,128)(2,1)S(1)} %pad_maximum_fusion.4), channel_id=1, source_target_pairs={{0,136},{128,0},{8,128},{136,8},{1,137},{129,1},{9,129},{137,9},{2... | collective-permute-start | bytes 1179656 | tf_op jit(solution)/shard_map/ppermute | solution.py:36
  61.0 3.8 %collective-permute-start.25 = (bf16[768,1536]{1,0:T(8,128)(2,1)S(1)}, bf16[768,1536]{1,0:T(8,128)(2,1)S(1)}, u32[]{:S(2)}, u32[]{:S(2)}) collective-permute-start(bf16[768,1536]{1,0:T(8,128)(2,1)S(1)} %constant_dynamic-update-slice_fusion.17.refs_12_), channel_id=1, source_target_pairs={{0,16},{16,0},{1,17},{17,1},{2,18},{18,2},{3,19},{19,3},{4,20},{20... | collective-permute-start | bytes 7077896 | tf_op jit(solution)/shard_map/ppermute | solution.py:49
  64.8 2.0 %shard_map.51 = (f32[512,1536]{1,0:T(8,128)S(1)}, bf16[512,1536]{1,0:T(8,128)(2,1)S(1)}) custom-call(f32[768,1536]{1,0:T(8,128)S(1)} %shard_map.50.early_ref, bf16[256,1536]{1,0:T(8,128)(2,1)S(1)} %constant_dynamic-update-slice_fusion.13.grads_ref.refs_1_, bf16[1536,1536]{1,0:T(8,128)(2,1)S(1)} %bitcast.1), custom_call_target="tpu_custom_call" | custom-call | flops 1207959552 | bytes 8388608 | tf_op jit(solution)/shard_map/pallas_call | solution.py:109
  66.8 2.2 %collective-permute-done.22.refs_4_ = bf16[128,1536]{1,0:T(8,128)(2,1)S(1)} collective-permute-done((bf16[128,1536]{1,0:T(8,128)(2,1)S(1)}, bf16[128,1536]{1,0:T(8,128)(2,1)S(1)}, u32[]{:S(2)}, u32[]{:S(2)}) %collective-permute-start.22) | collective-permute-done | bytes 393248 | tf_op jit(solution)/shard_map/ppermute | solution.py:36
  69.0 4.6 %collective-permute-start.24 = (bf16[512,1536]{1,0:T(8,128)(2,1)S(1)}, bf16[512,1536]{1,0:T(8,128)(2,1)S(1)}, u32[]{:S(2)}, u32[]{:S(2)}) collective-permute-start(bf16[512,1536]{1,0:T(8,128)(2,1)S(1)} %get-tuple-element.66), channel_id=1, source_target_pairs={{0,16},{16,0},{1,17},{17,1},{2,18},{18,2},{3,19},{19,3},{4,20},{20... | collective-permute-start | bytes 4718600 | tf_op jit(solution)/shard_map/ppermute | solution.py:49
  73.6 3.0 %collective-permute-done.24 = bf16[512,1536]{1,0:T(8,128)(2,1)S(1)} collective-permute-done((bf16[512,1536]{1,0:T(8,128)(2,1)S(1)}, bf16[512,1536]{1,0:T(8,128)(2,1)S(1)}, u32[]{:S(2)}, u32[]{:S(2)}) %collective-permute-start.24) | collective-permute-done | bytes 1572896 | tf_op jit(solution)/shard_map/ppermute | solution.py:49
  77.1 1.5 %collective-permute-start.29 = (bf16[64,1536]{1,0:T(8,128)(2,1)S(1)}, bf16[64,1536]{1,0:T(8,128)(2,1)S(1)}, u32[]{:S(2)}, u32[]{:S(2)}) collective-permute-start(bf16[64,1536]{1,0:T(8,128)(2,1)S(1)} %pad_maximum_fusion.5), channel_id=1, source_target_pairs={{0,128},{128,8},{8,136},{136,0},{1,129},{129,9},{9,137},{137,1},{2... | collective-permute-start | bytes 589832 | tf_op jit(solution)/shard_map/ppermute | solution.py:36
  78.6 2.8 %collective-permute-start.26 = (bf16[128,1536]{1,0:T(8,128)(2,1)S(1)}, bf16[128,1536]{1,0:T(8,128)(2,1)S(1)}, u32[]{:S(2)}, u32[]{:S(2)}) collective-permute-start(bf16[128,1536]{1,0:T(8,128)(2,1)S(1)} %get-tuple-element.71), channel_id=1, source_target_pairs={{0,64},{32,96},{64,0},{96,32},{1,65},{33,97},{65,1},{97,33},{2,66}... | collective-permute-start | bytes 1179656 | tf_op jit(solution)/shard_map/ppermute | solution.py:40
  81.4 1.6 %collective-permute-start.27 = (bf16[128,1536]{1,0:T(8,128)(2,1)S(1)}, bf16[128,1536]{1,0:T(8,128)(2,1)S(1)}, u32[]{:S(2)}, u32[]{:S(2)}) collective-permute-start(bf16[128,1536]{1,0:T(8,128)(2,1)S(1)} %get-tuple-element.72), channel_id=1, source_target_pairs={{0,32},{32,64},{64,96},{96,0},{1,33},{33,65},{65,97},{97,1},{2,34}... | collective-permute-start | bytes 1179656 | tf_op jit(solution)/shard_map/ppermute | solution.py:40
  84.3 13.5 %shard_map.52 = bf16[1536,1536]{1,0:T(8,128)(2,1)} custom-call(bf16[768,1536]{1,0:T(8,128)(2,1)S(1)} %slice_dynamic-update-slice_fusion.2.grads_ref.refs_0_, bf16[256,1536]{1,0:T(8,128)(2,1)S(1)} %constant_dynamic-update-slice_fusion.13.grads_ref.refs_1_, bf16[192,1536]{1,0:T(8,128)(2,1)S(1)} %collective-permute-done.11.refs_2_, ...), custom_call_target="tpu_custom_call" | custom-call | flops 9663676416 | bytes 17825792 | tf_op jit(solution)/shard_map/pallas_call | solution.py:170
  97.8 1.8 %collective-permute-done.27 = bf16[128,1536]{1,0:T(8,128)(2,1)S(1)} collective-permute-done((bf16[128,1536]{1,0:T(8,128)(2,1)S(1)}, bf16[128,1536]{1,0:T(8,128)(2,1)S(1)}, u32[]{:S(2)}, u32[]{:S(2)}) %collective-permute-start.27) | collective-permute-done | bytes 393248 | tf_op jit(solution)/shard_map/ppermute | solution.py:40
  100.0 1.5 %fusion.7 = bf16[128,1536]{1,0:T(8,128)(2,1)} fusion(bf16[128,1536]{1,0:T(8,128)(2,1)S(1)} %copy-done, bf16[128,1536]{1,0:T(8,128)(2,1)S(1)} %collective-permute-done.26, bf16[128,1536]{1,0:T(8,128)(2,1)S(1)} %collective-permute-done.28, bf16[128,1536]{1,0:T(8,128)(2,1)S(1)} %collective-permute-done.27, f32[512,1536]{1,0:T(8,128)S(1)} %get-tuple-element.65, ...), kind=kLoop, calls=%fused_computation.14 | loop fusion | flops 5505024 | bytes 3145728 | tf_op jit(solution)/shard_map/convert_element_type | solution.py:243
  (74 shorter events, 7.0 us)
Async XLA Ops:
  1.9 15.0 %collective-permute-start = (bf16[128,1536]{1,0:T(8,128)(2,1)S(1)}, bf16[128,1536]{1,0:T(8,128)(2,1)S(1)}, u32[]{:S(2)}, u32[]{:S(2)}) collective-permute-start(bf16[128,1536]{1,0:T(8,128)(2,1)S(1)} %fusion.2), channel_id=1, source_target_pairs={{0,16},{16,0},{1,17},{17,1},{2,18},{18,2},{3,19},{19,3},{4,20},{20... | collective-permute-start | bytes 1179656 | tf_op jit(solution)/shard_map/ppermute | solution.py:49
  5.2 10.5 %collective-permute-start.2 = (bf16[64,1536]{1,0:T(8,128)(2,1)}, bf16[64,1536]{1,0:T(8,128)(2,1)S(1)}, u32[]{:S(2)}, u32[]{:S(2)}) collective-permute-start(bf16[64,1536]{1,0:T(8,128)(2,1)} %param.4), channel_id=1, source_target_pairs={{0,7},{1,0},{2,1},{3,2},{4,3},{5,4},{6,5},{7,6},{8,15},{9,8},{10,9... | collective-permute-start | bytes 589832 | tf_op jit(solution)/shard_map/ppermute | solution.py:29
  9.1 7.6 %collective-permute-start.1 = (bf16[64,1536]{1,0:T(8,128)(2,1)}, bf16[64,1536]{1,0:T(8,128)(2,1)S(1)}, u32[]{:S(2)}, u32[]{:S(2)}) collective-permute-start(bf16[64,1536]{1,0:T(8,128)(2,1)} %param.4), channel_id=1, source_target_pairs={{0,1},{1,2},{2,3},{3,4},{4,5},{5,6},{6,7},{7,0},{8,9},{9,10},{10,1... | collective-permute-start | bytes 589832 | tf_op jit(solution)/shard_map/ppermute | solution.py:29
  9.1 7.8 %collective-permute-start.3 = (bf16[64,1536]{1,0:T(8,128)(2,1)}, bf16[64,1536]{1,0:T(8,128)(2,1)S(1)}, u32[]{:S(2)}, u32[]{:S(2)}) collective-permute-start(bf16[64,1536]{1,0:T(8,128)(2,1)} %param.4), channel_id=1, source_target_pairs={{0,8},{128,136},{8,0},{136,128},{1,9},{129,137},{9,1},{137,129},{2... | collective-permute-start | bytes 589832 | tf_op jit(solution)/shard_map/ppermute | solution.py:36
  11.8 11.8 %collective-permute-start.8 = (bf16[128,1536]{1,0:T(8,128)(2,1)S(1)}, bf16[128,1536]{1,0:T(8,128)(2,1)S(1)}, u32[]{:S(2)}, u32[]{:S(2)}) collective-permute-start(bf16[128,1536]{1,0:T(8,128)(2,1)S(1)} %fusion.2), channel_id=1, source_target_pairs={{0,64},{32,96},{64,0},{96,32},{1,65},{33,97},{65,1},{97,33},{2,66}... | collective-permute-start | bytes 1179656 | tf_op jit(solution)/shard_map/ppermute | solution.py:40
  16.9 9.4 %collective-permute-start.6 = (bf16[128,1536]{1,0:T(8,128)(2,1)S(1)}, bf16[128,1536]{1,0:T(8,128)(2,1)S(1)}, u32[]{:S(2)}, u32[]{:S(2)}) collective-permute-start(bf16[128,1536]{1,0:T(8,128)(2,1)S(1)} %fusion.2), channel_id=1, source_target_pairs={{0,128},{128,0},{1,129},{129,1},{2,130},{130,2},{3,131},{131,3},{4... | collective-permute-start | bytes 1179656 | tf_op jit(solution)/shard_map/ppermute | solution.py:49
  18.1 32.4 %slice-start = ((s8[4718592]{0:T(1024)(128)(4,1)}), s8[4194304]{0:T(1024)(128)(4,1)S(1)}, s32[]{:S(2)}) async-start(s8[4718592]{0:T(1024)(128)(4,1)} %bitcast), calls=%async_computation | async-start | bytes 8388608
  18.2 16.2 %collective-permute-start.7 = (bf16[256,1536]{1,0:T(8,128)(2,1)S(1)}, bf16[256,1536]{1,0:T(8,128)(2,1)S(1)}, u32[]{:S(2)}, u32[]{:S(2)}) collective-permute-start(bf16[256,1536]{1,0:T(8,128)(2,1)S(1)} %constant_dynamic-update-slice_fusion.refs_10_), channel_id=1, source_target_pairs={{0,32},{16,112},{32,64},{48,16},{64,96},{80,48},{96,0},{112,80},{1... | collective-permute-start | bytes 2359304 | tf_op jit(solution)/shard_map/ppermute | solution.py:45
  21.1 10.5 %collective-permute-start.5 = (bf16[128,1536]{1,0:T(8,128)(2,1)S(1)}, bf16[128,1536]{1,0:T(8,128)(2,1)S(1)}, u32[]{:S(2)}, u32[]{:S(2)}) collective-permute-start(bf16[128,1536]{1,0:T(8,128)(2,1)S(1)} %get-tuple-element.109), channel_id=1, source_target_pairs={{0,7},{1,0},{2,1},{3,2},{4,3},{5,4},{6,5},{7,6},{8,15},{9,8},{10,9... | collective-permute-start | bytes 1179656 | tf_op jit(solution)/shard_map/ppermute | solution.py:29
  23.5 10.9 %collective-permute-start.4 = (bf16[128,1536]{1,0:T(8,128)(2,1)S(1)}, bf16[128,1536]{1,0:T(8,128)(2,1)S(1)}, u32[]{:S(2)}, u32[]{:S(2)}) collective-permute-start(bf16[128,1536]{1,0:T(8,128)(2,1)S(1)} %get-tuple-element.110), channel_id=1, source_target_pairs={{0,1},{1,2},{2,3},{3,4},{4,5},{5,6},{6,7},{7,0},{8,9},{9,10},{10,1... | collective-permute-start | bytes 1179656 | tf_op jit(solution)/shard_map/ppermute | solution.py:29
  23.6 15.5 %collective-permute-start.12 = (bf16[192,1536]{1,0:T(8,128)(2,1)S(1)}, bf16[192,1536]{1,0:T(8,128)(2,1)S(1)}, u32[]{:S(2)}, u32[]{:S(2)}) collective-permute-start(bf16[192,1536]{1,0:T(8,128)(2,1)S(1)} %get-tuple-element.104), channel_id=1, source_target_pairs={{0,136},{128,0},{8,128},{136,8},{1,137},{129,1},{9,129},{137,9},{2... | collective-permute-start | bytes 1769480 | tf_op jit(solution)/shard_map/ppermute | solution.py:36
  26.4 12.7 %collective-permute-start.11 = (bf16[192,1536]{1,0:T(8,128)(2,1)S(1)}, bf16[192,1536]{1,0:T(8,128)(2,1)S(1)}, u32[]{:S(2)}, u32[]{:S(2)}) collective-permute-start(bf16[192,1536]{1,0:T(8,128)(2,1)S(1)} %get-tuple-element.104), channel_id=1, source_target_pairs={{0,128},{128,8},{8,136},{136,0},{1,129},{129,9},{9,137},{137,1},{2... | collective-permute-start | bytes 1769480 | tf_op jit(solution)/shard_map/ppermute | solution.py:36
  34.4 10.9 %collective-permute-start.14 = (bf16[128,1536]{1,0:T(8,128)(2,1)S(1)}, bf16[128,1536]{1,0:T(8,128)(2,1)S(1)}, u32[]{:S(2)}, u32[]{:S(2)}) collective-permute-start(bf16[128,1536]{1,0:T(8,128)(2,1)S(1)} %collective-permute-done.6), channel_id=1, source_target_pairs={{0,64},{32,96},{64,0},{96,32},{1,65},{33,97},{65,1},{97,33},{2,66}... | collective-permute-start | bytes 1179656 | tf_op jit(solution)/shard_map/ppermute | solution.py:40
  34.8 10.5 %collective-permute-start.9 = (bf16[128,1536]{1,0:T(8,128)(2,1)S(1)}, bf16[128,1536]{1,0:T(8,128)(2,1)S(1)}, u32[]{:S(2)}, u32[]{:S(2)}) collective-permute-start(bf16[128,1536]{1,0:T(8,128)(2,1)S(1)} %collective-permute-done.4), channel_id=1, source_target_pairs={{0,1},{1,2},{2,3},{3,4},{4,5},{5,6},{6,7},{7,0},{8,9},{9,10},{10,1... | collective-permute-start | bytes 1179656 | tf_op jit(solution)/shard_map/ppermute | solution.py:29
  34.8 10.5 %collective-permute-start.10 = (bf16[128,1536]{1,0:T(8,128)(2,1)S(1)}, bf16[128,1536]{1,0:T(8,128)(2,1)S(1)}, u32[]{:S(2)}, u32[]{:S(2)}) collective-permute-start(bf16[128,1536]{1,0:T(8,128)(2,1)S(1)} %collective-permute-done.5), channel_id=1, source_target_pairs={{0,7},{1,0},{2,1},{3,2},{4,3},{5,4},{6,5},{7,6},{8,15},{9,8},{10,9... | collective-permute-start | bytes 1179656 | tf_op jit(solution)/shard_map/ppermute | solution.py:29
  39.1 5.7 %collective-permute-start.13 = (bf16[128,1536]{1,0:T(8,128)(2,1)S(1)}, bf16[128,1536]{1,0:T(8,128)(2,1)S(1)}, u32[]{:S(2)}, u32[]{:S(2)}) collective-permute-start(bf16[128,1536]{1,0:T(8,128)(2,1)S(1)} %collective-permute-done.6), channel_id=1, source_target_pairs={{0,16},{16,0},{1,17},{17,1},{2,18},{18,2},{3,19},{19,3},{4,20},{20... | collective-permute-start | bytes 1179656 | tf_op jit(solution)/shard_map/ppermute | solution.py:49
  43.4 14.9 %collective-permute-start.21 = (bf16[128,1536]{1,0:T(8,128)(2,1)S(1)}, bf16[128,1536]{1,0:T(8,128)(2,1)S(1)}, u32[]{:S(2)}, u32[]{:S(2)}) collective-permute-start(bf16[128,1536]{1,0:T(8,128)(2,1)S(1)} %pad_maximum_fusion.3), channel_id=1, source_target_pairs={{0,136},{128,0},{8,128},{136,8},{1,137},{129,1},{9,129},{137,9},{2... | collective-permute-start | bytes 1179656 | tf_op jit(solution)/shard_map/ppermute | solution.py:36
  44.8 16.0 %collective-permute-start.20 = (bf16[128,1536]{1,0:T(8,128)(2,1)S(1)}, bf16[128,1536]{1,0:T(8,128)(2,1)S(1)}, u32[]{:S(2)}, u32[]{:S(2)}) collective-permute-start(bf16[128,1536]{1,0:T(8,128)(2,1)S(1)} %pad_maximum_fusion.3), channel_id=1, source_target_pairs={{0,128},{128,8},{8,136},{136,0},{1,129},{129,9},{9,137},{137,1},{2... | collective-permute-start | bytes 1179656 | tf_op jit(solution)/shard_map/ppermute | solution.py:36
  45.4 9.9 %collective-permute-start.16 = (bf16[96,1536]{1,0:T(8,128)(2,1)S(1)}, bf16[96,1536]{1,0:T(8,128)(2,1)S(1)}, u32[]{:S(2)}, u32[]{:S(2)}) collective-permute-start(bf16[96,1536]{1,0:T(8,128)(2,1)S(1)} %slice.77), channel_id=1, source_target_pairs={{0,7},{1,0},{2,1},{3,2},{4,3},{5,4},{6,5},{7,6},{8,15},{9,8},{10,9... | collective-permute-start | bytes 884744 | tf_op jit(solution)/shard_map/ppermute | solution.py:29
  47.9 7.4 %collective-permute-start.15 = (bf16[96,1536]{1,0:T(8,128)(2,1)S(1)}, bf16[96,1536]{1,0:T(8,128)(2,1)S(1)}, u32[]{:S(2)}, u32[]{:S(2)}) collective-permute-start(bf16[96,1536]{1,0:T(8,128)(2,1)S(1)} %slice.76), channel_id=1, source_target_pairs={{0,1},{1,2},{2,3},{3,4},{4,5},{5,6},{6,7},{7,0},{8,9},{9,10},{10,1... | collective-permute-start | bytes 884744 | tf_op jit(solution)/shard_map/ppermute | solution.py:29
  47.9 13.0 %collective-permute-start.19 = (bf16[256,1536]{1,0:T(8,128)(2,1)S(1)}, bf16[256,1536]{1,0:T(8,128)(2,1)S(1)}, u32[]{:S(2)}, u32[]{:S(2)}) collective-permute-start(bf16[256,1536]{1,0:T(8,128)(2,1)S(1)} %pad_maximum_fusion.refs_11_), channel_id=1, source_target_pairs={{0,32},{16,112},{32,64},{48,16},{64,96},{80,48},{96,0},{112,80},{1... | collective-permute-start | bytes 2359304 | tf_op jit(solution)/shard_map/ppermute | solution.py:45
  55.4 5.5 %collective-permute-start.17 = (bf16[32,1536]{1,0:T(8,128)(2,1)S(1)}, bf16[32,1536]{1,0:T(8,128)(2,1)S(1)}, u32[]{:S(2)}, u32[]{:S(2)}) collective-permute-start(bf16[32,1536]{1,0:T(8,128)(2,1)S(1)} %get-tuple-element.99), channel_id=1, source_target_pairs={{0,1},{1,2},{2,3},{3,4},{4,5},{5,6},{6,7},{7,0},{8,9},{9,10},{10,1... | collective-permute-start | bytes 294920 | tf_op jit(solution)/shard_map/ppermute | solution.py:29
  55.5 5.4 %collective-permute-start.18 = (bf16[32,1536]{1,0:T(8,128)(2,1)S(1)}, bf16[32,1536]{1,0:T(8,128)(2,1)S(1)}, u32[]{:S(2)}, u32[]{:S(2)}) collective-permute-start(bf16[32,1536]{1,0:T(8,128)(2,1)S(1)} %get-tuple-element.102), channel_id=1, source_target_pairs={{0,7},{1,0},{2,1},{3,2},{4,3},{5,4},{6,5},{7,6},{8,15},{9,8},{10,9... | collective-permute-start | bytes 294920 | tf_op jit(solution)/shard_map/ppermute | solution.py:29
  58.3 8.5 %collective-permute-start.23 = (bf16[128,1536]{1,0:T(8,128)(2,1)S(1)}, bf16[128,1536]{1,0:T(8,128)(2,1)S(1)}, u32[]{:S(2)}, u32[]{:S(2)}) collective-permute-start(bf16[128,1536]{1,0:T(8,128)(2,1)S(1)} %pad_maximum_fusion.4), channel_id=1, source_target_pairs={{0,136},{128,0},{8,128},{136,8},{1,137},{129,1},{9,129},{137,9},{2... | collective-permute-start | bytes 1179656 | tf_op jit(solution)/shard_map/ppermute | solution.py:36
  60.8 8.1 %collective-permute-start.22 = (bf16[128,1536]{1,0:T(8,128)(2,1)S(1)}, bf16[128,1536]{1,0:T(8,128)(2,1)S(1)}, u32[]{:S(2)}, u32[]{:S(2)}) collective-permute-start(bf16[128,1536]{1,0:T(8,128)(2,1)S(1)} %pad_maximum_fusion.4), channel_id=1, source_target_pairs={{0,128},{128,8},{8,136},{136,0},{1,129},{129,9},{9,137},{137,1},{2... | collective-permute-start | bytes 1179656 | tf_op jit(solution)/shard_map/ppermute | solution.py:36
  61.0 16.0 %collective-permute-start.25 = (bf16[768,1536]{1,0:T(8,128)(2,1)S(1)}, bf16[768,1536]{1,0:T(8,128)(2,1)S(1)}, u32[]{:S(2)}, u32[]{:S(2)}) collective-permute-start(bf16[768,1536]{1,0:T(8,128)(2,1)S(1)} %constant_dynamic-update-slice_fusion.17.refs_12_), channel_id=1, source_target_pairs={{0,16},{16,0},{1,17},{17,1},{2,18},{18,2},{3,19},{19,3},{4,20},{20... | collective-permute-start | bytes 7077896 | tf_op jit(solution)/shard_map/ppermute | solution.py:49
  69.0 7.6 %collective-permute-start.24 = (bf16[512,1536]{1,0:T(8,128)(2,1)S(1)}, bf16[512,1536]{1,0:T(8,128)(2,1)S(1)}, u32[]{:S(2)}, u32[]{:S(2)}) collective-permute-start(bf16[512,1536]{1,0:T(8,128)(2,1)S(1)} %get-tuple-element.66), channel_id=1, source_target_pairs={{0,16},{16,0},{1,17},{17,1},{2,18},{18,2},{3,19},{19,3},{4,20},{20... | collective-permute-start | bytes 4718600 | tf_op jit(solution)/shard_map/ppermute | solution.py:49
  77.0 7.1 %collective-permute-start.30 = (bf16[64,1536]{1,0:T(8,128)(2,1)S(1)}, bf16[64,1536]{1,0:T(8,128)(2,1)S(1)}, u32[]{:S(2)}, u32[]{:S(2)}) collective-permute-start(bf16[64,1536]{1,0:T(8,128)(2,1)S(1)} %pad_maximum_fusion.5), channel_id=1, source_target_pairs={{0,136},{128,0},{8,128},{136,8},{1,137},{129,1},{9,129},{137,9},{2... | collective-permute-start | bytes 589832 | tf_op jit(solution)/shard_map/ppermute | solution.py:36
  77.1 7.2 %collective-permute-start.29 = (bf16[64,1536]{1,0:T(8,128)(2,1)S(1)}, bf16[64,1536]{1,0:T(8,128)(2,1)S(1)}, u32[]{:S(2)}, u32[]{:S(2)}) collective-permute-start(bf16[64,1536]{1,0:T(8,128)(2,1)S(1)} %pad_maximum_fusion.5), channel_id=1, source_target_pairs={{0,128},{128,8},{8,136},{136,0},{1,129},{129,9},{9,137},{137,1},{2... | collective-permute-start | bytes 589832 | tf_op jit(solution)/shard_map/ppermute | solution.py:36
  78.6 19.2 %collective-permute-start.26 = (bf16[128,1536]{1,0:T(8,128)(2,1)S(1)}, bf16[128,1536]{1,0:T(8,128)(2,1)S(1)}, u32[]{:S(2)}, u32[]{:S(2)}) collective-permute-start(bf16[128,1536]{1,0:T(8,128)(2,1)S(1)} %get-tuple-element.71), channel_id=1, source_target_pairs={{0,64},{32,96},{64,0},{96,32},{1,65},{33,97},{65,1},{97,33},{2,66}... | collective-permute-start | bytes 1179656 | tf_op jit(solution)/shard_map/ppermute | solution.py:40
  81.4 18.1 %collective-permute-start.27 = (bf16[128,1536]{1,0:T(8,128)(2,1)S(1)}, bf16[128,1536]{1,0:T(8,128)(2,1)S(1)}, u32[]{:S(2)}, u32[]{:S(2)}) collective-permute-start(bf16[128,1536]{1,0:T(8,128)(2,1)S(1)} %get-tuple-element.72), channel_id=1, source_target_pairs={{0,32},{32,64},{64,96},{96,0},{1,33},{33,65},{65,97},{97,1},{2,34}... | collective-permute-start | bytes 1179656 | tf_op jit(solution)/shard_map/ppermute | solution.py:40
  83.0 17.0 %collective-permute-start.28 = (bf16[128,1536]{1,0:T(8,128)(2,1)S(1)}, bf16[128,1536]{1,0:T(8,128)(2,1)S(1)}, u32[]{:S(2)}, u32[]{:S(2)}) collective-permute-start(bf16[128,1536]{1,0:T(8,128)(2,1)S(1)} %get-tuple-element.73), channel_id=1, source_target_pairs={{0,96},{32,0},{64,32},{96,64},{1,97},{33,1},{65,33},{97,65},{2,98}... | collective-permute-start | bytes 1179656 | tf_op jit(solution)/shard_map/ppermute | solution.py:40
  (2 other events, 30.1 us)

commit v7 on v6

--- a/solution.py
+++ b/solution.py
@@ -57,8 +57,8 @@
 
 
 VMEM = pl.BlockSpec(memory_space=pltpu.VMEM)
-EARLY = [(0, k) for k in range(7)] + [(1, k) for k in range(5)]
-LATE = [(0, 7), (1, 5), (1, 6), (1, 7)]
+EARLY = [(0, k) for k in range(8)] + [(1, k) for k in range(5)]
+LATE = [(1, 5), (1, 6), (1, 7)]
 
 
 def early_kernel(grads_ref, w_ref, out_ref):
@@ -111,22 +111,22 @@
         in_specs=[VMEM] * 3,
         out_specs=[VMEM] * 2,
         out_shape=[jax.ShapeDtypeStruct((512, 1536), F32), jax.ShapeDtypeStruct((512, 1536), BF)],
-        scratch_shapes=[pltpu.VMEM((256, 1536), F32)],
+        scratch_shapes=[pltpu.VMEM((64 * len(LATE), 1536), F32)],
         compiler_params=pltpu.CompilerParams(vmem_limit_bytes=8 << 20),
-        cost_estimate=pl.CostEstimate(flops=2 * 256 * 1536 * 1536, bytes_accessed=8 << 20, transcendentals=0),
+        cost_estimate=pl.CostEstimate(flops=2 * 192 * 1536 * 1536, bytes_accessed=8 << 20, transcendentals=0),
     )(early, grads, weight)
 
 
 PIECES = [
     [(2 * far, OWN[j]) for far, j in EARLY],
     [(2 * far, OWN[j]) for far, j in LATE],
-    *[[(dx, OWN[j]) for j in group] for dx in (3, 1) for group in ((0, 1, 2), (3, 4), (5, 6), (7,))],
+    *[[(dx, OWN[j]) for j in group] for dx in (3, 1) for group in ((0, 1, 2), (3, 4), (7, 5, 6))],
 ]
 
 
 def weight_kernel(*refs):
-    pieces, acts_refs = refs[:10], refs[10:14]
-    out_ref, grads, acts = refs[14:]
+    pieces, acts_refs = refs[:8], refs[8:13]
+    out_ref, grads, acts = refs[13:]
     y, c, xl, xh, z = (lax.axis_index(a) for a in ("y", "c", "xl", "xh", "z"))
 
     @pl.when(pl.program_id(0) == 0)
@@ -153,7 +153,18 @@
 
             @pl.when((dy == 4 - back) | ((dy == 2) & (away == 1)))
             def _():
-                copy(3, 3 * other + jnp.where(dy == 2, 2, 1 - away))
+                if other:
+
+                    @pl.when(dy == 2)
+                    def _():
+                        copy(3, 3)
+
+                    @pl.when(dy != 2)
+                    def _():
+                        copy(4, 1 - away)
+
+                else:
+                    copy(3, jnp.where(dy == 2, 2, 1 - away))
 
     lanes = pl.ds(pl.multiple_of(pl.program_id(0) * 256, 256), 256)
     start = 0
@@ -170,7 +181,7 @@
     return pl.pallas_call(
         weight_kernel,
         grid=(1536 // step,),
-        in_specs=[VMEM] * 14,
+        in_specs=[VMEM] * 13,
         out_specs=pl.BlockSpec((step, 1536), lambda m: (m, 0)),
         out_shape=jax.ShapeDtypeStruct((1536, 1536), BF),
         scratch_shapes=[pltpu.VMEM((2048, step), BF), pltpu.VMEM((2048, 1536), BF)],
@@ -185,59 +196,60 @@
     activation = gelu_tanh(pre_wide).astype(BF)
 
     up1, down1, far = along_z(g, 1), along_z(g, -1), along_x(g, 2)
+    opposite = along_z(g, 4)
     act_c = swap(activation, "c")
     hop_2 = along_y(activation, 2)
-    activation, act_c, up1, down1, far = tie(activation, act_c, up1, down1, far)
+    activation, act_c, up1, down1, far, opposite = tie(activation, act_c, up1, down1, far, opposite)
 
     up2 = along_z(jnp.concatenate([far, up1]), 1)
     down2 = along_z(jnp.concatenate([down1, far]), -1)
     other_rep = swap(activation, "xl")
     chip = jnp.concatenate([activation, act_c])
+    near = jnp.concatenate([g, up1, down1])
     hop_1 = round_y(chip)
+    other_rep, near = tie(other_rep, near)
+    left_a, right_a = along_x(near, 1), along_x(near, -1)
+    far_opposite = along_x(opposite, 2)
     up2, down2, other_rep, hop_1, hop_2 = tie(up2, down2, other_rep, hop_1, hop_2)
 
     up3, down3 = along_z(up2, 1), along_z(down2, -1)
-    near = jnp.concatenate([g, up1, down1])
-    left_a, right_a = along_x(near, 1), along_x(near, -1)
     hop_4 = along_y(other_rep, 2)
     other_rep, left_a, right_a = tie(other_rep, left_a, right_a)
     other_chip = jnp.concatenate([other_rep, swap(other_rep, "c")])
-    up3, down3, left_a, right_a, other_chip, hop_4 = tie(up3, down3, left_a, right_a, other_chip, hop_4)
-
-    up4, down4 = along_z(up3[:96], 1), along_z(down3[32:], -1)
     middle = jnp.concatenate([up2[64:], down2[:64]])
     left_b, right_b = along_x(middle, 1), along_x(middle, -1)
+    up3, down3, left_a, right_a, other_chip, far_opposite = tie(
+        up3, down3, left_a, right_a, other_chip, far_opposite
+    )
+
+    up4, down4 = along_z(up3[:64], 1), along_z(down3[64:], -1)
     hop_3 = round_y(other_chip)
-    up4, down4 = tie(up4, down4)
-    own = [g, up1, down1, up2[64:], down2[:64], up3[64:], down3[:64]]
+    own = [g, up1, down1, up2[64:], down2[:64], up3[64:], down3[:64], opposite]
     second = [far, up2[:64], down2[64:], up3[:64], down3[64:]]
     grads_early = jnp.concatenate(own + second)
     early = early_partial(grads_early, down_weight)
-
-    up5, down5 = along_z(up4[:32], 1), along_z(down4[64:], -1)
-    last = jnp.concatenate([up4[64:], down4[:32]])
-    third = jnp.concatenate([up3[64:], down3[:64]])
+    third = jnp.concatenate([opposite, up3[64:], down3[:64]])
     left_c, right_c = along_x(third, 1), along_x(third, -1)
-    up5, down5, early, hop_3, left_b, right_b = tie(up5, down5, early, hop_3, left_b, right_b)
-
-    grads_late = jnp.concatenate([last, up4[:64], down4[32:], up5, down5])
+    up4, down4, early, left_b, right_b, hop_4 = tie(up4, down4, early, left_b, right_b, hop_4)
+    swap_a = swap(jnp.concatenate([hop_1, hop_2, hop_4]), "c")
+
+    grads_late = jnp.concatenate([up4, down4, far_opposite])
     mine, other = late_partial(early, grads_late, down_weight)
-    mine, other, left_c, right_c = tie(mine, other, left_c, right_c)
+    other, hop_3 = tie(other, hop_3)
     other = swap(other, "c")
-    came = jnp.concatenate([hop_1, hop_2, hop_3, hop_4])
-    swapped = swap(came, "c")
+    swap_b = swap(hop_3, "c")
 
     def summed(block):
         return mine[128 * block : 128 * block + 128] + other[128 * block : 128 * block + 128].astype(F32)
 
     to_above, to_below, to_across = summed(1).astype(BF), summed(3).astype(BF), summed(2).astype(BF)
-    to_above, to_below, to_across, swapped, last = tie(to_above, to_below, to_across, swapped, last)
-    left_d, right_d = along_x(last, 1), along_x(last, -1)
+    to_above, to_below, to_across, swap_a, swap_b = tie(to_above, to_below, to_across, swap_a, swap_b)
     from_across = along_y(to_across, 2)
     from_below, from_above = along_y(to_above, 1), along_y(to_below, -1)
 
-    arrived = [left_a, left_b, left_c, left_d, right_a, right_b, right_c, right_d]
-    weight_grad = weight_gradient([grads_early, grads_late, *arrived], [chip, other_chip, came, swapped])
+    arrived = [left_a, left_b, left_c, right_a, right_b, right_c]
+    came = jnp.concatenate([hop_1, hop_2, hop_3, hop_4])
+    weight_grad = weight_gradient([grads_early, grads_late, *arrived], [chip, other_chip, came, swap_a, swap_b])
     from_across, from_below, from_above, weight_grad = tie(from_across, from_below, from_above, weight_grad)
     grad_act = summed(0) + from_below.astype(F32) + from_above.astype(F32) + from_across.astype(F32)
     pre_grad = (grad_act * gelu_slope(pre_wide)).astype(BF)

time: 102 us -> 112 us (1.098)
  waiting for transfers between devices: 18.2 us -> 25.1 us
  starting transfers between devices: 57.1 us -> 59.9 us
    ppermute x9 -> x8, waiting for transfers between devices: 4.27 us -> 9.99 us  [along_x(): lax.ppermute(a, ('xl', 'xh'), [(place(x), place((x + d) % 4)) for x in ra...]
    ppermute x5 -> x6, starting transfers between devices: 17.1 us -> 11.7 us  [swap(): return lax.ppermute(a, axis, [(0, 1), (1, 0)])]
    ppermute x10 -> x9, starting transfers between devices: 14.2 us -> 18.9 us  [along_z(): return lax.ppermute(a, 'z', [(i, (i + d) % Z) for i in range(Z)])]
    ppermute x2, waiting for transfers between devices: 0.01 us -> 3.36 us  [round_y(): lax.ppermute(a, ('y', 'c'), [(s[0] * C + s[1], t[0] * C + t[1]) for s, t...]
    ppermute x9 -> x8, starting transfers between devices: 11.7 us -> 14.3 us  [along_x(): lax.ppermute(a, ('xl', 'xh'), [(place(x), place((x + d) % 4)) for x in ra...]
    ppermute x5, waiting for transfers between devices: 2.19 us -> 0.01 us  [along_y(): return lax.ppermute(a, 'y', [(i, (i + d) % Y) for i in range(Y)])]
    ppermute x10 -> x9, waiting for transfers between devices: 7.82 us -> 7.91 us  [along_z(): return lax.ppermute(a, 'z', [(i, (i + d) % Z) for i in range(Z)])]
    ppermute x5 -> x6, waiting for transfers between devices: 3.9 us -> 3.87 us  [swap(): return lax.ppermute(a, axis, [(0, 1), (1, 0)])]
  transfers between devices with their start and end apart: 31 -> 30, of which waited for: 11 -> 8; matrix products, arithmetic and copies ran while one was open for 2% -> 2% of each run, Pallas kernels for 20% -> 18%
where the time goes in v7:
time: 112 us; the launch traced here: 111 us
  starting transfers between devices  59.9 us (53%)
  waiting for transfers between devices  25.1 us (22%)
  Pallas kernels  20.3 us (18%)
  other arithmetic  3.6 us (3%)
  local copies, waits for them, and re-layouts  1.34 us (1%)
    ppermute x9, starting transfers between devices, along_z(): return lax.ppermute(a, 'z', [(i, (i + d) % Z) for i in range(Z)])  18.9 us
    ppermute x8, starting transfers between devices, along_x(): lax.ppermute(a, ('xl', 'xh'), [(place(x), place((x + d) % 4)) for x in ra...  14.3 us
    pallas_call x1, Pallas kernels, weight_gradient(): pl.pallas_call(weight_kernel, grid=(1536 // step,), in_specs=[VMEM] * 13,...  13.5 us
    ppermute x6, starting transfers between devices, swap(): return lax.ppermute(a, axis, [(0, 1), (1, 0)])  11.7 us
    ppermute x8, waiting for transfers between devices, along_x(): lax.ppermute(a, ('xl', 'xh'), [(place(x), place((x + d) % 4)) for x in ra...  9.99 us
    ppermute x5, starting transfers between devices, along_y(): return lax.ppermute(a, 'y', [(i, (i + d) % Y) for i in range(Y)])  9.85 us
    ppermute x9, waiting for transfers between devices, along_z(): return lax.ppermute(a, 'z', [(i, (i + d) % Z) for i in range(Z)])  7.91 us
    ppermute x2, starting transfers between devices, round_y(): lax.ppermute(a, ('y', 'c'), [(s[0] * C + s[1], t[0] * C + t[1]) for s, t...  5.13 us
  transfers between devices with their start and end apart: 30, of which 8 were waited for; matrix products, arithmetic and copies ran while one was open for 2% of the time, Pallas kernels for 18%

profile of v7, /device:TPU:1, one launch (start us, length us, event | category | flops | bytes accessed | tf_op | source)
XLA Modules:
  0.0 111.2 jit_solution(18235610598078618786)
XLA Ops:
  2.0 3.3 %collective-permute-start = (bf16[128,1536]{1,0:T(8,128)(2,1)S(1)}, bf16[128,1536]{1,0:T(8,128)(2,1)S(1)}, u32[]{:S(2)}, u32[]{:S(2)}) collective-permute-start(bf16[128,1536]{1,0:T(8,128)(2,1)S(1)} %fusion.2), channel_id=1, source_target_pairs={{0,16},{16,0},{1,17},{17,1},{2,18},{18,2},{3,19},{19,3},{4,20},{20... | collective-permute-start | bytes 1179656 | tf_op jit(solution)/shard_map/ppermute | solution.py:49
  5.3 3.8 %collective-permute-start.2 = (bf16[64,1536]{1,0:T(8,128)(2,1)}, bf16[64,1536]{1,0:T(8,128)(2,1)S(1)}, u32[]{:S(2)}, u32[]{:S(2)}) collective-permute-start(bf16[64,1536]{1,0:T(8,128)(2,1)} %param.4), channel_id=1, source_target_pairs={{0,7},{1,0},{2,1},{3,2},{4,3},{5,4},{6,5},{7,6},{8,15},{9,8},{10,9... | collective-permute-start | bytes 589832 | tf_op jit(solution)/shard_map/ppermute | solution.py:29
  9.1 2.7 %collective-permute-start.3 = (bf16[64,1536]{1,0:T(8,128)(2,1)}, bf16[64,1536]{1,0:T(8,128)(2,1)S(1)}, u32[]{:S(2)}, u32[]{:S(2)}) collective-permute-start(bf16[64,1536]{1,0:T(8,128)(2,1)} %param.4), channel_id=1, source_target_pairs={{0,8},{128,136},{8,0},{136,128},{1,9},{129,137},{9,1},{137,129},{2... | collective-permute-start | bytes 589832 | tf_op jit(solution)/shard_map/ppermute | solution.py:36
  11.9 4.0 %collective-permute-start.4 = (bf16[64,1536]{1,0:T(8,128)(2,1)}, bf16[64,1536]{1,0:T(8,128)(2,1)S(1)}, u32[]{:S(2)}, u32[]{:S(2)}) collective-permute-start(bf16[64,1536]{1,0:T(8,128)(2,1)} %param.4), channel_id=1, source_target_pairs={{0,4},{1,5},{2,6},{3,7},{4,0},{5,1},{6,2},{7,3},{8,12},{9,13},{10,... | collective-permute-start | bytes 589832 | tf_op jit(solution)/shard_map/ppermute | solution.py:29
  16.9 3.0 %collective-permute-start.9 = (bf16[128,1536]{1,0:T(8,128)(2,1)S(1)}, bf16[128,1536]{1,0:T(8,128)(2,1)S(1)}, u32[]{:S(2)}, u32[]{:S(2)}) collective-permute-start(bf16[128,1536]{1,0:T(8,128)(2,1)S(1)} %fusion.2), channel_id=1, source_target_pairs={{0,64},{32,96},{64,0},{96,32},{1,65},{33,97},{65,1},{97,33},{2,66}... | collective-permute-start | bytes 1179656 | tf_op jit(solution)/shard_map/ppermute | solution.py:40
  19.9 5.2 %collective-permute-done.4 = bf16[64,1536]{1,0:T(8,128)(2,1)S(1)} collective-permute-done((bf16[64,1536]{1,0:T(8,128)(2,1)}, bf16[64,1536]{1,0:T(8,128)(2,1)S(1)}, u32[]{:S(2)}, u32[]{:S(2)}) %collective-permute-start.4) | collective-permute-done | bytes 196640 | tf_op jit(solution)/shard_map/ppermute | solution.py:29
  25.4 2.8 %collective-permute-start.8 = (bf16[256,1536]{1,0:T(8,128)(2,1)S(1)}, bf16[256,1536]{1,0:T(8,128)(2,1)S(1)}, u32[]{:S(2)}, u32[]{:S(2)}) collective-permute-start(bf16[256,1536]{1,0:T(8,128)(2,1)S(1)} %constant_dynamic-update-slice_fusion.refs_8_), channel_id=1, source_target_pairs={{0,32},{16,112},{32,64},{48,16},{64,96},{80,48},{96,0},{112,80},{1... | collective-permute-start | bytes 2359304 | tf_op jit(solution)/shard_map/ppermute | solution.py:45
  28.3 1.9 %collective-permute-start.5 = (bf16[128,1536]{1,0:T(8,128)(2,1)S(1)}, bf16[128,1536]{1,0:T(8,128)(2,1)S(1)}, u32[]{:S(2)}, u32[]{:S(2)}) collective-permute-start(bf16[128,1536]{1,0:T(8,128)(2,1)S(1)} %get-tuple-element.98), channel_id=1, source_target_pairs={{0,1},{1,2},{2,3},{3,4},{4,5},{5,6},{6,7},{7,0},{8,9},{9,10},{10,1... | collective-permute-start | bytes 1179656 | tf_op jit(solution)/shard_map/ppermute | solution.py:29
  31.1 2.0 %collective-permute-done.7 = bf16[128,1536]{1,0:T(8,128)(2,1)S(1)} collective-permute-done((bf16[128,1536]{1,0:T(8,128)(2,1)S(1)}, bf16[128,1536]{1,0:T(8,128)(2,1)S(1)}, u32[]{:S(2)}, u32[]{:S(2)}) %collective-permute-start.7) | collective-permute-done | bytes 393248 | tf_op jit(solution)/shard_map/ppermute | solution.py:49
  33.5 2.4 %collective-permute-start.13 = (bf16[192,1536]{1,0:T(8,128)(2,1)S(1)}, bf16[192,1536]{1,0:T(8,128)(2,1)S(1)}, u32[]{:S(2)}, u32[]{:S(2)}) collective-permute-start(bf16[192,1536]{1,0:T(8,128)(2,1)S(1)} %pad_maximum_fusion.3), channel_id=1, source_target_pairs={{0,136},{128,0},{8,128},{136,8},{1,137},{129,1},{9,129},{137,9},{2... | collective-permute-start | bytes 1769480 | tf_op jit(solution)/shard_map/ppermute | solution.py:36
  35.9 2.7 %collective-permute-done.5 = bf16[128,1536]{1,0:T(8,128)(2,1)S(1)} collective-permute-done((bf16[128,1536]{1,0:T(8,128)(2,1)S(1)}, bf16[128,1536]{1,0:T(8,128)(2,1)S(1)}, u32[]{:S(2)}, u32[]{:S(2)}) %collective-permute-start.5) | collective-permute-done | bytes 393248 | tf_op jit(solution)/shard_map/ppermute | solution.py:29
  38.6 2.5 %collective-permute-start.15 = (bf16[64,1536]{1,0:T(8,128)(2,1)S(1)}, bf16[64,1536]{1,0:T(8,128)(2,1)S(1)}, u32[]{:S(2)}, u32[]{:S(2)}) collective-permute-start(bf16[64,1536]{1,0:T(8,128)(2,1)S(1)} %collective-permute-done.4), channel_id=1, source_target_pairs={{0,8},{128,136},{8,0},{136,128},{1,9},{129,137},{9,1},{137,129},{2... | collective-permute-start | bytes 589832 | tf_op jit(solution)/shard_map/ppermute | solution.py:36
  41.1 1.8 %collective-permute-start.10 = (bf16[128,1536]{1,0:T(8,128)(2,1)S(1)}, bf16[128,1536]{1,0:T(8,128)(2,1)S(1)}, u32[]{:S(2)}, u32[]{:S(2)}) collective-permute-start(bf16[128,1536]{1,0:T(8,128)(2,1)S(1)} %collective-permute-done.5), channel_id=1, source_target_pairs={{0,1},{1,2},{2,3},{3,4},{4,5},{5,6},{6,7},{7,0},{8,9},{9,10},{10,1... | collective-permute-start | bytes 1179656 | tf_op jit(solution)/shard_map/ppermute | solution.py:29
  43.8 2.0 %collective-permute-done.12.refs_2_ = bf16[192,1536]{1,0:T(8,128)(2,1)S(1)} collective-permute-done((bf16[192,1536]{1,0:T(8,128)(2,1)S(1)}, bf16[192,1536]{1,0:T(8,128)(2,1)S(1)}, u32[]{:S(2)}, u32[]{:S(2)}) %collective-permute-start.12) | collective-permute-done | bytes 589856 | tf_op jit(solution)/shard_map/ppermute | solution.py:36
  45.8 2.3 %collective-permute-done.13.refs_5_ = bf16[192,1536]{1,0:T(8,128)(2,1)S(1)} collective-permute-done((bf16[192,1536]{1,0:T(8,128)(2,1)S(1)}, bf16[192,1536]{1,0:T(8,128)(2,1)S(1)}, u32[]{:S(2)}, u32[]{:S(2)}) %collective-permute-start.13) | collective-permute-done | bytes 589856 | tf_op jit(solution)/shard_map/ppermute | solution.py:36
  48.1 5.1 %collective-permute-start.14 = (bf16[128,1536]{1,0:T(8,128)(2,1)S(1)}, bf16[128,1536]{1,0:T(8,128)(2,1)S(1)}, u32[]{:S(2)}, u32[]{:S(2)}) collective-permute-start(bf16[128,1536]{1,0:T(8,128)(2,1)S(1)} %collective-permute-done.7), channel_id=1, source_target_pairs={{0,16},{16,0},{1,17},{17,1},{2,18},{18,2},{3,19},{19,3},{4,20},{20... | collective-permute-start | bytes 1179656 | tf_op jit(solution)/shard_map/ppermute | solution.py:49
  53.3 3.6 %collective-permute-start.18 = (bf16[128,1536]{1,0:T(8,128)(2,1)S(1)}, bf16[128,1536]{1,0:T(8,128)(2,1)S(1)}, u32[]{:S(2)}, u32[]{:S(2)}) collective-permute-start(bf16[128,1536]{1,0:T(8,128)(2,1)S(1)} %pad_maximum_fusion.7), channel_id=1, source_target_pairs={{0,128},{128,8},{8,136},{136,0},{1,129},{129,9},{9,137},{137,1},{2... | collective-permute-start | bytes 1179656 | tf_op jit(solution)/shard_map/ppermute | solution.py:36
  57.0 3.0 %collective-permute-start.20 = (bf16[128,1536]{1,0:T(8,128)(2,1)S(1)}, bf16[128,1536]{1,0:T(8,128)(2,1)S(1)}, u32[]{:S(2)}, u32[]{:S(2)}) collective-permute-start(bf16[128,1536]{1,0:T(8,128)(2,1)S(1)} %collective-permute-done.7), channel_id=1, source_target_pairs={{0,64},{32,96},{64,0},{96,32},{1,65},{33,97},{65,1},{97,33},{2,66}... | collective-permute-start | bytes 1179656 | tf_op jit(solution)/shard_map/ppermute | solution.py:40
  60.2 3.7 %collective-permute-start.16 = (bf16[64,1536]{1,0:T(8,128)(2,1)S(1)}, bf16[64,1536]{1,0:T(8,128)(2,1)S(1)}, u32[]{:S(2)}, u32[]{:S(2)}) collective-permute-start(bf16[64,1536]{1,0:T(8,128)(2,1)S(1)} %get-tuple-element.89), channel_id=1, source_target_pairs={{0,1},{1,2},{2,3},{3,4},{4,5},{5,6},{6,7},{7,0},{8,9},{9,10},{10,1... | collective-permute-start | bytes 589832 | tf_op jit(solution)/shard_map/ppermute | solution.py:29
  63.9 2.0 %collective-permute-start.17 = (bf16[64,1536]{1,0:T(8,128)(2,1)S(1)}, bf16[64,1536]{1,0:T(8,128)(2,1)S(1)}, u32[]{:S(2)}, u32[]{:S(2)}) collective-permute-start(bf16[64,1536]{1,0:T(8,128)(2,1)S(1)} %get-tuple-element.92), channel_id=1, source_target_pairs={{0,7},{1,0},{2,1},{3,2},{4,3},{5,4},{6,5},{7,6},{8,15},{9,8},{10,9... | collective-permute-start | bytes 589832 | tf_op jit(solution)/shard_map/ppermute | solution.py:29
  65.9 2.3 %collective-permute-start.21 = (bf16[256,1536]{1,0:T(8,128)(2,1)S(1)}, bf16[256,1536]{1,0:T(8,128)(2,1)S(1)}, u32[]{:S(2)}, u32[]{:S(2)}) collective-permute-start(bf16[256,1536]{1,0:T(8,128)(2,1)S(1)} %pad_maximum_fusion.2.refs_9_), channel_id=1, source_target_pairs={{0,32},{16,112},{32,64},{48,16},{64,96},{80,48},{96,0},{112,80},{1... | collective-permute-start | bytes 2359304 | tf_op jit(solution)/shard_map/ppermute | solution.py:45
  68.2 5.1 %shard_map.50.early_ref = f32[832,1536]{1,0:T(8,128)S(1)} custom-call(bf16[832,1536]{1,0:T(8,128)(2,1)S(1)} %get-tuple-element.91.grads_ref.refs_0_, bf16[1536,1536]{1,0:T(8,128)(2,1)S(1)} %copy-done), custom_call_target="tpu_custom_call" | custom-call | flops 3925868544 | bytes 12582912 | tf_op jit(solution)/shard_map/pallas_call | solution.py:71
  73.4 1.7 %shard_map.51 = (f32[512,1536]{1,0:T(8,128)S(1)}, bf16[512,1536]{1,0:T(8,128)(2,1)S(1)}) custom-call(f32[832,1536]{1,0:T(8,128)S(1)} %shard_map.50.early_ref, bf16[192,1536]{1,0:T(8,128)(2,1)S(1)} %constant_dynamic-update-slice_fusion.13.grads_ref.refs_1_, bf16[1536,1536]{1,0:T(8,128)(2,1)S(1)} %copy-done), custom_call_target="tpu_custom_call" | custom-call | flops 905969664 | bytes 8388608 | tf_op jit(solution)/shard_map/pallas_call | solution.py:109
  75.1 3.4 %collective-permute-done.21 = bf16[256,1536]{1,0:T(8,128)(2,1)S(1)} collective-permute-done((bf16[256,1536]{1,0:T(8,128)(2,1)S(1)}, bf16[256,1536]{1,0:T(8,128)(2,1)S(1)}, u32[]{:S(2)}, u32[]{:S(2)}) %collective-permute-start.21) | collective-permute-done | bytes 786464 | tf_op jit(solution)/shard_map/ppermute | solution.py:45
  78.5 1.8 %collective-permute-start.22 = (bf16[512,1536]{1,0:T(8,128)(2,1)S(1)}, bf16[512,1536]{1,0:T(8,128)(2,1)S(1)}, u32[]{:S(2)}, u32[]{:S(2)}) collective-permute-start(bf16[512,1536]{1,0:T(8,128)(2,1)S(1)} %get-tuple-element.66), channel_id=1, source_target_pairs={{0,16},{16,0},{1,17},{17,1},{2,18},{18,2},{3,19},{19,3},{4,20},{20... | collective-permute-start | bytes 4718600 | tf_op jit(solution)/shard_map/ppermute | solution.py:49
  80.5 1.4 %collective-permute-start.28 = (bf16[192,1536]{1,0:T(8,128)(2,1)S(1)}, bf16[192,1536]{1,0:T(8,128)(2,1)S(1)}, u32[]{:S(2)}, u32[]{:S(2)}) collective-permute-start(bf16[192,1536]{1,0:T(8,128)(2,1)S(1)} %pad_maximum_fusion.4), channel_id=1, source_target_pairs={{0,128},{128,8},{8,136},{136,0},{1,129},{129,9},{9,137},{137,1},{2... | collective-permute-start | bytes 1769480 | tf_op jit(solution)/shard_map/ppermute | solution.py:36
  82.0 1.3 %collective-permute-start.29 = (bf16[192,1536]{1,0:T(8,128)(2,1)S(1)}, bf16[192,1536]{1,0:T(8,128)(2,1)S(1)}, u32[]{:S(2)}, u32[]{:S(2)}) collective-permute-start(bf16[192,1536]{1,0:T(8,128)(2,1)S(1)} %pad_maximum_fusion.4), channel_id=1, source_target_pairs={{0,136},{128,0},{8,128},{136,8},{1,137},{129,1},{9,129},{137,9},{2... | collective-permute-start | bytes 1769480 | tf_op jit(solution)/shard_map/ppermute | solution.py:36
  84.9 1.8 %collective-permute-done.24.refs_12_ = bf16[256,1536]{1,0:T(8,128)(2,1)S(1)} collective-permute-done((bf16[256,1536]{1,0:T(8,128)(2,1)S(1)}, bf16[256,1536]{1,0:T(8,128)(2,1)S(1)}, u32[]{:S(2)}, u32[]{:S(2)}) %collective-permute-start.24) | collective-permute-done | bytes 786464 | tf_op jit(solution)/shard_map/ppermute | solution.py:49
  88.1 2.4 %collective-permute-start.27 = (bf16[128,1536]{1,0:T(8,128)(2,1)S(1)}, bf16[128,1536]{1,0:T(8,128)(2,1)S(1)}, u32[]{:S(2)}, u32[]{:S(2)}) collective-permute-start(bf16[128,1536]{1,0:T(8,128)(2,1)S(1)} %get-tuple-element.73), channel_id=1, source_target_pairs={{0,96},{32,0},{64,32},{96,64},{1,97},{33,1},{65,33},{97,65},{2,98}... | collective-permute-start | bytes 1179656 | tf_op jit(solution)/shard_map/ppermute | solution.py:40
  90.6 5.7 %collective-permute-done.28.refs_4_ = bf16[192,1536]{1,0:T(8,128)(2,1)S(1)} collective-permute-done((bf16[192,1536]{1,0:T(8,128)(2,1)S(1)}, bf16[192,1536]{1,0:T(8,128)(2,1)S(1)}, u32[]{:S(2)}, u32[]{:S(2)}) %collective-permute-start.28) | collective-permute-done | bytes 589856 | tf_op jit(solution)/shard_map/ppermute | solution.py:36
  96.2 13.5 %shard_map.52 = bf16[1536,1536]{1,0:T(8,128)(2,1)} custom-call(bf16[832,1536]{1,0:T(8,128)(2,1)S(1)} %get-tuple-element.91.grads_ref.refs_0_, bf16[192,1536]{1,0:T(8,128)(2,1)S(1)} %constant_dynamic-update-slice_fusion.13.grads_ref.refs_1_, bf16[192,1536]{1,0:T(8,128)(2,1)S(1)} %collective-permute-done.12.refs_2_, ...), custom_call_target="tpu_custom_call" | custom-call | flops 9663676416 | bytes 17825792 | tf_op jit(solution)/shard_map/pallas_call | solution.py:181
  109.7 1.5 %fusion.7 = bf16[128,1536]{1,0:T(8,128)(2,1)} fusion(bf16[128,1536]{1,0:T(8,128)(2,1)S(1)} %copy-done.1, bf16[128,1536]{1,0:T(8,128)(2,1)S(1)} %collective-permute-done.25, bf16[128,1536]{1,0:T(8,128)(2,1)S(1)} %collective-permute-done.27, bf16[128,1536]{1,0:T(8,128)(2,1)S(1)} %collective-permute-done.26, f32[512,1536]{1,0:T(8,128)S(1)} %get-tuple-element.63, ...), kind=kLoop, calls=%fused_computation.16 | loop fusion | flops 5505024 | bytes 3145728 | tf_op jit(solution)/shard_map/convert_element_type | solution.py:255
  (65 shorter events, 8.5 us)
Async XLA Ops:
  0.6 30.4 %copy-start.2 = (bf16[64,1536]{1,0:T(8,128)(2,1)S(1)}, bf16[64,1536]{1,0:T(8,128)(2,1)}, u32[]{:S(2)}) copy-start(bf16[64,1536]{1,0:T(8,128)(2,1)} %param.4) | copy-start | bytes 589828
  2.0 23.1 %collective-permute-start = (bf16[128,1536]{1,0:T(8,128)(2,1)S(1)}, bf16[128,1536]{1,0:T(8,128)(2,1)S(1)}, u32[]{:S(2)}, u32[]{:S(2)}) collective-permute-start(bf16[128,1536]{1,0:T(8,128)(2,1)S(1)} %fusion.2), channel_id=1, source_target_pairs={{0,16},{16,0},{1,17},{17,1},{2,18},{18,2},{3,19},{19,3},{4,20},{20... | collective-permute-start | bytes 1179656 | tf_op jit(solution)/shard_map/ppermute | solution.py:49
  5.3 11.6 %collective-permute-start.1 = (bf16[64,1536]{1,0:T(8,128)(2,1)}, bf16[64,1536]{1,0:T(8,128)(2,1)S(1)}, u32[]{:S(2)}, u32[]{:S(2)}) collective-permute-start(bf16[64,1536]{1,0:T(8,128)(2,1)} %param.4), channel_id=1, source_target_pairs={{0,1},{1,2},{2,3},{3,4},{4,5},{5,6},{6,7},{7,0},{8,9},{9,10},{10,1... | collective-permute-start | bytes 589832 | tf_op jit(solution)/shard_map/ppermute | solution.py:29
  5.3 14.6 %collective-permute-start.2 = (bf16[64,1536]{1,0:T(8,128)(2,1)}, bf16[64,1536]{1,0:T(8,128)(2,1)S(1)}, u32[]{:S(2)}, u32[]{:S(2)}) collective-permute-start(bf16[64,1536]{1,0:T(8,128)(2,1)} %param.4), channel_id=1, source_target_pairs={{0,7},{1,0},{2,1},{3,2},{4,3},{5,4},{6,5},{7,6},{8,15},{9,8},{10,9... | collective-permute-start | bytes 589832 | tf_op jit(solution)/shard_map/ppermute | solution.py:29
  9.1 10.8 %collective-permute-start.3 = (bf16[64,1536]{1,0:T(8,128)(2,1)}, bf16[64,1536]{1,0:T(8,128)(2,1)S(1)}, u32[]{:S(2)}, u32[]{:S(2)}) collective-permute-start(bf16[64,1536]{1,0:T(8,128)(2,1)} %param.4), channel_id=1, source_target_pairs={{0,8},{128,136},{8,0},{136,128},{1,9},{129,137},{9,1},{137,129},{2... | collective-permute-start | bytes 589832 | tf_op jit(solution)/shard_map/ppermute | solution.py:36
  11.9 13.2 %collective-permute-start.4 = (bf16[64,1536]{1,0:T(8,128)(2,1)}, bf16[64,1536]{1,0:T(8,128)(2,1)S(1)}, u32[]{:S(2)}, u32[]{:S(2)}) collective-permute-start(bf16[64,1536]{1,0:T(8,128)(2,1)} %param.4), channel_id=1, source_target_pairs={{0,4},{1,5},{2,6},{3,7},{4,0},{5,1},{6,2},{7,3},{8,12},{9,13},{10,... | collective-permute-start | bytes 589832 | tf_op jit(solution)/shard_map/ppermute | solution.py:29
  16.9 16.6 %collective-permute-start.9 = (bf16[128,1536]{1,0:T(8,128)(2,1)S(1)}, bf16[128,1536]{1,0:T(8,128)(2,1)S(1)}, u32[]{:S(2)}, u32[]{:S(2)}) collective-permute-start(bf16[128,1536]{1,0:T(8,128)(2,1)S(1)} %fusion.2), channel_id=1, source_target_pairs={{0,64},{32,96},{64,0},{96,32},{1,65},{33,97},{65,1},{97,33},{2,66}... | collective-permute-start | bytes 1179656 | tf_op jit(solution)/shard_map/ppermute | solution.py:40
  25.1 8.1 %collective-permute-start.7 = (bf16[128,1536]{1,0:T(8,128)(2,1)S(1)}, bf16[128,1536]{1,0:T(8,128)(2,1)S(1)}, u32[]{:S(2)}, u32[]{:S(2)}) collective-permute-start(bf16[128,1536]{1,0:T(8,128)(2,1)S(1)} %fusion.2), channel_id=1, source_target_pairs={{0,128},{128,0},{1,129},{129,1},{2,130},{130,2},{3,131},{131,3},{4... | collective-permute-start | bytes 1179656 | tf_op jit(solution)/shard_map/ppermute | solution.py:49
  25.4 15.6 %collective-permute-start.8 = (bf16[256,1536]{1,0:T(8,128)(2,1)S(1)}, bf16[256,1536]{1,0:T(8,128)(2,1)S(1)}, u32[]{:S(2)}, u32[]{:S(2)}) collective-permute-start(bf16[256,1536]{1,0:T(8,128)(2,1)S(1)} %constant_dynamic-update-slice_fusion.refs_8_), channel_id=1, source_target_pairs={{0,32},{16,112},{32,64},{48,16},{64,96},{80,48},{96,0},{112,80},{1... | collective-permute-start | bytes 2359304 | tf_op jit(solution)/shard_map/ppermute | solution.py:45
  28.3 10.3 %collective-permute-start.5 = (bf16[128,1536]{1,0:T(8,128)(2,1)S(1)}, bf16[128,1536]{1,0:T(8,128)(2,1)S(1)}, u32[]{:S(2)}, u32[]{:S(2)}) collective-permute-start(bf16[128,1536]{1,0:T(8,128)(2,1)S(1)} %get-tuple-element.98), channel_id=1, source_target_pairs={{0,1},{1,2},{2,3},{3,4},{4,5},{5,6},{6,7},{7,0},{8,9},{9,10},{10,1... | collective-permute-start | bytes 1179656 | tf_op jit(solution)/shard_map/ppermute | solution.py:29
  30.2 10.9 %collective-permute-start.6 = (bf16[128,1536]{1,0:T(8,128)(2,1)S(1)}, bf16[128,1536]{1,0:T(8,128)(2,1)S(1)}, u32[]{:S(2)}, u32[]{:S(2)}) collective-permute-start(bf16[128,1536]{1,0:T(8,128)(2,1)S(1)} %get-tuple-element.97), channel_id=1, source_target_pairs={{0,7},{1,0},{2,1},{3,2},{4,3},{5,4},{6,5},{7,6},{8,15},{9,8},{10,9... | collective-permute-start | bytes 1179656 | tf_op jit(solution)/shard_map/ppermute | solution.py:29
  33.2 12.6 %collective-permute-start.12 = (bf16[192,1536]{1,0:T(8,128)(2,1)S(1)}, bf16[192,1536]{1,0:T(8,128)(2,1)S(1)}, u32[]{:S(2)}, u32[]{:S(2)}) collective-permute-start(bf16[192,1536]{1,0:T(8,128)(2,1)S(1)} %pad_maximum_fusion.3), channel_id=1, source_target_pairs={{0,128},{128,8},{8,136},{136,0},{1,129},{129,9},{9,137},{137,1},{2... | collective-permute-start | bytes 1769480 | tf_op jit(solution)/shard_map/ppermute | solution.py:36
  33.5 14.6 %collective-permute-start.13 = (bf16[192,1536]{1,0:T(8,128)(2,1)S(1)}, bf16[192,1536]{1,0:T(8,128)(2,1)S(1)}, u32[]{:S(2)}, u32[]{:S(2)}) collective-permute-start(bf16[192,1536]{1,0:T(8,128)(2,1)S(1)} %pad_maximum_fusion.3), channel_id=1, source_target_pairs={{0,136},{128,0},{8,128},{136,8},{1,137},{129,1},{9,129},{137,9},{2... | collective-permute-start | bytes 1769480 | tf_op jit(solution)/shard_map/ppermute | solution.py:36
  38.6 18.4 %collective-permute-start.15 = (bf16[64,1536]{1,0:T(8,128)(2,1)S(1)}, bf16[64,1536]{1,0:T(8,128)(2,1)S(1)}, u32[]{:S(2)}, u32[]{:S(2)}) collective-permute-start(bf16[64,1536]{1,0:T(8,128)(2,1)S(1)} %collective-permute-done.4), channel_id=1, source_target_pairs={{0,8},{128,136},{8,0},{136,128},{1,9},{129,137},{9,1},{137,129},{2... | collective-permute-start | bytes 589832 | tf_op jit(solution)/shard_map/ppermute | solution.py:36
  41.1 18.9 %collective-permute-start.10 = (bf16[128,1536]{1,0:T(8,128)(2,1)S(1)}, bf16[128,1536]{1,0:T(8,128)(2,1)S(1)}, u32[]{:S(2)}, u32[]{:S(2)}) collective-permute-start(bf16[128,1536]{1,0:T(8,128)(2,1)S(1)} %collective-permute-done.5), channel_id=1, source_target_pairs={{0,1},{1,2},{2,3},{3,4},{4,5},{5,6},{6,7},{7,0},{8,9},{9,10},{10,1... | collective-permute-start | bytes 1179656 | tf_op jit(solution)/shard_map/ppermute | solution.py:29
  42.8 17.2 %collective-permute-start.11 = (bf16[128,1536]{1,0:T(8,128)(2,1)S(1)}, bf16[128,1536]{1,0:T(8,128)(2,1)S(1)}, u32[]{:S(2)}, u32[]{:S(2)}) collective-permute-start(bf16[128,1536]{1,0:T(8,128)(2,1)S(1)} %collective-permute-done.6), channel_id=1, source_target_pairs={{0,7},{1,0},{2,1},{3,2},{4,3},{5,4},{6,5},{7,6},{8,15},{9,8},{10,9... | collective-permute-start | bytes 1179656 | tf_op jit(solution)/shard_map/ppermute | solution.py:29
  48.1 8.8 %collective-permute-start.14 = (bf16[128,1536]{1,0:T(8,128)(2,1)S(1)}, bf16[128,1536]{1,0:T(8,128)(2,1)S(1)}, u32[]{:S(2)}, u32[]{:S(2)}) collective-permute-start(bf16[128,1536]{1,0:T(8,128)(2,1)S(1)} %collective-permute-done.7), channel_id=1, source_target_pairs={{0,16},{16,0},{1,17},{17,1},{2,18},{18,2},{3,19},{19,3},{4,20},{20... | collective-permute-start | bytes 1179656 | tf_op jit(solution)/shard_map/ppermute | solution.py:49
  53.3 12.6 %collective-permute-start.18 = (bf16[128,1536]{1,0:T(8,128)(2,1)S(1)}, bf16[128,1536]{1,0:T(8,128)(2,1)S(1)}, u32[]{:S(2)}, u32[]{:S(2)}) collective-permute-start(bf16[128,1536]{1,0:T(8,128)(2,1)S(1)} %pad_maximum_fusion.7), channel_id=1, source_target_pairs={{0,128},{128,8},{8,136},{136,0},{1,129},{129,9},{9,137},{137,1},{2... | collective-permute-start | bytes 1179656 | tf_op jit(solution)/shard_map/ppermute | solution.py:36
  56.9 16.4 %collective-permute-start.19 = (bf16[128,1536]{1,0:T(8,128)(2,1)S(1)}, bf16[128,1536]{1,0:T(8,128)(2,1)S(1)}, u32[]{:S(2)}, u32[]{:S(2)}) collective-permute-start(bf16[128,1536]{1,0:T(8,128)(2,1)S(1)} %pad_maximum_fusion.7), channel_id=1, source_target_pairs={{0,136},{128,0},{8,128},{136,8},{1,137},{129,1},{9,129},{137,9},{2... | collective-permute-start | bytes 1179656 | tf_op jit(solution)/shard_map/ppermute | solution.py:36
  57.0 16.3 %collective-permute-start.20 = (bf16[128,1536]{1,0:T(8,128)(2,1)S(1)}, bf16[128,1536]{1,0:T(8,128)(2,1)S(1)}, u32[]{:S(2)}, u32[]{:S(2)}) collective-permute-start(bf16[128,1536]{1,0:T(8,128)(2,1)S(1)} %collective-permute-done.7), channel_id=1, source_target_pairs={{0,64},{32,96},{64,0},{96,32},{1,65},{33,97},{65,1},{97,33},{2,66}... | collective-permute-start | bytes 1179656 | tf_op jit(solution)/shard_map/ppermute | solution.py:40
  60.2 13.1 %collective-permute-start.16 = (bf16[64,1536]{1,0:T(8,128)(2,1)S(1)}, bf16[64,1536]{1,0:T(8,128)(2,1)S(1)}, u32[]{:S(2)}, u32[]{:S(2)}) collective-permute-start(bf16[64,1536]{1,0:T(8,128)(2,1)S(1)} %get-tuple-element.89), channel_id=1, source_target_pairs={{0,1},{1,2},{2,3},{3,4},{4,5},{5,6},{6,7},{7,0},{8,9},{9,10},{10,1... | collective-permute-start | bytes 589832 | tf_op jit(solution)/shard_map/ppermute | solution.py:29
  63.9 9.4 %collective-permute-start.17 = (bf16[64,1536]{1,0:T(8,128)(2,1)S(1)}, bf16[64,1536]{1,0:T(8,128)(2,1)S(1)}, u32[]{:S(2)}, u32[]{:S(2)}) collective-permute-start(bf16[64,1536]{1,0:T(8,128)(2,1)S(1)} %get-tuple-element.92), channel_id=1, source_target_pairs={{0,7},{1,0},{2,1},{3,2},{4,3},{5,4},{6,5},{7,6},{8,15},{9,8},{10,9... | collective-permute-start | bytes 589832 | tf_op jit(solution)/shard_map/ppermute | solution.py:29
  65.9 12.6 %collective-permute-start.21 = (bf16[256,1536]{1,0:T(8,128)(2,1)S(1)}, bf16[256,1536]{1,0:T(8,128)(2,1)S(1)}, u32[]{:S(2)}, u32[]{:S(2)}) collective-permute-start(bf16[256,1536]{1,0:T(8,128)(2,1)S(1)} %pad_maximum_fusion.2.refs_9_), channel_id=1, source_target_pairs={{0,32},{16,112},{32,64},{48,16},{64,96},{80,48},{96,0},{112,80},{1... | collective-permute-start | bytes 2359304 | tf_op jit(solution)/shard_map/ppermute | solution.py:45
  78.5 6.0 %collective-permute-start.22 = (bf16[512,1536]{1,0:T(8,128)(2,1)S(1)}, bf16[512,1536]{1,0:T(8,128)(2,1)S(1)}, u32[]{:S(2)}, u32[]{:S(2)}) collective-permute-start(bf16[512,1536]{1,0:T(8,128)(2,1)S(1)} %get-tuple-element.66), channel_id=1, source_target_pairs={{0,16},{16,0},{1,17},{17,1},{2,18},{18,2},{3,19},{19,3},{4,20},{20... | collective-permute-start | bytes 4718600 | tf_op jit(solution)/shard_map/ppermute | solution.py:49
  80.4 6.3 %collective-permute-start.23 = (bf16[512,1536]{1,0:T(8,128)(2,1)S(1)}, bf16[512,1536]{1,0:T(8,128)(2,1)S(1)}, u32[]{:S(2)}, u32[]{:S(2)}) collective-permute-start(bf16[512,1536]{1,0:T(8,128)(2,1)S(1)} %pad_maximum_fusion.1), channel_id=1, source_target_pairs={{0,16},{16,0},{1,17},{17,1},{2,18},{18,2},{3,19},{19,3},{4,20},{20... | collective-permute-start | bytes 4718600 | tf_op jit(solution)/shard_map/ppermute | solution.py:49
  80.5 15.7 %collective-permute-start.28 = (bf16[192,1536]{1,0:T(8,128)(2,1)S(1)}, bf16[192,1536]{1,0:T(8,128)(2,1)S(1)}, u32[]{:S(2)}, u32[]{:S(2)}) collective-permute-start(bf16[192,1536]{1,0:T(8,128)(2,1)S(1)} %pad_maximum_fusion.4), channel_id=1, source_target_pairs={{0,128},{128,8},{8,136},{136,0},{1,129},{129,9},{9,137},{137,1},{2... | collective-permute-start | bytes 1769480 | tf_op jit(solution)/shard_map/ppermute | solution.py:36
  82.0 14.3 %collective-permute-start.29 = (bf16[192,1536]{1,0:T(8,128)(2,1)S(1)}, bf16[192,1536]{1,0:T(8,128)(2,1)S(1)}, u32[]{:S(2)}, u32[]{:S(2)}) collective-permute-start(bf16[192,1536]{1,0:T(8,128)(2,1)S(1)} %pad_maximum_fusion.4), channel_id=1, source_target_pairs={{0,136},{128,0},{8,128},{136,8},{1,137},{129,1},{9,129},{137,9},{2... | collective-permute-start | bytes 1769480 | tf_op jit(solution)/shard_map/ppermute | solution.py:36
  83.3 3.4 %collective-permute-start.24 = (bf16[256,1536]{1,0:T(8,128)(2,1)S(1)}, bf16[256,1536]{1,0:T(8,128)(2,1)S(1)}, u32[]{:S(2)}, u32[]{:S(2)}) collective-permute-start(bf16[256,1536]{1,0:T(8,128)(2,1)S(1)} %collective-permute-done.21), channel_id=1, source_target_pairs={{0,16},{16,0},{1,17},{17,1},{2,18},{18,2},{3,19},{19,3},{4,20},{20... | collective-permute-start | bytes 2359304 | tf_op jit(solution)/shard_map/ppermute | solution.py:49
  86.7 23.0 %copy-start.1 = (bf16[128,1536]{1,0:T(8,128)(2,1)S(1)}, bf16[128,1536]{1,0:T(8,128)(2,1)}, u32[]{:S(2)}) copy-start(bf16[128,1536]{1,0:T(8,128)(2,1)} %param.3) | copy-start | bytes 1179652
  86.7 23.0 %collective-permute-start.25 = (bf16[128,1536]{1,0:T(8,128)(2,1)S(1)}, bf16[128,1536]{1,0:T(8,128)(2,1)S(1)}, u32[]{:S(2)}, u32[]{:S(2)}) collective-permute-start(bf16[128,1536]{1,0:T(8,128)(2,1)S(1)} %get-tuple-element.71), channel_id=1, source_target_pairs={{0,64},{32,96},{64,0},{96,32},{1,65},{33,97},{65,1},{97,33},{2,66}... | collective-permute-start | bytes 1179656 | tf_op jit(solution)/shard_map/ppermute | solution.py:40
  87.9 21.8 %collective-permute-start.26 = (bf16[128,1536]{1,0:T(8,128)(2,1)S(1)}, bf16[128,1536]{1,0:T(8,128)(2,1)S(1)}, u32[]{:S(2)}, u32[]{:S(2)}) collective-permute-start(bf16[128,1536]{1,0:T(8,128)(2,1)S(1)} %get-tuple-element.72), channel_id=1, source_target_pairs={{0,32},{32,64},{64,96},{96,0},{1,33},{33,65},{65,97},{97,1},{2,34}... | collective-permute-start | bytes 1179656 | tf_op jit(solution)/shard_map/ppermute | solution.py:40
  88.1 21.6 %collective-permute-start.27 = (bf16[128,1536]{1,0:T(8,128)(2,1)S(1)}, bf16[128,1536]{1,0:T(8,128)(2,1)S(1)}, u32[]{:S(2)}, u32[]{:S(2)}) collective-permute-start(bf16[128,1536]{1,0:T(8,128)(2,1)S(1)} %get-tuple-element.73), channel_id=1, source_target_pairs={{0,96},{32,0},{64,32},{96,64},{1,97},{33,1},{65,33},{97,65},{2,98}... | collective-permute-start | bytes 1179656 | tf_op jit(solution)/shard_map/ppermute | solution.py:40
  (1 other events, 11.3 us)

commit v8 on v6

--- a/solution.py
+++ b/solution.py
@@ -187,28 +187,30 @@
     up1, down1, far = along_z(g, 1), along_z(g, -1), along_x(g, 2)
     act_c = swap(activation, "c")
     hop_2 = along_y(activation, 2)
-    activation, act_c, up1, down1, far = tie(activation, act_c, up1, down1, far)
+    activation, up1, down1, far = tie(activation, up1, down1, far)
 
     up2 = along_z(jnp.concatenate([far, up1]), 1)
     down2 = along_z(jnp.concatenate([down1, far]), -1)
     other_rep = swap(activation, "xl")
     chip = jnp.concatenate([activation, act_c])
+    near = jnp.concatenate([g, up1, down1])
+    other_rep, chip, near = tie(other_rep, chip, near)
     hop_1 = round_y(chip)
-    up2, down2, other_rep, hop_1, hop_2 = tie(up2, down2, other_rep, hop_1, hop_2)
+    left_a, right_a = along_x(near, 1), along_x(near, -1)
+    up2, down2, hop_2 = tie(up2, down2, hop_2)
 
     up3, down3 = along_z(up2, 1), along_z(down2, -1)
-    near = jnp.concatenate([g, up1, down1])
-    left_a, right_a = along_x(near, 1), along_x(near, -1)
-    hop_4 = along_y(other_rep, 2)
     other_rep, left_a, right_a = tie(other_rep, left_a, right_a)
     other_chip = jnp.concatenate([other_rep, swap(other_rep, "c")])
-    up3, down3, left_a, right_a, other_chip, hop_4 = tie(up3, down3, left_a, right_a, other_chip, hop_4)
+    up3, down3, left_a, right_a, other_rep, other_chip, hop_1 = tie(
+        up3, down3, left_a, right_a, other_rep, other_chip, hop_1
+    )
 
     up4, down4 = along_z(up3[:96], 1), along_z(down3[32:], -1)
     middle = jnp.concatenate([up2[64:], down2[:64]])
     left_b, right_b = along_x(middle, 1), along_x(middle, -1)
-    hop_3 = round_y(other_chip)
-    up4, down4 = tie(up4, down4)
+    hop_4 = along_y(other_rep, 2)
+    up4, down4, other_chip = tie(up4, down4, other_chip)
     own = [g, up1, down1, up2[64:], down2[:64], up3[64:], down3[:64]]
     second = [far, up2[:64], down2[64:], up3[:64], down3[64:]]
     grads_early = jnp.concatenate(own + second)
@@ -218,21 +220,24 @@
     last = jnp.concatenate([up4[64:], down4[:32]])
     third = jnp.concatenate([up3[64:], down3[:64]])
     left_c, right_c = along_x(third, 1), along_x(third, -1)
-    up5, down5, early, hop_3, left_b, right_b = tie(up5, down5, early, hop_3, left_b, right_b)
+    hop_3 = round_y(other_chip)
+    up5, down5, early, left_b, right_b, hop_4 = tie(up5, down5, early, left_b, right_b, hop_4)
 
     grads_late = jnp.concatenate([last, up4[:64], down4[32:], up5, down5])
     mine, other = late_partial(early, grads_late, down_weight)
-    mine, other, left_c, right_c = tie(mine, other, left_c, right_c)
+    mine, other, left_c, right_c, hop_3, last = tie(mine, other, left_c, right_c, hop_3, last)
     other = swap(other, "c")
+    left_d, right_d = along_x(last, 1), along_x(last, -1)
+
+    def summed(block):
+        return mine[128 * block : 128 * block + 128] + other[128 * block : 128 * block + 128].astype(F32)
+
+    to_above, to_below, to_across = summed(1).astype(BF), summed(3).astype(BF), summed(2).astype(BF)
+    to_above, to_below, to_across, hop_3, left_d, right_d = tie(
+        to_above, to_below, to_across, hop_3, left_d, right_d
+    )
     came = jnp.concatenate([hop_1, hop_2, hop_3, hop_4])
     swapped = swap(came, "c")
-
-    def summed(block):
-        return mine[128 * block : 128 * block + 128] + other[128 * block : 128 * block + 128].astype(F32)
-
-    to_above, to_below, to_across = summed(1).astype(BF), summed(3).astype(BF), summed(2).astype(BF)
-    to_above, to_below, to_across, swapped, last = tie(to_above, to_below, to_across, swapped, last)
-    left_d, right_d = along_x(last, 1), along_x(last, -1)
     from_across = along_y(to_across, 2)
     from_below, from_above = along_y(to_above, 1), along_y(to_below, -1)
 

time: 102 us -> 108 us (1.059)
  waiting for transfers between devices: 18.2 us -> 34.5 us
  starting transfers between devices: 57.1 us -> 47.6 us
    ppermute x9, waiting for transfers between devices: 4.27 us -> 15.8 us  [along_x(): lax.ppermute(a, ('xl', 'xh'), [(place(x), place((x + d) % 4)) for x in ra...]
    ppermute x5, starting transfers between devices: 17.1 us -> 11.3 us  [swap(): return lax.ppermute(a, axis, [(0, 1), (1, 0)])]
    ppermute x2, starting transfers between devices: 5.2 us -> 0.01 us  [round_y(): lax.ppermute(a, ('y', 'c'), [(s[0] * C + s[1], t[0] * C + t[1]) for s, t...]
    ppermute x10, starting transfers between devices: 14.2 us -> 19.1 us  [along_z(): return lax.ppermute(a, 'z', [(i, (i + d) % Z) for i in range(Z)])]
    ppermute x5, waiting for transfers between devices: 3.9 us -> 7.51 us  [swap(): return lax.ppermute(a, axis, [(0, 1), (1, 0)])]
    ppermute x9, starting transfers between devices: 11.7 us -> 9.4 us  [along_x(): lax.ppermute(a, ('xl', 'xh'), [(place(x), place((x + d) % 4)) for x in ra...]
  transfers between devices with their start and end apart: 31 -> 31, of which waited for: 11 -> 16; matrix products, arithmetic and copies ran while one was open for 2% -> 3% of each run, Pallas kernels for 20% -> 19%
where the time goes in v8:
time: 108 us
  starting transfers between devices  47.6 us (44%)
  waiting for transfers between devices  34.5 us (32%)
  Pallas kernels  20.2 us (19%)
  other arithmetic  3.34 us (3%)
  local copies, waits for them, and re-layouts  1.46 us (1%)
    ppermute x10, starting transfers between devices, along_z(): return lax.ppermute(a, 'z', [(i, (i + d) % Z) for i in range(Z)])  19.1 us
    ppermute x9, waiting for transfers between devices, along_x(): lax.ppermute(a, ('xl', 'xh'), [(place(x), place((x + d) % 4)) for x in ra...  15.8 us
    pallas_call x1, Pallas kernels, weight_gradient(): pl.pallas_call(weight_kernel, grid=(1536 // step,), in_specs=[VMEM] * 14,...  13.5 us
    ppermute x5, starting transfers between devices, swap(): return lax.ppermute(a, axis, [(0, 1), (1, 0)])  11.3 us
    ppermute x9, starting transfers between devices, along_x(): lax.ppermute(a, ('xl', 'xh'), [(place(x), place((x + d) % 4)) for x in ra...  9.4 us
    ppermute x10, waiting for transfers between devices, along_z(): return lax.ppermute(a, 'z', [(i, (i + d) % Z) for i in range(Z)])  8.35 us
    ppermute x5, starting transfers between devices, along_y(): return lax.ppermute(a, 'y', [(i, (i + d) % Y) for i in range(Y)])  7.81 us
    ppermute x5, waiting for transfers between devices, swap(): return lax.ppermute(a, axis, [(0, 1), (1, 0)])  7.51 us
  transfers between devices with their start and end apart: 31, of which 16 were waited for; matrix products, arithmetic and copies ran while one was open for 3% of the time, Pallas kernels for 19%

profile of v8, /device:TPU:1, one launch (start us, length us, event | category | flops | bytes accessed | tf_op | source)
XLA Modules:
  0.0 108.1 jit_solution(15483843657903903702)
XLA Ops:
  0.6 3.7 %collective-permute-start.2 = (bf16[64,1536]{1,0:T(8,128)(2,1)}, bf16[64,1536]{1,0:T(8,128)(2,1)S(1)}, u32[]{:S(2)}, u32[]{:S(2)}) collective-permute-start(bf16[64,1536]{1,0:T(8,128)(2,1)} %param.4), channel_id=1, source_target_pairs={{0,8},{128,136},{8,0},{136,128},{1,9},{129,137},{9,1},{137,129},{2... | collective-permute-start | bytes 589832 | tf_op jit(solution)/shard_map/ppermute | solution.py:36
  4.3 5.6 %collective-permute-start.1 = (bf16[64,1536]{1,0:T(8,128)(2,1)}, bf16[64,1536]{1,0:T(8,128)(2,1)S(1)}, u32[]{:S(2)}, u32[]{:S(2)}) collective-permute-start(bf16[64,1536]{1,0:T(8,128)(2,1)} %param.4), channel_id=1, source_target_pairs={{0,7},{1,0},{2,1},{3,2},{4,3},{5,4},{6,5},{7,6},{8,15},{9,8},{10,9... | collective-permute-start | bytes 589832 | tf_op jit(solution)/shard_map/ppermute | solution.py:29
  9.9 1.3 %fusion.2 = bf16[128,1536]{1,0:T(8,128)(2,1)S(1)} fusion(bf16[128,1536]{1,0:T(8,128)(2,1)} %param.3), kind=kLoop, calls=%fused_computation.9 | loop fusion | flops 1966080 | bytes 786432 | tf_op jit(solution)/shard_map/convert_element_type | solution.py:185
  11.2 1.3 %collective-permute-start.9 = (bf16[128,1536]{1,0:T(8,128)(2,1)S(1)}, bf16[128,1536]{1,0:T(8,128)(2,1)S(1)}, u32[]{:S(2)}, u32[]{:S(2)}) collective-permute-start(bf16[128,1536]{1,0:T(8,128)(2,1)S(1)} %fusion.2), channel_id=1, source_target_pairs={{0,16},{16,0},{1,17},{17,1},{2,18},{18,2},{3,19},{19,3},{4,20},{20... | collective-permute-start | bytes 1179656 | tf_op jit(solution)/shard_map/ppermute | solution.py:49
  12.5 2.9 %collective-permute-start.5 = (bf16[128,1536]{1,0:T(8,128)(2,1)S(1)}, bf16[128,1536]{1,0:T(8,128)(2,1)S(1)}, u32[]{:S(2)}, u32[]{:S(2)}) collective-permute-start(bf16[128,1536]{1,0:T(8,128)(2,1)S(1)} %fusion.2), channel_id=1, source_target_pairs={{0,64},{32,96},{64,0},{96,32},{1,65},{33,97},{65,1},{97,33},{2,66}... | collective-permute-start | bytes 1179656 | tf_op jit(solution)/shard_map/ppermute | solution.py:40
  16.8 3.0 %collective-permute-start.4 = (bf16[128,1536]{1,0:T(8,128)(2,1)S(1)}, bf16[128,1536]{1,0:T(8,128)(2,1)S(1)}, u32[]{:S(2)}, u32[]{:S(2)}) collective-permute-start(bf16[128,1536]{1,0:T(8,128)(2,1)S(1)} %get-tuple-element.113), channel_id=1, source_target_pairs={{0,7},{1,0},{2,1},{3,2},{4,3},{5,4},{6,5},{7,6},{8,15},{9,8},{10,9... | collective-permute-start | bytes 1179656 | tf_op jit(solution)/shard_map/ppermute | solution.py:29
  20.0 4.9 %collective-permute-done.8 = bf16[128,1536]{1,0:T(8,128)(2,1)S(1)} collective-permute-done((bf16[128,1536]{1,0:T(8,128)(2,1)S(1)}, bf16[128,1536]{1,0:T(8,128)(2,1)S(1)}, u32[]{:S(2)}, u32[]{:S(2)}) %collective-permute-start.8) | collective-permute-done | bytes 393248 | tf_op jit(solution)/shard_map/ppermute | solution.py:49
  26.4 1.3 %collective-permute-done.4 = bf16[128,1536]{1,0:T(8,128)(2,1)S(1)} collective-permute-done((bf16[128,1536]{1,0:T(8,128)(2,1)S(1)}, bf16[128,1536]{1,0:T(8,128)(2,1)S(1)}, u32[]{:S(2)}, u32[]{:S(2)}) %collective-permute-start.4) | collective-permute-done | bytes 393248 | tf_op jit(solution)/shard_map/ppermute | solution.py:29
  27.7 3.1 %collective-permute-done.3 = bf16[128,1536]{1,0:T(8,128)(2,1)S(1)} collective-permute-done((bf16[128,1536]{1,0:T(8,128)(2,1)S(1)}, bf16[128,1536]{1,0:T(8,128)(2,1)S(1)}, u32[]{:S(2)}, u32[]{:S(2)}) %collective-permute-start.3) | collective-permute-done | bytes 393248 | tf_op jit(solution)/shard_map/ppermute | solution.py:29
  30.8 2.7 %collective-permute-start.7 = (bf16[128,1536]{1,0:T(8,128)(2,1)S(1)}, bf16[128,1536]{1,0:T(8,128)(2,1)S(1)}, u32[]{:S(2)}, u32[]{:S(2)}) collective-permute-start(bf16[128,1536]{1,0:T(8,128)(2,1)S(1)} %collective-permute-done.4), channel_id=1, source_target_pairs={{0,7},{1,0},{2,1},{3,2},{4,3},{5,4},{6,5},{7,6},{8,15},{9,8},{10,9... | collective-permute-start | bytes 1179656 | tf_op jit(solution)/shard_map/ppermute | solution.py:29
  33.5 3.2 %collective-permute-done.11.refs_6_ = bf16[192,1536]{1,0:T(8,128)(2,1)S(1)} collective-permute-done((bf16[192,1536]{1,0:T(8,128)(2,1)S(1)}, bf16[192,1536]{1,0:T(8,128)(2,1)S(1)}, u32[]{:S(2)}, u32[]{:S(2)}) %collective-permute-start.11) | collective-permute-done | bytes 589856 | tf_op jit(solution)/shard_map/ppermute | solution.py:36
  36.7 1.8 %collective-permute-done.10.refs_2_ = bf16[192,1536]{1,0:T(8,128)(2,1)S(1)} collective-permute-done((bf16[192,1536]{1,0:T(8,128)(2,1)S(1)}, bf16[192,1536]{1,0:T(8,128)(2,1)S(1)}, u32[]{:S(2)}, u32[]{:S(2)}) %collective-permute-start.10) | collective-permute-done | bytes 589856 | tf_op jit(solution)/shard_map/ppermute | solution.py:36
  38.5 4.3 %collective-permute-start.12 = (bf16[128,1536]{1,0:T(8,128)(2,1)S(1)}, bf16[128,1536]{1,0:T(8,128)(2,1)S(1)}, u32[]{:S(2)}, u32[]{:S(2)}) collective-permute-start(bf16[128,1536]{1,0:T(8,128)(2,1)S(1)} %collective-permute-done.8), channel_id=1, source_target_pairs={{0,16},{16,0},{1,17},{17,1},{2,18},{18,2},{3,19},{19,3},{4,20},{20... | collective-permute-start | bytes 1179656 | tf_op jit(solution)/shard_map/ppermute | solution.py:49
  42.9 1.2 %collective-permute-done.12 = bf16[128,1536]{1,0:T(8,128)(2,1)S(1)} collective-permute-done((bf16[128,1536]{1,0:T(8,128)(2,1)S(1)}, bf16[128,1536]{1,0:T(8,128)(2,1)S(1)}, u32[]{:S(2)}, u32[]{:S(2)}) %collective-permute-start.12) | collective-permute-done | bytes 393248 | tf_op jit(solution)/shard_map/ppermute | solution.py:49
  44.7 4.9 %collective-permute-start.15 = (bf16[96,1536]{1,0:T(8,128)(2,1)S(1)}, bf16[96,1536]{1,0:T(8,128)(2,1)S(1)}, u32[]{:S(2)}, u32[]{:S(2)}) collective-permute-start(bf16[96,1536]{1,0:T(8,128)(2,1)S(1)} %slice.77), channel_id=1, source_target_pairs={{0,7},{1,0},{2,1},{3,2},{4,3},{5,4},{6,5},{7,6},{8,15},{9,8},{10,9... | collective-permute-start | bytes 884744 | tf_op jit(solution)/shard_map/ppermute | solution.py:29
  49.8 4.8 %shard_map.50.early_ref = f32[768,1536]{1,0:T(8,128)S(1)} custom-call(bf16[768,1536]{1,0:T(8,128)(2,1)S(1)} %slice_dynamic-update-slice_fusion.2.grads_ref.refs_0_, bf16[1536,1536]{1,0:T(8,128)(2,1)S(1)} %copy-done), custom_call_target="tpu_custom_call" | custom-call | flops 3623878656 | bytes 12582912 | tf_op jit(solution)/shard_map/pallas_call | solution.py:71
  55.4 3.1 %collective-permute-done.14 = bf16[96,1536]{1,0:T(8,128)(2,1)S(1)} collective-permute-done((bf16[96,1536]{1,0:T(8,128)(2,1)S(1)}, bf16[96,1536]{1,0:T(8,128)(2,1)S(1)}, u32[]{:S(2)}, u32[]{:S(2)}) %collective-permute-start.14) | collective-permute-done | bytes 294944 | tf_op jit(solution)/shard_map/ppermute | solution.py:29
  58.7 2.7 %collective-permute-start.17 = (bf16[32,1536]{1,0:T(8,128)(2,1)S(1)}, bf16[32,1536]{1,0:T(8,128)(2,1)S(1)}, u32[]{:S(2)}, u32[]{:S(2)}) collective-permute-start(bf16[32,1536]{1,0:T(8,128)(2,1)S(1)} %get-tuple-element.112), channel_id=1, source_target_pairs={{0,7},{1,0},{2,1},{3,2},{4,3},{5,4},{6,5},{7,6},{8,15},{9,8},{10,9... | collective-permute-start | bytes 294920 | tf_op jit(solution)/shard_map/ppermute | solution.py:29
  61.5 2.4 %collective-permute-start.22 = (bf16[128,1536]{1,0:T(8,128)(2,1)S(1)}, bf16[128,1536]{1,0:T(8,128)(2,1)S(1)}, u32[]{:S(2)}, u32[]{:S(2)}) collective-permute-start(bf16[128,1536]{1,0:T(8,128)(2,1)S(1)} %pad_maximum_fusion.6), channel_id=1, source_target_pairs={{0,136},{128,0},{8,128},{136,8},{1,137},{129,1},{9,129},{137,9},{2... | collective-permute-start | bytes 1179656 | tf_op jit(solution)/shard_map/ppermute | solution.py:36
  63.9 2.0 %shard_map.51 = (f32[512,1536]{1,0:T(8,128)S(1)}, bf16[512,1536]{1,0:T(8,128)(2,1)S(1)}) custom-call(f32[768,1536]{1,0:T(8,128)S(1)} %shard_map.50.early_ref, bf16[256,1536]{1,0:T(8,128)(2,1)S(1)} %constant_dynamic-update-slice_fusion.8.grads_ref.refs_1_, bf16[1536,1536]{1,0:T(8,128)(2,1)S(1)} %copy-done), custom_call_target="tpu_custom_call" | custom-call | flops 1207959552 | bytes 8388608 | tf_op jit(solution)/shard_map/pallas_call | solution.py:109
  65.9 3.3 %collective-permute-done.22.refs_8_ = bf16[128,1536]{1,0:T(8,128)(2,1)S(1)} collective-permute-done((bf16[128,1536]{1,0:T(8,128)(2,1)S(1)}, bf16[128,1536]{1,0:T(8,128)(2,1)S(1)}, u32[]{:S(2)}, u32[]{:S(2)}) %collective-permute-start.22) | collective-permute-done | bytes 393248 | tf_op jit(solution)/shard_map/ppermute | solution.py:36
  69.2 3.1 %collective-permute-done.21.refs_4_ = bf16[128,1536]{1,0:T(8,128)(2,1)S(1)} collective-permute-done((bf16[128,1536]{1,0:T(8,128)(2,1)S(1)}, bf16[128,1536]{1,0:T(8,128)(2,1)S(1)}, u32[]{:S(2)}, u32[]{:S(2)}) %collective-permute-start.21) | collective-permute-done | bytes 393248 | tf_op jit(solution)/shard_map/ppermute | solution.py:36
  72.3 4.3 %collective-permute-start.24 = (bf16[512,1536]{1,0:T(8,128)(2,1)S(1)}, bf16[512,1536]{1,0:T(8,128)(2,1)S(1)}, u32[]{:S(2)}, u32[]{:S(2)}) collective-permute-start(bf16[512,1536]{1,0:T(8,128)(2,1)S(1)} %get-tuple-element.74), channel_id=1, source_target_pairs={{0,16},{16,0},{1,17},{17,1},{2,18},{18,2},{3,19},{19,3},{4,20},{20... | collective-permute-start | bytes 4718600 | tf_op jit(solution)/shard_map/ppermute | solution.py:49
  76.8 1.5 %collective-permute-start.25 = (bf16[64,1536]{1,0:T(8,128)(2,1)S(1)}, bf16[64,1536]{1,0:T(8,128)(2,1)S(1)}, u32[]{:S(2)}, u32[]{:S(2)}) collective-permute-start(bf16[64,1536]{1,0:T(8,128)(2,1)S(1)} %pad_maximum_fusion.7), channel_id=1, source_target_pairs={{0,128},{128,8},{8,136},{136,0},{1,129},{129,9},{9,137},{137,1},{2... | collective-permute-start | bytes 589832 | tf_op jit(solution)/shard_map/ppermute | solution.py:36
  78.2 1.4 %collective-permute-done.24 = bf16[512,1536]{1,0:T(8,128)(2,1)S(1)} collective-permute-done((bf16[512,1536]{1,0:T(8,128)(2,1)S(1)}, bf16[512,1536]{1,0:T(8,128)(2,1)S(1)}, u32[]{:S(2)}, u32[]{:S(2)}) %collective-permute-start.24) | collective-permute-done | bytes 1572896 | tf_op jit(solution)/shard_map/ppermute | solution.py:49
  80.0 3.3 %collective-permute-done.26.refs_9_ = bf16[64,1536]{1,0:T(8,128)(2,1)S(1)} collective-permute-done((bf16[64,1536]{1,0:T(8,128)(2,1)S(1)}, bf16[64,1536]{1,0:T(8,128)(2,1)S(1)}, u32[]{:S(2)}, u32[]{:S(2)}) %collective-permute-start.26) | collective-permute-done | bytes 196640 | tf_op jit(solution)/shard_map/ppermute | solution.py:36
  84.5 1.1 %collective-permute-start.30 = (bf16[768,1536]{1,0:T(8,128)(2,1)S(1)}, bf16[768,1536]{1,0:T(8,128)(2,1)S(1)}, u32[]{:S(2)}, u32[]{:S(2)}) collective-permute-start(bf16[768,1536]{1,0:T(8,128)(2,1)S(1)} %constant_dynamic-update-slice_fusion.12.refs_12_), channel_id=1, source_target_pairs={{0,16},{16,0},{1,17},{17,1},{2,18},{18,2},{3,19},{19,3},{4,20},{20... | collective-permute-start | bytes 7077896 | tf_op jit(solution)/shard_map/ppermute | solution.py:49
  85.6 2.2 %collective-permute-start.27 = (bf16[128,1536]{1,0:T(8,128)(2,1)S(1)}, bf16[128,1536]{1,0:T(8,128)(2,1)S(1)}, u32[]{:S(2)}, u32[]{:S(2)}) collective-permute-start(bf16[128,1536]{1,0:T(8,128)(2,1)S(1)} %get-tuple-element.77), channel_id=1, source_target_pairs={{0,64},{32,96},{64,0},{96,32},{1,65},{33,97},{65,1},{97,33},{2,66}... | collective-permute-start | bytes 1179656 | tf_op jit(solution)/shard_map/ppermute | solution.py:40
  88.1 2.4 %collective-permute-start.29 = (bf16[128,1536]{1,0:T(8,128)(2,1)S(1)}, bf16[128,1536]{1,0:T(8,128)(2,1)S(1)}, u32[]{:S(2)}, u32[]{:S(2)}) collective-permute-start(bf16[128,1536]{1,0:T(8,128)(2,1)S(1)} %get-tuple-element.79), channel_id=1, source_target_pairs={{0,96},{32,0},{64,32},{96,64},{1,97},{33,1},{65,33},{97,65},{2,98}... | collective-permute-start | bytes 1179656 | tf_op jit(solution)/shard_map/ppermute | solution.py:40
  90.5 13.5 %shard_map.52 = bf16[1536,1536]{1,0:T(8,128)(2,1)} custom-call(bf16[768,1536]{1,0:T(8,128)(2,1)S(1)} %slice_dynamic-update-slice_fusion.2.grads_ref.refs_0_, bf16[256,1536]{1,0:T(8,128)(2,1)S(1)} %constant_dynamic-update-slice_fusion.8.grads_ref.refs_1_, bf16[192,1536]{1,0:T(8,128)(2,1)S(1)} %collective-permute-done.10.refs_2_, ...), custom_call_target="tpu_custom_call" | custom-call | flops 9663676416 | bytes 17825792 | tf_op jit(solution)/shard_map/pallas_call | solution.py:170
  103.9 2.6 %collective-permute-done.28 = bf16[128,1536]{1,0:T(8,128)(2,1)S(1)} collective-permute-done((bf16[128,1536]{1,0:T(8,128)(2,1)S(1)}, bf16[128,1536]{1,0:T(8,128)(2,1)S(1)}, u32[]{:S(2)}, u32[]{:S(2)}) %collective-permute-start.28) | collective-permute-done | bytes 393248 | tf_op jit(solution)/shard_map/ppermute | solution.py:40
  106.6 1.5 %fusion.7 = bf16[128,1536]{1,0:T(8,128)(2,1)} fusion(bf16[128,1536]{1,0:T(8,128)(2,1)S(1)} %copy-done.1, bf16[128,1536]{1,0:T(8,128)(2,1)S(1)} %collective-permute-done.27, bf16[128,1536]{1,0:T(8,128)(2,1)S(1)} %collective-permute-done.29, bf16[128,1536]{1,0:T(8,128)(2,1)S(1)} %collective-permute-done.28, f32[512,1536]{1,0:T(8,128)S(1)} %get-tuple-element.73, ...), kind=kLoop, calls=%fused_computation.14 | loop fusion | flops 5505024 | bytes 3145728 | tf_op jit(solution)/shard_map/convert_element_type | solution.py:248
  (73 shorter events, 6.8 us)
Async XLA Ops:
  0.6 15.7 %collective-permute-start.2 = (bf16[64,1536]{1,0:T(8,128)(2,1)}, bf16[64,1536]{1,0:T(8,128)(2,1)S(1)}, u32[]{:S(2)}, u32[]{:S(2)}) collective-permute-start(bf16[64,1536]{1,0:T(8,128)(2,1)} %param.4), channel_id=1, source_target_pairs={{0,8},{128,136},{8,0},{136,128},{1,9},{129,137},{9,1},{137,129},{2... | collective-permute-start | bytes 589832 | tf_op jit(solution)/shard_map/ppermute | solution.py:36
  4.3 12.1 %collective-permute-start.1 = (bf16[64,1536]{1,0:T(8,128)(2,1)}, bf16[64,1536]{1,0:T(8,128)(2,1)S(1)}, u32[]{:S(2)}, u32[]{:S(2)}) collective-permute-start(bf16[64,1536]{1,0:T(8,128)(2,1)} %param.4), channel_id=1, source_target_pairs={{0,7},{1,0},{2,1},{3,2},{4,3},{5,4},{6,5},{7,6},{8,15},{9,8},{10,9... | collective-permute-start | bytes 589832 | tf_op jit(solution)/shard_map/ppermute | solution.py:29
  9.9 6.6 %collective-permute-start = (bf16[64,1536]{1,0:T(8,128)(2,1)}, bf16[64,1536]{1,0:T(8,128)(2,1)S(1)}, u32[]{:S(2)}, u32[]{:S(2)}) collective-permute-start(bf16[64,1536]{1,0:T(8,128)(2,1)} %param.4), channel_id=1, source_target_pairs={{0,1},{1,2},{2,3},{3,4},{4,5},{5,6},{6,7},{7,0},{8,9},{9,10},{10,1... | collective-permute-start | bytes 589832 | tf_op jit(solution)/shard_map/ppermute | solution.py:29
  11.2 8.8 %collective-permute-start.9 = (bf16[128,1536]{1,0:T(8,128)(2,1)S(1)}, bf16[128,1536]{1,0:T(8,128)(2,1)S(1)}, u32[]{:S(2)}, u32[]{:S(2)}) collective-permute-start(bf16[128,1536]{1,0:T(8,128)(2,1)S(1)} %fusion.2), channel_id=1, source_target_pairs={{0,16},{16,0},{1,17},{17,1},{2,18},{18,2},{3,19},{19,3},{4,20},{20... | collective-permute-start | bytes 1179656 | tf_op jit(solution)/shard_map/ppermute | solution.py:49
  12.5 13.9 %collective-permute-start.5 = (bf16[128,1536]{1,0:T(8,128)(2,1)S(1)}, bf16[128,1536]{1,0:T(8,128)(2,1)S(1)}, u32[]{:S(2)}, u32[]{:S(2)}) collective-permute-start(bf16[128,1536]{1,0:T(8,128)(2,1)S(1)} %fusion.2), channel_id=1, source_target_pairs={{0,64},{32,96},{64,0},{96,32},{1,65},{33,97},{65,1},{97,33},{2,66}... | collective-permute-start | bytes 1179656 | tf_op jit(solution)/shard_map/ppermute | solution.py:40
  16.5 8.5 %collective-permute-start.8 = (bf16[128,1536]{1,0:T(8,128)(2,1)S(1)}, bf16[128,1536]{1,0:T(8,128)(2,1)S(1)}, u32[]{:S(2)}, u32[]{:S(2)}) collective-permute-start(bf16[128,1536]{1,0:T(8,128)(2,1)S(1)} %fusion.2), channel_id=1, source_target_pairs={{0,128},{128,0},{1,129},{129,1},{2,130},{130,2},{3,131},{131,3},{4... | collective-permute-start | bytes 1179656 | tf_op jit(solution)/shard_map/ppermute | solution.py:49
  16.8 10.8 %collective-permute-start.4 = (bf16[128,1536]{1,0:T(8,128)(2,1)S(1)}, bf16[128,1536]{1,0:T(8,128)(2,1)S(1)}, u32[]{:S(2)}, u32[]{:S(2)}) collective-permute-start(bf16[128,1536]{1,0:T(8,128)(2,1)S(1)} %get-tuple-element.113), channel_id=1, source_target_pairs={{0,7},{1,0},{2,1},{3,2},{4,3},{5,4},{6,5},{7,6},{8,15},{9,8},{10,9... | collective-permute-start | bytes 1179656 | tf_op jit(solution)/shard_map/ppermute | solution.py:29
  19.9 10.9 %collective-permute-start.3 = (bf16[128,1536]{1,0:T(8,128)(2,1)S(1)}, bf16[128,1536]{1,0:T(8,128)(2,1)S(1)}, u32[]{:S(2)}, u32[]{:S(2)}) collective-permute-start(bf16[128,1536]{1,0:T(8,128)(2,1)S(1)} %get-tuple-element.114), channel_id=1, source_target_pairs={{0,1},{1,2},{2,3},{3,4},{4,5},{5,6},{6,7},{7,0},{8,9},{9,10},{10,1... | collective-permute-start | bytes 1179656 | tf_op jit(solution)/shard_map/ppermute | solution.py:29
  24.9 11.7 %collective-permute-start.11 = (bf16[192,1536]{1,0:T(8,128)(2,1)S(1)}, bf16[192,1536]{1,0:T(8,128)(2,1)S(1)}, u32[]{:S(2)}, u32[]{:S(2)}) collective-permute-start(bf16[192,1536]{1,0:T(8,128)(2,1)S(1)} %pad_maximum_fusion.2), channel_id=1, source_target_pairs={{0,136},{128,0},{8,128},{136,8},{1,137},{129,1},{9,129},{137,9},{2... | collective-permute-start | bytes 1769480 | tf_op jit(solution)/shard_map/ppermute | solution.py:36
  25.8 12.7 %collective-permute-start.10 = (bf16[192,1536]{1,0:T(8,128)(2,1)S(1)}, bf16[192,1536]{1,0:T(8,128)(2,1)S(1)}, u32[]{:S(2)}, u32[]{:S(2)}) collective-permute-start(bf16[192,1536]{1,0:T(8,128)(2,1)S(1)} %pad_maximum_fusion.2), channel_id=1, source_target_pairs={{0,128},{128,8},{8,136},{136,0},{1,129},{129,9},{9,137},{137,1},{2... | collective-permute-start | bytes 1769480 | tf_op jit(solution)/shard_map/ppermute | solution.py:36
  30.8 13.6 %collective-permute-start.6 = (bf16[128,1536]{1,0:T(8,128)(2,1)S(1)}, bf16[128,1536]{1,0:T(8,128)(2,1)S(1)}, u32[]{:S(2)}, u32[]{:S(2)}) collective-permute-start(bf16[128,1536]{1,0:T(8,128)(2,1)S(1)} %collective-permute-done.3), channel_id=1, source_target_pairs={{0,1},{1,2},{2,3},{3,4},{4,5},{5,6},{6,7},{7,0},{8,9},{9,10},{10,1... | collective-permute-start | bytes 1179656 | tf_op jit(solution)/shard_map/ppermute | solution.py:29
  30.8 13.6 %collective-permute-start.7 = (bf16[128,1536]{1,0:T(8,128)(2,1)S(1)}, bf16[128,1536]{1,0:T(8,128)(2,1)S(1)}, u32[]{:S(2)}, u32[]{:S(2)}) collective-permute-start(bf16[128,1536]{1,0:T(8,128)(2,1)S(1)} %collective-permute-done.4), channel_id=1, source_target_pairs={{0,7},{1,0},{2,1},{3,2},{4,3},{5,4},{6,5},{7,6},{8,15},{9,8},{10,9... | collective-permute-start | bytes 1179656 | tf_op jit(solution)/shard_map/ppermute | solution.py:29
  33.5 11.1 %collective-permute-start.13 = (bf16[256,1536]{1,0:T(8,128)(2,1)S(1)}, bf16[256,1536]{1,0:T(8,128)(2,1)S(1)}, u32[]{:S(2)}, u32[]{:S(2)}) collective-permute-start(bf16[256,1536]{1,0:T(8,128)(2,1)S(1)} %pad_maximum_fusion.refs_10_), channel_id=1, source_target_pairs={{0,32},{16,112},{32,64},{48,16},{64,96},{80,48},{96,0},{112,80},{1... | collective-permute-start | bytes 2359304 | tf_op jit(solution)/shard_map/ppermute | solution.py:45
  38.5 5.6 %collective-permute-start.12 = (bf16[128,1536]{1,0:T(8,128)(2,1)S(1)}, bf16[128,1536]{1,0:T(8,128)(2,1)S(1)}, u32[]{:S(2)}, u32[]{:S(2)}) collective-permute-start(bf16[128,1536]{1,0:T(8,128)(2,1)S(1)} %collective-permute-done.8), channel_id=1, source_target_pairs={{0,16},{16,0},{1,17},{17,1},{2,18},{18,2},{3,19},{19,3},{4,20},{20... | collective-permute-start | bytes 1179656 | tf_op jit(solution)/shard_map/ppermute | solution.py:49
  42.8 15.9 %collective-permute-start.19 = (bf16[128,1536]{1,0:T(8,128)(2,1)S(1)}, bf16[128,1536]{1,0:T(8,128)(2,1)S(1)}, u32[]{:S(2)}, u32[]{:S(2)}) collective-permute-start(bf16[128,1536]{1,0:T(8,128)(2,1)S(1)} %pad_maximum_fusion.5), channel_id=1, source_target_pairs={{0,136},{128,0},{8,128},{136,8},{1,137},{129,1},{9,129},{137,9},{2... | collective-permute-start | bytes 1179656 | tf_op jit(solution)/shard_map/ppermute | solution.py:36
  44.1 17.4 %collective-permute-start.18 = (bf16[128,1536]{1,0:T(8,128)(2,1)S(1)}, bf16[128,1536]{1,0:T(8,128)(2,1)S(1)}, u32[]{:S(2)}, u32[]{:S(2)}) collective-permute-start(bf16[128,1536]{1,0:T(8,128)(2,1)S(1)} %pad_maximum_fusion.5), channel_id=1, source_target_pairs={{0,128},{128,8},{8,136},{136,0},{1,129},{129,9},{9,137},{137,1},{2... | collective-permute-start | bytes 1179656 | tf_op jit(solution)/shard_map/ppermute | solution.py:36
  44.7 10.8 %collective-permute-start.15 = (bf16[96,1536]{1,0:T(8,128)(2,1)S(1)}, bf16[96,1536]{1,0:T(8,128)(2,1)S(1)}, u32[]{:S(2)}, u32[]{:S(2)}) collective-permute-start(bf16[96,1536]{1,0:T(8,128)(2,1)S(1)} %slice.77), channel_id=1, source_target_pairs={{0,7},{1,0},{2,1},{3,2},{4,3},{5,4},{6,5},{7,6},{8,15},{9,8},{10,9... | collective-permute-start | bytes 884744 | tf_op jit(solution)/shard_map/ppermute | solution.py:29
  49.6 8.9 %collective-permute-start.14 = (bf16[96,1536]{1,0:T(8,128)(2,1)S(1)}, bf16[96,1536]{1,0:T(8,128)(2,1)S(1)}, u32[]{:S(2)}, u32[]{:S(2)}) collective-permute-start(bf16[96,1536]{1,0:T(8,128)(2,1)S(1)} %slice.76), channel_id=1, source_target_pairs={{0,1},{1,2},{2,3},{3,4},{4,5},{5,6},{6,7},{7,0},{8,9},{9,10},{10,1... | collective-permute-start | bytes 884744 | tf_op jit(solution)/shard_map/ppermute | solution.py:29
  49.6 14.2 %collective-permute-start.20 = (bf16[128,1536]{1,0:T(8,128)(2,1)S(1)}, bf16[128,1536]{1,0:T(8,128)(2,1)S(1)}, u32[]{:S(2)}, u32[]{:S(2)}) collective-permute-start(bf16[128,1536]{1,0:T(8,128)(2,1)S(1)} %collective-permute-done.8), channel_id=1, source_target_pairs={{0,64},{32,96},{64,0},{96,32},{1,65},{33,97},{65,1},{97,33},{2,66}... | collective-permute-start | bytes 1179656 | tf_op jit(solution)/shard_map/ppermute | solution.py:40
  58.5 13.8 %collective-permute-start.23 = (bf16[256,1536]{1,0:T(8,128)(2,1)S(1)}, bf16[256,1536]{1,0:T(8,128)(2,1)S(1)}, u32[]{:S(2)}, u32[]{:S(2)}) collective-permute-start(bf16[256,1536]{1,0:T(8,128)(2,1)S(1)} %pad_maximum_fusion.1.refs_11_), channel_id=1, source_target_pairs={{0,32},{16,112},{32,64},{48,16},{64,96},{80,48},{96,0},{112,80},{1... | collective-permute-start | bytes 2359304 | tf_op jit(solution)/shard_map/ppermute | solution.py:45
  58.5 5.3 %collective-permute-start.16 = (bf16[32,1536]{1,0:T(8,128)(2,1)S(1)}, bf16[32,1536]{1,0:T(8,128)(2,1)S(1)}, u32[]{:S(2)}, u32[]{:S(2)}) collective-permute-start(bf16[32,1536]{1,0:T(8,128)(2,1)S(1)} %get-tuple-element.109), channel_id=1, source_target_pairs={{0,1},{1,2},{2,3},{3,4},{4,5},{5,6},{6,7},{7,0},{8,9},{9,10},{10,1... | collective-permute-start | bytes 294920 | tf_op jit(solution)/shard_map/ppermute | solution.py:29
  58.7 5.2 %collective-permute-start.17 = (bf16[32,1536]{1,0:T(8,128)(2,1)S(1)}, bf16[32,1536]{1,0:T(8,128)(2,1)S(1)}, u32[]{:S(2)}, u32[]{:S(2)}) collective-permute-start(bf16[32,1536]{1,0:T(8,128)(2,1)S(1)} %get-tuple-element.112), channel_id=1, source_target_pairs={{0,7},{1,0},{2,1},{3,2},{4,3},{5,4},{6,5},{7,6},{8,15},{9,8},{10,9... | collective-permute-start | bytes 294920 | tf_op jit(solution)/shard_map/ppermute | solution.py:29
  61.5 7.7 %collective-permute-start.22 = (bf16[128,1536]{1,0:T(8,128)(2,1)S(1)}, bf16[128,1536]{1,0:T(8,128)(2,1)S(1)}, u32[]{:S(2)}, u32[]{:S(2)}) collective-permute-start(bf16[128,1536]{1,0:T(8,128)(2,1)S(1)} %pad_maximum_fusion.6), channel_id=1, source_target_pairs={{0,136},{128,0},{8,128},{136,8},{1,137},{129,1},{9,129},{137,9},{2... | collective-permute-start | bytes 1179656 | tf_op jit(solution)/shard_map/ppermute | solution.py:36
  63.9 8.5 %collective-permute-start.21 = (bf16[128,1536]{1,0:T(8,128)(2,1)S(1)}, bf16[128,1536]{1,0:T(8,128)(2,1)S(1)}, u32[]{:S(2)}, u32[]{:S(2)}) collective-permute-start(bf16[128,1536]{1,0:T(8,128)(2,1)S(1)} %pad_maximum_fusion.6), channel_id=1, source_target_pairs={{0,128},{128,8},{8,136},{136,0},{1,129},{129,9},{9,137},{137,1},{2... | collective-permute-start | bytes 1179656 | tf_op jit(solution)/shard_map/ppermute | solution.py:36
  72.3 7.3 %collective-permute-start.24 = (bf16[512,1536]{1,0:T(8,128)(2,1)S(1)}, bf16[512,1536]{1,0:T(8,128)(2,1)S(1)}, u32[]{:S(2)}, u32[]{:S(2)}) collective-permute-start(bf16[512,1536]{1,0:T(8,128)(2,1)S(1)} %get-tuple-element.74), channel_id=1, source_target_pairs={{0,16},{16,0},{1,17},{17,1},{2,18},{18,2},{3,19},{19,3},{4,20},{20... | collective-permute-start | bytes 4718600 | tf_op jit(solution)/shard_map/ppermute | solution.py:49
  76.7 6.6 %collective-permute-start.26 = (bf16[64,1536]{1,0:T(8,128)(2,1)S(1)}, bf16[64,1536]{1,0:T(8,128)(2,1)S(1)}, u32[]{:S(2)}, u32[]{:S(2)}) collective-permute-start(bf16[64,1536]{1,0:T(8,128)(2,1)S(1)} %pad_maximum_fusion.7), channel_id=1, source_target_pairs={{0,136},{128,0},{8,128},{136,8},{1,137},{129,1},{9,129},{137,9},{2... | collective-permute-start | bytes 589832 | tf_op jit(solution)/shard_map/ppermute | solution.py:36
  76.8 7.6 %collective-permute-start.25 = (bf16[64,1536]{1,0:T(8,128)(2,1)S(1)}, bf16[64,1536]{1,0:T(8,128)(2,1)S(1)}, u32[]{:S(2)}, u32[]{:S(2)}) collective-permute-start(bf16[64,1536]{1,0:T(8,128)(2,1)S(1)} %pad_maximum_fusion.7), channel_id=1, source_target_pairs={{0,128},{128,8},{8,136},{136,0},{1,129},{129,9},{9,137},{137,1},{2... | collective-permute-start | bytes 589832 | tf_op jit(solution)/shard_map/ppermute | solution.py:36
  84.5 22.1 %copy-start.1 = (bf16[128,1536]{1,0:T(8,128)(2,1)S(1)}, bf16[128,1536]{1,0:T(8,128)(2,1)}, u32[]{:S(2)}) copy-start(bf16[128,1536]{1,0:T(8,128)(2,1)} %param.3) | copy-start | bytes 1179652
  84.5 6.0 %collective-permute-start.30 = (bf16[768,1536]{1,0:T(8,128)(2,1)S(1)}, bf16[768,1536]{1,0:T(8,128)(2,1)S(1)}, u32[]{:S(2)}, u32[]{:S(2)}) collective-permute-start(bf16[768,1536]{1,0:T(8,128)(2,1)S(1)} %constant_dynamic-update-slice_fusion.12.refs_12_), channel_id=1, source_target_pairs={{0,16},{16,0},{1,17},{17,1},{2,18},{18,2},{3,19},{19,3},{4,20},{20... | collective-permute-start | bytes 7077896 | tf_op jit(solution)/shard_map/ppermute | solution.py:49
  85.6 18.4 %collective-permute-start.27 = (bf16[128,1536]{1,0:T(8,128)(2,1)S(1)}, bf16[128,1536]{1,0:T(8,128)(2,1)S(1)}, u32[]{:S(2)}, u32[]{:S(2)}) collective-permute-start(bf16[128,1536]{1,0:T(8,128)(2,1)S(1)} %get-tuple-element.77), channel_id=1, source_target_pairs={{0,64},{32,96},{64,0},{96,32},{1,65},{33,97},{65,1},{97,33},{2,66}... | collective-permute-start | bytes 1179656 | tf_op jit(solution)/shard_map/ppermute | solution.py:40
  87.8 18.8 %collective-permute-start.28 = (bf16[128,1536]{1,0:T(8,128)(2,1)S(1)}, bf16[128,1536]{1,0:T(8,128)(2,1)S(1)}, u32[]{:S(2)}, u32[]{:S(2)}) collective-permute-start(bf16[128,1536]{1,0:T(8,128)(2,1)S(1)} %get-tuple-element.78), channel_id=1, source_target_pairs={{0,32},{32,64},{64,96},{96,0},{1,33},{33,65},{65,97},{97,1},{2,34}... | collective-permute-start | bytes 1179656 | tf_op jit(solution)/shard_map/ppermute | solution.py:40
  88.1 18.5 %collective-permute-start.29 = (bf16[128,1536]{1,0:T(8,128)(2,1)S(1)}, bf16[128,1536]{1,0:T(8,128)(2,1)S(1)}, u32[]{:S(2)}, u32[]{:S(2)}) collective-permute-start(bf16[128,1536]{1,0:T(8,128)(2,1)S(1)} %get-tuple-element.79), channel_id=1, source_target_pairs={{0,96},{32,0},{64,32},{96,64},{1,97},{33,1},{65,33},{97,65},{2,98}... | collective-permute-start | bytes 1179656 | tf_op jit(solution)/shard_map/ppermute | solution.py:40
  (2 other events, 24.5 us)

commit v9 on v8

--- a/solution.py
+++ b/solution.py
@@ -1,3 +1,5 @@
+import functools
+
 import jax
 import jax.numpy as jnp
 from jax import lax
@@ -120,18 +122,18 @@
 PIECES = [
     [(2 * far, OWN[j]) for far, j in EARLY],
     [(2 * far, OWN[j]) for far, j in LATE],
-    *[[(dx, OWN[j]) for j in group] for dx in (3, 1) for group in ((0, 1, 2), (3, 4), (5, 6), (7,))],
+    *[[(dx, OWN[j]) for j in group] for group in ((0, 1, 2), (3, 4), (5, 6, 7)) for dx in (3, 1)],
 ]
 
 
-def weight_kernel(*refs):
-    pieces, acts_refs = refs[:10], refs[10:14]
-    out_ref, grads, acts = refs[14:]
+def weight_kernel(layout, *refs):
+    pieces, acts_refs = refs[: len(layout)], refs[len(layout) : len(layout) + 4]
+    *sum_ref, out_ref, grads, acts = refs[len(layout) + 4 :]
     y, c, xl, xh, z = (lax.axis_index(a) for a in ("y", "c", "xl", "xh", "z"))
 
     @pl.when(pl.program_id(0) == 0)
     def _():
-        for k, (dx, dz) in enumerate(shard for piece in PIECES for shard in piece):
+        for k, (dx, dz) in enumerate(shard for piece in layout for shard in piece):
             xp = lax.rem(2 * xh + xl + dx, 4)
             zp = lax.rem(z + dz + 8, 8)
             dy = lax.rem(2 * (xp // 2) + zp // 4 + 4 - y, 4)
@@ -157,26 +159,29 @@
 
     lanes = pl.ds(pl.multiple_of(pl.program_id(0) * 256, 256), 256)
     start = 0
-    for piece, ref in zip(PIECES, pieces):
+    for piece, ref in zip(layout, pieces):
         grads[start : start + 64 * len(piece), :] = ref[:, lanes]
         start += 64 * len(piece)
-    out_ref[...] = lax.dot_general(
-        grads[...], acts[...], (((0,), (0,)), ((), ())), preferred_element_type=F32
-    ).astype(BF)
-
-
-def weight_gradient(pieces, acts):
-    step = 256
+    product = lax.dot_general(grads[...], acts[...], (((0,), (0,)), ((), ())), preferred_element_type=F32)
+    if sum_ref:
+        product = product + sum_ref[0][...]
+    out_ref[...] = product.astype(out_ref.dtype)
+
+
+def weight_product(layout, pieces, acts, so_far):
+    step, count = 256, 64 * sum(len(piece) for piece in layout)
+    block = pl.BlockSpec((step, 1536), lambda m: (m, 0))
+    last = so_far is not None
     return pl.pallas_call(
-        weight_kernel,
+        functools.partial(weight_kernel, layout),
         grid=(1536 // step,),
-        in_specs=[VMEM] * 14,
-        out_specs=pl.BlockSpec((step, 1536), lambda m: (m, 0)),
-        out_shape=jax.ShapeDtypeStruct((1536, 1536), BF),
-        scratch_shapes=[pltpu.VMEM((2048, step), BF), pltpu.VMEM((2048, 1536), BF)],
+        in_specs=[VMEM] * (len(pieces) + 4) + [block] * last,
+        out_specs=block,
+        out_shape=jax.ShapeDtypeStruct((1536, 1536), BF if last else F32),
+        scratch_shapes=[pltpu.VMEM((count, step), BF), pltpu.VMEM((count, 1536), BF)],
         compiler_params=pltpu.CompilerParams(vmem_limit_bytes=18 << 20),
-        cost_estimate=pl.CostEstimate(flops=2 * 2048 * 1536 * 1536, bytes_accessed=17 << 20, transcendentals=0),
-    )(*pieces, *acts)
+        cost_estimate=pl.CostEstimate(flops=2 * count * 1536 * 1536, bytes_accessed=12 << 20, transcendentals=0),
+    )(*pieces, *acts, *([so_far] if last else []))
 
 
 def per_device(pre_act, out_grad, down_weight):
@@ -194,9 +199,9 @@
     other_rep = swap(activation, "xl")
     chip = jnp.concatenate([activation, act_c])
     near = jnp.concatenate([g, up1, down1])
-    other_rep, chip, near = tie(other_rep, chip, near)
+    left_a, right_a = along_x(near, 1), along_x(near, -1)
+    other_rep, chip = tie(other_rep, chip)
     hop_1 = round_y(chip)
-    left_a, right_a = along_x(near, 1), along_x(near, -1)
     up2, down2, hop_2 = tie(up2, down2, hop_2)
 
     up3, down3 = along_z(up2, 1), along_z(down2, -1)
@@ -218,31 +223,28 @@
 
     up5, down5 = along_z(up4[:32], 1), along_z(down4[64:], -1)
     last = jnp.concatenate([up4[64:], down4[:32]])
-    third = jnp.concatenate([up3[64:], down3[:64]])
-    left_c, right_c = along_x(third, 1), along_x(third, -1)
     hop_3 = round_y(other_chip)
     up5, down5, early, left_b, right_b, hop_4 = tie(up5, down5, early, left_b, right_b, hop_4)
 
     grads_late = jnp.concatenate([last, up4[:64], down4[32:], up5, down5])
     mine, other = late_partial(early, grads_late, down_weight)
-    mine, other, left_c, right_c, hop_3, last = tie(mine, other, left_c, right_c, hop_3, last)
+    mine, other, hop_3, last = tie(mine, other, hop_3, last)
     other = swap(other, "c")
-    left_d, right_d = along_x(last, 1), along_x(last, -1)
+    came = jnp.concatenate([hop_1, hop_2, hop_3, hop_4])
+    swapped = swap(came, "c")
+    third = jnp.concatenate([up3[64:], down3[:64], last])
+    left_c, right_c = along_x(third, 1), along_x(third, -1)
 
     def summed(block):
         return mine[128 * block : 128 * block + 128] + other[128 * block : 128 * block + 128].astype(F32)
 
     to_above, to_below, to_across = summed(1).astype(BF), summed(3).astype(BF), summed(2).astype(BF)
-    to_above, to_below, to_across, hop_3, left_d, right_d = tie(
-        to_above, to_below, to_across, hop_3, left_d, right_d
-    )
-    came = jnp.concatenate([hop_1, hop_2, hop_3, hop_4])
-    swapped = swap(came, "c")
     from_across = along_y(to_across, 2)
     from_below, from_above = along_y(to_above, 1), along_y(to_below, -1)
 
-    arrived = [left_a, left_b, left_c, left_d, right_a, right_b, right_c, right_d]
-    weight_grad = weight_gradient([grads_early, grads_late, *arrived], [chip, other_chip, came, swapped])
+    acts = [chip, other_chip, came, swapped]
+    weight_sum = weight_product(PIECES[:5], [grads_early, grads_late, left_a, right_a, left_b], acts, None)
+    weight_grad = weight_product(PIECES[5:], [right_b, left_c, right_c], acts, weight_sum)
     from_across, from_below, from_above, weight_grad = tie(from_across, from_below, from_above, weight_grad)
     grad_act = summed(0) + from_below.astype(F32) + from_above.astype(F32) + from_across.astype(F32)
     pre_grad = (grad_act * gelu_slope(pre_wide)).astype(BF)

time: 108 us -> 103 us (0.954)
  starting transfers between devices: 47.6 us -> 42.9 us
  waiting for transfers between devices: 34.5 us -> 32.1 us
  Pallas kernels: 20.2 us -> 22 us
    ppermute x9 -> x7, waiting for transfers between devices: 15.8 us -> 9.33 us  [along_x(): lax.ppermute(a, ('xl', 'xh'), [(place(x), place((x + d) % 4)) for x in ra...]
    ppermute x2, waiting for transfers between devices: 0.17 us -> 5.59 us  [round_y(): lax.ppermute(a, ('y', 'c'), [(s[0] * C + s[1], t[0] * C + t[1]) for s, t...]
    ppermute x10, waiting for transfers between devices: 8.35 us -> 4.13 us  [along_z(): return lax.ppermute(a, 'z', [(i, (i + d) % Z) for i in range(Z)])]
    ppermute x5, waiting for transfers between devices: 7.51 us -> 10.6 us  [swap(): return lax.ppermute(a, axis, [(0, 1), (1, 0)])]
    ppermute x10, starting transfers between devices: 19.1 us -> 16.5 us  [along_z(): return lax.ppermute(a, 'z', [(i, (i + d) % Z) for i in range(Z)])]
    ppermute x5, starting transfers between devices: 11.3 us -> 9.15 us  [swap(): return lax.ppermute(a, axis, [(0, 1), (1, 0)])]
    pallas_call x1 -> x2, Pallas kernels: 13.5 us -> 15.2 us  [weight_product(): pl.pallas_call(functools.partial(weight_kernel, layout), grid=(1536 // st...]
    ppermute x2, starting transfers between devices: 0.01 us -> 1.7 us  [round_y(): lax.ppermute(a, ('y', 'c'), [(s[0] * C + s[1], t[0] * C + t[1]) for s, t...]
  transfers between devices with their start and end apart: 31 -> 29, of which waited for: 16 -> 10; matrix products, arithmetic and copies ran while one was open for 3% -> 3% of each run, Pallas kernels for 19% -> 21%
where the time goes in v9:
time: 103 us
  starting transfers between devices  42.9 us (42%)
  waiting for transfers between devices  32.1 us (31%)
  Pallas kernels  22 us (21%)
  other arithmetic  3.32 us (3%)
  local copies, waits for them, and re-layouts  1.5 us (1%)
  between operations  1.03 us (1%)
    ppermute x10, starting transfers between devices, along_z(): return lax.ppermute(a, 'z', [(i, (i + d) % Z) for i in range(Z)])  16.5 us
    pallas_call x2, Pallas kernels, weight_product(): pl.pallas_call(functools.partial(weight_kernel, layout), grid=(1536 // st...  15.2 us
    ppermute x5, waiting for transfers between devices, swap(): return lax.ppermute(a, axis, [(0, 1), (1, 0)])  10.6 us
    ppermute x7, waiting for transfers between devices, along_x(): lax.ppermute(a, ('xl', 'xh'), [(place(x), place((x + d) % 4)) for x in ra...  9.33 us
    ppermute x5, starting transfers between devices, swap(): return lax.ppermute(a, axis, [(0, 1), (1, 0)])  9.15 us
    ppermute x7, starting transfers between devices, along_x(): lax.ppermute(a, ('xl', 'xh'), [(place(x), place((x + d) % 4)) for x in ra...  8.34 us
    ppermute x5, starting transfers between devices, along_y(): return lax.ppermute(a, 'y', [(i, (i + d) % Y) for i in range(Y)])  7.22 us
    ppermute x2, waiting for transfers between devices, round_y(): lax.ppermute(a, ('y', 'c'), [(s[0] * C + s[1], t[0] * C + t[1]) for s, t...  5.59 us
  transfers between devices with their start and end apart: 29, of which 10 were waited for; matrix products, arithmetic and copies ran while one was open for 3% of the time, Pallas kernels for 21%

profile of v9, /device:TPU:1, one launch (start us, length us, event | category | flops | bytes accessed | tf_op | source)
XLA Modules:
  0.0 102.9 jit_solution(7499994086229569640)
XLA Ops:
  0.6 2.5 %collective-permute-start = (bf16[64,1536]{1,0:T(8,128)(2,1)}, bf16[64,1536]{1,0:T(8,128)(2,1)S(1)}, u32[]{:S(2)}, u32[]{:S(2)}) collective-permute-start(bf16[64,1536]{1,0:T(8,128)(2,1)} %param.4), channel_id=1, source_target_pairs={{0,1},{1,2},{2,3},{3,4},{4,5},{5,6},{6,7},{7,0},{8,9},{9,10},{10,1... | collective-permute-start | bytes 589832 | tf_op jit(solution)/shard_map/ppermute | solution.py:31
  3.2 4.0 %collective-permute-start.1 = (bf16[64,1536]{1,0:T(8,128)(2,1)}, bf16[64,1536]{1,0:T(8,128)(2,1)S(1)}, u32[]{:S(2)}, u32[]{:S(2)}) collective-permute-start(bf16[64,1536]{1,0:T(8,128)(2,1)} %param.4), channel_id=1, source_target_pairs={{0,7},{1,0},{2,1},{3,2},{4,3},{5,4},{6,5},{7,6},{8,15},{9,8},{10,9... | collective-permute-start | bytes 589832 | tf_op jit(solution)/shard_map/ppermute | solution.py:31
  7.2 2.7 %collective-permute-start.2 = (bf16[64,1536]{1,0:T(8,128)(2,1)}, bf16[64,1536]{1,0:T(8,128)(2,1)S(1)}, u32[]{:S(2)}, u32[]{:S(2)}) collective-permute-start(bf16[64,1536]{1,0:T(8,128)(2,1)} %param.4), channel_id=1, source_target_pairs={{0,8},{128,136},{8,0},{136,128},{1,9},{129,137},{9,1},{137,129},{2... | collective-permute-start | bytes 589832 | tf_op jit(solution)/shard_map/ppermute | solution.py:38
  9.9 1.3 %fusion.2 = bf16[128,1536]{1,0:T(8,128)(2,1)S(1)} fusion(bf16[128,1536]{1,0:T(8,128)(2,1)} %param.3), kind=kLoop, calls=%fused_computation.9 | loop fusion | flops 1966080 | bytes 786432 | tf_op jit(solution)/shard_map/convert_element_type | solution.py:190
  11.2 1.3 %collective-permute-start.9 = (bf16[128,1536]{1,0:T(8,128)(2,1)S(1)}, bf16[128,1536]{1,0:T(8,128)(2,1)S(1)}, u32[]{:S(2)}, u32[]{:S(2)}) collective-permute-start(bf16[128,1536]{1,0:T(8,128)(2,1)S(1)} %fusion.2), channel_id=1, source_target_pairs={{0,16},{16,0},{1,17},{17,1},{2,18},{18,2},{3,19},{19,3},{4,20},{20... | collective-permute-start | bytes 1179656 | tf_op jit(solution)/shard_map/ppermute | solution.py:51
  12.5 2.9 %collective-permute-start.5 = (bf16[128,1536]{1,0:T(8,128)(2,1)S(1)}, bf16[128,1536]{1,0:T(8,128)(2,1)S(1)}, u32[]{:S(2)}, u32[]{:S(2)}) collective-permute-start(bf16[128,1536]{1,0:T(8,128)(2,1)S(1)} %fusion.2), channel_id=1, source_target_pairs={{0,64},{32,96},{64,0},{96,32},{1,65},{33,97},{65,1},{97,33},{2,66}... | collective-permute-start | bytes 1179656 | tf_op jit(solution)/shard_map/ppermute | solution.py:42
  17.0 2.7 %collective-permute-start.4 = (bf16[128,1536]{1,0:T(8,128)(2,1)S(1)}, bf16[128,1536]{1,0:T(8,128)(2,1)S(1)}, u32[]{:S(2)}, u32[]{:S(2)}) collective-permute-start(bf16[128,1536]{1,0:T(8,128)(2,1)S(1)} %get-tuple-element.101), channel_id=1, source_target_pairs={{0,7},{1,0},{2,1},{3,2},{4,3},{5,4},{6,5},{7,6},{8,15},{9,8},{10,9... | collective-permute-start | bytes 1179656 | tf_op jit(solution)/shard_map/ppermute | solution.py:31
  19.8 1.2 %collective-permute-start.10 = (bf16[192,1536]{1,0:T(8,128)(2,1)S(1)}, bf16[192,1536]{1,0:T(8,128)(2,1)S(1)}, u32[]{:S(2)}, u32[]{:S(2)}) collective-permute-start(bf16[192,1536]{1,0:T(8,128)(2,1)S(1)} %get-tuple-element.96), channel_id=1, source_target_pairs={{0,128},{128,8},{8,136},{136,0},{1,129},{129,9},{9,137},{137,1},{2... | collective-permute-start | bytes 1769480 | tf_op jit(solution)/shard_map/ppermute | solution.py:38
  21.0 5.9 %collective-permute-done.8 = bf16[128,1536]{1,0:T(8,128)(2,1)S(1)} collective-permute-done((bf16[128,1536]{1,0:T(8,128)(2,1)S(1)}, bf16[128,1536]{1,0:T(8,128)(2,1)S(1)}, u32[]{:S(2)}, u32[]{:S(2)}) %collective-permute-start.8) | collective-permute-done | bytes 393248 | tf_op jit(solution)/shard_map/ppermute | solution.py:51
  27.0 1.0 collective-permute-done.3
  28.0 2.7 %collective-permute-start.7 = (bf16[128,1536]{1,0:T(8,128)(2,1)S(1)}, bf16[128,1536]{1,0:T(8,128)(2,1)S(1)}, u32[]{:S(2)}, u32[]{:S(2)}) collective-permute-start(bf16[128,1536]{1,0:T(8,128)(2,1)S(1)} %collective-permute-done.4), channel_id=1, source_target_pairs={{0,7},{1,0},{2,1},{3,2},{4,3},{5,4},{6,5},{7,6},{8,15},{9,8},{10,9... | collective-permute-start | bytes 1179656 | tf_op jit(solution)/shard_map/ppermute | solution.py:31
  31.2 6.2 %collective-permute-done.10.refs_2_ = bf16[192,1536]{1,0:T(8,128)(2,1)S(1)} collective-permute-done((bf16[192,1536]{1,0:T(8,128)(2,1)S(1)}, bf16[192,1536]{1,0:T(8,128)(2,1)S(1)}, u32[]{:S(2)}, u32[]{:S(2)}) %collective-permute-start.10) | collective-permute-done | bytes 589856 | tf_op jit(solution)/shard_map/ppermute | solution.py:38
  37.4 3.1 %collective-permute-done.11.refs_3_ = bf16[192,1536]{1,0:T(8,128)(2,1)S(1)} collective-permute-done((bf16[192,1536]{1,0:T(8,128)(2,1)S(1)}, bf16[192,1536]{1,0:T(8,128)(2,1)S(1)}, u32[]{:S(2)}, u32[]{:S(2)}) %collective-permute-start.11) | collective-permute-done | bytes 589856 | tf_op jit(solution)/shard_map/ppermute | solution.py:38
  40.5 2.1 %collective-permute-start.12 = (bf16[128,1536]{1,0:T(8,128)(2,1)S(1)}, bf16[128,1536]{1,0:T(8,128)(2,1)S(1)}, u32[]{:S(2)}, u32[]{:S(2)}) collective-permute-start(bf16[128,1536]{1,0:T(8,128)(2,1)S(1)} %collective-permute-done.8), channel_id=1, source_target_pairs={{0,16},{16,0},{1,17},{17,1},{2,18},{18,2},{3,19},{19,3},{4,20},{20... | collective-permute-start | bytes 1179656 | tf_op jit(solution)/shard_map/ppermute | solution.py:51
  42.8 1.1 %collective-permute-done.12 = bf16[128,1536]{1,0:T(8,128)(2,1)S(1)} collective-permute-done((bf16[128,1536]{1,0:T(8,128)(2,1)S(1)}, bf16[128,1536]{1,0:T(8,128)(2,1)S(1)}, u32[]{:S(2)}, u32[]{:S(2)}) %collective-permute-start.12) | collective-permute-done | bytes 393248 | tf_op jit(solution)/shard_map/ppermute | solution.py:51
  44.0 1.5 %collective-permute-start.19 = (bf16[128,1536]{1,0:T(8,128)(2,1)S(1)}, bf16[128,1536]{1,0:T(8,128)(2,1)S(1)}, u32[]{:S(2)}, u32[]{:S(2)}) collective-permute-start(bf16[128,1536]{1,0:T(8,128)(2,1)S(1)} %pad_maximum_fusion.5), channel_id=1, source_target_pairs={{0,136},{128,0},{8,128},{136,8},{1,137},{129,1},{9,129},{137,9},{2... | collective-permute-start | bytes 1179656 | tf_op jit(solution)/shard_map/ppermute | solution.py:38
  45.9 2.7 %collective-permute-start.15 = (bf16[96,1536]{1,0:T(8,128)(2,1)S(1)}, bf16[96,1536]{1,0:T(8,128)(2,1)S(1)}, u32[]{:S(2)}, u32[]{:S(2)}) collective-permute-start(bf16[96,1536]{1,0:T(8,128)(2,1)S(1)} %slice.77), channel_id=1, source_target_pairs={{0,7},{1,0},{2,1},{3,2},{4,3},{5,4},{6,5},{7,6},{8,15},{9,8},{10,9... | collective-permute-start | bytes 884744 | tf_op jit(solution)/shard_map/ppermute | solution.py:31
  48.8 1.4 %collective-permute-start.20 = (bf16[128,1536]{1,0:T(8,128)(2,1)S(1)}, bf16[128,1536]{1,0:T(8,128)(2,1)S(1)}, u32[]{:S(2)}, u32[]{:S(2)}) collective-permute-start(bf16[128,1536]{1,0:T(8,128)(2,1)S(1)} %collective-permute-done.8), channel_id=1, source_target_pairs={{0,64},{32,96},{64,0},{96,32},{1,65},{33,97},{65,1},{97,33},{2,66}... | collective-permute-start | bytes 1179656 | tf_op jit(solution)/shard_map/ppermute | solution.py:42
  50.3 4.8 %shard_map.50.early_ref = f32[768,1536]{1,0:T(8,128)S(1)} custom-call(bf16[768,1536]{1,0:T(8,128)(2,1)S(1)} %slice_dynamic-update-slice_fusion.2.grads_ref.refs_0_, bf16[1536,1536]{1,0:T(8,128)(2,1)S(1)} %bitcast.1), custom_call_target="tpu_custom_call" | custom-call | flops 3623878656 | bytes 12582912 | tf_op jit(solution)/shard_map/pallas_call | solution.py:73
  56.8 1.2 %collective-permute-start.21 = (bf16[256,1536]{1,0:T(8,128)(2,1)S(1)}, bf16[256,1536]{1,0:T(8,128)(2,1)S(1)}, u32[]{:S(2)}, u32[]{:S(2)}) collective-permute-start(bf16[256,1536]{1,0:T(8,128)(2,1)S(1)} %pad_maximum_fusion.1.refs_6_.refs_4_), channel_id=1, source_target_pairs={{0,32},{16,112},{32,64},{48,16},{64,96},{80,48},{96,0},{112,80},{1... | collective-permute-start | bytes 2359304 | tf_op jit(solution)/shard_map/ppermute | solution.py:47
  58.0 1.1 %collective-permute-done.17 = bf16[32,1536]{1,0:T(8,128)(2,1)S(1)} collective-permute-done((bf16[32,1536]{1,0:T(8,128)(2,1)S(1)}, bf16[32,1536]{1,0:T(8,128)(2,1)S(1)}, u32[]{:S(2)}, u32[]{:S(2)}) %collective-permute-start.17) | collective-permute-done | bytes 98336 | tf_op jit(solution)/shard_map/ppermute | solution.py:31
  59.1 2.0 %collective-permute-done.16 = bf16[32,1536]{1,0:T(8,128)(2,1)S(1)} collective-permute-done((bf16[32,1536]{1,0:T(8,128)(2,1)S(1)}, bf16[32,1536]{1,0:T(8,128)(2,1)S(1)}, u32[]{:S(2)}, u32[]{:S(2)}) %collective-permute-start.16) | collective-permute-done | bytes 98336 | tf_op jit(solution)/shard_map/ppermute | solution.py:31
  61.1 2.0 %shard_map.51 = (f32[512,1536]{1,0:T(8,128)S(1)}, bf16[512,1536]{1,0:T(8,128)(2,1)S(1)}) custom-call(f32[768,1536]{1,0:T(8,128)S(1)} %shard_map.50.early_ref, bf16[256,1536]{1,0:T(8,128)(2,1)S(1)} %constant_dynamic-update-slice_fusion.11.grads_ref.refs_1_, bf16[1536,1536]{1,0:T(8,128)(2,1)S(1)} %bitcast.1), custom_call_target="tpu_custom_call" | custom-call | flops 1207959552 | bytes 8388608 | tf_op jit(solution)/shard_map/pallas_call | solution.py:111
  63.1 5.6 %collective-permute-done.21 = bf16[256,1536]{1,0:T(8,128)(2,1)S(1)} collective-permute-done((bf16[256,1536]{1,0:T(8,128)(2,1)S(1)}, bf16[256,1536]{1,0:T(8,128)(2,1)S(1)}, u32[]{:S(2)}, u32[]{:S(2)}) %collective-permute-start.21) | collective-permute-done | bytes 786464 | tf_op jit(solution)/shard_map/ppermute | solution.py:47
  68.8 5.2 %collective-permute-start.28 = (bf16[768,1536]{1,0:T(8,128)(2,1)S(1)}, bf16[768,1536]{1,0:T(8,128)(2,1)S(1)}, u32[]{:S(2)}, u32[]{:S(2)}) collective-permute-start(bf16[768,1536]{1,0:T(8,128)(2,1)S(1)} %constant_dynamic-update-slice_fusion.15.refs_7_.refs_5_), channel_id=1, source_target_pairs={{0,16},{16,0},{1,17},{17,1},{2,18},{18,2},{3,19},{19,3},{4,20},{20... | collective-permute-start | bytes 7077896 | tf_op jit(solution)/shard_map/ppermute | solution.py:51
  74.3 2.7 %collective-permute-start.27 = (bf16[192,1536]{1,0:T(8,128)(2,1)S(1)}, bf16[192,1536]{1,0:T(8,128)(2,1)S(1)}, u32[]{:S(2)}, u32[]{:S(2)}) collective-permute-start(bf16[192,1536]{1,0:T(8,128)(2,1)S(1)} %pad_maximum_fusion.2), channel_id=1, source_target_pairs={{0,136},{128,0},{8,128},{136,8},{1,137},{129,1},{9,129},{137,9},{2... | collective-permute-start | bytes 1769480 | tf_op jit(solution)/shard_map/ppermute | solution.py:38
  76.9 3.5 %collective-permute-done.22 = bf16[512,1536]{1,0:T(8,128)(2,1)S(1)} collective-permute-done((bf16[512,1536]{1,0:T(8,128)(2,1)S(1)}, bf16[512,1536]{1,0:T(8,128)(2,1)S(1)}, u32[]{:S(2)}, u32[]{:S(2)}) %collective-permute-start.22) | collective-permute-done | bytes 1572896 | tf_op jit(solution)/shard_map/ppermute | solution.py:51
  81.0 2.6 %collective-permute-start.25 = (bf16[128,1536]{1,0:T(8,128)(2,1)S(1)}, bf16[128,1536]{1,0:T(8,128)(2,1)S(1)}, u32[]{:S(2)}, u32[]{:S(2)}) collective-permute-start(bf16[128,1536]{1,0:T(8,128)(2,1)S(1)} %get-tuple-element.78), channel_id=1, source_target_pairs={{0,96},{32,0},{64,32},{96,64},{1,97},{33,1},{65,33},{97,65},{2,98}... | collective-permute-start | bytes 1179656 | tf_op jit(solution)/shard_map/ppermute | solution.py:42
  83.6 9.7 %shard_map.52.refs_7_ = f32[1536,1536]{1,0:T(8,128)S(1)} custom-call(bf16[768,1536]{1,0:T(8,128)(2,1)S(1)} %slice_dynamic-update-slice_fusion.2.grads_ref.refs_0_, bf16[256,1536]{1,0:T(8,128)(2,1)S(1)} %constant_dynamic-update-slice_fusion.11.grads_ref.refs_1_, bf16[192,1536]{1,0:T(8,128)(2,1)S(1)} %collective-permute-done.10.refs_2_, ...), custom_call_target="tpu_custom_call" | custom-call | flops 7247757312 | bytes 12582912 | tf_op jit(solution)/shard_map/pallas_call | solution.py:175
  93.4 5.5 %shard_map.53 = bf16[1536,1536]{1,0:T(8,128)(2,1)} custom-call(bf16[128,1536]{1,0:T(8,128)(2,1)S(1)} %collective-permute-done.19.refs_0_, bf16[192,1536]{1,0:T(8,128)(2,1)S(1)} %collective-permute-done.26.refs_1_, bf16[192,1536]{1,0:T(8,128)(2,1)S(1)} %collective-permute-done.27.refs_2_, bf16[256,1536]{1,0:T(8,128)(2,1)S(1)} %pad_maximum_fusion.refs_5_.refs_3_, ...), custom_call_target="tpu_custom_call" | custom-call | flops 2415919104 | bytes 12582912 | tf_op jit(solution)/shard_map/pallas_call | solution.py:175
  98.9 2.5 %collective-permute-done.24 = bf16[128,1536]{1,0:T(8,128)(2,1)S(1)} collective-permute-done((bf16[128,1536]{1,0:T(8,128)(2,1)S(1)}, bf16[128,1536]{1,0:T(8,128)(2,1)S(1)}, u32[]{:S(2)}, u32[]{:S(2)}) %collective-permute-start.24) | collective-permute-done | bytes 393248 | tf_op jit(solution)/shard_map/ppermute | solution.py:42
  101.4 1.5 %fusion.7 = bf16[128,1536]{1,0:T(8,128)(2,1)} fusion(bf16[128,1536]{1,0:T(8,128)(2,1)S(1)} %copy-done, bf16[128,1536]{1,0:T(8,128)(2,1)S(1)} %collective-permute-done.23, bf16[128,1536]{1,0:T(8,128)(2,1)S(1)} %collective-permute-done.25, bf16[128,1536]{1,0:T(8,128)(2,1)S(1)} %collective-permute-done.24, f32[512,1536]{1,0:T(8,128)S(1)} %get-tuple-element.63, ...), kind=kLoop, calls=%fused_computation.14 | loop fusion | flops 5505024 | bytes 3145728 | tf_op jit(solution)/shard_map/convert_element_type | solution.py:250
  (70 shorter events, 5.5 us)
Async XLA Ops:
  0.6 15.8 %collective-permute-start = (bf16[64,1536]{1,0:T(8,128)(2,1)}, bf16[64,1536]{1,0:T(8,128)(2,1)S(1)}, u32[]{:S(2)}, u32[]{:S(2)}) collective-permute-start(bf16[64,1536]{1,0:T(8,128)(2,1)} %param.4), channel_id=1, source_target_pairs={{0,1},{1,2},{2,3},{3,4},{4,5},{5,6},{6,7},{7,0},{8,9},{9,10},{10,1... | collective-permute-start | bytes 589832 | tf_op jit(solution)/shard_map/ppermute | solution.py:31
  3.2 13.3 %collective-permute-start.1 = (bf16[64,1536]{1,0:T(8,128)(2,1)}, bf16[64,1536]{1,0:T(8,128)(2,1)S(1)}, u32[]{:S(2)}, u32[]{:S(2)}) collective-permute-start(bf16[64,1536]{1,0:T(8,128)(2,1)} %param.4), channel_id=1, source_target_pairs={{0,7},{1,0},{2,1},{3,2},{4,3},{5,4},{6,5},{7,6},{8,15},{9,8},{10,9... | collective-permute-start | bytes 589832 | tf_op jit(solution)/shard_map/ppermute | solution.py:31
  7.2 9.2 %collective-permute-start.2 = (bf16[64,1536]{1,0:T(8,128)(2,1)}, bf16[64,1536]{1,0:T(8,128)(2,1)S(1)}, u32[]{:S(2)}, u32[]{:S(2)}) collective-permute-start(bf16[64,1536]{1,0:T(8,128)(2,1)} %param.4), channel_id=1, source_target_pairs={{0,8},{128,136},{8,0},{136,128},{1,9},{129,137},{9,1},{137,129},{2... | collective-permute-start | bytes 589832 | tf_op jit(solution)/shard_map/ppermute | solution.py:38
  11.2 8.5 %collective-permute-start.9 = (bf16[128,1536]{1,0:T(8,128)(2,1)S(1)}, bf16[128,1536]{1,0:T(8,128)(2,1)S(1)}, u32[]{:S(2)}, u32[]{:S(2)}) collective-permute-start(bf16[128,1536]{1,0:T(8,128)(2,1)S(1)} %fusion.2), channel_id=1, source_target_pairs={{0,16},{16,0},{1,17},{17,1},{2,18},{18,2},{3,19},{19,3},{4,20},{20... | collective-permute-start | bytes 1179656 | tf_op jit(solution)/shard_map/ppermute | solution.py:51
  12.5 14.4 %collective-permute-start.5 = (bf16[128,1536]{1,0:T(8,128)(2,1)S(1)}, bf16[128,1536]{1,0:T(8,128)(2,1)S(1)}, u32[]{:S(2)}, u32[]{:S(2)}) collective-permute-start(bf16[128,1536]{1,0:T(8,128)(2,1)S(1)} %fusion.2), channel_id=1, source_target_pairs={{0,64},{32,96},{64,0},{96,32},{1,65},{33,97},{65,1},{97,33},{2,66}... | collective-permute-start | bytes 1179656 | tf_op jit(solution)/shard_map/ppermute | solution.py:42
  16.5 10.4 %collective-permute-start.8 = (bf16[128,1536]{1,0:T(8,128)(2,1)S(1)}, bf16[128,1536]{1,0:T(8,128)(2,1)S(1)}, u32[]{:S(2)}, u32[]{:S(2)}) collective-permute-start(bf16[128,1536]{1,0:T(8,128)(2,1)S(1)} %fusion.2), channel_id=1, source_target_pairs={{0,128},{128,0},{1,129},{129,1},{2,130},{130,2},{3,131},{131,3},{4... | collective-permute-start | bytes 1179656 | tf_op jit(solution)/shard_map/ppermute | solution.py:51
  16.9 33.5 %slice-start = ((s8[4718592]{0:T(1024)(128)(4,1)}), s8[4194304]{0:T(1024)(128)(4,1)S(1)}, s32[]{:S(2)}) async-start(s8[4718592]{0:T(1024)(128)(4,1)} %bitcast), calls=%async_computation | async-start | bytes 8388608
  16.9 11.0 %collective-permute-start.3 = (bf16[128,1536]{1,0:T(8,128)(2,1)S(1)}, bf16[128,1536]{1,0:T(8,128)(2,1)S(1)}, u32[]{:S(2)}, u32[]{:S(2)}) collective-permute-start(bf16[128,1536]{1,0:T(8,128)(2,1)S(1)} %get-tuple-element.102), channel_id=1, source_target_pairs={{0,1},{1,2},{2,3},{3,4},{4,5},{5,6},{6,7},{7,0},{8,9},{9,10},{10,1... | collective-permute-start | bytes 1179656 | tf_op jit(solution)/shard_map/ppermute | solution.py:31
  17.0 11.0 %collective-permute-start.4 = (bf16[128,1536]{1,0:T(8,128)(2,1)S(1)}, bf16[128,1536]{1,0:T(8,128)(2,1)S(1)}, u32[]{:S(2)}, u32[]{:S(2)}) collective-permute-start(bf16[128,1536]{1,0:T(8,128)(2,1)S(1)} %get-tuple-element.101), channel_id=1, source_target_pairs={{0,7},{1,0},{2,1},{3,2},{4,3},{5,4},{6,5},{7,6},{8,15},{9,8},{10,9... | collective-permute-start | bytes 1179656 | tf_op jit(solution)/shard_map/ppermute | solution.py:31
  19.8 17.6 %collective-permute-start.10 = (bf16[192,1536]{1,0:T(8,128)(2,1)S(1)}, bf16[192,1536]{1,0:T(8,128)(2,1)S(1)}, u32[]{:S(2)}, u32[]{:S(2)}) collective-permute-start(bf16[192,1536]{1,0:T(8,128)(2,1)S(1)} %get-tuple-element.96), channel_id=1, source_target_pairs={{0,128},{128,8},{8,136},{136,0},{1,129},{129,9},{9,137},{137,1},{2... | collective-permute-start | bytes 1769480 | tf_op jit(solution)/shard_map/ppermute | solution.py:38
  26.9 13.6 %collective-permute-start.11 = (bf16[192,1536]{1,0:T(8,128)(2,1)S(1)}, bf16[192,1536]{1,0:T(8,128)(2,1)S(1)}, u32[]{:S(2)}, u32[]{:S(2)}) collective-permute-start(bf16[192,1536]{1,0:T(8,128)(2,1)S(1)} %get-tuple-element.96), channel_id=1, source_target_pairs={{0,136},{128,0},{8,128},{136,8},{1,137},{129,1},{9,129},{137,9},{2... | collective-permute-start | bytes 1769480 | tf_op jit(solution)/shard_map/ppermute | solution.py:38
  28.0 17.6 %collective-permute-start.6 = (bf16[128,1536]{1,0:T(8,128)(2,1)S(1)}, bf16[128,1536]{1,0:T(8,128)(2,1)S(1)}, u32[]{:S(2)}, u32[]{:S(2)}) collective-permute-start(bf16[128,1536]{1,0:T(8,128)(2,1)S(1)} %collective-permute-done.3), channel_id=1, source_target_pairs={{0,1},{1,2},{2,3},{3,4},{4,5},{5,6},{6,7},{7,0},{8,9},{9,10},{10,1... | collective-permute-start | bytes 1179656 | tf_op jit(solution)/shard_map/ppermute | solution.py:31
  28.0 17.6 %collective-permute-start.7 = (bf16[128,1536]{1,0:T(8,128)(2,1)S(1)}, bf16[128,1536]{1,0:T(8,128)(2,1)S(1)}, u32[]{:S(2)}, u32[]{:S(2)}) collective-permute-start(bf16[128,1536]{1,0:T(8,128)(2,1)S(1)} %collective-permute-done.4), channel_id=1, source_target_pairs={{0,7},{1,0},{2,1},{3,2},{4,3},{5,4},{6,5},{7,6},{8,15},{9,8},{10,9... | collective-permute-start | bytes 1179656 | tf_op jit(solution)/shard_map/ppermute | solution.py:31
  30.7 14.9 %collective-permute-start.13 = (bf16[256,1536]{1,0:T(8,128)(2,1)S(1)}, bf16[256,1536]{1,0:T(8,128)(2,1)S(1)}, u32[]{:S(2)}, u32[]{:S(2)}) collective-permute-start(bf16[256,1536]{1,0:T(8,128)(2,1)S(1)} %pad_maximum_fusion.refs_5_.refs_3_), channel_id=1, source_target_pairs={{0,32},{16,112},{32,64},{48,16},{64,96},{80,48},{96,0},{112,80},{1... | collective-permute-start | bytes 2359304 | tf_op jit(solution)/shard_map/ppermute | solution.py:47
  40.5 3.5 %collective-permute-start.12 = (bf16[128,1536]{1,0:T(8,128)(2,1)S(1)}, bf16[128,1536]{1,0:T(8,128)(2,1)S(1)}, u32[]{:S(2)}, u32[]{:S(2)}) collective-permute-start(bf16[128,1536]{1,0:T(8,128)(2,1)S(1)} %collective-permute-done.8), channel_id=1, source_target_pairs={{0,16},{16,0},{1,17},{17,1},{2,18},{18,2},{3,19},{19,3},{4,20},{20... | collective-permute-start | bytes 1179656 | tf_op jit(solution)/shard_map/ppermute | solution.py:51
  42.7 7.6 %slice-start.1 = ((s8[4718592]{0:T(1024)(128)(4,1)}), s8[524288]{0:T(1024)(128)(4,1)S(1)}, s32[]{:S(2)}) async-start(s8[4718592]{0:T(1024)(128)(4,1)} %bitcast), calls=%async_computation.1 | async-start | bytes 1048576
  42.7 14.1 %collective-permute-start.18 = (bf16[128,1536]{1,0:T(8,128)(2,1)S(1)}, bf16[128,1536]{1,0:T(8,128)(2,1)S(1)}, u32[]{:S(2)}, u32[]{:S(2)}) collective-permute-start(bf16[128,1536]{1,0:T(8,128)(2,1)S(1)} %pad_maximum_fusion.5), channel_id=1, source_target_pairs={{0,128},{128,8},{8,136},{136,0},{1,129},{129,9},{9,137},{137,1},{2... | collective-permute-start | bytes 1179656 | tf_op jit(solution)/shard_map/ppermute | solution.py:38
  44.0 14.0 %collective-permute-start.19 = (bf16[128,1536]{1,0:T(8,128)(2,1)S(1)}, bf16[128,1536]{1,0:T(8,128)(2,1)S(1)}, u32[]{:S(2)}, u32[]{:S(2)}) collective-permute-start(bf16[128,1536]{1,0:T(8,128)(2,1)S(1)} %pad_maximum_fusion.5), channel_id=1, source_target_pairs={{0,136},{128,0},{8,128},{136,8},{1,137},{129,1},{9,129},{137,9},{2... | collective-permute-start | bytes 1179656 | tf_op jit(solution)/shard_map/ppermute | solution.py:38
  45.6 9.5 %collective-permute-start.14 = (bf16[96,1536]{1,0:T(8,128)(2,1)S(1)}, bf16[96,1536]{1,0:T(8,128)(2,1)S(1)}, u32[]{:S(2)}, u32[]{:S(2)}) collective-permute-start(bf16[96,1536]{1,0:T(8,128)(2,1)S(1)} %slice.76), channel_id=1, source_target_pairs={{0,1},{1,2},{2,3},{3,4},{4,5},{5,6},{6,7},{7,0},{8,9},{9,10},{10,1... | collective-permute-start | bytes 884744 | tf_op jit(solution)/shard_map/ppermute | solution.py:31
  45.9 9.2 %collective-permute-start.15 = (bf16[96,1536]{1,0:T(8,128)(2,1)S(1)}, bf16[96,1536]{1,0:T(8,128)(2,1)S(1)}, u32[]{:S(2)}, u32[]{:S(2)}) collective-permute-start(bf16[96,1536]{1,0:T(8,128)(2,1)S(1)} %slice.77), channel_id=1, source_target_pairs={{0,7},{1,0},{2,1},{3,2},{4,3},{5,4},{6,5},{7,6},{8,15},{9,8},{10,9... | collective-permute-start | bytes 884744 | tf_op jit(solution)/shard_map/ppermute | solution.py:31
  48.8 12.3 %collective-permute-start.20 = (bf16[128,1536]{1,0:T(8,128)(2,1)S(1)}, bf16[128,1536]{1,0:T(8,128)(2,1)S(1)}, u32[]{:S(2)}, u32[]{:S(2)}) collective-permute-start(bf16[128,1536]{1,0:T(8,128)(2,1)S(1)} %collective-permute-done.8), channel_id=1, source_target_pairs={{0,64},{32,96},{64,0},{96,32},{1,65},{33,97},{65,1},{97,33},{2,66}... | collective-permute-start | bytes 1179656 | tf_op jit(solution)/shard_map/ppermute | solution.py:42
  55.2 3.8 %collective-permute-start.17 = (bf16[32,1536]{1,0:T(8,128)(2,1)S(1)}, bf16[32,1536]{1,0:T(8,128)(2,1)S(1)}, u32[]{:S(2)}, u32[]{:S(2)}) collective-permute-start(bf16[32,1536]{1,0:T(8,128)(2,1)S(1)} %get-tuple-element.94), channel_id=1, source_target_pairs={{0,7},{1,0},{2,1},{3,2},{4,3},{5,4},{6,5},{7,6},{8,15},{9,8},{10,9... | collective-permute-start | bytes 294920 | tf_op jit(solution)/shard_map/ppermute | solution.py:31
  56.1 5.0 %collective-permute-start.16 = (bf16[32,1536]{1,0:T(8,128)(2,1)S(1)}, bf16[32,1536]{1,0:T(8,128)(2,1)S(1)}, u32[]{:S(2)}, u32[]{:S(2)}) collective-permute-start(bf16[32,1536]{1,0:T(8,128)(2,1)S(1)} %get-tuple-element.91), channel_id=1, source_target_pairs={{0,1},{1,2},{2,3},{3,4},{4,5},{5,6},{6,7},{7,0},{8,9},{9,10},{10,1... | collective-permute-start | bytes 294920 | tf_op jit(solution)/shard_map/ppermute | solution.py:31
  56.8 11.9 %collective-permute-start.21 = (bf16[256,1536]{1,0:T(8,128)(2,1)S(1)}, bf16[256,1536]{1,0:T(8,128)(2,1)S(1)}, u32[]{:S(2)}, u32[]{:S(2)}) collective-permute-start(bf16[256,1536]{1,0:T(8,128)(2,1)S(1)} %pad_maximum_fusion.1.refs_6_.refs_4_), channel_id=1, source_target_pairs={{0,32},{16,112},{32,64},{48,16},{64,96},{80,48},{96,0},{112,80},{1... | collective-permute-start | bytes 2359304 | tf_op jit(solution)/shard_map/ppermute | solution.py:47
  68.8 12.2 %collective-permute-start.28 = (bf16[768,1536]{1,0:T(8,128)(2,1)S(1)}, bf16[768,1536]{1,0:T(8,128)(2,1)S(1)}, u32[]{:S(2)}, u32[]{:S(2)}) collective-permute-start(bf16[768,1536]{1,0:T(8,128)(2,1)S(1)} %constant_dynamic-update-slice_fusion.15.refs_7_.refs_5_), channel_id=1, source_target_pairs={{0,16},{16,0},{1,17},{17,1},{2,18},{18,2},{3,19},{19,3},{4,20},{20... | collective-permute-start | bytes 7077896 | tf_op jit(solution)/shard_map/ppermute | solution.py:51
  74.0 6.4 %collective-permute-start.22 = (bf16[512,1536]{1,0:T(8,128)(2,1)S(1)}, bf16[512,1536]{1,0:T(8,128)(2,1)S(1)}, u32[]{:S(2)}, u32[]{:S(2)}) collective-permute-start(bf16[512,1536]{1,0:T(8,128)(2,1)S(1)} %get-tuple-element.64), channel_id=1, source_target_pairs={{0,16},{16,0},{1,17},{17,1},{2,18},{18,2},{3,19},{19,3},{4,20},{20... | collective-permute-start | bytes 4718600 | tf_op jit(solution)/shard_map/ppermute | solution.py:51
  74.2 19.2 %collective-permute-start.26 = (bf16[192,1536]{1,0:T(8,128)(2,1)S(1)}, bf16[192,1536]{1,0:T(8,128)(2,1)S(1)}, u32[]{:S(2)}, u32[]{:S(2)}) collective-permute-start(bf16[192,1536]{1,0:T(8,128)(2,1)S(1)} %pad_maximum_fusion.2), channel_id=1, source_target_pairs={{0,128},{128,8},{8,136},{136,0},{1,129},{129,9},{9,137},{137,1},{2... | collective-permute-start | bytes 1769480 | tf_op jit(solution)/shard_map/ppermute | solution.py:38
  74.3 19.1 %collective-permute-start.27 = (bf16[192,1536]{1,0:T(8,128)(2,1)S(1)}, bf16[192,1536]{1,0:T(8,128)(2,1)S(1)}, u32[]{:S(2)}, u32[]{:S(2)}) collective-permute-start(bf16[192,1536]{1,0:T(8,128)(2,1)S(1)} %pad_maximum_fusion.2), channel_id=1, source_target_pairs={{0,136},{128,0},{8,128},{136,8},{1,137},{129,1},{9,129},{137,9},{2... | collective-permute-start | bytes 1769480 | tf_op jit(solution)/shard_map/ppermute | solution.py:38
  80.8 18.1 %collective-permute-start.23 = (bf16[128,1536]{1,0:T(8,128)(2,1)S(1)}, bf16[128,1536]{1,0:T(8,128)(2,1)S(1)}, u32[]{:S(2)}, u32[]{:S(2)}) collective-permute-start(bf16[128,1536]{1,0:T(8,128)(2,1)S(1)} %get-tuple-element.80), channel_id=1, source_target_pairs={{0,64},{32,96},{64,0},{96,32},{1,65},{33,97},{65,1},{97,33},{2,66}... | collective-permute-start | bytes 1179656 | tf_op jit(solution)/shard_map/ppermute | solution.py:42
  80.9 20.5 %collective-permute-start.24 = (bf16[128,1536]{1,0:T(8,128)(2,1)S(1)}, bf16[128,1536]{1,0:T(8,128)(2,1)S(1)}, u32[]{:S(2)}, u32[]{:S(2)}) collective-permute-start(bf16[128,1536]{1,0:T(8,128)(2,1)S(1)} %get-tuple-element.79), channel_id=1, source_target_pairs={{0,32},{32,64},{64,96},{96,0},{1,33},{33,65},{65,97},{97,1},{2,34}... | collective-permute-start | bytes 1179656 | tf_op jit(solution)/shard_map/ppermute | solution.py:42
  81.0 20.4 %collective-permute-start.25 = (bf16[128,1536]{1,0:T(8,128)(2,1)S(1)}, bf16[128,1536]{1,0:T(8,128)(2,1)S(1)}, u32[]{:S(2)}, u32[]{:S(2)}) collective-permute-start(bf16[128,1536]{1,0:T(8,128)(2,1)S(1)} %get-tuple-element.78), channel_id=1, source_target_pairs={{0,96},{32,0},{64,32},{96,64},{1,97},{33,1},{65,33},{97,65},{2,98}... | collective-permute-start | bytes 1179656 | tf_op jit(solution)/shard_map/ppermute | solution.py:42
  93.4 8.1 %copy-start = (bf16[128,1536]{1,0:T(8,128)(2,1)S(1)}, bf16[128,1536]{1,0:T(8,128)(2,1)}, u32[]{:S(2)}) copy-start(bf16[128,1536]{1,0:T(8,128)(2,1)} %param.3) | copy-start | bytes 1179652

commit v10 on v9

--- a/solution.py
+++ b/solution.py
@@ -201,21 +201,19 @@
     near = jnp.concatenate([g, up1, down1])
     left_a, right_a = along_x(near, 1), along_x(near, -1)
     other_rep, chip = tie(other_rep, chip)
-    hop_1 = round_y(chip)
     up2, down2, hop_2 = tie(up2, down2, hop_2)
 
     up3, down3 = along_z(up2, 1), along_z(down2, -1)
+    hop_4 = along_y(other_rep, 2)
     other_rep, left_a, right_a = tie(other_rep, left_a, right_a)
     other_chip = jnp.concatenate([other_rep, swap(other_rep, "c")])
-    up3, down3, left_a, right_a, other_rep, other_chip, hop_1 = tie(
-        up3, down3, left_a, right_a, other_rep, other_chip, hop_1
-    )
+    up3, down3, left_a, right_a, other_chip, hop_4 = tie(up3, down3, left_a, right_a, other_chip, hop_4)
 
     up4, down4 = along_z(up3[:96], 1), along_z(down3[32:], -1)
     middle = jnp.concatenate([up2[64:], down2[:64]])
     left_b, right_b = along_x(middle, 1), along_x(middle, -1)
-    hop_4 = along_y(other_rep, 2)
-    up4, down4, other_chip = tie(up4, down4, other_chip)
+    hops = round_y(jnp.concatenate([chip, other_chip]))
+    up4, down4 = tie(up4, down4)
     own = [g, up1, down1, up2[64:], down2[:64], up3[64:], down3[:64]]
     second = [far, up2[:64], down2[64:], up3[:64], down3[64:]]
     grads_early = jnp.concatenate(own + second)
@@ -223,14 +221,14 @@
 
     up5, down5 = along_z(up4[:32], 1), along_z(down4[64:], -1)
     last = jnp.concatenate([up4[64:], down4[:32]])
-    hop_3 = round_y(other_chip)
-    up5, down5, early, left_b, right_b, hop_4 = tie(up5, down5, early, left_b, right_b, hop_4)
+    up5, down5, early, left_b, right_b = tie(up5, down5, early, left_b, right_b)
 
     grads_late = jnp.concatenate([last, up4[:64], down4[32:], up5, down5])
     mine, other = late_partial(early, grads_late, down_weight)
-    mine, other, hop_3, last = tie(mine, other, hop_3, last)
+    mine, other, hops, last = tie(mine, other, hops, last)
     other = swap(other, "c")
-    came = jnp.concatenate([hop_1, hop_2, hop_3, hop_4])
+    other, hops = tie(other, hops)
+    came = jnp.concatenate([hops[:256], hop_2, hops[256:], hop_4])
     swapped = swap(came, "c")
     third = jnp.concatenate([up3[64:], down3[:64], last])
     left_c, right_c = along_x(third, 1), along_x(third, -1)

time: 103 us -> 101 us (0.981)
  starting transfers between devices: 42.9 us -> 40.9 us
    ppermute x10, waiting for transfers between devices: 4.13 us -> 6.1 us  [along_z(): return lax.ppermute(a, 'z', [(i, (i + d) % Z) for i in range(Z)])]
    ppermute x2 -> x1, waiting for transfers between devices: 5.59 us -> 3.86 us  [round_y(): lax.ppermute(a, ('y', 'c'), [(s[0] * C + s[1], t[0] * C + t[1]) for s, t...]
    ppermute x5, starting transfers between devices: 9.15 us -> 7.48 us  [swap(): return lax.ppermute(a, axis, [(0, 1), (1, 0)])]
  transfers between devices with their start and end apart: 29 -> 28, of which waited for: 10 -> 13; matrix products, arithmetic and copies ran while one was open for 3% -> 3% of each run, Pallas kernels for 21% -> 22%
where the time goes in v10:
time: 101 us
  starting transfers between devices  40.9 us (40%)
  waiting for transfers between devices  32.3 us (32%)
  Pallas kernels  21.9 us (22%)
  other arithmetic  3.59 us (4%)
  local copies, waits for them, and re-layouts  1.44 us (1%)
    ppermute x10, starting transfers between devices, along_z(): return lax.ppermute(a, 'z', [(i, (i + d) % Z) for i in range(Z)])  17.5 us
    pallas_call x2, Pallas kernels, weight_product(): pl.pallas_call(functools.partial(weight_kernel, layout), grid=(1536 // st...  15.1 us
    ppermute x5, waiting for transfers between devices, swap(): return lax.ppermute(a, axis, [(0, 1), (1, 0)])  10.4 us
    ppermute x7, waiting for transfers between devices, along_x(): lax.ppermute(a, ('xl', 'xh'), [(place(x), place((x + d) % 4)) for x in ra...  9.39 us
    ppermute x7, starting transfers between devices, along_x(): lax.ppermute(a, ('xl', 'xh'), [(place(x), place((x + d) % 4)) for x in ra...  8.34 us
    ppermute x5, starting transfers between devices, swap(): return lax.ppermute(a, axis, [(0, 1), (1, 0)])  7.48 us
    ppermute x5, starting transfers between devices, along_y(): return lax.ppermute(a, 'y', [(i, (i + d) % Y) for i in range(Y)])  6.31 us
    ppermute x10, waiting for transfers between devices, along_z(): return lax.ppermute(a, 'z', [(i, (i + d) % Z) for i in range(Z)])  6.1 us
  transfers between devices with their start and end apart: 28, of which 13 were waited for; matrix products, arithmetic and copies ran while one was open for 3% of the time, Pallas kernels for 22%

profile of v10, /device:TPU:1, one launch (start us, length us, event | category | flops | bytes accessed | tf_op | source)
XLA Modules:
  0.0 101.1 jit_solution(3216579554634865154)
XLA Ops:
  0.6 2.5 %collective-permute-start = (bf16[64,1536]{1,0:T(8,128)(2,1)}, bf16[64,1536]{1,0:T(8,128)(2,1)S(1)}, u32[]{:S(2)}, u32[]{:S(2)}) collective-permute-start(bf16[64,1536]{1,0:T(8,128)(2,1)} %param.4), channel_id=1, source_target_pairs={{0,1},{1,2},{2,3},{3,4},{4,5},{5,6},{6,7},{7,0},{8,9},{9,10},{10,1... | collective-permute-start | bytes 589832 | tf_op jit(solution)/shard_map/ppermute | solution.py:31
  3.2 4.0 %collective-permute-start.1 = (bf16[64,1536]{1,0:T(8,128)(2,1)}, bf16[64,1536]{1,0:T(8,128)(2,1)S(1)}, u32[]{:S(2)}, u32[]{:S(2)}) collective-permute-start(bf16[64,1536]{1,0:T(8,128)(2,1)} %param.4), channel_id=1, source_target_pairs={{0,7},{1,0},{2,1},{3,2},{4,3},{5,4},{6,5},{7,6},{8,15},{9,8},{10,9... | collective-permute-start | bytes 589832 | tf_op jit(solution)/shard_map/ppermute | solution.py:31
  7.2 2.7 %collective-permute-start.2 = (bf16[64,1536]{1,0:T(8,128)(2,1)}, bf16[64,1536]{1,0:T(8,128)(2,1)S(1)}, u32[]{:S(2)}, u32[]{:S(2)}) collective-permute-start(bf16[64,1536]{1,0:T(8,128)(2,1)} %param.4), channel_id=1, source_target_pairs={{0,8},{128,136},{8,0},{136,128},{1,9},{129,137},{9,1},{137,129},{2... | collective-permute-start | bytes 589832 | tf_op jit(solution)/shard_map/ppermute | solution.py:38
  9.9 1.3 %fusion.2 = bf16[128,1536]{1,0:T(8,128)(2,1)S(1)} fusion(bf16[128,1536]{1,0:T(8,128)(2,1)} %param.3), kind=kLoop, calls=%fused_computation.11 | loop fusion | flops 1966080 | bytes 786432 | tf_op jit(solution)/shard_map/convert_element_type | solution.py:190
  11.2 1.3 %collective-permute-start.9 = (bf16[128,1536]{1,0:T(8,128)(2,1)S(1)}, bf16[128,1536]{1,0:T(8,128)(2,1)S(1)}, u32[]{:S(2)}, u32[]{:S(2)}) collective-permute-start(bf16[128,1536]{1,0:T(8,128)(2,1)S(1)} %fusion.2), channel_id=1, source_target_pairs={{0,16},{16,0},{1,17},{17,1},{2,18},{18,2},{3,19},{19,3},{4,20},{20... | collective-permute-start | bytes 1179656 | tf_op jit(solution)/shard_map/ppermute | solution.py:51
  12.5 2.9 %collective-permute-start.5 = (bf16[128,1536]{1,0:T(8,128)(2,1)S(1)}, bf16[128,1536]{1,0:T(8,128)(2,1)S(1)}, u32[]{:S(2)}, u32[]{:S(2)}) collective-permute-start(bf16[128,1536]{1,0:T(8,128)(2,1)S(1)} %fusion.2), channel_id=1, source_target_pairs={{0,64},{32,96},{64,0},{96,32},{1,65},{33,97},{65,1},{97,33},{2,66}... | collective-permute-start | bytes 1179656 | tf_op jit(solution)/shard_map/ppermute | solution.py:42
  17.0 2.7 %collective-permute-start.4 = (bf16[128,1536]{1,0:T(8,128)(2,1)S(1)}, bf16[128,1536]{1,0:T(8,128)(2,1)S(1)}, u32[]{:S(2)}, u32[]{:S(2)}) collective-permute-start(bf16[128,1536]{1,0:T(8,128)(2,1)S(1)} %get-tuple-element.101), channel_id=1, source_target_pairs={{0,7},{1,0},{2,1},{3,2},{4,3},{5,4},{6,5},{7,6},{8,15},{9,8},{10,9... | collective-permute-start | bytes 1179656 | tf_op jit(solution)/shard_map/ppermute | solution.py:31
  19.8 1.2 %collective-permute-start.10 = (bf16[192,1536]{1,0:T(8,128)(2,1)S(1)}, bf16[192,1536]{1,0:T(8,128)(2,1)S(1)}, u32[]{:S(2)}, u32[]{:S(2)}) collective-permute-start(bf16[192,1536]{1,0:T(8,128)(2,1)S(1)} %get-tuple-element.96), channel_id=1, source_target_pairs={{0,128},{128,8},{8,136},{136,0},{1,129},{129,9},{9,137},{137,1},{2... | collective-permute-start | bytes 1769480 | tf_op jit(solution)/shard_map/ppermute | solution.py:38
  21.0 5.9 %collective-permute-done.8 = bf16[128,1536]{1,0:T(8,128)(2,1)S(1)} collective-permute-done((bf16[128,1536]{1,0:T(8,128)(2,1)S(1)}, bf16[128,1536]{1,0:T(8,128)(2,1)S(1)}, u32[]{:S(2)}, u32[]{:S(2)}) %collective-permute-start.8) | collective-permute-done | bytes 393248 | tf_op jit(solution)/shard_map/ppermute | solution.py:51
  27.0 1.0 %collective-permute-done.3 = bf16[128,1536]{1,0:T(8,128)(2,1)S(1)} collective-permute-done((bf16[128,1536]{1,0:T(8,128)(2,1)S(1)}, bf16[128,1536]{1,0:T(8,128)(2,1)S(1)}, u32[]{:S(2)}, u32[]{:S(2)}) %collective-permute-start.3) | collective-permute-done | bytes 393248 | tf_op jit(solution)/shard_map/ppermute | solution.py:31
  28.0 2.7 %collective-permute-start.7 = (bf16[128,1536]{1,0:T(8,128)(2,1)S(1)}, bf16[128,1536]{1,0:T(8,128)(2,1)S(1)}, u32[]{:S(2)}, u32[]{:S(2)}) collective-permute-start(bf16[128,1536]{1,0:T(8,128)(2,1)S(1)} %collective-permute-done.4), channel_id=1, source_target_pairs={{0,7},{1,0},{2,1},{3,2},{4,3},{5,4},{6,5},{7,6},{8,15},{9,8},{10,9... | collective-permute-start | bytes 1179656 | tf_op jit(solution)/shard_map/ppermute | solution.py:31
  31.4 6.0 %collective-permute-done.10.refs_2_ = bf16[192,1536]{1,0:T(8,128)(2,1)S(1)} collective-permute-done((bf16[192,1536]{1,0:T(8,128)(2,1)S(1)}, bf16[192,1536]{1,0:T(8,128)(2,1)S(1)}, u32[]{:S(2)}, u32[]{:S(2)}) %collective-permute-start.10) | collective-permute-done | bytes 589856 | tf_op jit(solution)/shard_map/ppermute | solution.py:38
  37.4 3.1 %collective-permute-done.11.refs_3_ = bf16[192,1536]{1,0:T(8,128)(2,1)S(1)} collective-permute-done((bf16[192,1536]{1,0:T(8,128)(2,1)S(1)}, bf16[192,1536]{1,0:T(8,128)(2,1)S(1)}, u32[]{:S(2)}, u32[]{:S(2)}) %collective-permute-start.11) | collective-permute-done | bytes 589856 | tf_op jit(solution)/shard_map/ppermute | solution.py:38
  40.5 2.1 %collective-permute-start.12 = (bf16[128,1536]{1,0:T(8,128)(2,1)S(1)}, bf16[128,1536]{1,0:T(8,128)(2,1)S(1)}, u32[]{:S(2)}, u32[]{:S(2)}) collective-permute-start(bf16[128,1536]{1,0:T(8,128)(2,1)S(1)} %collective-permute-done.8), channel_id=1, source_target_pairs={{0,16},{16,0},{1,17},{17,1},{2,18},{18,2},{3,19},{19,3},{4,20},{20... | collective-permute-start | bytes 1179656 | tf_op jit(solution)/shard_map/ppermute | solution.py:51
  42.8 1.1 %collective-permute-done.12 = bf16[128,1536]{1,0:T(8,128)(2,1)S(1)} collective-permute-done((bf16[128,1536]{1,0:T(8,128)(2,1)S(1)}, bf16[128,1536]{1,0:T(8,128)(2,1)S(1)}, u32[]{:S(2)}, u32[]{:S(2)}) %collective-permute-start.12) | collective-permute-done | bytes 393248 | tf_op jit(solution)/shard_map/ppermute | solution.py:51
  44.0 1.5 %collective-permute-start.19 = (bf16[128,1536]{1,0:T(8,128)(2,1)S(1)}, bf16[128,1536]{1,0:T(8,128)(2,1)S(1)}, u32[]{:S(2)}, u32[]{:S(2)}) collective-permute-start(bf16[128,1536]{1,0:T(8,128)(2,1)S(1)} %pad_maximum_fusion.7), channel_id=1, source_target_pairs={{0,136},{128,0},{8,128},{136,8},{1,137},{129,1},{9,129},{137,9},{2... | collective-permute-start | bytes 1179656 | tf_op jit(solution)/shard_map/ppermute | solution.py:38
  45.9 2.7 %collective-permute-start.15 = (bf16[96,1536]{1,0:T(8,128)(2,1)S(1)}, bf16[96,1536]{1,0:T(8,128)(2,1)S(1)}, u32[]{:S(2)}, u32[]{:S(2)}) collective-permute-start(bf16[96,1536]{1,0:T(8,128)(2,1)S(1)} %slice.83), channel_id=1, source_target_pairs={{0,7},{1,0},{2,1},{3,2},{4,3},{5,4},{6,5},{7,6},{8,15},{9,8},{10,9... | collective-permute-start | bytes 884744 | tf_op jit(solution)/shard_map/ppermute | solution.py:31
  48.9 1.2 %collective-permute-start.20 = (bf16[512,1536]{1,0:T(8,128)(2,1)S(1)}, bf16[512,1536]{1,0:T(8,128)(2,1)S(1)}, u32[]{:S(2)}, u32[]{:S(2)}) collective-permute-start(bf16[512,1536]{1,0:T(8,128)(2,1)S(1)} %pad_maximum_fusion.1), channel_id=1, source_target_pairs={{0,32},{16,112},{32,64},{48,16},{64,96},{80,48},{96,0},{112,80},{1... | collective-permute-start | bytes 4718600 | tf_op jit(solution)/shard_map/ppermute | solution.py:47
  50.2 4.8 %shard_map.50.early_ref = f32[768,1536]{1,0:T(8,128)S(1)} custom-call(bf16[768,1536]{1,0:T(8,128)(2,1)S(1)} %slice_dynamic-update-slice_fusion.2.grads_ref.refs_0_, bf16[1536,1536]{1,0:T(8,128)(2,1)S(1)} %bitcast.1), custom_call_target="tpu_custom_call" | custom-call | flops 3623878656 | bytes 12582912 | tf_op jit(solution)/shard_map/pallas_call | solution.py:73
  55.2 2.5 %collective-permute-start.17 = (bf16[32,1536]{1,0:T(8,128)(2,1)S(1)}, bf16[32,1536]{1,0:T(8,128)(2,1)S(1)}, u32[]{:S(2)}, u32[]{:S(2)}) collective-permute-start(bf16[32,1536]{1,0:T(8,128)(2,1)S(1)} %get-tuple-element.94), channel_id=1, source_target_pairs={{0,7},{1,0},{2,1},{3,2},{4,3},{5,4},{6,5},{7,6},{8,15},{9,8},{10,9... | collective-permute-start | bytes 294920 | tf_op jit(solution)/shard_map/ppermute | solution.py:31
  57.7 1.6 %collective-permute-done.17 = bf16[32,1536]{1,0:T(8,128)(2,1)S(1)} collective-permute-done((bf16[32,1536]{1,0:T(8,128)(2,1)S(1)}, bf16[32,1536]{1,0:T(8,128)(2,1)S(1)}, u32[]{:S(2)}, u32[]{:S(2)}) %collective-permute-start.17) | collective-permute-done | bytes 98336 | tf_op jit(solution)/shard_map/ppermute | solution.py:31
  59.3 3.3 %collective-permute-done.16 = bf16[32,1536]{1,0:T(8,128)(2,1)S(1)} collective-permute-done((bf16[32,1536]{1,0:T(8,128)(2,1)S(1)}, bf16[32,1536]{1,0:T(8,128)(2,1)S(1)}, u32[]{:S(2)}, u32[]{:S(2)}) %collective-permute-start.16) | collective-permute-done | bytes 98336 | tf_op jit(solution)/shard_map/ppermute | solution.py:31
  62.7 2.0 %shard_map.51 = (f32[512,1536]{1,0:T(8,128)S(1)}, bf16[512,1536]{1,0:T(8,128)(2,1)S(1)}) custom-call(f32[768,1536]{1,0:T(8,128)S(1)} %shard_map.50.early_ref, bf16[256,1536]{1,0:T(8,128)(2,1)S(1)} %constant_dynamic-update-slice_fusion.11.grads_ref.refs_1_, bf16[1536,1536]{1,0:T(8,128)(2,1)S(1)} %bitcast.1), custom_call_target="tpu_custom_call" | custom-call | flops 1207959552 | bytes 8388608 | tf_op jit(solution)/shard_map/pallas_call | solution.py:111
  64.7 3.9 %collective-permute-done.20 = bf16[512,1536]{1,0:T(8,128)(2,1)S(1)} collective-permute-done((bf16[512,1536]{1,0:T(8,128)(2,1)S(1)}, bf16[512,1536]{1,0:T(8,128)(2,1)S(1)}, u32[]{:S(2)}, u32[]{:S(2)}) %collective-permute-start.20) | collective-permute-done | bytes 1572896 | tf_op jit(solution)/shard_map/ppermute | solution.py:47
  68.6 3.2 %collective-permute-start.21 = (bf16[512,1536]{1,0:T(8,128)(2,1)S(1)}, bf16[512,1536]{1,0:T(8,128)(2,1)S(1)}, u32[]{:S(2)}, u32[]{:S(2)}) collective-permute-start(bf16[512,1536]{1,0:T(8,128)(2,1)S(1)} %get-tuple-element.61), channel_id=1, source_target_pairs={{0,16},{16,0},{1,17},{17,1},{2,18},{18,2},{3,19},{19,3},{4,20},{20... | collective-permute-start | bytes 4718600 | tf_op jit(solution)/shard_map/ppermute | solution.py:51
  71.7 3.0 %collective-permute-done.21 = bf16[512,1536]{1,0:T(8,128)(2,1)S(1)} collective-permute-done((bf16[512,1536]{1,0:T(8,128)(2,1)S(1)}, bf16[512,1536]{1,0:T(8,128)(2,1)S(1)}, u32[]{:S(2)}, u32[]{:S(2)}) %collective-permute-start.21) | collective-permute-done | bytes 1572896 | tf_op jit(solution)/shard_map/ppermute | solution.py:51
  75.7 2.6 %collective-permute-start.26 = (bf16[192,1536]{1,0:T(8,128)(2,1)S(1)}, bf16[192,1536]{1,0:T(8,128)(2,1)S(1)}, u32[]{:S(2)}, u32[]{:S(2)}) collective-permute-start(bf16[192,1536]{1,0:T(8,128)(2,1)S(1)} %pad_maximum_fusion.4), channel_id=1, source_target_pairs={{0,136},{128,0},{8,128},{136,8},{1,137},{129,1},{9,129},{137,9},{2... | collective-permute-start | bytes 1769480 | tf_op jit(solution)/shard_map/ppermute | solution.py:38
  79.7 2.0 %collective-permute-start.24 = (bf16[128,1536]{1,0:T(8,128)(2,1)S(1)}, bf16[128,1536]{1,0:T(8,128)(2,1)S(1)}, u32[]{:S(2)}, u32[]{:S(2)}) collective-permute-start(bf16[128,1536]{1,0:T(8,128)(2,1)S(1)} %get-tuple-element.76), channel_id=1, source_target_pairs={{0,96},{32,0},{64,32},{96,64},{1,97},{33,1},{65,33},{97,65},{2,98}... | collective-permute-start | bytes 1179656 | tf_op jit(solution)/shard_map/ppermute | solution.py:42
  81.6 9.7 %shard_map.52.refs_7_ = f32[1536,1536]{1,0:T(8,128)S(1)} custom-call(bf16[768,1536]{1,0:T(8,128)(2,1)S(1)} %slice_dynamic-update-slice_fusion.2.grads_ref.refs_0_, bf16[256,1536]{1,0:T(8,128)(2,1)S(1)} %constant_dynamic-update-slice_fusion.11.grads_ref.refs_1_, bf16[192,1536]{1,0:T(8,128)(2,1)S(1)} %collective-permute-done.10.refs_2_, ...), custom_call_target="tpu_custom_call" | custom-call | flops 7247757312 | bytes 12582912 | tf_op jit(solution)/shard_map/pallas_call | solution.py:175
  91.6 5.4 %shard_map.53 = bf16[1536,1536]{1,0:T(8,128)(2,1)} custom-call(bf16[128,1536]{1,0:T(8,128)(2,1)S(1)} %collective-permute-done.19.refs_0_, bf16[192,1536]{1,0:T(8,128)(2,1)S(1)} %collective-permute-done.25.refs_1_, bf16[192,1536]{1,0:T(8,128)(2,1)S(1)} %collective-permute-done.26.refs_2_, bf16[256,1536]{1,0:T(8,128)(2,1)S(1)} %pad_maximum_fusion.2.refs_5_.refs_3_, ...), custom_call_target="tpu_custom_call" | custom-call | flops 2415919104 | bytes 12582912 | tf_op jit(solution)/shard_map/pallas_call | solution.py:175
  97.1 2.5 %collective-permute-done.23 = bf16[128,1536]{1,0:T(8,128)(2,1)S(1)} collective-permute-done((bf16[128,1536]{1,0:T(8,128)(2,1)S(1)}, bf16[128,1536]{1,0:T(8,128)(2,1)S(1)}, u32[]{:S(2)}, u32[]{:S(2)}) %collective-permute-start.23) | collective-permute-done | bytes 393248 | tf_op jit(solution)/shard_map/ppermute | solution.py:42
  99.6 1.5 %fusion.7 = bf16[128,1536]{1,0:T(8,128)(2,1)} fusion(bf16[128,1536]{1,0:T(8,128)(2,1)S(1)} %copy-done, bf16[128,1536]{1,0:T(8,128)(2,1)S(1)} %collective-permute-done.22, bf16[128,1536]{1,0:T(8,128)(2,1)S(1)} %collective-permute-done.24, bf16[128,1536]{1,0:T(8,128)(2,1)S(1)} %collective-permute-done.23, f32[512,1536]{1,0:T(8,128)S(1)} %get-tuple-element.60, ...), kind=kLoop, calls=%fused_computation.16 | loop fusion | flops 5505024 | bytes 3145728 | tf_op jit(solution)/shard_map/convert_element_type | solution.py:248
  (67 shorter events, 5.9 us)
Async XLA Ops:
  0.6 15.8 %collective-permute-start = (bf16[64,1536]{1,0:T(8,128)(2,1)}, bf16[64,1536]{1,0:T(8,128)(2,1)S(1)}, u32[]{:S(2)}, u32[]{:S(2)}) collective-permute-start(bf16[64,1536]{1,0:T(8,128)(2,1)} %param.4), channel_id=1, source_target_pairs={{0,1},{1,2},{2,3},{3,4},{4,5},{5,6},{6,7},{7,0},{8,9},{9,10},{10,1... | collective-permute-start | bytes 589832 | tf_op jit(solution)/shard_map/ppermute | solution.py:31
  3.2 13.3 %collective-permute-start.1 = (bf16[64,1536]{1,0:T(8,128)(2,1)}, bf16[64,1536]{1,0:T(8,128)(2,1)S(1)}, u32[]{:S(2)}, u32[]{:S(2)}) collective-permute-start(bf16[64,1536]{1,0:T(8,128)(2,1)} %param.4), channel_id=1, source_target_pairs={{0,7},{1,0},{2,1},{3,2},{4,3},{5,4},{6,5},{7,6},{8,15},{9,8},{10,9... | collective-permute-start | bytes 589832 | tf_op jit(solution)/shard_map/ppermute | solution.py:31
  7.2 9.2 %collective-permute-start.2 = (bf16[64,1536]{1,0:T(8,128)(2,1)}, bf16[64,1536]{1,0:T(8,128)(2,1)S(1)}, u32[]{:S(2)}, u32[]{:S(2)}) collective-permute-start(bf16[64,1536]{1,0:T(8,128)(2,1)} %param.4), channel_id=1, source_target_pairs={{0,8},{128,136},{8,0},{136,128},{1,9},{129,137},{9,1},{137,129},{2... | collective-permute-start | bytes 589832 | tf_op jit(solution)/shard_map/ppermute | solution.py:38
  11.2 8.5 %collective-permute-start.9 = (bf16[128,1536]{1,0:T(8,128)(2,1)S(1)}, bf16[128,1536]{1,0:T(8,128)(2,1)S(1)}, u32[]{:S(2)}, u32[]{:S(2)}) collective-permute-start(bf16[128,1536]{1,0:T(8,128)(2,1)S(1)} %fusion.2), channel_id=1, source_target_pairs={{0,16},{16,0},{1,17},{17,1},{2,18},{18,2},{3,19},{19,3},{4,20},{20... | collective-permute-start | bytes 1179656 | tf_op jit(solution)/shard_map/ppermute | solution.py:51
  12.5 14.4 %collective-permute-start.5 = (bf16[128,1536]{1,0:T(8,128)(2,1)S(1)}, bf16[128,1536]{1,0:T(8,128)(2,1)S(1)}, u32[]{:S(2)}, u32[]{:S(2)}) collective-permute-start(bf16[128,1536]{1,0:T(8,128)(2,1)S(1)} %fusion.2), channel_id=1, source_target_pairs={{0,64},{32,96},{64,0},{96,32},{1,65},{33,97},{65,1},{97,33},{2,66}... | collective-permute-start | bytes 1179656 | tf_op jit(solution)/shard_map/ppermute | solution.py:42
  16.5 10.4 %collective-permute-start.8 = (bf16[128,1536]{1,0:T(8,128)(2,1)S(1)}, bf16[128,1536]{1,0:T(8,128)(2,1)S(1)}, u32[]{:S(2)}, u32[]{:S(2)}) collective-permute-start(bf16[128,1536]{1,0:T(8,128)(2,1)S(1)} %fusion.2), channel_id=1, source_target_pairs={{0,128},{128,0},{1,129},{129,1},{2,130},{130,2},{3,131},{131,3},{4... | collective-permute-start | bytes 1179656 | tf_op jit(solution)/shard_map/ppermute | solution.py:51
  16.9 33.3 %slice-start = ((s8[4718592]{0:T(1024)(128)(4,1)}), s8[4194304]{0:T(1024)(128)(4,1)S(1)}, s32[]{:S(2)}) async-start(s8[4718592]{0:T(1024)(128)(4,1)} %bitcast), calls=%async_computation | async-start | bytes 8388608
  16.9 11.0 %collective-permute-start.3 = (bf16[128,1536]{1,0:T(8,128)(2,1)S(1)}, bf16[128,1536]{1,0:T(8,128)(2,1)S(1)}, u32[]{:S(2)}, u32[]{:S(2)}) collective-permute-start(bf16[128,1536]{1,0:T(8,128)(2,1)S(1)} %get-tuple-element.102), channel_id=1, source_target_pairs={{0,1},{1,2},{2,3},{3,4},{4,5},{5,6},{6,7},{7,0},{8,9},{9,10},{10,1... | collective-permute-start | bytes 1179656 | tf_op jit(solution)/shard_map/ppermute | solution.py:31
  17.0 11.0 %collective-permute-start.4 = (bf16[128,1536]{1,0:T(8,128)(2,1)S(1)}, bf16[128,1536]{1,0:T(8,128)(2,1)S(1)}, u32[]{:S(2)}, u32[]{:S(2)}) collective-permute-start(bf16[128,1536]{1,0:T(8,128)(2,1)S(1)} %get-tuple-element.101), channel_id=1, source_target_pairs={{0,7},{1,0},{2,1},{3,2},{4,3},{5,4},{6,5},{7,6},{8,15},{9,8},{10,9... | collective-permute-start | bytes 1179656 | tf_op jit(solution)/shard_map/ppermute | solution.py:31
  19.8 17.6 %collective-permute-start.10 = (bf16[192,1536]{1,0:T(8,128)(2,1)S(1)}, bf16[192,1536]{1,0:T(8,128)(2,1)S(1)}, u32[]{:S(2)}, u32[]{:S(2)}) collective-permute-start(bf16[192,1536]{1,0:T(8,128)(2,1)S(1)} %get-tuple-element.96), channel_id=1, source_target_pairs={{0,128},{128,8},{8,136},{136,0},{1,129},{129,9},{9,137},{137,1},{2... | collective-permute-start | bytes 1769480 | tf_op jit(solution)/shard_map/ppermute | solution.py:38
  26.9 13.6 %collective-permute-start.11 = (bf16[192,1536]{1,0:T(8,128)(2,1)S(1)}, bf16[192,1536]{1,0:T(8,128)(2,1)S(1)}, u32[]{:S(2)}, u32[]{:S(2)}) collective-permute-start(bf16[192,1536]{1,0:T(8,128)(2,1)S(1)} %get-tuple-element.96), channel_id=1, source_target_pairs={{0,136},{128,0},{8,128},{136,8},{1,137},{129,1},{9,129},{137,9},{2... | collective-permute-start | bytes 1769480 | tf_op jit(solution)/shard_map/ppermute | solution.py:38
  28.0 17.6 %collective-permute-start.6 = (bf16[128,1536]{1,0:T(8,128)(2,1)S(1)}, bf16[128,1536]{1,0:T(8,128)(2,1)S(1)}, u32[]{:S(2)}, u32[]{:S(2)}) collective-permute-start(bf16[128,1536]{1,0:T(8,128)(2,1)S(1)} %collective-permute-done.3), channel_id=1, source_target_pairs={{0,1},{1,2},{2,3},{3,4},{4,5},{5,6},{6,7},{7,0},{8,9},{9,10},{10,1... | collective-permute-start | bytes 1179656 | tf_op jit(solution)/shard_map/ppermute | solution.py:31
  28.0 17.6 %collective-permute-start.7 = (bf16[128,1536]{1,0:T(8,128)(2,1)S(1)}, bf16[128,1536]{1,0:T(8,128)(2,1)S(1)}, u32[]{:S(2)}, u32[]{:S(2)}) collective-permute-start(bf16[128,1536]{1,0:T(8,128)(2,1)S(1)} %collective-permute-done.4), channel_id=1, source_target_pairs={{0,7},{1,0},{2,1},{3,2},{4,3},{5,4},{6,5},{7,6},{8,15},{9,8},{10,9... | collective-permute-start | bytes 1179656 | tf_op jit(solution)/shard_map/ppermute | solution.py:31
  30.7 14.9 %collective-permute-start.13 = (bf16[128,1536]{1,0:T(8,128)(2,1)S(1)}, bf16[128,1536]{1,0:T(8,128)(2,1)S(1)}, u32[]{:S(2)}, u32[]{:S(2)}) collective-permute-start(bf16[128,1536]{1,0:T(8,128)(2,1)S(1)} %collective-permute-done.8), channel_id=1, source_target_pairs={{0,64},{32,96},{64,0},{96,32},{1,65},{33,97},{65,1},{97,33},{2,66}... | collective-permute-start | bytes 1179656 | tf_op jit(solution)/shard_map/ppermute | solution.py:42
  40.5 3.5 %collective-permute-start.12 = (bf16[128,1536]{1,0:T(8,128)(2,1)S(1)}, bf16[128,1536]{1,0:T(8,128)(2,1)S(1)}, u32[]{:S(2)}, u32[]{:S(2)}) collective-permute-start(bf16[128,1536]{1,0:T(8,128)(2,1)S(1)} %collective-permute-done.8), channel_id=1, source_target_pairs={{0,16},{16,0},{1,17},{17,1},{2,18},{18,2},{3,19},{19,3},{4,20},{20... | collective-permute-start | bytes 1179656 | tf_op jit(solution)/shard_map/ppermute | solution.py:51
  42.7 7.5 %slice-start.1 = ((s8[4718592]{0:T(1024)(128)(4,1)}), s8[524288]{0:T(1024)(128)(4,1)S(1)}, s32[]{:S(2)}) async-start(s8[4718592]{0:T(1024)(128)(4,1)} %bitcast), calls=%async_computation.1 | async-start | bytes 1048576
  42.7 15.0 %collective-permute-start.18 = (bf16[128,1536]{1,0:T(8,128)(2,1)S(1)}, bf16[128,1536]{1,0:T(8,128)(2,1)S(1)}, u32[]{:S(2)}, u32[]{:S(2)}) collective-permute-start(bf16[128,1536]{1,0:T(8,128)(2,1)S(1)} %pad_maximum_fusion.7), channel_id=1, source_target_pairs={{0,128},{128,8},{8,136},{136,0},{1,129},{129,9},{9,137},{137,1},{2... | collective-permute-start | bytes 1179656 | tf_op jit(solution)/shard_map/ppermute | solution.py:38
  44.0 13.7 %collective-permute-start.19 = (bf16[128,1536]{1,0:T(8,128)(2,1)S(1)}, bf16[128,1536]{1,0:T(8,128)(2,1)S(1)}, u32[]{:S(2)}, u32[]{:S(2)}) collective-permute-start(bf16[128,1536]{1,0:T(8,128)(2,1)S(1)} %pad_maximum_fusion.7), channel_id=1, source_target_pairs={{0,136},{128,0},{8,128},{136,8},{1,137},{129,1},{9,129},{137,9},{2... | collective-permute-start | bytes 1179656 | tf_op jit(solution)/shard_map/ppermute | solution.py:38
  45.6 9.5 %collective-permute-start.14 = (bf16[96,1536]{1,0:T(8,128)(2,1)S(1)}, bf16[96,1536]{1,0:T(8,128)(2,1)S(1)}, u32[]{:S(2)}, u32[]{:S(2)}) collective-permute-start(bf16[96,1536]{1,0:T(8,128)(2,1)S(1)} %slice.82), channel_id=1, source_target_pairs={{0,1},{1,2},{2,3},{3,4},{4,5},{5,6},{6,7},{7,0},{8,9},{9,10},{10,1... | collective-permute-start | bytes 884744 | tf_op jit(solution)/shard_map/ppermute | solution.py:31
  45.9 9.2 %collective-permute-start.15 = (bf16[96,1536]{1,0:T(8,128)(2,1)S(1)}, bf16[96,1536]{1,0:T(8,128)(2,1)S(1)}, u32[]{:S(2)}, u32[]{:S(2)}) collective-permute-start(bf16[96,1536]{1,0:T(8,128)(2,1)S(1)} %slice.83), channel_id=1, source_target_pairs={{0,7},{1,0},{2,1},{3,2},{4,3},{5,4},{6,5},{7,6},{8,15},{9,8},{10,9... | collective-permute-start | bytes 884744 | tf_op jit(solution)/shard_map/ppermute | solution.py:31
  48.9 19.6 %collective-permute-start.20 = (bf16[512,1536]{1,0:T(8,128)(2,1)S(1)}, bf16[512,1536]{1,0:T(8,128)(2,1)S(1)}, u32[]{:S(2)}, u32[]{:S(2)}) collective-permute-start(bf16[512,1536]{1,0:T(8,128)(2,1)S(1)} %pad_maximum_fusion.1), channel_id=1, source_target_pairs={{0,32},{16,112},{32,64},{48,16},{64,96},{80,48},{96,0},{112,80},{1... | collective-permute-start | bytes 4718600 | tf_op jit(solution)/shard_map/ppermute | solution.py:47
  55.2 4.2 %collective-permute-start.17 = (bf16[32,1536]{1,0:T(8,128)(2,1)S(1)}, bf16[32,1536]{1,0:T(8,128)(2,1)S(1)}, u32[]{:S(2)}, u32[]{:S(2)}) collective-permute-start(bf16[32,1536]{1,0:T(8,128)(2,1)S(1)} %get-tuple-element.94), channel_id=1, source_target_pairs={{0,7},{1,0},{2,1},{3,2},{4,3},{5,4},{6,5},{7,6},{8,15},{9,8},{10,9... | collective-permute-start | bytes 294920 | tf_op jit(solution)/shard_map/ppermute | solution.py:31
  57.7 5.0 %collective-permute-start.16 = (bf16[32,1536]{1,0:T(8,128)(2,1)S(1)}, bf16[32,1536]{1,0:T(8,128)(2,1)S(1)}, u32[]{:S(2)}, u32[]{:S(2)}) collective-permute-start(bf16[32,1536]{1,0:T(8,128)(2,1)S(1)} %get-tuple-element.91), channel_id=1, source_target_pairs={{0,1},{1,2},{2,3},{3,4},{4,5},{5,6},{6,7},{7,0},{8,9},{9,10},{10,1... | collective-permute-start | bytes 294920 | tf_op jit(solution)/shard_map/ppermute | solution.py:31
  68.6 6.2 %collective-permute-start.21 = (bf16[512,1536]{1,0:T(8,128)(2,1)S(1)}, bf16[512,1536]{1,0:T(8,128)(2,1)S(1)}, u32[]{:S(2)}, u32[]{:S(2)}) collective-permute-start(bf16[512,1536]{1,0:T(8,128)(2,1)S(1)} %get-tuple-element.61), channel_id=1, source_target_pairs={{0,16},{16,0},{1,17},{17,1},{2,18},{18,2},{3,19},{19,3},{4,20},{20... | collective-permute-start | bytes 4718600 | tf_op jit(solution)/shard_map/ppermute | solution.py:51
  75.0 4.6 %collective-permute-start.27 = (bf16[768,1536]{1,0:T(8,128)(2,1)S(1)}, bf16[768,1536]{1,0:T(8,128)(2,1)S(1)}, u32[]{:S(2)}, u32[]{:S(2)}) collective-permute-start(bf16[768,1536]{1,0:T(8,128)(2,1)S(1)} %pad_maximum_fusion.refs_7_.refs_5_), channel_id=1, source_target_pairs={{0,16},{16,0},{1,17},{17,1},{2,18},{18,2},{3,19},{19,3},{4,20},{20... | collective-permute-start | bytes 7077896 | tf_op jit(solution)/shard_map/ppermute | solution.py:51
  75.5 16.1 %collective-permute-start.25 = (bf16[192,1536]{1,0:T(8,128)(2,1)S(1)}, bf16[192,1536]{1,0:T(8,128)(2,1)S(1)}, u32[]{:S(2)}, u32[]{:S(2)}) collective-permute-start(bf16[192,1536]{1,0:T(8,128)(2,1)S(1)} %pad_maximum_fusion.4), channel_id=1, source_target_pairs={{0,128},{128,8},{8,136},{136,0},{1,129},{129,9},{9,137},{137,1},{2... | collective-permute-start | bytes 1769480 | tf_op jit(solution)/shard_map/ppermute | solution.py:38
  75.7 15.9 %collective-permute-start.26 = (bf16[192,1536]{1,0:T(8,128)(2,1)S(1)}, bf16[192,1536]{1,0:T(8,128)(2,1)S(1)}, u32[]{:S(2)}, u32[]{:S(2)}) collective-permute-start(bf16[192,1536]{1,0:T(8,128)(2,1)S(1)} %pad_maximum_fusion.4), channel_id=1, source_target_pairs={{0,136},{128,0},{8,128},{136,8},{1,137},{129,1},{9,129},{137,9},{2... | collective-permute-start | bytes 1769480 | tf_op jit(solution)/shard_map/ppermute | solution.py:38
  78.6 18.4 %collective-permute-start.22 = (bf16[128,1536]{1,0:T(8,128)(2,1)S(1)}, bf16[128,1536]{1,0:T(8,128)(2,1)S(1)}, u32[]{:S(2)}, u32[]{:S(2)}) collective-permute-start(bf16[128,1536]{1,0:T(8,128)(2,1)S(1)} %get-tuple-element.78), channel_id=1, source_target_pairs={{0,64},{32,96},{64,0},{96,32},{1,65},{33,97},{65,1},{97,33},{2,66}... | collective-permute-start | bytes 1179656 | tf_op jit(solution)/shard_map/ppermute | solution.py:42
  79.0 20.6 %collective-permute-start.23 = (bf16[128,1536]{1,0:T(8,128)(2,1)S(1)}, bf16[128,1536]{1,0:T(8,128)(2,1)S(1)}, u32[]{:S(2)}, u32[]{:S(2)}) collective-permute-start(bf16[128,1536]{1,0:T(8,128)(2,1)S(1)} %get-tuple-element.77), channel_id=1, source_target_pairs={{0,32},{32,64},{64,96},{96,0},{1,33},{33,65},{65,97},{97,1},{2,34}... | collective-permute-start | bytes 1179656 | tf_op jit(solution)/shard_map/ppermute | solution.py:42
  79.7 19.9 %collective-permute-start.24 = (bf16[128,1536]{1,0:T(8,128)(2,1)S(1)}, bf16[128,1536]{1,0:T(8,128)(2,1)S(1)}, u32[]{:S(2)}, u32[]{:S(2)}) collective-permute-start(bf16[128,1536]{1,0:T(8,128)(2,1)S(1)} %get-tuple-element.76), channel_id=1, source_target_pairs={{0,96},{32,0},{64,32},{96,64},{1,97},{33,1},{65,33},{97,65},{2,98}... | collective-permute-start | bytes 1179656 | tf_op jit(solution)/shard_map/ppermute | solution.py:42
  91.4 8.2 %copy-start = (bf16[128,1536]{1,0:T(8,128)(2,1)S(1)}, bf16[128,1536]{1,0:T(8,128)(2,1)}, u32[]{:S(2)}) copy-start(bf16[128,1536]{1,0:T(8,128)(2,1)} %param.3) | copy-start | bytes 1179652

commit v11 on v10

--- a/solution.py
+++ b/solution.py
@@ -127,8 +127,8 @@
 
 
 def weight_kernel(layout, *refs):
-    pieces, acts_refs = refs[: len(layout)], refs[len(layout) : len(layout) + 4]
-    *sum_ref, out_ref, grads, acts = refs[len(layout) + 4 :]
+    pieces, acts_refs = refs[: len(layout)], refs[len(layout) : len(layout) + 7]
+    *sum_ref, out_ref, grads, acts = refs[len(layout) + 7 :]
     y, c, xl, xh, z = (lax.axis_index(a) for a in ("y", "c", "xl", "xh", "z"))
 
     @pl.when(pl.program_id(0) == 0)
@@ -149,13 +149,21 @@
             def _():
                 copy(other, away)
 
-            @pl.when((dy == back) | ((dy == 2) & (away == 0)))
-            def _():
-                copy(2, 3 * other + jnp.where(dy == 2, 2, away))
-
-            @pl.when((dy == 4 - back) | ((dy == 2) & (away == 1)))
-            def _():
-                copy(3, 3 * other + jnp.where(dy == 2, 2, 1 - away))
+            @pl.when(dy == back)
+            def _():
+                copy(2, 2 * other + away)
+
+            @pl.when(dy == 4 - back)
+            def _():
+                copy(3, 2 * other + 1 - away)
+
+            @pl.when((dy == 2) & (away == 0))
+            def _():
+                copy(4 + other, 0)
+
+            @pl.when((dy == 2) & (away == 1))
+            def _():
+                copy(6, other)
 
     lanes = pl.ds(pl.multiple_of(pl.program_id(0) * 256, 256), 256)
     start = 0
@@ -175,7 +183,7 @@
     return pl.pallas_call(
         functools.partial(weight_kernel, layout),
         grid=(1536 // step,),
-        in_specs=[VMEM] * (len(pieces) + 4) + [block] * last,
+        in_specs=[VMEM] * (len(pieces) + 7) + [block] * last,
         out_specs=block,
         out_shape=jax.ShapeDtypeStruct((1536, 1536), BF if last else F32),
         scratch_shapes=[pltpu.VMEM((count, step), BF), pltpu.VMEM((count, 1536), BF)],
@@ -225,11 +233,12 @@
 
     grads_late = jnp.concatenate([last, up4[:64], down4[32:], up5, down5])
     mine, other = late_partial(early, grads_late, down_weight)
-    mine, other, hops, last = tie(mine, other, hops, last)
+    mine, other, hop_2, hop_4, last = tie(mine, other, hop_2, hop_4, last)
+    swap_a = swap(jnp.concatenate([hop_2, hop_4]), "c")
+    other, hops, swap_a = tie(other, hops, swap_a)
     other = swap(other, "c")
     other, hops = tie(other, hops)
-    came = jnp.concatenate([hops[:256], hop_2, hops[256:], hop_4])
-    swapped = swap(came, "c")
+    swap_b = swap(hops, "c")
     third = jnp.concatenate([up3[64:], down3[:64], last])
     left_c, right_c = along_x(third, 1), along_x(third, -1)
 
@@ -240,7 +249,7 @@
     from_across = along_y(to_across, 2)
     from_below, from_above = along_y(to_above, 1), along_y(to_below, -1)
 
-    acts = [chip, other_chip, came, swapped]
+    acts = [chip, other_chip, hops, swap_b, hop_2, hop_4, swap_a]
     weight_sum = weight_product(PIECES[:5], [grads_early, grads_late, left_a, right_a, left_b], acts, None)
     weight_grad = weight_product(PIECES[5:], [right_b, left_c, right_c], acts, weight_sum)
     from_across, from_below, from_above, weight_grad = tie(from_across, from_below, from_above, weight_grad)

time: 101 us -> 101 us (level)
  waiting for transfers between devices: 32.3 us -> 29.7 us
  starting transfers between devices: 40.9 us -> 43 us
    ppermute x1, waiting for transfers between devices: 3.86 us -> 0.01 us  [round_y(): lax.ppermute(a, ('y', 'c'), [(s[0] * C + s[1], t[0] * C + t[1]) for s, t...]
    ppermute x5 -> x6, starting transfers between devices: 7.48 us -> 9.28 us  [swap(): return lax.ppermute(a, axis, [(0, 1), (1, 0)])]
    ppermute x5 -> x6, waiting for transfers between devices: 10.4 us -> 12 us  [swap(): return lax.ppermute(a, axis, [(0, 1), (1, 0)])]
  transfers between devices with their start and end apart: 28 -> 29, of which waited for: 13 -> 11; matrix products, arithmetic and copies ran while one was open for 3% -> 3% of each run, Pallas kernels for 22% -> 22%
where the time goes in v11:
time: 101 us
  starting transfers between devices  43 us (43%)
  waiting for transfers between devices  29.7 us (29%)
  Pallas kernels  22.2 us (22%)
  other arithmetic  3.47 us (3%)
  local copies, waits for them, and re-layouts  1.34 us (1%)
    ppermute x10, starting transfers between devices, along_z(): return lax.ppermute(a, 'z', [(i, (i + d) % Z) for i in range(Z)])  17.5 us
    pallas_call x2, Pallas kernels, weight_product(): pl.pallas_call(functools.partial(weight_kernel, layout), grid=(1536 // st...  15.5 us
    ppermute x6, waiting for transfers between devices, swap(): return lax.ppermute(a, axis, [(0, 1), (1, 0)])  12 us
    ppermute x6, starting transfers between devices, swap(): return lax.ppermute(a, axis, [(0, 1), (1, 0)])  9.28 us
    ppermute x7, waiting for transfers between devices, along_x(): lax.ppermute(a, ('xl', 'xh'), [(place(x), place((x + d) % 4)) for x in ra...  9.2 us
    ppermute x7, starting transfers between devices, along_x(): lax.ppermute(a, ('xl', 'xh'), [(place(x), place((x + d) % 4)) for x in ra...  8.34 us
    ppermute x5, starting transfers between devices, along_y(): return lax.ppermute(a, 'y', [(i, (i + d) % Y) for i in range(Y)])  6.61 us
    ppermute x10, waiting for transfers between devices, along_z(): return lax.ppermute(a, 'z', [(i, (i + d) % Z) for i in range(Z)])  6.1 us
  transfers between devices with their start and end apart: 29, of which 11 were waited for; matrix products, arithmetic and copies ran while one was open for 3% of the time, Pallas kernels for 22%

profile of v11, /device:TPU:1, one launch (start us, length us, event | category | flops | bytes accessed | tf_op | source)
XLA Modules:
  0.0 100.7 jit_solution(6899963677806558049)
XLA Ops:
  0.6 2.5 %collective-permute-start = (bf16[64,1536]{1,0:T(8,128)(2,1)}, bf16[64,1536]{1,0:T(8,128)(2,1)S(1)}, u32[]{:S(2)}, u32[]{:S(2)}) collective-permute-start(bf16[64,1536]{1,0:T(8,128)(2,1)} %param.4), channel_id=1, source_target_pairs={{0,1},{1,2},{2,3},{3,4},{4,5},{5,6},{6,7},{7,0},{8,9},{9,10},{10,1... | collective-permute-start | bytes 589832 | tf_op jit(solution)/shard_map/ppermute | solution.py:31
  3.2 4.0 %collective-permute-start.1 = (bf16[64,1536]{1,0:T(8,128)(2,1)}, bf16[64,1536]{1,0:T(8,128)(2,1)S(1)}, u32[]{:S(2)}, u32[]{:S(2)}) collective-permute-start(bf16[64,1536]{1,0:T(8,128)(2,1)} %param.4), channel_id=1, source_target_pairs={{0,7},{1,0},{2,1},{3,2},{4,3},{5,4},{6,5},{7,6},{8,15},{9,8},{10,9... | collective-permute-start | bytes 589832 | tf_op jit(solution)/shard_map/ppermute | solution.py:31
  7.2 2.7 %collective-permute-start.2 = (bf16[64,1536]{1,0:T(8,128)(2,1)}, bf16[64,1536]{1,0:T(8,128)(2,1)S(1)}, u32[]{:S(2)}, u32[]{:S(2)}) collective-permute-start(bf16[64,1536]{1,0:T(8,128)(2,1)} %param.4), channel_id=1, source_target_pairs={{0,8},{128,136},{8,0},{136,128},{1,9},{129,137},{9,1},{137,129},{2... | collective-permute-start | bytes 589832 | tf_op jit(solution)/shard_map/ppermute | solution.py:38
  9.9 1.3 %fusion.2 = bf16[128,1536]{1,0:T(8,128)(2,1)S(1)} fusion(bf16[128,1536]{1,0:T(8,128)(2,1)} %param.3), kind=kLoop, calls=%fused_computation.10 | loop fusion | flops 1966080 | bytes 786432 | tf_op jit(solution)/shard_map/convert_element_type | solution.py:198
  11.2 1.3 %collective-permute-start.9 = (bf16[128,1536]{1,0:T(8,128)(2,1)S(1)}, bf16[128,1536]{1,0:T(8,128)(2,1)S(1)}, u32[]{:S(2)}, u32[]{:S(2)}) collective-permute-start(bf16[128,1536]{1,0:T(8,128)(2,1)S(1)} %fusion.2), channel_id=1, source_target_pairs={{0,16},{16,0},{1,17},{17,1},{2,18},{18,2},{3,19},{19,3},{4,20},{20... | collective-permute-start | bytes 1179656 | tf_op jit(solution)/shard_map/ppermute | solution.py:51
  12.5 2.9 %collective-permute-start.5 = (bf16[128,1536]{1,0:T(8,128)(2,1)S(1)}, bf16[128,1536]{1,0:T(8,128)(2,1)S(1)}, u32[]{:S(2)}, u32[]{:S(2)}) collective-permute-start(bf16[128,1536]{1,0:T(8,128)(2,1)S(1)} %fusion.2), channel_id=1, source_target_pairs={{0,64},{32,96},{64,0},{96,32},{1,65},{33,97},{65,1},{97,33},{2,66}... | collective-permute-start | bytes 1179656 | tf_op jit(solution)/shard_map/ppermute | solution.py:42
  17.0 2.7 %collective-permute-start.4 = (bf16[128,1536]{1,0:T(8,128)(2,1)S(1)}, bf16[128,1536]{1,0:T(8,128)(2,1)S(1)}, u32[]{:S(2)}, u32[]{:S(2)}) collective-permute-start(bf16[128,1536]{1,0:T(8,128)(2,1)S(1)} %get-tuple-element.107), channel_id=1, source_target_pairs={{0,7},{1,0},{2,1},{3,2},{4,3},{5,4},{6,5},{7,6},{8,15},{9,8},{10,9... | collective-permute-start | bytes 1179656 | tf_op jit(solution)/shard_map/ppermute | solution.py:31
  19.8 1.2 %collective-permute-start.10 = (bf16[192,1536]{1,0:T(8,128)(2,1)S(1)}, bf16[192,1536]{1,0:T(8,128)(2,1)S(1)}, u32[]{:S(2)}, u32[]{:S(2)}) collective-permute-start(bf16[192,1536]{1,0:T(8,128)(2,1)S(1)} %get-tuple-element.102), channel_id=1, source_target_pairs={{0,128},{128,8},{8,136},{136,0},{1,129},{129,9},{9,137},{137,1},{2... | collective-permute-start | bytes 1769480 | tf_op jit(solution)/shard_map/ppermute | solution.py:38
  21.0 5.9 %collective-permute-done.8 = bf16[128,1536]{1,0:T(8,128)(2,1)S(1)} collective-permute-done((bf16[128,1536]{1,0:T(8,128)(2,1)S(1)}, bf16[128,1536]{1,0:T(8,128)(2,1)S(1)}, u32[]{:S(2)}, u32[]{:S(2)}) %collective-permute-start.8) | collective-permute-done | bytes 393248 | tf_op jit(solution)/shard_map/ppermute | solution.py:51
  28.0 2.7 %collective-permute-start.7 = (bf16[128,1536]{1,0:T(8,128)(2,1)S(1)}, bf16[128,1536]{1,0:T(8,128)(2,1)S(1)}, u32[]{:S(2)}, u32[]{:S(2)}) collective-permute-start(bf16[128,1536]{1,0:T(8,128)(2,1)S(1)} %collective-permute-done.4), channel_id=1, source_target_pairs={{0,7},{1,0},{2,1},{3,2},{4,3},{5,4},{6,5},{7,6},{8,15},{9,8},{10,9... | collective-permute-start | bytes 1179656 | tf_op jit(solution)/shard_map/ppermute | solution.py:31
  31.4 6.0 %collective-permute-done.10.refs_2_ = bf16[192,1536]{1,0:T(8,128)(2,1)S(1)} collective-permute-done((bf16[192,1536]{1,0:T(8,128)(2,1)S(1)}, bf16[192,1536]{1,0:T(8,128)(2,1)S(1)}, u32[]{:S(2)}, u32[]{:S(2)}) %collective-permute-start.10) | collective-permute-done | bytes 589856 | tf_op jit(solution)/shard_map/ppermute | solution.py:38
  37.4 3.1 %collective-permute-done.11.refs_3_ = bf16[192,1536]{1,0:T(8,128)(2,1)S(1)} collective-permute-done((bf16[192,1536]{1,0:T(8,128)(2,1)S(1)}, bf16[192,1536]{1,0:T(8,128)(2,1)S(1)}, u32[]{:S(2)}, u32[]{:S(2)}) %collective-permute-start.11) | collective-permute-done | bytes 589856 | tf_op jit(solution)/shard_map/ppermute | solution.py:38
  40.5 2.1 %collective-permute-start.12 = (bf16[128,1536]{1,0:T(8,128)(2,1)S(1)}, bf16[128,1536]{1,0:T(8,128)(2,1)S(1)}, u32[]{:S(2)}, u32[]{:S(2)}) collective-permute-start(bf16[128,1536]{1,0:T(8,128)(2,1)S(1)} %collective-permute-done.8), channel_id=1, source_target_pairs={{0,16},{16,0},{1,17},{17,1},{2,18},{18,2},{3,19},{19,3},{4,20},{20... | collective-permute-start | bytes 1179656 | tf_op jit(solution)/shard_map/ppermute | solution.py:51
  42.8 1.1 %collective-permute-done.12 = bf16[128,1536]{1,0:T(8,128)(2,1)S(1)} collective-permute-done((bf16[128,1536]{1,0:T(8,128)(2,1)S(1)}, bf16[128,1536]{1,0:T(8,128)(2,1)S(1)}, u32[]{:S(2)}, u32[]{:S(2)}) %collective-permute-start.12) | collective-permute-done | bytes 393248 | tf_op jit(solution)/shard_map/ppermute | solution.py:51
  44.0 1.5 %collective-permute-start.19 = (bf16[128,1536]{1,0:T(8,128)(2,1)S(1)}, bf16[128,1536]{1,0:T(8,128)(2,1)S(1)}, u32[]{:S(2)}, u32[]{:S(2)}) collective-permute-start(bf16[128,1536]{1,0:T(8,128)(2,1)S(1)} %pad_maximum_fusion.7), channel_id=1, source_target_pairs={{0,136},{128,0},{8,128},{136,8},{1,137},{129,1},{9,129},{137,9},{2... | collective-permute-start | bytes 1179656 | tf_op jit(solution)/shard_map/ppermute | solution.py:38
  45.9 2.7 %collective-permute-start.15 = (bf16[96,1536]{1,0:T(8,128)(2,1)S(1)}, bf16[96,1536]{1,0:T(8,128)(2,1)S(1)}, u32[]{:S(2)}, u32[]{:S(2)}) collective-permute-start(bf16[96,1536]{1,0:T(8,128)(2,1)S(1)} %slice.77), channel_id=1, source_target_pairs={{0,7},{1,0},{2,1},{3,2},{4,3},{5,4},{6,5},{7,6},{8,15},{9,8},{10,9... | collective-permute-start | bytes 884744 | tf_op jit(solution)/shard_map/ppermute | solution.py:31
  48.9 1.2 %collective-permute-start.20 = (bf16[512,1536]{1,0:T(8,128)(2,1)S(1)}, bf16[512,1536]{1,0:T(8,128)(2,1)S(1)}, u32[]{:S(2)}, u32[]{:S(2)}) collective-permute-start(bf16[512,1536]{1,0:T(8,128)(2,1)S(1)} %pad_maximum_fusion), channel_id=1, source_target_pairs={{0,32},{16,112},{32,64},{48,16},{64,96},{80,48},{96,0},{112,80},{1... | collective-permute-start | bytes 4718600 | tf_op jit(solution)/shard_map/ppermute | solution.py:47
  50.2 4.8 %shard_map.50.early_ref = f32[768,1536]{1,0:T(8,128)S(1)} custom-call(bf16[768,1536]{1,0:T(8,128)(2,1)S(1)} %slice_dynamic-update-slice_fusion.2.grads_ref.refs_0_, bf16[1536,1536]{1,0:T(8,128)(2,1)S(1)} %bitcast.1), custom_call_target="tpu_custom_call" | custom-call | flops 3623878656 | bytes 12582912 | tf_op jit(solution)/shard_map/pallas_call | solution.py:73
  55.2 2.5 %collective-permute-start.17 = (bf16[32,1536]{1,0:T(8,128)(2,1)S(1)}, bf16[32,1536]{1,0:T(8,128)(2,1)S(1)}, u32[]{:S(2)}, u32[]{:S(2)}) collective-permute-start(bf16[32,1536]{1,0:T(8,128)(2,1)S(1)} %get-tuple-element.100), channel_id=1, source_target_pairs={{0,7},{1,0},{2,1},{3,2},{4,3},{5,4},{6,5},{7,6},{8,15},{9,8},{10,9... | collective-permute-start | bytes 294920 | tf_op jit(solution)/shard_map/ppermute | solution.py:31
  57.7 1.6 %collective-permute-done.17 = bf16[32,1536]{1,0:T(8,128)(2,1)S(1)} collective-permute-done((bf16[32,1536]{1,0:T(8,128)(2,1)S(1)}, bf16[32,1536]{1,0:T(8,128)(2,1)S(1)}, u32[]{:S(2)}, u32[]{:S(2)}) %collective-permute-start.17) | collective-permute-done | bytes 98336 | tf_op jit(solution)/shard_map/ppermute | solution.py:31
  59.3 3.3 %collective-permute-done.16 = bf16[32,1536]{1,0:T(8,128)(2,1)S(1)} collective-permute-done((bf16[32,1536]{1,0:T(8,128)(2,1)S(1)}, bf16[32,1536]{1,0:T(8,128)(2,1)S(1)}, u32[]{:S(2)}, u32[]{:S(2)}) %collective-permute-start.16) | collective-permute-done | bytes 98336 | tf_op jit(solution)/shard_map/ppermute | solution.py:31
  62.7 2.0 %shard_map.51 = (f32[512,1536]{1,0:T(8,128)S(1)}, bf16[512,1536]{1,0:T(8,128)(2,1)S(1)}) custom-call(f32[768,1536]{1,0:T(8,128)S(1)} %shard_map.50.early_ref, bf16[256,1536]{1,0:T(8,128)(2,1)S(1)} %constant_dynamic-update-slice_fusion.11.grads_ref.refs_1_, bf16[1536,1536]{1,0:T(8,128)(2,1)S(1)} %bitcast.1), custom_call_target="tpu_custom_call" | custom-call | flops 1207959552 | bytes 8388608 | tf_op jit(solution)/shard_map/pallas_call | solution.py:111
  64.8 2.9 %collective-permute-start.21 = (bf16[256,1536]{1,0:T(8,128)(2,1)S(1)}, bf16[256,1536]{1,0:T(8,128)(2,1)S(1)}, u32[]{:S(2)}, u32[]{:S(2)}) collective-permute-start(bf16[256,1536]{1,0:T(8,128)(2,1)S(1)} %pad_maximum_fusion.3), channel_id=1, source_target_pairs={{0,16},{16,0},{1,17},{17,1},{2,18},{18,2},{3,19},{19,3},{4,20},{20... | collective-permute-start | bytes 2359304 | tf_op jit(solution)/shard_map/ppermute | solution.py:51
  67.7 1.9 %collective-permute-done.21.refs_11_.refs_9_ = bf16[256,1536]{1,0:T(8,128)(2,1)S(1)} collective-permute-done((bf16[256,1536]{1,0:T(8,128)(2,1)S(1)}, bf16[256,1536]{1,0:T(8,128)(2,1)S(1)}, u32[]{:S(2)}, u32[]{:S(2)}) %collective-permute-start.21) | collective-permute-done | bytes 786464 | tf_op jit(solution)/shard_map/ppermute | solution.py:51
  69.6 2.1 %collective-permute-start.22 = (bf16[512,1536]{1,0:T(8,128)(2,1)S(1)}, bf16[512,1536]{1,0:T(8,128)(2,1)S(1)}, u32[]{:S(2)}, u32[]{:S(2)}) collective-permute-start(bf16[512,1536]{1,0:T(8,128)(2,1)S(1)} %get-tuple-element.70), channel_id=1, source_target_pairs={{0,16},{16,0},{1,17},{17,1},{2,18},{18,2},{3,19},{19,3},{4,20},{20... | collective-permute-start | bytes 4718600 | tf_op jit(solution)/shard_map/ppermute | solution.py:51
  71.7 3.0 %collective-permute-done.22 = bf16[512,1536]{1,0:T(8,128)(2,1)S(1)} collective-permute-done((bf16[512,1536]{1,0:T(8,128)(2,1)S(1)}, bf16[512,1536]{1,0:T(8,128)(2,1)S(1)}, u32[]{:S(2)}, u32[]{:S(2)}) %collective-permute-start.22) | collective-permute-done | bytes 1572896 | tf_op jit(solution)/shard_map/ppermute | solution.py:51
  75.3 2.6 %collective-permute-start.27 = (bf16[192,1536]{1,0:T(8,128)(2,1)S(1)}, bf16[192,1536]{1,0:T(8,128)(2,1)S(1)}, u32[]{:S(2)}, u32[]{:S(2)}) collective-permute-start(bf16[192,1536]{1,0:T(8,128)(2,1)S(1)} %pad_maximum_fusion.4), channel_id=1, source_target_pairs={{0,136},{128,0},{8,128},{136,8},{1,137},{129,1},{9,129},{137,9},{2... | collective-permute-start | bytes 1769480 | tf_op jit(solution)/shard_map/ppermute | solution.py:38
  79.0 2.3 %collective-permute-start.25 = (bf16[128,1536]{1,0:T(8,128)(2,1)S(1)}, bf16[128,1536]{1,0:T(8,128)(2,1)S(1)}, u32[]{:S(2)}, u32[]{:S(2)}) collective-permute-start(bf16[128,1536]{1,0:T(8,128)(2,1)S(1)} %get-tuple-element.84), channel_id=1, source_target_pairs={{0,96},{32,0},{64,32},{96,64},{1,97},{33,1},{65,33},{97,65},{2,98}... | collective-permute-start | bytes 1179656 | tf_op jit(solution)/shard_map/ppermute | solution.py:42
  81.3 9.9 %shard_map.52.refs_10_ = f32[1536,1536]{1,0:T(8,128)S(1)} custom-call(bf16[768,1536]{1,0:T(8,128)(2,1)S(1)} %slice_dynamic-update-slice_fusion.2.grads_ref.refs_0_, bf16[256,1536]{1,0:T(8,128)(2,1)S(1)} %constant_dynamic-update-slice_fusion.11.grads_ref.refs_1_, bf16[192,1536]{1,0:T(8,128)(2,1)S(1)} %collective-permute-done.10.refs_2_, ...), custom_call_target="tpu_custom_call" | custom-call | flops 7247757312 | bytes 12582912 | tf_op jit(solution)/shard_map/pallas_call | solution.py:183
  91.3 5.6 %shard_map.53 = bf16[1536,1536]{1,0:T(8,128)(2,1)} custom-call(bf16[128,1536]{1,0:T(8,128)(2,1)S(1)} %collective-permute-done.19.refs_0_, bf16[192,1536]{1,0:T(8,128)(2,1)S(1)} %collective-permute-done.26.refs_1_, bf16[192,1536]{1,0:T(8,128)(2,1)S(1)} %collective-permute-done.27.refs_2_, bf16[256,1536]{1,0:T(8,128)(2,1)S(1)} %pad_maximum_fusion.1.refs_5_.refs_3_, ...), custom_call_target="tpu_custom_call" | custom-call | flops 2415919104 | bytes 12582912 | tf_op jit(solution)/shard_map/pallas_call | solution.py:183
  96.8 2.4 %collective-permute-done.24 = bf16[128,1536]{1,0:T(8,128)(2,1)S(1)} collective-permute-done((bf16[128,1536]{1,0:T(8,128)(2,1)S(1)}, bf16[128,1536]{1,0:T(8,128)(2,1)S(1)}, u32[]{:S(2)}, u32[]{:S(2)}) %collective-permute-start.24) | collective-permute-done | bytes 393248 | tf_op jit(solution)/shard_map/ppermute | solution.py:42
  99.2 1.5 %fusion.7 = bf16[128,1536]{1,0:T(8,128)(2,1)} fusion(bf16[128,1536]{1,0:T(8,128)(2,1)S(1)} %copy-done, bf16[128,1536]{1,0:T(8,128)(2,1)S(1)} %collective-permute-done.23, bf16[128,1536]{1,0:T(8,128)(2,1)S(1)} %collective-permute-done.25, bf16[128,1536]{1,0:T(8,128)(2,1)S(1)} %collective-permute-done.24, f32[512,1536]{1,0:T(8,128)S(1)} %get-tuple-element.64, ...), kind=kLoop, calls=%fused_computation.15 | loop fusion | flops 5505024 | bytes 3145728 | tf_op jit(solution)/shard_map/convert_element_type | solution.py:257
  (68 shorter events, 6.1 us)
Async XLA Ops:
  0.6 15.8 %collective-permute-start = (bf16[64,1536]{1,0:T(8,128)(2,1)}, bf16[64,1536]{1,0:T(8,128)(2,1)S(1)}, u32[]{:S(2)}, u32[]{:S(2)}) collective-permute-start(bf16[64,1536]{1,0:T(8,128)(2,1)} %param.4), channel_id=1, source_target_pairs={{0,1},{1,2},{2,3},{3,4},{4,5},{5,6},{6,7},{7,0},{8,9},{9,10},{10,1... | collective-permute-start | bytes 589832 | tf_op jit(solution)/shard_map/ppermute | solution.py:31
  3.2 13.3 %collective-permute-start.1 = (bf16[64,1536]{1,0:T(8,128)(2,1)}, bf16[64,1536]{1,0:T(8,128)(2,1)S(1)}, u32[]{:S(2)}, u32[]{:S(2)}) collective-permute-start(bf16[64,1536]{1,0:T(8,128)(2,1)} %param.4), channel_id=1, source_target_pairs={{0,7},{1,0},{2,1},{3,2},{4,3},{5,4},{6,5},{7,6},{8,15},{9,8},{10,9... | collective-permute-start | bytes 589832 | tf_op jit(solution)/shard_map/ppermute | solution.py:31
  7.2 9.2 %collective-permute-start.2 = (bf16[64,1536]{1,0:T(8,128)(2,1)}, bf16[64,1536]{1,0:T(8,128)(2,1)S(1)}, u32[]{:S(2)}, u32[]{:S(2)}) collective-permute-start(bf16[64,1536]{1,0:T(8,128)(2,1)} %param.4), channel_id=1, source_target_pairs={{0,8},{128,136},{8,0},{136,128},{1,9},{129,137},{9,1},{137,129},{2... | collective-permute-start | bytes 589832 | tf_op jit(solution)/shard_map/ppermute | solution.py:38
  11.2 8.5 %collective-permute-start.9 = (bf16[128,1536]{1,0:T(8,128)(2,1)S(1)}, bf16[128,1536]{1,0:T(8,128)(2,1)S(1)}, u32[]{:S(2)}, u32[]{:S(2)}) collective-permute-start(bf16[128,1536]{1,0:T(8,128)(2,1)S(1)} %fusion.2), channel_id=1, source_target_pairs={{0,16},{16,0},{1,17},{17,1},{2,18},{18,2},{3,19},{19,3},{4,20},{20... | collective-permute-start | bytes 1179656 | tf_op jit(solution)/shard_map/ppermute | solution.py:51
  12.5 14.4 %collective-permute-start.5 = (bf16[128,1536]{1,0:T(8,128)(2,1)S(1)}, bf16[128,1536]{1,0:T(8,128)(2,1)S(1)}, u32[]{:S(2)}, u32[]{:S(2)}) collective-permute-start(bf16[128,1536]{1,0:T(8,128)(2,1)S(1)} %fusion.2), channel_id=1, source_target_pairs={{0,64},{32,96},{64,0},{96,32},{1,65},{33,97},{65,1},{97,33},{2,66}... | collective-permute-start | bytes 1179656 | tf_op jit(solution)/shard_map/ppermute | solution.py:42
  16.5 10.4 %collective-permute-start.8 = (bf16[128,1536]{1,0:T(8,128)(2,1)S(1)}, bf16[128,1536]{1,0:T(8,128)(2,1)S(1)}, u32[]{:S(2)}, u32[]{:S(2)}) collective-permute-start(bf16[128,1536]{1,0:T(8,128)(2,1)S(1)} %fusion.2), channel_id=1, source_target_pairs={{0,128},{128,0},{1,129},{129,1},{2,130},{130,2},{3,131},{131,3},{4... | collective-permute-start | bytes 1179656 | tf_op jit(solution)/shard_map/ppermute | solution.py:51
  16.9 33.3 %slice-start = ((s8[4718592]{0:T(1024)(128)(4,1)}), s8[4194304]{0:T(1024)(128)(4,1)S(1)}, s32[]{:S(2)}) async-start(s8[4718592]{0:T(1024)(128)(4,1)} %bitcast), calls=%async_computation | async-start | bytes 8388608
  16.9 11.0 %collective-permute-start.3 = (bf16[128,1536]{1,0:T(8,128)(2,1)S(1)}, bf16[128,1536]{1,0:T(8,128)(2,1)S(1)}, u32[]{:S(2)}, u32[]{:S(2)}) collective-permute-start(bf16[128,1536]{1,0:T(8,128)(2,1)S(1)} %get-tuple-element.108), channel_id=1, source_target_pairs={{0,1},{1,2},{2,3},{3,4},{4,5},{5,6},{6,7},{7,0},{8,9},{9,10},{10,1... | collective-permute-start | bytes 1179656 | tf_op jit(solution)/shard_map/ppermute | solution.py:31
  17.0 11.0 %collective-permute-start.4 = (bf16[128,1536]{1,0:T(8,128)(2,1)S(1)}, bf16[128,1536]{1,0:T(8,128)(2,1)S(1)}, u32[]{:S(2)}, u32[]{:S(2)}) collective-permute-start(bf16[128,1536]{1,0:T(8,128)(2,1)S(1)} %get-tuple-element.107), channel_id=1, source_target_pairs={{0,7},{1,0},{2,1},{3,2},{4,3},{5,4},{6,5},{7,6},{8,15},{9,8},{10,9... | collective-permute-start | bytes 1179656 | tf_op jit(solution)/shard_map/ppermute | solution.py:31
  19.8 17.6 %collective-permute-start.10 = (bf16[192,1536]{1,0:T(8,128)(2,1)S(1)}, bf16[192,1536]{1,0:T(8,128)(2,1)S(1)}, u32[]{:S(2)}, u32[]{:S(2)}) collective-permute-start(bf16[192,1536]{1,0:T(8,128)(2,1)S(1)} %get-tuple-element.102), channel_id=1, source_target_pairs={{0,128},{128,8},{8,136},{136,0},{1,129},{129,9},{9,137},{137,1},{2... | collective-permute-start | bytes 1769480 | tf_op jit(solution)/shard_map/ppermute | solution.py:38
  26.9 13.6 %collective-permute-start.11 = (bf16[192,1536]{1,0:T(8,128)(2,1)S(1)}, bf16[192,1536]{1,0:T(8,128)(2,1)S(1)}, u32[]{:S(2)}, u32[]{:S(2)}) collective-permute-start(bf16[192,1536]{1,0:T(8,128)(2,1)S(1)} %get-tuple-element.102), channel_id=1, source_target_pairs={{0,136},{128,0},{8,128},{136,8},{1,137},{129,1},{9,129},{137,9},{2... | collective-permute-start | bytes 1769480 | tf_op jit(solution)/shard_map/ppermute | solution.py:38
  28.0 17.6 %collective-permute-start.6 = (bf16[128,1536]{1,0:T(8,128)(2,1)S(1)}, bf16[128,1536]{1,0:T(8,128)(2,1)S(1)}, u32[]{:S(2)}, u32[]{:S(2)}) collective-permute-start(bf16[128,1536]{1,0:T(8,128)(2,1)S(1)} %collective-permute-done.3), channel_id=1, source_target_pairs={{0,1},{1,2},{2,3},{3,4},{4,5},{5,6},{6,7},{7,0},{8,9},{9,10},{10,1... | collective-permute-start | bytes 1179656 | tf_op jit(solution)/shard_map/ppermute | solution.py:31
  28.0 17.6 %collective-permute-start.7 = (bf16[128,1536]{1,0:T(8,128)(2,1)S(1)}, bf16[128,1536]{1,0:T(8,128)(2,1)S(1)}, u32[]{:S(2)}, u32[]{:S(2)}) collective-permute-start(bf16[128,1536]{1,0:T(8,128)(2,1)S(1)} %collective-permute-done.4), channel_id=1, source_target_pairs={{0,7},{1,0},{2,1},{3,2},{4,3},{5,4},{6,5},{7,6},{8,15},{9,8},{10,9... | collective-permute-start | bytes 1179656 | tf_op jit(solution)/shard_map/ppermute | solution.py:31
  30.7 14.9 %collective-permute-start.13 = (bf16[128,1536]{1,0:T(8,128)(2,1)S(1)}, bf16[128,1536]{1,0:T(8,128)(2,1)S(1)}, u32[]{:S(2)}, u32[]{:S(2)}) collective-permute-start(bf16[128,1536]{1,0:T(8,128)(2,1)S(1)} %collective-permute-done.8), channel_id=1, source_target_pairs={{0,64},{32,96},{64,0},{96,32},{1,65},{33,97},{65,1},{97,33},{2,66}... | collective-permute-start | bytes 1179656 | tf_op jit(solution)/shard_map/ppermute | solution.py:42
  40.5 3.5 %collective-permute-start.12 = (bf16[128,1536]{1,0:T(8,128)(2,1)S(1)}, bf16[128,1536]{1,0:T(8,128)(2,1)S(1)}, u32[]{:S(2)}, u32[]{:S(2)}) collective-permute-start(bf16[128,1536]{1,0:T(8,128)(2,1)S(1)} %collective-permute-done.8), channel_id=1, source_target_pairs={{0,16},{16,0},{1,17},{17,1},{2,18},{18,2},{3,19},{19,3},{4,20},{20... | collective-permute-start | bytes 1179656 | tf_op jit(solution)/shard_map/ppermute | solution.py:51
  42.7 7.5 %slice-start.1 = ((s8[4718592]{0:T(1024)(128)(4,1)}), s8[524288]{0:T(1024)(128)(4,1)S(1)}, s32[]{:S(2)}) async-start(s8[4718592]{0:T(1024)(128)(4,1)} %bitcast), calls=%async_computation.1 | async-start | bytes 1048576
  42.7 15.0 %collective-permute-start.18 = (bf16[128,1536]{1,0:T(8,128)(2,1)S(1)}, bf16[128,1536]{1,0:T(8,128)(2,1)S(1)}, u32[]{:S(2)}, u32[]{:S(2)}) collective-permute-start(bf16[128,1536]{1,0:T(8,128)(2,1)S(1)} %pad_maximum_fusion.7), channel_id=1, source_target_pairs={{0,128},{128,8},{8,136},{136,0},{1,129},{129,9},{9,137},{137,1},{2... | collective-permute-start | bytes 1179656 | tf_op jit(solution)/shard_map/ppermute | solution.py:38
  44.0 13.7 %collective-permute-start.19 = (bf16[128,1536]{1,0:T(8,128)(2,1)S(1)}, bf16[128,1536]{1,0:T(8,128)(2,1)S(1)}, u32[]{:S(2)}, u32[]{:S(2)}) collective-permute-start(bf16[128,1536]{1,0:T(8,128)(2,1)S(1)} %pad_maximum_fusion.7), channel_id=1, source_target_pairs={{0,136},{128,0},{8,128},{136,8},{1,137},{129,1},{9,129},{137,9},{2... | collective-permute-start | bytes 1179656 | tf_op jit(solution)/shard_map/ppermute | solution.py:38
  45.6 9.5 %collective-permute-start.14 = (bf16[96,1536]{1,0:T(8,128)(2,1)S(1)}, bf16[96,1536]{1,0:T(8,128)(2,1)S(1)}, u32[]{:S(2)}, u32[]{:S(2)}) collective-permute-start(bf16[96,1536]{1,0:T(8,128)(2,1)S(1)} %slice.76), channel_id=1, source_target_pairs={{0,1},{1,2},{2,3},{3,4},{4,5},{5,6},{6,7},{7,0},{8,9},{9,10},{10,1... | collective-permute-start | bytes 884744 | tf_op jit(solution)/shard_map/ppermute | solution.py:31
  45.9 9.2 %collective-permute-start.15 = (bf16[96,1536]{1,0:T(8,128)(2,1)S(1)}, bf16[96,1536]{1,0:T(8,128)(2,1)S(1)}, u32[]{:S(2)}, u32[]{:S(2)}) collective-permute-start(bf16[96,1536]{1,0:T(8,128)(2,1)S(1)} %slice.77), channel_id=1, source_target_pairs={{0,7},{1,0},{2,1},{3,2},{4,3},{5,4},{6,5},{7,6},{8,15},{9,8},{10,9... | collective-permute-start | bytes 884744 | tf_op jit(solution)/shard_map/ppermute | solution.py:31
  48.9 20.7 %collective-permute-start.20 = (bf16[512,1536]{1,0:T(8,128)(2,1)S(1)}, bf16[512,1536]{1,0:T(8,128)(2,1)S(1)}, u32[]{:S(2)}, u32[]{:S(2)}) collective-permute-start(bf16[512,1536]{1,0:T(8,128)(2,1)S(1)} %pad_maximum_fusion), channel_id=1, source_target_pairs={{0,32},{16,112},{32,64},{48,16},{64,96},{80,48},{96,0},{112,80},{1... | collective-permute-start | bytes 4718600 | tf_op jit(solution)/shard_map/ppermute | solution.py:47
  55.2 4.2 %collective-permute-start.17 = (bf16[32,1536]{1,0:T(8,128)(2,1)S(1)}, bf16[32,1536]{1,0:T(8,128)(2,1)S(1)}, u32[]{:S(2)}, u32[]{:S(2)}) collective-permute-start(bf16[32,1536]{1,0:T(8,128)(2,1)S(1)} %get-tuple-element.100), channel_id=1, source_target_pairs={{0,7},{1,0},{2,1},{3,2},{4,3},{5,4},{6,5},{7,6},{8,15},{9,8},{10,9... | collective-permute-start | bytes 294920 | tf_op jit(solution)/shard_map/ppermute | solution.py:31
  57.7 5.0 %collective-permute-start.16 = (bf16[32,1536]{1,0:T(8,128)(2,1)S(1)}, bf16[32,1536]{1,0:T(8,128)(2,1)S(1)}, u32[]{:S(2)}, u32[]{:S(2)}) collective-permute-start(bf16[32,1536]{1,0:T(8,128)(2,1)S(1)} %get-tuple-element.97), channel_id=1, source_target_pairs={{0,1},{1,2},{2,3},{3,4},{4,5},{5,6},{6,7},{7,0},{8,9},{9,10},{10,1... | collective-permute-start | bytes 294920 | tf_op jit(solution)/shard_map/ppermute | solution.py:31
  64.8 4.9 %collective-permute-start.21 = (bf16[256,1536]{1,0:T(8,128)(2,1)S(1)}, bf16[256,1536]{1,0:T(8,128)(2,1)S(1)}, u32[]{:S(2)}, u32[]{:S(2)}) collective-permute-start(bf16[256,1536]{1,0:T(8,128)(2,1)S(1)} %pad_maximum_fusion.3), channel_id=1, source_target_pairs={{0,16},{16,0},{1,17},{17,1},{2,18},{18,2},{3,19},{19,3},{4,20},{20... | collective-permute-start | bytes 2359304 | tf_op jit(solution)/shard_map/ppermute | solution.py:51
  69.6 5.2 %collective-permute-start.22 = (bf16[512,1536]{1,0:T(8,128)(2,1)S(1)}, bf16[512,1536]{1,0:T(8,128)(2,1)S(1)}, u32[]{:S(2)}, u32[]{:S(2)}) collective-permute-start(bf16[512,1536]{1,0:T(8,128)(2,1)S(1)} %get-tuple-element.70), channel_id=1, source_target_pairs={{0,16},{16,0},{1,17},{17,1},{2,18},{18,2},{3,19},{19,3},{4,20},{20... | collective-permute-start | bytes 4718600 | tf_op jit(solution)/shard_map/ppermute | solution.py:51
  74.8 4.2 %collective-permute-start.28 = (bf16[512,1536]{1,0:T(8,128)(2,1)S(1)}, bf16[512,1536]{1,0:T(8,128)(2,1)S(1)}, u32[]{:S(2)}, u32[]{:S(2)}) collective-permute-start(bf16[512,1536]{1,0:T(8,128)(2,1)S(1)} %collective-permute-done.20.refs_7_.refs_5_), channel_id=1, source_target_pairs={{0,16},{16,0},{1,17},{17,1},{2,18},{18,2},{3,19},{19,3},{4,20},{20... | collective-permute-start | bytes 4718600 | tf_op jit(solution)/shard_map/ppermute | solution.py:51
  75.2 16.1 %collective-permute-start.26 = (bf16[192,1536]{1,0:T(8,128)(2,1)S(1)}, bf16[192,1536]{1,0:T(8,128)(2,1)S(1)}, u32[]{:S(2)}, u32[]{:S(2)}) collective-permute-start(bf16[192,1536]{1,0:T(8,128)(2,1)S(1)} %pad_maximum_fusion.4), channel_id=1, source_target_pairs={{0,128},{128,8},{8,136},{136,0},{1,129},{129,9},{9,137},{137,1},{2... | collective-permute-start | bytes 1769480 | tf_op jit(solution)/shard_map/ppermute | solution.py:38
  75.3 15.9 %collective-permute-start.27 = (bf16[192,1536]{1,0:T(8,128)(2,1)S(1)}, bf16[192,1536]{1,0:T(8,128)(2,1)S(1)}, u32[]{:S(2)}, u32[]{:S(2)}) collective-permute-start(bf16[192,1536]{1,0:T(8,128)(2,1)S(1)} %pad_maximum_fusion.4), channel_id=1, source_target_pairs={{0,136},{128,0},{8,128},{136,8},{1,137},{129,1},{9,129},{137,9},{2... | collective-permute-start | bytes 1769480 | tf_op jit(solution)/shard_map/ppermute | solution.py:38
  78.3 18.5 %collective-permute-start.23 = (bf16[128,1536]{1,0:T(8,128)(2,1)S(1)}, bf16[128,1536]{1,0:T(8,128)(2,1)S(1)}, u32[]{:S(2)}, u32[]{:S(2)}) collective-permute-start(bf16[128,1536]{1,0:T(8,128)(2,1)S(1)} %get-tuple-element.86), channel_id=1, source_target_pairs={{0,64},{32,96},{64,0},{96,32},{1,65},{33,97},{65,1},{97,33},{2,66}... | collective-permute-start | bytes 1179656 | tf_op jit(solution)/shard_map/ppermute | solution.py:42
  78.6 20.6 %collective-permute-start.24 = (bf16[128,1536]{1,0:T(8,128)(2,1)S(1)}, bf16[128,1536]{1,0:T(8,128)(2,1)S(1)}, u32[]{:S(2)}, u32[]{:S(2)}) collective-permute-start(bf16[128,1536]{1,0:T(8,128)(2,1)S(1)} %get-tuple-element.85), channel_id=1, source_target_pairs={{0,32},{32,64},{64,96},{96,0},{1,33},{33,65},{65,97},{97,1},{2,34}... | collective-permute-start | bytes 1179656 | tf_op jit(solution)/shard_map/ppermute | solution.py:42
  79.0 20.2 %collective-permute-start.25 = (bf16[128,1536]{1,0:T(8,128)(2,1)S(1)}, bf16[128,1536]{1,0:T(8,128)(2,1)S(1)}, u32[]{:S(2)}, u32[]{:S(2)}) collective-permute-start(bf16[128,1536]{1,0:T(8,128)(2,1)S(1)} %get-tuple-element.84), channel_id=1, source_target_pairs={{0,96},{32,0},{64,32},{96,64},{1,97},{33,1},{65,33},{97,65},{2,98}... | collective-permute-start | bytes 1179656 | tf_op jit(solution)/shard_map/ppermute | solution.py:42
  91.2 8.0 %copy-start = (bf16[128,1536]{1,0:T(8,128)(2,1)S(1)}, bf16[128,1536]{1,0:T(8,128)(2,1)}, u32[]{:S(2)}) copy-start(bf16[128,1536]{1,0:T(8,128)(2,1)} %param.3) | copy-start | bytes 1179652

commit v12 on v11

--- a/solution.py
+++ b/solution.py
@@ -172,8 +172,9 @@
         start += 64 * len(piece)
     product = lax.dot_general(grads[...], acts[...], (((0,), (0,)), ((), ())), preferred_element_type=F32)
     if sum_ref:
-        product = product + sum_ref[0][...]
-    out_ref[...] = product.astype(out_ref.dtype)
+        out_ref[...] = (product + sum_ref[0][lanes, :]).astype(BF)
+    else:
+        out_ref[lanes, :] = product
 
 
 def weight_product(layout, pieces, acts, so_far):
@@ -183,8 +184,8 @@
     return pl.pallas_call(
         functools.partial(weight_kernel, layout),
         grid=(1536 // step,),
-        in_specs=[VMEM] * (len(pieces) + 7) + [block] * last,
-        out_specs=block,
+        in_specs=[VMEM] * (len(pieces) + 7 + last),
+        out_specs=block if last else VMEM,
         out_shape=jax.ShapeDtypeStruct((1536, 1536), BF if last else F32),
         scratch_shapes=[pltpu.VMEM((count, step), BF), pltpu.VMEM((count, 1536), BF)],
         compiler_params=pltpu.CompilerParams(vmem_limit_bytes=18 << 20),
@@ -196,6 +197,7 @@
     pre_wide = pre_act.astype(F32)
     g = out_grad
     activation = gelu_tanh(pre_wide).astype(BF)
+    slope = gelu_slope(pre_wide)
 
     up1, down1, far = along_z(g, 1), along_z(g, -1), along_x(g, 2)
     act_c = swap(activation, "c")
@@ -209,7 +211,7 @@
     near = jnp.concatenate([g, up1, down1])
     left_a, right_a = along_x(near, 1), along_x(near, -1)
     other_rep, chip = tie(other_rep, chip)
-    up2, down2, hop_2 = tie(up2, down2, hop_2)
+    up2, down2, hop_2, slope = tie(up2, down2, hop_2, slope)
 
     up3, down3 = along_z(up2, 1), along_z(down2, -1)
     hop_4 = along_y(other_rep, 2)
@@ -254,7 +256,7 @@
     weight_grad = weight_product(PIECES[5:], [right_b, left_c, right_c], acts, weight_sum)
     from_across, from_below, from_above, weight_grad = tie(from_across, from_below, from_above, weight_grad)
     grad_act = summed(0) + from_below.astype(F32) + from_above.astype(F32) + from_across.astype(F32)
-    pre_grad = (grad_act * gelu_slope(pre_wide)).astype(BF)
+    pre_grad = (grad_act * slope).astype(BF)
     return (pre_grad, weight_grad)
 
 

time: 101 us -> 100 us (0.990)
    convert_element_type x2 -> x1, other arithmetic: 2.74 us -> 1.03 us  [per_device(): pre_grad = (grad_act * slope).astype(BF)]
    add x0 -> x1, other arithmetic: none -> 1.52 us  [gelu_slope(): 0.5 * (1.0 + inner)]
  transfers between devices with their start and end apart: 29 -> 29, of which waited for: 11 -> 12; matrix products, arithmetic and copies ran while one was open for 3% -> 4% of each run, Pallas kernels for 22% -> 22%
where the time goes in v12:
time: 100 us
  starting transfers between devices  42.4 us (42%)
  waiting for transfers between devices  30.1 us (30%)
  Pallas kernels  22.1 us (22%)
  other arithmetic  3.28 us (3%)
  local copies, waits for them, and re-layouts  1.33 us (1%)
    ppermute x10, starting transfers between devices, along_z(): return lax.ppermute(a, 'z', [(i, (i + d) % Z) for i in range(Z)])  17.5 us
    pallas_call x2, Pallas kernels, weight_product(): pl.pallas_call(functools.partial(weight_kernel, layout), grid=(1536 // st...  15.4 us
    ppermute x6, waiting for transfers between devices, swap(): return lax.ppermute(a, axis, [(0, 1), (1, 0)])  11.7 us
    ppermute x7, waiting for transfers between devices, along_x(): lax.ppermute(a, ('xl', 'xh'), [(place(x), place((x + d) % 4)) for x in ra...  9.61 us
    ppermute x6, starting transfers between devices, swap(): return lax.ppermute(a, axis, [(0, 1), (1, 0)])  9.28 us
    ppermute x7, starting transfers between devices, along_x(): lax.ppermute(a, ('xl', 'xh'), [(place(x), place((x + d) % 4)) for x in ra...  8.68 us
    ppermute x10, waiting for transfers between devices, along_z(): return lax.ppermute(a, 'z', [(i, (i + d) % Z) for i in range(Z)])  6.54 us
    ppermute x5, starting transfers between devices, along_y(): return lax.ppermute(a, 'y', [(i, (i + d) % Y) for i in range(Y)])  5.96 us
  transfers between devices with their start and end apart: 29, of which 12 were waited for; matrix products, arithmetic and copies ran while one was open for 4% of the time, Pallas kernels for 22%

profile of v12, /device:TPU:1, one launch (start us, length us, event | category | flops | bytes accessed | tf_op | source)
XLA Modules:
  0.0 100.2 jit_solution(10170659106590218347)
XLA Ops:
  0.6 2.5 %collective-permute-start = (bf16[64,1536]{1,0:T(8,128)(2,1)}, bf16[64,1536]{1,0:T(8,128)(2,1)S(1)}, u32[]{:S(2)}, u32[]{:S(2)}) collective-permute-start(bf16[64,1536]{1,0:T(8,128)(2,1)} %param.4), channel_id=1, source_target_pairs={{0,1},{1,2},{2,3},{3,4},{4,5},{5,6},{6,7},{7,0},{8,9},{9,10},{10,1... | collective-permute-start | bytes 589832 | tf_op jit(solution)/shard_map/ppermute | solution.py:31
  3.2 4.0 %collective-permute-start.1 = (bf16[64,1536]{1,0:T(8,128)(2,1)}, bf16[64,1536]{1,0:T(8,128)(2,1)S(1)}, u32[]{:S(2)}, u32[]{:S(2)}) collective-permute-start(bf16[64,1536]{1,0:T(8,128)(2,1)} %param.4), channel_id=1, source_target_pairs={{0,7},{1,0},{2,1},{3,2},{4,3},{5,4},{6,5},{7,6},{8,15},{9,8},{10,9... | collective-permute-start | bytes 589832 | tf_op jit(solution)/shard_map/ppermute | solution.py:31
  7.2 2.7 %collective-permute-start.2 = (bf16[64,1536]{1,0:T(8,128)(2,1)}, bf16[64,1536]{1,0:T(8,128)(2,1)S(1)}, u32[]{:S(2)}, u32[]{:S(2)}) collective-permute-start(bf16[64,1536]{1,0:T(8,128)(2,1)} %param.4), channel_id=1, source_target_pairs={{0,8},{128,136},{8,0},{136,128},{1,9},{129,137},{9,1},{137,129},{2... | collective-permute-start | bytes 589832 | tf_op jit(solution)/shard_map/ppermute | solution.py:38
  9.9 1.5 %fusion.5 = (f32[128,1536]{1,0:T(8,128)S(1)}, bf16[128,1536]{1,0:T(8,128)(2,1)S(1)}) fusion(bf16[128,1536]{1,0:T(8,128)(2,1)} %param.3), kind=kLoop, calls=%fused_computation.13 | loop fusion | flops 3932160 | bytes 1572864 | tf_op jit(solution)/shard_map/add | solution.py:25
  11.5 1.3 %collective-permute-start.9 = (bf16[128,1536]{1,0:T(8,128)(2,1)S(1)}, bf16[128,1536]{1,0:T(8,128)(2,1)S(1)}, u32[]{:S(2)}, u32[]{:S(2)}) collective-permute-start(bf16[128,1536]{1,0:T(8,128)(2,1)S(1)} %get-tuple-element.49), channel_id=1, source_target_pairs={{0,16},{16,0},{1,17},{17,1},{2,18},{18,2},{3,19},{19,3},{4,20},{20... | collective-permute-start | bytes 1179656 | tf_op jit(solution)/shard_map/ppermute | solution.py:51
  12.8 2.9 %collective-permute-start.5 = (bf16[128,1536]{1,0:T(8,128)(2,1)S(1)}, bf16[128,1536]{1,0:T(8,128)(2,1)S(1)}, u32[]{:S(2)}, u32[]{:S(2)}) collective-permute-start(bf16[128,1536]{1,0:T(8,128)(2,1)S(1)} %get-tuple-element.49), channel_id=1, source_target_pairs={{0,64},{32,96},{64,0},{96,32},{1,65},{33,97},{65,1},{97,33},{2,66}... | collective-permute-start | bytes 1179656 | tf_op jit(solution)/shard_map/ppermute | solution.py:42
  17.3 2.7 %collective-permute-start.4 = (bf16[128,1536]{1,0:T(8,128)(2,1)S(1)}, bf16[128,1536]{1,0:T(8,128)(2,1)S(1)}, u32[]{:S(2)}, u32[]{:S(2)}) collective-permute-start(bf16[128,1536]{1,0:T(8,128)(2,1)S(1)} %get-tuple-element.111), channel_id=1, source_target_pairs={{0,7},{1,0},{2,1},{3,2},{4,3},{5,4},{6,5},{7,6},{8,15},{9,8},{10,9... | collective-permute-start | bytes 1179656 | tf_op jit(solution)/shard_map/ppermute | solution.py:31
  20.0 1.2 %collective-permute-start.10 = (bf16[192,1536]{1,0:T(8,128)(2,1)S(1)}, bf16[192,1536]{1,0:T(8,128)(2,1)S(1)}, u32[]{:S(2)}, u32[]{:S(2)}) collective-permute-start(bf16[192,1536]{1,0:T(8,128)(2,1)S(1)} %get-tuple-element.106), channel_id=1, source_target_pairs={{0,128},{128,8},{8,136},{136,0},{1,129},{129,9},{9,137},{137,1},{2... | collective-permute-start | bytes 1769480 | tf_op jit(solution)/shard_map/ppermute | solution.py:38
  21.2 5.9 %collective-permute-done.8 = bf16[128,1536]{1,0:T(8,128)(2,1)S(1)} collective-permute-done((bf16[128,1536]{1,0:T(8,128)(2,1)S(1)}, bf16[128,1536]{1,0:T(8,128)(2,1)S(1)}, u32[]{:S(2)}, u32[]{:S(2)}) %collective-permute-start.8) | collective-permute-done | bytes 393248 | tf_op jit(solution)/shard_map/ppermute | solution.py:51
  27.3 1.2 %collective-permute-done.3 = bf16[128,1536]{1,0:T(8,128)(2,1)S(1)} collective-permute-done((bf16[128,1536]{1,0:T(8,128)(2,1)S(1)}, bf16[128,1536]{1,0:T(8,128)(2,1)S(1)}, u32[]{:S(2)}, u32[]{:S(2)}) %collective-permute-start.3) | collective-permute-done | bytes 393248 | tf_op jit(solution)/shard_map/ppermute | solution.py:31
  28.5 2.7 %collective-permute-start.7 = (bf16[128,1536]{1,0:T(8,128)(2,1)S(1)}, bf16[128,1536]{1,0:T(8,128)(2,1)S(1)}, u32[]{:S(2)}, u32[]{:S(2)}) collective-permute-start(bf16[128,1536]{1,0:T(8,128)(2,1)S(1)} %collective-permute-done.4), channel_id=1, source_target_pairs={{0,7},{1,0},{2,1},{3,2},{4,3},{5,4},{6,5},{7,6},{8,15},{9,8},{10,9... | collective-permute-start | bytes 1179656 | tf_op jit(solution)/shard_map/ppermute | solution.py:31
  31.4 6.5 %collective-permute-done.10.refs_2_ = bf16[192,1536]{1,0:T(8,128)(2,1)S(1)} collective-permute-done((bf16[192,1536]{1,0:T(8,128)(2,1)S(1)}, bf16[192,1536]{1,0:T(8,128)(2,1)S(1)}, u32[]{:S(2)}, u32[]{:S(2)}) %collective-permute-start.10) | collective-permute-done | bytes 589856 | tf_op jit(solution)/shard_map/ppermute | solution.py:38
  37.9 2.9 %collective-permute-done.11.refs_3_ = bf16[192,1536]{1,0:T(8,128)(2,1)S(1)} collective-permute-done((bf16[192,1536]{1,0:T(8,128)(2,1)S(1)}, bf16[192,1536]{1,0:T(8,128)(2,1)S(1)}, u32[]{:S(2)}, u32[]{:S(2)}) %collective-permute-start.11) | collective-permute-done | bytes 589856 | tf_op jit(solution)/shard_map/ppermute | solution.py:38
  40.8 2.1 %collective-permute-start.12 = (bf16[128,1536]{1,0:T(8,128)(2,1)S(1)}, bf16[128,1536]{1,0:T(8,128)(2,1)S(1)}, u32[]{:S(2)}, u32[]{:S(2)}) collective-permute-start(bf16[128,1536]{1,0:T(8,128)(2,1)S(1)} %collective-permute-done.8), channel_id=1, source_target_pairs={{0,16},{16,0},{1,17},{17,1},{2,18},{18,2},{3,19},{19,3},{4,20},{20... | collective-permute-start | bytes 1179656 | tf_op jit(solution)/shard_map/ppermute | solution.py:51
  44.2 1.5 %collective-permute-start.19 = (bf16[128,1536]{1,0:T(8,128)(2,1)S(1)}, bf16[128,1536]{1,0:T(8,128)(2,1)S(1)}, u32[]{:S(2)}, u32[]{:S(2)}) collective-permute-start(bf16[128,1536]{1,0:T(8,128)(2,1)S(1)} %pad_maximum_fusion.7), channel_id=1, source_target_pairs={{0,136},{128,0},{8,128},{136,8},{1,137},{129,1},{9,129},{137,9},{2... | collective-permute-start | bytes 1179656 | tf_op jit(solution)/shard_map/ppermute | solution.py:38
  46.1 2.7 %collective-permute-start.15 = (bf16[96,1536]{1,0:T(8,128)(2,1)S(1)}, bf16[96,1536]{1,0:T(8,128)(2,1)S(1)}, u32[]{:S(2)}, u32[]{:S(2)}) collective-permute-start(bf16[96,1536]{1,0:T(8,128)(2,1)S(1)} %slice.77), channel_id=1, source_target_pairs={{0,7},{1,0},{2,1},{3,2},{4,3},{5,4},{6,5},{7,6},{8,15},{9,8},{10,9... | collective-permute-start | bytes 884744 | tf_op jit(solution)/shard_map/ppermute | solution.py:31
  49.2 1.0 collective-permute-start.20
  50.2 4.8 %shard_map.50.early_ref = f32[768,1536]{1,0:T(8,128)S(1)} custom-call(bf16[768,1536]{1,0:T(8,128)(2,1)S(1)} %slice_dynamic-update-slice_fusion.2.grads_ref.refs_0_, bf16[1536,1536]{1,0:T(8,128)(2,1)S(1)} %bitcast.1), custom_call_target="tpu_custom_call" | custom-call | flops 3623878656 | bytes 12582912 | tf_op jit(solution)/shard_map/pallas_call | solution.py:73
  55.4 2.5 %collective-permute-start.17 = (bf16[32,1536]{1,0:T(8,128)(2,1)S(1)}, bf16[32,1536]{1,0:T(8,128)(2,1)S(1)}, u32[]{:S(2)}, u32[]{:S(2)}) collective-permute-start(bf16[32,1536]{1,0:T(8,128)(2,1)S(1)} %get-tuple-element.104), channel_id=1, source_target_pairs={{0,7},{1,0},{2,1},{3,2},{4,3},{5,4},{6,5},{7,6},{8,15},{9,8},{10,9... | collective-permute-start | bytes 294920 | tf_op jit(solution)/shard_map/ppermute | solution.py:31
  58.0 1.6 %collective-permute-done.17 = bf16[32,1536]{1,0:T(8,128)(2,1)S(1)} collective-permute-done((bf16[32,1536]{1,0:T(8,128)(2,1)S(1)}, bf16[32,1536]{1,0:T(8,128)(2,1)S(1)}, u32[]{:S(2)}, u32[]{:S(2)}) %collective-permute-start.17) | collective-permute-done | bytes 98336 | tf_op jit(solution)/shard_map/ppermute | solution.py:31
  59.6 3.3 %collective-permute-done.16 = bf16[32,1536]{1,0:T(8,128)(2,1)S(1)} collective-permute-done((bf16[32,1536]{1,0:T(8,128)(2,1)S(1)}, bf16[32,1536]{1,0:T(8,128)(2,1)S(1)}, u32[]{:S(2)}, u32[]{:S(2)}) %collective-permute-start.16) | collective-permute-done | bytes 98336 | tf_op jit(solution)/shard_map/ppermute | solution.py:31
  62.9 2.0 %shard_map.51 = (f32[512,1536]{1,0:T(8,128)S(1)}, bf16[512,1536]{1,0:T(8,128)(2,1)S(1)}) custom-call(f32[768,1536]{1,0:T(8,128)S(1)} %shard_map.50.early_ref, bf16[256,1536]{1,0:T(8,128)(2,1)S(1)} %constant_dynamic-update-slice_fusion.11.grads_ref.refs_1_, bf16[1536,1536]{1,0:T(8,128)(2,1)S(1)} %bitcast.1), custom_call_target="tpu_custom_call" | custom-call | flops 1207959552 | bytes 8388608 | tf_op jit(solution)/shard_map/pallas_call | solution.py:111
  65.0 2.9 %collective-permute-start.21 = (bf16[256,1536]{1,0:T(8,128)(2,1)S(1)}, bf16[256,1536]{1,0:T(8,128)(2,1)S(1)}, u32[]{:S(2)}, u32[]{:S(2)}) collective-permute-start(bf16[256,1536]{1,0:T(8,128)(2,1)S(1)} %pad_maximum_fusion.3), channel_id=1, source_target_pairs={{0,16},{16,0},{1,17},{17,1},{2,18},{18,2},{3,19},{19,3},{4,20},{20... | collective-permute-start | bytes 2359304 | tf_op jit(solution)/shard_map/ppermute | solution.py:51
  68.0 1.9 %collective-permute-done.21.refs_11_.refs_9_ = bf16[256,1536]{1,0:T(8,128)(2,1)S(1)} collective-permute-done((bf16[256,1536]{1,0:T(8,128)(2,1)S(1)}, bf16[256,1536]{1,0:T(8,128)(2,1)S(1)}, u32[]{:S(2)}, u32[]{:S(2)}) %collective-permute-start.21) | collective-permute-done | bytes 786464 | tf_op jit(solution)/shard_map/ppermute | solution.py:51
  69.9 2.1 %collective-permute-start.22 = (bf16[512,1536]{1,0:T(8,128)(2,1)S(1)}, bf16[512,1536]{1,0:T(8,128)(2,1)S(1)}, u32[]{:S(2)}, u32[]{:S(2)}) collective-permute-start(bf16[512,1536]{1,0:T(8,128)(2,1)S(1)} %get-tuple-element.71), channel_id=1, source_target_pairs={{0,16},{16,0},{1,17},{17,1},{2,18},{18,2},{3,19},{19,3},{4,20},{20... | collective-permute-start | bytes 4718600 | tf_op jit(solution)/shard_map/ppermute | solution.py:51
  72.0 3.0 %collective-permute-done.22 = bf16[512,1536]{1,0:T(8,128)(2,1)S(1)} collective-permute-done((bf16[512,1536]{1,0:T(8,128)(2,1)S(1)}, bf16[512,1536]{1,0:T(8,128)(2,1)S(1)}, u32[]{:S(2)}, u32[]{:S(2)}) %collective-permute-start.22) | collective-permute-done | bytes 1572896 | tf_op jit(solution)/shard_map/ppermute | solution.py:51
  75.6 2.6 %collective-permute-start.27 = (bf16[192,1536]{1,0:T(8,128)(2,1)S(1)}, bf16[192,1536]{1,0:T(8,128)(2,1)S(1)}, u32[]{:S(2)}, u32[]{:S(2)}) collective-permute-start(bf16[192,1536]{1,0:T(8,128)(2,1)S(1)} %pad_maximum_fusion.4), channel_id=1, source_target_pairs={{0,136},{128,0},{8,128},{136,8},{1,137},{129,1},{9,129},{137,9},{2... | collective-permute-start | bytes 1769480 | tf_op jit(solution)/shard_map/ppermute | solution.py:38
  79.0 2.4 %collective-permute-start.25 = (bf16[128,1536]{1,0:T(8,128)(2,1)S(1)}, bf16[128,1536]{1,0:T(8,128)(2,1)S(1)}, u32[]{:S(2)}, u32[]{:S(2)}) collective-permute-start(bf16[128,1536]{1,0:T(8,128)(2,1)S(1)} %get-tuple-element.86), channel_id=1, source_target_pairs={{0,96},{32,0},{64,32},{96,64},{1,97},{33,1},{65,33},{97,65},{2,98}... | collective-permute-start | bytes 1179656 | tf_op jit(solution)/shard_map/ppermute | solution.py:42
  81.4 9.9 %shard_map.52.refs_10_ = f32[1536,1536]{1,0:T(8,128)S(1)} custom-call(bf16[768,1536]{1,0:T(8,128)(2,1)S(1)} %slice_dynamic-update-slice_fusion.2.grads_ref.refs_0_, bf16[256,1536]{1,0:T(8,128)(2,1)S(1)} %constant_dynamic-update-slice_fusion.11.grads_ref.refs_1_, bf16[192,1536]{1,0:T(8,128)(2,1)S(1)} %collective-permute-done.10.refs_2_, ...), custom_call_target="tpu_custom_call" | custom-call | flops 7247757312 | bytes 12582912 | tf_op jit(solution)/shard_map/pallas_call | solution.py:184
  91.5 5.5 %shard_map.53 = bf16[1536,1536]{1,0:T(8,128)(2,1)} custom-call(bf16[128,1536]{1,0:T(8,128)(2,1)S(1)} %collective-permute-done.19.refs_0_, bf16[192,1536]{1,0:T(8,128)(2,1)S(1)} %collective-permute-done.26.refs_1_, bf16[192,1536]{1,0:T(8,128)(2,1)S(1)} %collective-permute-done.27.refs_2_, bf16[256,1536]{1,0:T(8,128)(2,1)S(1)} %pad_maximum_fusion.1.refs_5_.refs_3_, ...), custom_call_target="tpu_custom_call" | custom-call | flops 2415919104 | bytes 12582912 | tf_op jit(solution)/shard_map/pallas_call | solution.py:184
  97.0 2.2 %collective-permute-done.24 = bf16[128,1536]{1,0:T(8,128)(2,1)S(1)} collective-permute-done((bf16[128,1536]{1,0:T(8,128)(2,1)S(1)}, bf16[128,1536]{1,0:T(8,128)(2,1)S(1)}, u32[]{:S(2)}, u32[]{:S(2)}) %collective-permute-start.24) | collective-permute-done | bytes 393248 | tf_op jit(solution)/shard_map/ppermute | solution.py:42
  99.2 1.0 %multiply_convert_fusion = bf16[128,1536]{1,0:T(8,128)(2,1)} fusion(f32[128,1536]{1,0:T(8,128)S(1)} %get-tuple-element.84, bf16[128,1536]{1,0:T(8,128)(2,1)S(1)} %collective-permute-done.23, bf16[128,1536]{1,0:T(8,128)(2,1)S(1)} %collective-permute-done.25, bf16[128,1536]{1,0:T(8,128)(2,1)S(1)} %collective-permute-done.24, ...), kind=kLoop, calls=%fused_computation.20 | loop fusion | flops 1966080 | bytes 3538944 | tf_op jit(solution)/shard_map/convert_element_type | solution.py:259
  (66 shorter events, 5.9 us)
Async XLA Ops:
  0.6 16.1 %collective-permute-start = (bf16[64,1536]{1,0:T(8,128)(2,1)}, bf16[64,1536]{1,0:T(8,128)(2,1)S(1)}, u32[]{:S(2)}, u32[]{:S(2)}) collective-permute-start(bf16[64,1536]{1,0:T(8,128)(2,1)} %param.4), channel_id=1, source_target_pairs={{0,1},{1,2},{2,3},{3,4},{4,5},{5,6},{6,7},{7,0},{8,9},{9,10},{10,1... | collective-permute-start | bytes 589832 | tf_op jit(solution)/shard_map/ppermute | solution.py:31
  3.2 13.5 %collective-permute-start.1 = (bf16[64,1536]{1,0:T(8,128)(2,1)}, bf16[64,1536]{1,0:T(8,128)(2,1)S(1)}, u32[]{:S(2)}, u32[]{:S(2)}) collective-permute-start(bf16[64,1536]{1,0:T(8,128)(2,1)} %param.4), channel_id=1, source_target_pairs={{0,7},{1,0},{2,1},{3,2},{4,3},{5,4},{6,5},{7,6},{8,15},{9,8},{10,9... | collective-permute-start | bytes 589832 | tf_op jit(solution)/shard_map/ppermute | solution.py:31
  7.2 9.5 %collective-permute-start.2 = (bf16[64,1536]{1,0:T(8,128)(2,1)}, bf16[64,1536]{1,0:T(8,128)(2,1)S(1)}, u32[]{:S(2)}, u32[]{:S(2)}) collective-permute-start(bf16[64,1536]{1,0:T(8,128)(2,1)} %param.4), channel_id=1, source_target_pairs={{0,8},{128,136},{8,0},{136,128},{1,9},{129,137},{9,1},{137,129},{2... | collective-permute-start | bytes 589832 | tf_op jit(solution)/shard_map/ppermute | solution.py:38
  11.5 8.5 %collective-permute-start.9 = (bf16[128,1536]{1,0:T(8,128)(2,1)S(1)}, bf16[128,1536]{1,0:T(8,128)(2,1)S(1)}, u32[]{:S(2)}, u32[]{:S(2)}) collective-permute-start(bf16[128,1536]{1,0:T(8,128)(2,1)S(1)} %get-tuple-element.49), channel_id=1, source_target_pairs={{0,16},{16,0},{1,17},{17,1},{2,18},{18,2},{3,19},{19,3},{4,20},{20... | collective-permute-start | bytes 1179656 | tf_op jit(solution)/shard_map/ppermute | solution.py:51
  12.8 14.5 %collective-permute-start.5 = (bf16[128,1536]{1,0:T(8,128)(2,1)S(1)}, bf16[128,1536]{1,0:T(8,128)(2,1)S(1)}, u32[]{:S(2)}, u32[]{:S(2)}) collective-permute-start(bf16[128,1536]{1,0:T(8,128)(2,1)S(1)} %get-tuple-element.49), channel_id=1, source_target_pairs={{0,64},{32,96},{64,0},{96,32},{1,65},{33,97},{65,1},{97,33},{2,66}... | collective-permute-start | bytes 1179656 | tf_op jit(solution)/shard_map/ppermute | solution.py:42
  16.7 10.4 %collective-permute-start.8 = (bf16[128,1536]{1,0:T(8,128)(2,1)S(1)}, bf16[128,1536]{1,0:T(8,128)(2,1)S(1)}, u32[]{:S(2)}, u32[]{:S(2)}) collective-permute-start(bf16[128,1536]{1,0:T(8,128)(2,1)S(1)} %get-tuple-element.49), channel_id=1, source_target_pairs={{0,128},{128,0},{1,129},{129,1},{2,130},{130,2},{3,131},{131,3},{4... | collective-permute-start | bytes 1179656 | tf_op jit(solution)/shard_map/ppermute | solution.py:51
  17.1 33.0 %slice-start = ((s8[4718592]{0:T(1024)(128)(4,1)}), s8[4194304]{0:T(1024)(128)(4,1)S(1)}, s32[]{:S(2)}) async-start(s8[4718592]{0:T(1024)(128)(4,1)} %bitcast), calls=%async_computation | async-start | bytes 8388608
  17.2 11.3 %collective-permute-start.3 = (bf16[128,1536]{1,0:T(8,128)(2,1)S(1)}, bf16[128,1536]{1,0:T(8,128)(2,1)S(1)}, u32[]{:S(2)}, u32[]{:S(2)}) collective-permute-start(bf16[128,1536]{1,0:T(8,128)(2,1)S(1)} %get-tuple-element.112), channel_id=1, source_target_pairs={{0,1},{1,2},{2,3},{3,4},{4,5},{5,6},{6,7},{7,0},{8,9},{9,10},{10,1... | collective-permute-start | bytes 1179656 | tf_op jit(solution)/shard_map/ppermute | solution.py:31
  17.3 11.2 %collective-permute-start.4 = (bf16[128,1536]{1,0:T(8,128)(2,1)S(1)}, bf16[128,1536]{1,0:T(8,128)(2,1)S(1)}, u32[]{:S(2)}, u32[]{:S(2)}) collective-permute-start(bf16[128,1536]{1,0:T(8,128)(2,1)S(1)} %get-tuple-element.111), channel_id=1, source_target_pairs={{0,7},{1,0},{2,1},{3,2},{4,3},{5,4},{6,5},{7,6},{8,15},{9,8},{10,9... | collective-permute-start | bytes 1179656 | tf_op jit(solution)/shard_map/ppermute | solution.py:31
  20.0 17.9 %collective-permute-start.10 = (bf16[192,1536]{1,0:T(8,128)(2,1)S(1)}, bf16[192,1536]{1,0:T(8,128)(2,1)S(1)}, u32[]{:S(2)}, u32[]{:S(2)}) collective-permute-start(bf16[192,1536]{1,0:T(8,128)(2,1)S(1)} %get-tuple-element.106), channel_id=1, source_target_pairs={{0,128},{128,8},{8,136},{136,0},{1,129},{129,9},{9,137},{137,1},{2... | collective-permute-start | bytes 1769480 | tf_op jit(solution)/shard_map/ppermute | solution.py:38
  27.1 13.6 %collective-permute-start.11 = (bf16[192,1536]{1,0:T(8,128)(2,1)S(1)}, bf16[192,1536]{1,0:T(8,128)(2,1)S(1)}, u32[]{:S(2)}, u32[]{:S(2)}) collective-permute-start(bf16[192,1536]{1,0:T(8,128)(2,1)S(1)} %get-tuple-element.106), channel_id=1, source_target_pairs={{0,136},{128,0},{8,128},{136,8},{1,137},{129,1},{9,129},{137,9},{2... | collective-permute-start | bytes 1769480 | tf_op jit(solution)/shard_map/ppermute | solution.py:38
  28.5 17.3 %collective-permute-start.6 = (bf16[128,1536]{1,0:T(8,128)(2,1)S(1)}, bf16[128,1536]{1,0:T(8,128)(2,1)S(1)}, u32[]{:S(2)}, u32[]{:S(2)}) collective-permute-start(bf16[128,1536]{1,0:T(8,128)(2,1)S(1)} %collective-permute-done.3), channel_id=1, source_target_pairs={{0,1},{1,2},{2,3},{3,4},{4,5},{5,6},{6,7},{7,0},{8,9},{9,10},{10,1... | collective-permute-start | bytes 1179656 | tf_op jit(solution)/shard_map/ppermute | solution.py:31
  28.5 17.3 %collective-permute-start.7 = (bf16[128,1536]{1,0:T(8,128)(2,1)S(1)}, bf16[128,1536]{1,0:T(8,128)(2,1)S(1)}, u32[]{:S(2)}, u32[]{:S(2)}) collective-permute-start(bf16[128,1536]{1,0:T(8,128)(2,1)S(1)} %collective-permute-done.4), channel_id=1, source_target_pairs={{0,7},{1,0},{2,1},{3,2},{4,3},{5,4},{6,5},{7,6},{8,15},{9,8},{10,9... | collective-permute-start | bytes 1179656 | tf_op jit(solution)/shard_map/ppermute | solution.py:31
  31.2 14.6 %collective-permute-start.13 = (bf16[128,1536]{1,0:T(8,128)(2,1)S(1)}, bf16[128,1536]{1,0:T(8,128)(2,1)S(1)}, u32[]{:S(2)}, u32[]{:S(2)}) collective-permute-start(bf16[128,1536]{1,0:T(8,128)(2,1)S(1)} %collective-permute-done.8), channel_id=1, source_target_pairs={{0,64},{32,96},{64,0},{96,32},{1,65},{33,97},{65,1},{97,33},{2,66}... | collective-permute-start | bytes 1179656 | tf_op jit(solution)/shard_map/ppermute | solution.py:42
  40.8 3.5 %collective-permute-start.12 = (bf16[128,1536]{1,0:T(8,128)(2,1)S(1)}, bf16[128,1536]{1,0:T(8,128)(2,1)S(1)}, u32[]{:S(2)}, u32[]{:S(2)}) collective-permute-start(bf16[128,1536]{1,0:T(8,128)(2,1)S(1)} %collective-permute-done.8), channel_id=1, source_target_pairs={{0,16},{16,0},{1,17},{17,1},{2,18},{18,2},{3,19},{19,3},{4,20},{20... | collective-permute-start | bytes 1179656 | tf_op jit(solution)/shard_map/ppermute | solution.py:51
  43.0 7.2 %slice-start.1 = ((s8[4718592]{0:T(1024)(128)(4,1)}), s8[524288]{0:T(1024)(128)(4,1)S(1)}, s32[]{:S(2)}) async-start(s8[4718592]{0:T(1024)(128)(4,1)} %bitcast), calls=%async_computation.1 | async-start | bytes 1048576
  43.0 15.0 %collective-permute-start.18 = (bf16[128,1536]{1,0:T(8,128)(2,1)S(1)}, bf16[128,1536]{1,0:T(8,128)(2,1)S(1)}, u32[]{:S(2)}, u32[]{:S(2)}) collective-permute-start(bf16[128,1536]{1,0:T(8,128)(2,1)S(1)} %pad_maximum_fusion.7), channel_id=1, source_target_pairs={{0,128},{128,8},{8,136},{136,0},{1,129},{129,9},{9,137},{137,1},{2... | collective-permute-start | bytes 1179656 | tf_op jit(solution)/shard_map/ppermute | solution.py:38
  44.2 13.7 %collective-permute-start.19 = (bf16[128,1536]{1,0:T(8,128)(2,1)S(1)}, bf16[128,1536]{1,0:T(8,128)(2,1)S(1)}, u32[]{:S(2)}, u32[]{:S(2)}) collective-permute-start(bf16[128,1536]{1,0:T(8,128)(2,1)S(1)} %pad_maximum_fusion.7), channel_id=1, source_target_pairs={{0,136},{128,0},{8,128},{136,8},{1,137},{129,1},{9,129},{137,9},{2... | collective-permute-start | bytes 1179656 | tf_op jit(solution)/shard_map/ppermute | solution.py:38
  45.8 9.5 %collective-permute-start.14 = (bf16[96,1536]{1,0:T(8,128)(2,1)S(1)}, bf16[96,1536]{1,0:T(8,128)(2,1)S(1)}, u32[]{:S(2)}, u32[]{:S(2)}) collective-permute-start(bf16[96,1536]{1,0:T(8,128)(2,1)S(1)} %slice.76), channel_id=1, source_target_pairs={{0,1},{1,2},{2,3},{3,4},{4,5},{5,6},{6,7},{7,0},{8,9},{9,10},{10,1... | collective-permute-start | bytes 884744 | tf_op jit(solution)/shard_map/ppermute | solution.py:31
  46.1 9.2 %collective-permute-start.15 = (bf16[96,1536]{1,0:T(8,128)(2,1)S(1)}, bf16[96,1536]{1,0:T(8,128)(2,1)S(1)}, u32[]{:S(2)}, u32[]{:S(2)}) collective-permute-start(bf16[96,1536]{1,0:T(8,128)(2,1)S(1)} %slice.77), channel_id=1, source_target_pairs={{0,7},{1,0},{2,1},{3,2},{4,3},{5,4},{6,5},{7,6},{8,15},{9,8},{10,9... | collective-permute-start | bytes 884744 | tf_op jit(solution)/shard_map/ppermute | solution.py:31
  49.2 20.7 %collective-permute-start.20 = (bf16[512,1536]{1,0:T(8,128)(2,1)S(1)}, bf16[512,1536]{1,0:T(8,128)(2,1)S(1)}, u32[]{:S(2)}, u32[]{:S(2)}) collective-permute-start(bf16[512,1536]{1,0:T(8,128)(2,1)S(1)} %pad_maximum_fusion), channel_id=1, source_target_pairs={{0,32},{16,112},{32,64},{48,16},{64,96},{80,48},{96,0},{112,80},{1... | collective-permute-start | bytes 4718600 | tf_op jit(solution)/shard_map/ppermute | solution.py:47
  55.4 4.2 %collective-permute-start.17 = (bf16[32,1536]{1,0:T(8,128)(2,1)S(1)}, bf16[32,1536]{1,0:T(8,128)(2,1)S(1)}, u32[]{:S(2)}, u32[]{:S(2)}) collective-permute-start(bf16[32,1536]{1,0:T(8,128)(2,1)S(1)} %get-tuple-element.104), channel_id=1, source_target_pairs={{0,7},{1,0},{2,1},{3,2},{4,3},{5,4},{6,5},{7,6},{8,15},{9,8},{10,9... | collective-permute-start | bytes 294920 | tf_op jit(solution)/shard_map/ppermute | solution.py:31
  57.9 5.0 %collective-permute-start.16 = (bf16[32,1536]{1,0:T(8,128)(2,1)S(1)}, bf16[32,1536]{1,0:T(8,128)(2,1)S(1)}, u32[]{:S(2)}, u32[]{:S(2)}) collective-permute-start(bf16[32,1536]{1,0:T(8,128)(2,1)S(1)} %get-tuple-element.101), channel_id=1, source_target_pairs={{0,1},{1,2},{2,3},{3,4},{4,5},{5,6},{6,7},{7,0},{8,9},{9,10},{10,1... | collective-permute-start | bytes 294920 | tf_op jit(solution)/shard_map/ppermute | solution.py:31
  65.0 4.9 %collective-permute-start.21 = (bf16[256,1536]{1,0:T(8,128)(2,1)S(1)}, bf16[256,1536]{1,0:T(8,128)(2,1)S(1)}, u32[]{:S(2)}, u32[]{:S(2)}) collective-permute-start(bf16[256,1536]{1,0:T(8,128)(2,1)S(1)} %pad_maximum_fusion.3), channel_id=1, source_target_pairs={{0,16},{16,0},{1,17},{17,1},{2,18},{18,2},{3,19},{19,3},{4,20},{20... | collective-permute-start | bytes 2359304 | tf_op jit(solution)/shard_map/ppermute | solution.py:51
  69.9 5.2 %collective-permute-start.22 = (bf16[512,1536]{1,0:T(8,128)(2,1)S(1)}, bf16[512,1536]{1,0:T(8,128)(2,1)S(1)}, u32[]{:S(2)}, u32[]{:S(2)}) collective-permute-start(bf16[512,1536]{1,0:T(8,128)(2,1)S(1)} %get-tuple-element.71), channel_id=1, source_target_pairs={{0,16},{16,0},{1,17},{17,1},{2,18},{18,2},{3,19},{19,3},{4,20},{20... | collective-permute-start | bytes 4718600 | tf_op jit(solution)/shard_map/ppermute | solution.py:51
  75.0 4.0 %collective-permute-start.28 = (bf16[512,1536]{1,0:T(8,128)(2,1)S(1)}, bf16[512,1536]{1,0:T(8,128)(2,1)S(1)}, u32[]{:S(2)}, u32[]{:S(2)}) collective-permute-start(bf16[512,1536]{1,0:T(8,128)(2,1)S(1)} %collective-permute-done.20.refs_7_.refs_5_), channel_id=1, source_target_pairs={{0,16},{16,0},{1,17},{17,1},{2,18},{18,2},{3,19},{19,3},{4,20},{20... | collective-permute-start | bytes 4718600 | tf_op jit(solution)/shard_map/ppermute | solution.py:51
  75.4 16.1 %collective-permute-start.26 = (bf16[192,1536]{1,0:T(8,128)(2,1)S(1)}, bf16[192,1536]{1,0:T(8,128)(2,1)S(1)}, u32[]{:S(2)}, u32[]{:S(2)}) collective-permute-start(bf16[192,1536]{1,0:T(8,128)(2,1)S(1)} %pad_maximum_fusion.4), channel_id=1, source_target_pairs={{0,128},{128,8},{8,136},{136,0},{1,129},{129,9},{9,137},{137,1},{2... | collective-permute-start | bytes 1769480 | tf_op jit(solution)/shard_map/ppermute | solution.py:38
  75.6 15.9 %collective-permute-start.27 = (bf16[192,1536]{1,0:T(8,128)(2,1)S(1)}, bf16[192,1536]{1,0:T(8,128)(2,1)S(1)}, u32[]{:S(2)}, u32[]{:S(2)}) collective-permute-start(bf16[192,1536]{1,0:T(8,128)(2,1)S(1)} %pad_maximum_fusion.4), channel_id=1, source_target_pairs={{0,136},{128,0},{8,128},{136,8},{1,137},{129,1},{9,129},{137,9},{2... | collective-permute-start | bytes 1769480 | tf_op jit(solution)/shard_map/ppermute | solution.py:38
  78.5 18.5 %collective-permute-start.23 = (bf16[128,1536]{1,0:T(8,128)(2,1)S(1)}, bf16[128,1536]{1,0:T(8,128)(2,1)S(1)}, u32[]{:S(2)}, u32[]{:S(2)}) collective-permute-start(bf16[128,1536]{1,0:T(8,128)(2,1)S(1)} %get-tuple-element.88), channel_id=1, source_target_pairs={{0,64},{32,96},{64,0},{96,32},{1,65},{33,97},{65,1},{97,33},{2,66}... | collective-permute-start | bytes 1179656 | tf_op jit(solution)/shard_map/ppermute | solution.py:42
  78.6 20.5 %collective-permute-start.24 = (bf16[128,1536]{1,0:T(8,128)(2,1)S(1)}, bf16[128,1536]{1,0:T(8,128)(2,1)S(1)}, u32[]{:S(2)}, u32[]{:S(2)}) collective-permute-start(bf16[128,1536]{1,0:T(8,128)(2,1)S(1)} %get-tuple-element.87), channel_id=1, source_target_pairs={{0,32},{32,64},{64,96},{96,0},{1,33},{33,65},{65,97},{97,1},{2,34}... | collective-permute-start | bytes 1179656 | tf_op jit(solution)/shard_map/ppermute | solution.py:42
  79.0 20.2 %collective-permute-start.25 = (bf16[128,1536]{1,0:T(8,128)(2,1)S(1)}, bf16[128,1536]{1,0:T(8,128)(2,1)S(1)}, u32[]{:S(2)}, u32[]{:S(2)}) collective-permute-start(bf16[128,1536]{1,0:T(8,128)(2,1)S(1)} %get-tuple-element.86), channel_id=1, source_target_pairs={{0,96},{32,0},{64,32},{96,64},{1,97},{33,1},{65,33},{97,65},{2,98}... | collective-permute-start | bytes 1179656 | tf_op jit(solution)/shard_map/ppermute | solution.py:42

commit v13 on v12

--- a/solution.py
+++ b/solution.py
@@ -239,7 +239,6 @@
     swap_a = swap(jnp.concatenate([hop_2, hop_4]), "c")
     other, hops, swap_a = tie(other, hops, swap_a)
     other = swap(other, "c")
-    other, hops = tie(other, hops)
     swap_b = swap(hops, "c")
     third = jnp.concatenate([up3[64:], down3[:64], last])
     left_c, right_c = along_x(third, 1), along_x(third, -1)

time: 100 us -> 97.2 us (0.972)
  starting transfers between devices: 42.4 us -> 40.6 us
  waiting for transfers between devices: 30.1 us -> 28.6 us
    ppermute x5, starting transfers between devices: 5.96 us -> 4.51 us  [along_y(): return lax.ppermute(a, 'y', [(i, (i + d) % Y) for i in range(Y)])]
    ppermute x6, waiting for transfers between devices: 11.7 us -> 10.4 us  [swap(): return lax.ppermute(a, axis, [(0, 1), (1, 0)])]
  transfers between devices with their start and end apart: 29 -> 29, of which waited for: 12 -> 12; matrix products, arithmetic and copies ran while one was open for 4% -> 4% of each run, Pallas kernels for 22% -> 23%
where the time goes in v13:
time: 97.2 us; the launch traced here: 97.1 us
  starting transfers between devices  40.6 us (42%)
  waiting for transfers between devices  28.6 us (29%)
  Pallas kernels  22.2 us (23%)
  other arithmetic  3.28 us (3%)
  local copies, waits for them, and re-layouts  1.33 us (1%)
  between operations  0.98 us (1%)
    ppermute x10, starting transfers between devices, along_z(): return lax.ppermute(a, 'z', [(i, (i + d) % Z) for i in range(Z)])  17.5 us
    pallas_call x2, Pallas kernels, weight_product(): pl.pallas_call(functools.partial(weight_kernel, layout), grid=(1536 // st...  15.5 us
    ppermute x6, waiting for transfers between devices, swap(): return lax.ppermute(a, axis, [(0, 1), (1, 0)])  10.4 us
    ppermute x7, waiting for transfers between devices, along_x(): lax.ppermute(a, ('xl', 'xh'), [(place(x), place((x + d) % 4)) for x in ra...  9.41 us
    ppermute x6, starting transfers between devices, swap(): return lax.ppermute(a, axis, [(0, 1), (1, 0)])  8.91 us
    ppermute x7, starting transfers between devices, along_x(): lax.ppermute(a, ('xl', 'xh'), [(place(x), place((x + d) % 4)) for x in ra...  8.68 us
    ppermute x10, waiting for transfers between devices, along_z(): return lax.ppermute(a, 'z', [(i, (i + d) % Z) for i in range(Z)])  6.54 us
    pallas_call x1, Pallas kernels, early_partial(): pl.pallas_call(early_kernel, grid=(1536 // step,), in_specs=[pl.BlockSpec...  4.75 us
  transfers between devices with their start and end apart: 29, of which 12 were waited for; matrix products, arithmetic and copies ran while one was open for 4% of the time, Pallas kernels for 23%

profile of v13, /device:TPU:1, one launch (start us, length us, event | category | flops | bytes accessed | tf_op | source)
XLA Modules:
  0.0 97.1 jit_solution(14099211084561639670)
XLA Ops:
  0.6 2.5 %collective-permute-start = (bf16[64,1536]{1,0:T(8,128)(2,1)}, bf16[64,1536]{1,0:T(8,128)(2,1)S(1)}, u32[]{:S(2)}, u32[]{:S(2)}) collective-permute-start(bf16[64,1536]{1,0:T(8,128)(2,1)} %param.4), channel_id=1, source_target_pairs={{0,1},{1,2},{2,3},{3,4},{4,5},{5,6},{6,7},{7,0},{8,9},{9,10},{10,1... | collective-permute-start | bytes 589832 | tf_op jit(solution)/shard_map/ppermute | solution.py:31
  3.2 4.0 %collective-permute-start.1 = (bf16[64,1536]{1,0:T(8,128)(2,1)}, bf16[64,1536]{1,0:T(8,128)(2,1)S(1)}, u32[]{:S(2)}, u32[]{:S(2)}) collective-permute-start(bf16[64,1536]{1,0:T(8,128)(2,1)} %param.4), channel_id=1, source_target_pairs={{0,7},{1,0},{2,1},{3,2},{4,3},{5,4},{6,5},{7,6},{8,15},{9,8},{10,9... | collective-permute-start | bytes 589832 | tf_op jit(solution)/shard_map/ppermute | solution.py:31
  7.2 2.7 %collective-permute-start.2 = (bf16[64,1536]{1,0:T(8,128)(2,1)}, bf16[64,1536]{1,0:T(8,128)(2,1)S(1)}, u32[]{:S(2)}, u32[]{:S(2)}) collective-permute-start(bf16[64,1536]{1,0:T(8,128)(2,1)} %param.4), channel_id=1, source_target_pairs={{0,8},{128,136},{8,0},{136,128},{1,9},{129,137},{9,1},{137,129},{2... | collective-permute-start | bytes 589832 | tf_op jit(solution)/shard_map/ppermute | solution.py:38
  9.9 1.5 %fusion.5 = (f32[128,1536]{1,0:T(8,128)S(1)}, bf16[128,1536]{1,0:T(8,128)(2,1)S(1)}) fusion(bf16[128,1536]{1,0:T(8,128)(2,1)} %param.3), kind=kLoop, calls=%fused_computation.13 | loop fusion | flops 3932160 | bytes 1572864 | tf_op jit(solution)/shard_map/add | solution.py:25
  11.5 1.3 %collective-permute-start.9 = (bf16[128,1536]{1,0:T(8,128)(2,1)S(1)}, bf16[128,1536]{1,0:T(8,128)(2,1)S(1)}, u32[]{:S(2)}, u32[]{:S(2)}) collective-permute-start(bf16[128,1536]{1,0:T(8,128)(2,1)S(1)} %get-tuple-element.47), channel_id=1, source_target_pairs={{0,16},{16,0},{1,17},{17,1},{2,18},{18,2},{3,19},{19,3},{4,20},{20... | collective-permute-start | bytes 1179656 | tf_op jit(solution)/shard_map/ppermute | solution.py:51
  12.8 2.9 %collective-permute-start.5 = (bf16[128,1536]{1,0:T(8,128)(2,1)S(1)}, bf16[128,1536]{1,0:T(8,128)(2,1)S(1)}, u32[]{:S(2)}, u32[]{:S(2)}) collective-permute-start(bf16[128,1536]{1,0:T(8,128)(2,1)S(1)} %get-tuple-element.47), channel_id=1, source_target_pairs={{0,64},{32,96},{64,0},{96,32},{1,65},{33,97},{65,1},{97,33},{2,66}... | collective-permute-start | bytes 1179656 | tf_op jit(solution)/shard_map/ppermute | solution.py:42
  17.3 2.7 %collective-permute-start.4 = (bf16[128,1536]{1,0:T(8,128)(2,1)S(1)}, bf16[128,1536]{1,0:T(8,128)(2,1)S(1)}, u32[]{:S(2)}, u32[]{:S(2)}) collective-permute-start(bf16[128,1536]{1,0:T(8,128)(2,1)S(1)} %get-tuple-element.107), channel_id=1, source_target_pairs={{0,7},{1,0},{2,1},{3,2},{4,3},{5,4},{6,5},{7,6},{8,15},{9,8},{10,9... | collective-permute-start | bytes 1179656 | tf_op jit(solution)/shard_map/ppermute | solution.py:31
  20.0 1.2 %collective-permute-start.10 = (bf16[192,1536]{1,0:T(8,128)(2,1)S(1)}, bf16[192,1536]{1,0:T(8,128)(2,1)S(1)}, u32[]{:S(2)}, u32[]{:S(2)}) collective-permute-start(bf16[192,1536]{1,0:T(8,128)(2,1)S(1)} %get-tuple-element.102), channel_id=1, source_target_pairs={{0,128},{128,8},{8,136},{136,0},{1,129},{129,9},{9,137},{137,1},{2... | collective-permute-start | bytes 1769480 | tf_op jit(solution)/shard_map/ppermute | solution.py:38
  21.2 5.9 %collective-permute-done.8 = bf16[128,1536]{1,0:T(8,128)(2,1)S(1)} collective-permute-done((bf16[128,1536]{1,0:T(8,128)(2,1)S(1)}, bf16[128,1536]{1,0:T(8,128)(2,1)S(1)}, u32[]{:S(2)}, u32[]{:S(2)}) %collective-permute-start.8) | collective-permute-done | bytes 393248 | tf_op jit(solution)/shard_map/ppermute | solution.py:51
  27.3 1.2 %collective-permute-done.3 = bf16[128,1536]{1,0:T(8,128)(2,1)S(1)} collective-permute-done((bf16[128,1536]{1,0:T(8,128)(2,1)S(1)}, bf16[128,1536]{1,0:T(8,128)(2,1)S(1)}, u32[]{:S(2)}, u32[]{:S(2)}) %collective-permute-start.3) | collective-permute-done | bytes 393248 | tf_op jit(solution)/shard_map/ppermute | solution.py:31
  28.5 2.7 %collective-permute-start.7 = (bf16[128,1536]{1,0:T(8,128)(2,1)S(1)}, bf16[128,1536]{1,0:T(8,128)(2,1)S(1)}, u32[]{:S(2)}, u32[]{:S(2)}) collective-permute-start(bf16[128,1536]{1,0:T(8,128)(2,1)S(1)} %collective-permute-done.4), channel_id=1, source_target_pairs={{0,7},{1,0},{2,1},{3,2},{4,3},{5,4},{6,5},{7,6},{8,15},{9,8},{10,9... | collective-permute-start | bytes 1179656 | tf_op jit(solution)/shard_map/ppermute | solution.py:31
  31.4 6.5 %collective-permute-done.10.refs_2_ = bf16[192,1536]{1,0:T(8,128)(2,1)S(1)} collective-permute-done((bf16[192,1536]{1,0:T(8,128)(2,1)S(1)}, bf16[192,1536]{1,0:T(8,128)(2,1)S(1)}, u32[]{:S(2)}, u32[]{:S(2)}) %collective-permute-start.10) | collective-permute-done | bytes 589856 | tf_op jit(solution)/shard_map/ppermute | solution.py:38
  37.9 2.9 %collective-permute-done.11.refs_3_ = bf16[192,1536]{1,0:T(8,128)(2,1)S(1)} collective-permute-done((bf16[192,1536]{1,0:T(8,128)(2,1)S(1)}, bf16[192,1536]{1,0:T(8,128)(2,1)S(1)}, u32[]{:S(2)}, u32[]{:S(2)}) %collective-permute-start.11) | collective-permute-done | bytes 589856 | tf_op jit(solution)/shard_map/ppermute | solution.py:38
  40.8 2.1 %collective-permute-start.12 = (bf16[128,1536]{1,0:T(8,128)(2,1)S(1)}, bf16[128,1536]{1,0:T(8,128)(2,1)S(1)}, u32[]{:S(2)}, u32[]{:S(2)}) collective-permute-start(bf16[128,1536]{1,0:T(8,128)(2,1)S(1)} %collective-permute-done.8), channel_id=1, source_target_pairs={{0,16},{16,0},{1,17},{17,1},{2,18},{18,2},{3,19},{19,3},{4,20},{20... | collective-permute-start | bytes 1179656 | tf_op jit(solution)/shard_map/ppermute | solution.py:51
  44.2 1.5 %collective-permute-start.19 = (bf16[128,1536]{1,0:T(8,128)(2,1)S(1)}, bf16[128,1536]{1,0:T(8,128)(2,1)S(1)}, u32[]{:S(2)}, u32[]{:S(2)}) collective-permute-start(bf16[128,1536]{1,0:T(8,128)(2,1)S(1)} %pad_maximum_fusion.7), channel_id=1, source_target_pairs={{0,136},{128,0},{8,128},{136,8},{1,137},{129,1},{9,129},{137,9},{2... | collective-permute-start | bytes 1179656 | tf_op jit(solution)/shard_map/ppermute | solution.py:38
  46.1 2.7 %collective-permute-start.15 = (bf16[96,1536]{1,0:T(8,128)(2,1)S(1)}, bf16[96,1536]{1,0:T(8,128)(2,1)S(1)}, u32[]{:S(2)}, u32[]{:S(2)}) collective-permute-start(bf16[96,1536]{1,0:T(8,128)(2,1)S(1)} %slice.77), channel_id=1, source_target_pairs={{0,7},{1,0},{2,1},{3,2},{4,3},{5,4},{6,5},{7,6},{8,15},{9,8},{10,9... | collective-permute-start | bytes 884744 | tf_op jit(solution)/shard_map/ppermute | solution.py:31
  49.2 1.0 %collective-permute-start.20 = (bf16[512,1536]{1,0:T(8,128)(2,1)S(1)}, bf16[512,1536]{1,0:T(8,128)(2,1)S(1)}, u32[]{:S(2)}, u32[]{:S(2)}) collective-permute-start(bf16[512,1536]{1,0:T(8,128)(2,1)S(1)} %pad_maximum_fusion), channel_id=1, source_target_pairs={{0,32},{16,112},{32,64},{48,16},{64,96},{80,48},{96,0},{112,80},{1... | collective-permute-start | bytes 4718600 | tf_op jit(solution)/shard_map/ppermute | solution.py:47
  50.2 4.8 %shard_map.50.early_ref = f32[768,1536]{1,0:T(8,128)S(1)} custom-call(bf16[768,1536]{1,0:T(8,128)(2,1)S(1)} %slice_dynamic-update-slice_fusion.2.grads_ref.refs_0_, bf16[1536,1536]{1,0:T(8,128)(2,1)S(1)} %bitcast.1), custom_call_target="tpu_custom_call" | custom-call | flops 3623878656 | bytes 12582912 | tf_op jit(solution)/shard_map/pallas_call | solution.py:73
  55.4 2.5 %collective-permute-start.17 = (bf16[32,1536]{1,0:T(8,128)(2,1)S(1)}, bf16[32,1536]{1,0:T(8,128)(2,1)S(1)}, u32[]{:S(2)}, u32[]{:S(2)}) collective-permute-start(bf16[32,1536]{1,0:T(8,128)(2,1)S(1)} %get-tuple-element.100), channel_id=1, source_target_pairs={{0,7},{1,0},{2,1},{3,2},{4,3},{5,4},{6,5},{7,6},{8,15},{9,8},{10,9... | collective-permute-start | bytes 294920 | tf_op jit(solution)/shard_map/ppermute | solution.py:31
  58.0 1.6 %collective-permute-done.17 = bf16[32,1536]{1,0:T(8,128)(2,1)S(1)} collective-permute-done((bf16[32,1536]{1,0:T(8,128)(2,1)S(1)}, bf16[32,1536]{1,0:T(8,128)(2,1)S(1)}, u32[]{:S(2)}, u32[]{:S(2)}) %collective-permute-start.17) | collective-permute-done | bytes 98336 | tf_op jit(solution)/shard_map/ppermute | solution.py:31
  59.6 3.3 %collective-permute-done.16 = bf16[32,1536]{1,0:T(8,128)(2,1)S(1)} collective-permute-done((bf16[32,1536]{1,0:T(8,128)(2,1)S(1)}, bf16[32,1536]{1,0:T(8,128)(2,1)S(1)}, u32[]{:S(2)}, u32[]{:S(2)}) %collective-permute-start.16) | collective-permute-done | bytes 98336 | tf_op jit(solution)/shard_map/ppermute | solution.py:31
  62.9 2.0 %shard_map.51 = (f32[512,1536]{1,0:T(8,128)S(1)}, bf16[512,1536]{1,0:T(8,128)(2,1)S(1)}) custom-call(f32[768,1536]{1,0:T(8,128)S(1)} %shard_map.50.early_ref, bf16[256,1536]{1,0:T(8,128)(2,1)S(1)} %constant_dynamic-update-slice_fusion.11.grads_ref.refs_1_, bf16[1536,1536]{1,0:T(8,128)(2,1)S(1)} %bitcast.1), custom_call_target="tpu_custom_call" | custom-call | flops 1207959552 | bytes 8388608 | tf_op jit(solution)/shard_map/pallas_call | solution.py:111
  65.0 2.9 %collective-permute-start.21 = (bf16[256,1536]{1,0:T(8,128)(2,1)S(1)}, bf16[256,1536]{1,0:T(8,128)(2,1)S(1)}, u32[]{:S(2)}, u32[]{:S(2)}) collective-permute-start(bf16[256,1536]{1,0:T(8,128)(2,1)S(1)} %pad_maximum_fusion.3), channel_id=1, source_target_pairs={{0,16},{16,0},{1,17},{17,1},{2,18},{18,2},{3,19},{19,3},{4,20},{20... | collective-permute-start | bytes 2359304 | tf_op jit(solution)/shard_map/ppermute | solution.py:51
  68.0 1.9 %collective-permute-done.21.refs_11_.refs_9_ = bf16[256,1536]{1,0:T(8,128)(2,1)S(1)} collective-permute-done((bf16[256,1536]{1,0:T(8,128)(2,1)S(1)}, bf16[256,1536]{1,0:T(8,128)(2,1)S(1)}, u32[]{:S(2)}, u32[]{:S(2)}) %collective-permute-start.21) | collective-permute-done | bytes 786464 | tf_op jit(solution)/shard_map/ppermute | solution.py:51
  69.9 2.1 %collective-permute-start.22 = (bf16[512,1536]{1,0:T(8,128)(2,1)S(1)}, bf16[512,1536]{1,0:T(8,128)(2,1)S(1)}, u32[]{:S(2)}, u32[]{:S(2)}) collective-permute-start(bf16[512,1536]{1,0:T(8,128)(2,1)S(1)} %get-tuple-element.69), channel_id=1, source_target_pairs={{0,16},{16,0},{1,17},{17,1},{2,18},{18,2},{3,19},{19,3},{4,20},{20... | collective-permute-start | bytes 4718600 | tf_op jit(solution)/shard_map/ppermute | solution.py:51
  72.2 2.6 %collective-permute-start.27 = (bf16[192,1536]{1,0:T(8,128)(2,1)S(1)}, bf16[192,1536]{1,0:T(8,128)(2,1)S(1)}, u32[]{:S(2)}, u32[]{:S(2)}) collective-permute-start(bf16[192,1536]{1,0:T(8,128)(2,1)S(1)} %pad_maximum_fusion.4), channel_id=1, source_target_pairs={{0,136},{128,0},{8,128},{136,8},{1,137},{129,1},{9,129},{137,9},{2... | collective-permute-start | bytes 1769480 | tf_op jit(solution)/shard_map/ppermute | solution.py:38
  75.8 1.5 %collective-permute-done.28.refs_8_.refs_6_ = bf16[512,1536]{1,0:T(8,128)(2,1)S(1)} collective-permute-done((bf16[512,1536]{1,0:T(8,128)(2,1)S(1)}, bf16[512,1536]{1,0:T(8,128)(2,1)S(1)}, u32[]{:S(2)}, u32[]{:S(2)}) %collective-permute-start.28) | collective-permute-done | bytes 1572896 | tf_op jit(solution)/shard_map/ppermute | solution.py:51
  77.3 1.0 collective-permute-start.25
  78.2 9.9 %shard_map.52.refs_10_ = f32[1536,1536]{1,0:T(8,128)S(1)} custom-call(bf16[768,1536]{1,0:T(8,128)(2,1)S(1)} %slice_dynamic-update-slice_fusion.2.grads_ref.refs_0_, bf16[256,1536]{1,0:T(8,128)(2,1)S(1)} %constant_dynamic-update-slice_fusion.11.grads_ref.refs_1_, bf16[192,1536]{1,0:T(8,128)(2,1)S(1)} %collective-permute-done.10.refs_2_, ...), custom_call_target="tpu_custom_call" | custom-call | flops 7247757312 | bytes 12582912 | tf_op jit(solution)/shard_map/pallas_call | solution.py:184
  88.2 5.6 %shard_map.53 = bf16[1536,1536]{1,0:T(8,128)(2,1)} custom-call(bf16[128,1536]{1,0:T(8,128)(2,1)S(1)} %collective-permute-done.19.refs_0_, bf16[192,1536]{1,0:T(8,128)(2,1)S(1)} %collective-permute-done.26.refs_1_, bf16[192,1536]{1,0:T(8,128)(2,1)S(1)} %collective-permute-done.27.refs_2_, bf16[256,1536]{1,0:T(8,128)(2,1)S(1)} %pad_maximum_fusion.1.refs_5_.refs_3_, ...), custom_call_target="tpu_custom_call" | custom-call | flops 2415919104 | bytes 12582912 | tf_op jit(solution)/shard_map/pallas_call | solution.py:184
  93.8 2.3 %collective-permute-done.24 = bf16[128,1536]{1,0:T(8,128)(2,1)S(1)} collective-permute-done((bf16[128,1536]{1,0:T(8,128)(2,1)S(1)}, bf16[128,1536]{1,0:T(8,128)(2,1)S(1)}, u32[]{:S(2)}, u32[]{:S(2)}) %collective-permute-start.24) | collective-permute-done | bytes 393248 | tf_op jit(solution)/shard_map/ppermute | solution.py:42
  96.0 1.0 %multiply_convert_fusion = bf16[128,1536]{1,0:T(8,128)(2,1)} fusion(f32[128,1536]{1,0:T(8,128)S(1)} %get-tuple-element.80, bf16[128,1536]{1,0:T(8,128)(2,1)S(1)} %collective-permute-done.23, bf16[128,1536]{1,0:T(8,128)(2,1)S(1)} %collective-permute-done.25, bf16[128,1536]{1,0:T(8,128)(2,1)S(1)} %collective-permute-done.24, ...), kind=kLoop, calls=%fused_computation.20 | loop fusion | flops 1966080 | bytes 3538944 | tf_op jit(solution)/shard_map/convert_element_type | solution.py:258
  (66 shorter events, 5.6 us)
Async XLA Ops:
  0.6 16.1 %collective-permute-start = (bf16[64,1536]{1,0:T(8,128)(2,1)}, bf16[64,1536]{1,0:T(8,128)(2,1)S(1)}, u32[]{:S(2)}, u32[]{:S(2)}) collective-permute-start(bf16[64,1536]{1,0:T(8,128)(2,1)} %param.4), channel_id=1, source_target_pairs={{0,1},{1,2},{2,3},{3,4},{4,5},{5,6},{6,7},{7,0},{8,9},{9,10},{10,1... | collective-permute-start | bytes 589832 | tf_op jit(solution)/shard_map/ppermute | solution.py:31
  3.2 13.5 %collective-permute-start.1 = (bf16[64,1536]{1,0:T(8,128)(2,1)}, bf16[64,1536]{1,0:T(8,128)(2,1)S(1)}, u32[]{:S(2)}, u32[]{:S(2)}) collective-permute-start(bf16[64,1536]{1,0:T(8,128)(2,1)} %param.4), channel_id=1, source_target_pairs={{0,7},{1,0},{2,1},{3,2},{4,3},{5,4},{6,5},{7,6},{8,15},{9,8},{10,9... | collective-permute-start | bytes 589832 | tf_op jit(solution)/shard_map/ppermute | solution.py:31
  7.2 9.5 %collective-permute-start.2 = (bf16[64,1536]{1,0:T(8,128)(2,1)}, bf16[64,1536]{1,0:T(8,128)(2,1)S(1)}, u32[]{:S(2)}, u32[]{:S(2)}) collective-permute-start(bf16[64,1536]{1,0:T(8,128)(2,1)} %param.4), channel_id=1, source_target_pairs={{0,8},{128,136},{8,0},{136,128},{1,9},{129,137},{9,1},{137,129},{2... | collective-permute-start | bytes 589832 | tf_op jit(solution)/shard_map/ppermute | solution.py:38
  11.5 8.5 %collective-permute-start.9 = (bf16[128,1536]{1,0:T(8,128)(2,1)S(1)}, bf16[128,1536]{1,0:T(8,128)(2,1)S(1)}, u32[]{:S(2)}, u32[]{:S(2)}) collective-permute-start(bf16[128,1536]{1,0:T(8,128)(2,1)S(1)} %get-tuple-element.47), channel_id=1, source_target_pairs={{0,16},{16,0},{1,17},{17,1},{2,18},{18,2},{3,19},{19,3},{4,20},{20... | collective-permute-start | bytes 1179656 | tf_op jit(solution)/shard_map/ppermute | solution.py:51
  12.8 14.5 %collective-permute-start.5 = (bf16[128,1536]{1,0:T(8,128)(2,1)S(1)}, bf16[128,1536]{1,0:T(8,128)(2,1)S(1)}, u32[]{:S(2)}, u32[]{:S(2)}) collective-permute-start(bf16[128,1536]{1,0:T(8,128)(2,1)S(1)} %get-tuple-element.47), channel_id=1, source_target_pairs={{0,64},{32,96},{64,0},{96,32},{1,65},{33,97},{65,1},{97,33},{2,66}... | collective-permute-start | bytes 1179656 | tf_op jit(solution)/shard_map/ppermute | solution.py:42
  16.7 10.4 %collective-permute-start.8 = (bf16[128,1536]{1,0:T(8,128)(2,1)S(1)}, bf16[128,1536]{1,0:T(8,128)(2,1)S(1)}, u32[]{:S(2)}, u32[]{:S(2)}) collective-permute-start(bf16[128,1536]{1,0:T(8,128)(2,1)S(1)} %get-tuple-element.47), channel_id=1, source_target_pairs={{0,128},{128,0},{1,129},{129,1},{2,130},{130,2},{3,131},{131,3},{4... | collective-permute-start | bytes 1179656 | tf_op jit(solution)/shard_map/ppermute | solution.py:51
  17.1 33.0 %slice-start = ((s8[4718592]{0:T(1024)(128)(4,1)}), s8[4194304]{0:T(1024)(128)(4,1)S(1)}, s32[]{:S(2)}) async-start(s8[4718592]{0:T(1024)(128)(4,1)} %bitcast), calls=%async_computation | async-start | bytes 8388608
  17.2 11.3 %collective-permute-start.3 = (bf16[128,1536]{1,0:T(8,128)(2,1)S(1)}, bf16[128,1536]{1,0:T(8,128)(2,1)S(1)}, u32[]{:S(2)}, u32[]{:S(2)}) collective-permute-start(bf16[128,1536]{1,0:T(8,128)(2,1)S(1)} %get-tuple-element.108), channel_id=1, source_target_pairs={{0,1},{1,2},{2,3},{3,4},{4,5},{5,6},{6,7},{7,0},{8,9},{9,10},{10,1... | collective-permute-start | bytes 1179656 | tf_op jit(solution)/shard_map/ppermute | solution.py:31
  17.3 11.2 %collective-permute-start.4 = (bf16[128,1536]{1,0:T(8,128)(2,1)S(1)}, bf16[128,1536]{1,0:T(8,128)(2,1)S(1)}, u32[]{:S(2)}, u32[]{:S(2)}) collective-permute-start(bf16[128,1536]{1,0:T(8,128)(2,1)S(1)} %get-tuple-element.107), channel_id=1, source_target_pairs={{0,7},{1,0},{2,1},{3,2},{4,3},{5,4},{6,5},{7,6},{8,15},{9,8},{10,9... | collective-permute-start | bytes 1179656 | tf_op jit(solution)/shard_map/ppermute | solution.py:31
  20.0 17.9 %collective-permute-start.10 = (bf16[192,1536]{1,0:T(8,128)(2,1)S(1)}, bf16[192,1536]{1,0:T(8,128)(2,1)S(1)}, u32[]{:S(2)}, u32[]{:S(2)}) collective-permute-start(bf16[192,1536]{1,0:T(8,128)(2,1)S(1)} %get-tuple-element.102), channel_id=1, source_target_pairs={{0,128},{128,8},{8,136},{136,0},{1,129},{129,9},{9,137},{137,1},{2... | collective-permute-start | bytes 1769480 | tf_op jit(solution)/shard_map/ppermute | solution.py:38
  27.1 13.6 %collective-permute-start.11 = (bf16[192,1536]{1,0:T(8,128)(2,1)S(1)}, bf16[192,1536]{1,0:T(8,128)(2,1)S(1)}, u32[]{:S(2)}, u32[]{:S(2)}) collective-permute-start(bf16[192,1536]{1,0:T(8,128)(2,1)S(1)} %get-tuple-element.102), channel_id=1, source_target_pairs={{0,136},{128,0},{8,128},{136,8},{1,137},{129,1},{9,129},{137,9},{2... | collective-permute-start | bytes 1769480 | tf_op jit(solution)/shard_map/ppermute | solution.py:38
  28.5 17.3 %collective-permute-start.6 = (bf16[128,1536]{1,0:T(8,128)(2,1)S(1)}, bf16[128,1536]{1,0:T(8,128)(2,1)S(1)}, u32[]{:S(2)}, u32[]{:S(2)}) collective-permute-start(bf16[128,1536]{1,0:T(8,128)(2,1)S(1)} %collective-permute-done.3), channel_id=1, source_target_pairs={{0,1},{1,2},{2,3},{3,4},{4,5},{5,6},{6,7},{7,0},{8,9},{9,10},{10,1... | collective-permute-start | bytes 1179656 | tf_op jit(solution)/shard_map/ppermute | solution.py:31
  28.5 17.3 %collective-permute-start.7 = (bf16[128,1536]{1,0:T(8,128)(2,1)S(1)}, bf16[128,1536]{1,0:T(8,128)(2,1)S(1)}, u32[]{:S(2)}, u32[]{:S(2)}) collective-permute-start(bf16[128,1536]{1,0:T(8,128)(2,1)S(1)} %collective-permute-done.4), channel_id=1, source_target_pairs={{0,7},{1,0},{2,1},{3,2},{4,3},{5,4},{6,5},{7,6},{8,15},{9,8},{10,9... | collective-permute-start | bytes 1179656 | tf_op jit(solution)/shard_map/ppermute | solution.py:31
  31.2 14.6 %collective-permute-start.13 = (bf16[128,1536]{1,0:T(8,128)(2,1)S(1)}, bf16[128,1536]{1,0:T(8,128)(2,1)S(1)}, u32[]{:S(2)}, u32[]{:S(2)}) collective-permute-start(bf16[128,1536]{1,0:T(8,128)(2,1)S(1)} %collective-permute-done.8), channel_id=1, source_target_pairs={{0,64},{32,96},{64,0},{96,32},{1,65},{33,97},{65,1},{97,33},{2,66}... | collective-permute-start | bytes 1179656 | tf_op jit(solution)/shard_map/ppermute | solution.py:42
  40.8 3.5 %collective-permute-start.12 = (bf16[128,1536]{1,0:T(8,128)(2,1)S(1)}, bf16[128,1536]{1,0:T(8,128)(2,1)S(1)}, u32[]{:S(2)}, u32[]{:S(2)}) collective-permute-start(bf16[128,1536]{1,0:T(8,128)(2,1)S(1)} %collective-permute-done.8), channel_id=1, source_target_pairs={{0,16},{16,0},{1,17},{17,1},{2,18},{18,2},{3,19},{19,3},{4,20},{20... | collective-permute-start | bytes 1179656 | tf_op jit(solution)/shard_map/ppermute | solution.py:51
  43.0 7.2 %slice-start.1 = ((s8[4718592]{0:T(1024)(128)(4,1)}), s8[524288]{0:T(1024)(128)(4,1)S(1)}, s32[]{:S(2)}) async-start(s8[4718592]{0:T(1024)(128)(4,1)} %bitcast), calls=%async_computation.1 | async-start | bytes 1048576
  43.0 15.0 %collective-permute-start.18 = (bf16[128,1536]{1,0:T(8,128)(2,1)S(1)}, bf16[128,1536]{1,0:T(8,128)(2,1)S(1)}, u32[]{:S(2)}, u32[]{:S(2)}) collective-permute-start(bf16[128,1536]{1,0:T(8,128)(2,1)S(1)} %pad_maximum_fusion.7), channel_id=1, source_target_pairs={{0,128},{128,8},{8,136},{136,0},{1,129},{129,9},{9,137},{137,1},{2... | collective-permute-start | bytes 1179656 | tf_op jit(solution)/shard_map/ppermute | solution.py:38
  44.2 13.7 %collective-permute-start.19 = (bf16[128,1536]{1,0:T(8,128)(2,1)S(1)}, bf16[128,1536]{1,0:T(8,128)(2,1)S(1)}, u32[]{:S(2)}, u32[]{:S(2)}) collective-permute-start(bf16[128,1536]{1,0:T(8,128)(2,1)S(1)} %pad_maximum_fusion.7), channel_id=1, source_target_pairs={{0,136},{128,0},{8,128},{136,8},{1,137},{129,1},{9,129},{137,9},{2... | collective-permute-start | bytes 1179656 | tf_op jit(solution)/shard_map/ppermute | solution.py:38
  45.8 9.5 %collective-permute-start.14 = (bf16[96,1536]{1,0:T(8,128)(2,1)S(1)}, bf16[96,1536]{1,0:T(8,128)(2,1)S(1)}, u32[]{:S(2)}, u32[]{:S(2)}) collective-permute-start(bf16[96,1536]{1,0:T(8,128)(2,1)S(1)} %slice.76), channel_id=1, source_target_pairs={{0,1},{1,2},{2,3},{3,4},{4,5},{5,6},{6,7},{7,0},{8,9},{9,10},{10,1... | collective-permute-start | bytes 884744 | tf_op jit(solution)/shard_map/ppermute | solution.py:31
  46.1 9.2 %collective-permute-start.15 = (bf16[96,1536]{1,0:T(8,128)(2,1)S(1)}, bf16[96,1536]{1,0:T(8,128)(2,1)S(1)}, u32[]{:S(2)}, u32[]{:S(2)}) collective-permute-start(bf16[96,1536]{1,0:T(8,128)(2,1)S(1)} %slice.77), channel_id=1, source_target_pairs={{0,7},{1,0},{2,1},{3,2},{4,3},{5,4},{6,5},{7,6},{8,15},{9,8},{10,9... | collective-permute-start | bytes 884744 | tf_op jit(solution)/shard_map/ppermute | solution.py:31
  49.2 20.7 %collective-permute-start.20 = (bf16[512,1536]{1,0:T(8,128)(2,1)S(1)}, bf16[512,1536]{1,0:T(8,128)(2,1)S(1)}, u32[]{:S(2)}, u32[]{:S(2)}) collective-permute-start(bf16[512,1536]{1,0:T(8,128)(2,1)S(1)} %pad_maximum_fusion), channel_id=1, source_target_pairs={{0,32},{16,112},{32,64},{48,16},{64,96},{80,48},{96,0},{112,80},{1... | collective-permute-start | bytes 4718600 | tf_op jit(solution)/shard_map/ppermute | solution.py:47
  55.4 4.2 %collective-permute-start.17 = (bf16[32,1536]{1,0:T(8,128)(2,1)S(1)}, bf16[32,1536]{1,0:T(8,128)(2,1)S(1)}, u32[]{:S(2)}, u32[]{:S(2)}) collective-permute-start(bf16[32,1536]{1,0:T(8,128)(2,1)S(1)} %get-tuple-element.100), channel_id=1, source_target_pairs={{0,7},{1,0},{2,1},{3,2},{4,3},{5,4},{6,5},{7,6},{8,15},{9,8},{10,9... | collective-permute-start | bytes 294920 | tf_op jit(solution)/shard_map/ppermute | solution.py:31
  57.9 5.0 %collective-permute-start.16 = (bf16[32,1536]{1,0:T(8,128)(2,1)S(1)}, bf16[32,1536]{1,0:T(8,128)(2,1)S(1)}, u32[]{:S(2)}, u32[]{:S(2)}) collective-permute-start(bf16[32,1536]{1,0:T(8,128)(2,1)S(1)} %get-tuple-element.97), channel_id=1, source_target_pairs={{0,1},{1,2},{2,3},{3,4},{4,5},{5,6},{6,7},{7,0},{8,9},{9,10},{10,1... | collective-permute-start | bytes 294920 | tf_op jit(solution)/shard_map/ppermute | solution.py:31
  65.0 4.9 %collective-permute-start.21 = (bf16[256,1536]{1,0:T(8,128)(2,1)S(1)}, bf16[256,1536]{1,0:T(8,128)(2,1)S(1)}, u32[]{:S(2)}, u32[]{:S(2)}) collective-permute-start(bf16[256,1536]{1,0:T(8,128)(2,1)S(1)} %pad_maximum_fusion.3), channel_id=1, source_target_pairs={{0,16},{16,0},{1,17},{17,1},{2,18},{18,2},{3,19},{19,3},{4,20},{20... | collective-permute-start | bytes 2359304 | tf_op jit(solution)/shard_map/ppermute | solution.py:51
  69.9 5.2 %collective-permute-start.22 = (bf16[512,1536]{1,0:T(8,128)(2,1)S(1)}, bf16[512,1536]{1,0:T(8,128)(2,1)S(1)}, u32[]{:S(2)}, u32[]{:S(2)}) collective-permute-start(bf16[512,1536]{1,0:T(8,128)(2,1)S(1)} %get-tuple-element.69), channel_id=1, source_target_pairs={{0,16},{16,0},{1,17},{17,1},{2,18},{18,2},{3,19},{19,3},{4,20},{20... | collective-permute-start | bytes 4718600 | tf_op jit(solution)/shard_map/ppermute | solution.py:51
  72.0 5.3 %collective-permute-start.28 = (bf16[512,1536]{1,0:T(8,128)(2,1)S(1)}, bf16[512,1536]{1,0:T(8,128)(2,1)S(1)}, u32[]{:S(2)}, u32[]{:S(2)}) collective-permute-start(bf16[512,1536]{1,0:T(8,128)(2,1)S(1)} %collective-permute-done.20.refs_7_.refs_5_), channel_id=1, source_target_pairs={{0,16},{16,0},{1,17},{17,1},{2,18},{18,2},{3,19},{19,3},{4,20},{20... | collective-permute-start | bytes 4718600 | tf_op jit(solution)/shard_map/ppermute | solution.py:51
  72.0 16.1 %collective-permute-start.26 = (bf16[192,1536]{1,0:T(8,128)(2,1)S(1)}, bf16[192,1536]{1,0:T(8,128)(2,1)S(1)}, u32[]{:S(2)}, u32[]{:S(2)}) collective-permute-start(bf16[192,1536]{1,0:T(8,128)(2,1)S(1)} %pad_maximum_fusion.4), channel_id=1, source_target_pairs={{0,128},{128,8},{8,136},{136,0},{1,129},{129,9},{9,137},{137,1},{2... | collective-permute-start | bytes 1769480 | tf_op jit(solution)/shard_map/ppermute | solution.py:38
  72.2 16.0 %collective-permute-start.27 = (bf16[192,1536]{1,0:T(8,128)(2,1)S(1)}, bf16[192,1536]{1,0:T(8,128)(2,1)S(1)}, u32[]{:S(2)}, u32[]{:S(2)}) collective-permute-start(bf16[192,1536]{1,0:T(8,128)(2,1)S(1)} %pad_maximum_fusion.4), channel_id=1, source_target_pairs={{0,136},{128,0},{8,128},{136,8},{1,137},{129,1},{9,129},{137,9},{2... | collective-permute-start | bytes 1769480 | tf_op jit(solution)/shard_map/ppermute | solution.py:38
  75.4 18.4 %collective-permute-start.23 = (bf16[128,1536]{1,0:T(8,128)(2,1)S(1)}, bf16[128,1536]{1,0:T(8,128)(2,1)S(1)}, u32[]{:S(2)}, u32[]{:S(2)}) collective-permute-start(bf16[128,1536]{1,0:T(8,128)(2,1)S(1)} %get-tuple-element.84), channel_id=1, source_target_pairs={{0,64},{32,96},{64,0},{96,32},{1,65},{33,97},{65,1},{97,33},{2,66}... | collective-permute-start | bytes 1179656 | tf_op jit(solution)/shard_map/ppermute | solution.py:42
  75.5 20.5 %collective-permute-start.24 = (bf16[128,1536]{1,0:T(8,128)(2,1)S(1)}, bf16[128,1536]{1,0:T(8,128)(2,1)S(1)}, u32[]{:S(2)}, u32[]{:S(2)}) collective-permute-start(bf16[128,1536]{1,0:T(8,128)(2,1)S(1)} %get-tuple-element.83), channel_id=1, source_target_pairs={{0,32},{32,64},{64,96},{96,0},{1,33},{33,65},{65,97},{97,1},{2,34}... | collective-permute-start | bytes 1179656 | tf_op jit(solution)/shard_map/ppermute | solution.py:42
  77.3 18.7 %collective-permute-start.25 = (bf16[128,1536]{1,0:T(8,128)(2,1)S(1)}, bf16[128,1536]{1,0:T(8,128)(2,1)S(1)}, u32[]{:S(2)}, u32[]{:S(2)}) collective-permute-start(bf16[128,1536]{1,0:T(8,128)(2,1)S(1)} %get-tuple-element.82), channel_id=1, source_target_pairs={{0,96},{32,0},{64,32},{96,64},{1,97},{33,1},{65,33},{97,65},{2,98}... | collective-permute-start | bytes 1179656 | tf_op jit(solution)/shard_map/ppermute | solution.py:42
